TPU v7x, 32 devices: a whole 2x2x4 slice. The times are simulated.
32 devices in a mesh: dp: 8 (over y, x, core), section: 4 (over z).
Axes of the slice: x: 2, y: 2, z: 4, core: 2. Of those that a mesh axis runs over, the one named last changes fastest.
Arguments:
- inputs: bfloat16 [1024, 3072], P('dp'), may hold values from -6 to 6
- tiles: bfloat16 [4, 72, 128, 128], P('section'), may hold values from -0.3125 to 0.3125
- tile_rows: int32 [4, 72], P('section'), may hold values from 0 to 23, as said below
- out_grad: bfloat16 [1024, 3072], P('dp'), may hold values from -0.119628906 to 0.119628906
Outputs:
- weight_grad: float32 [128, 4, 72, 128], P('dp', 'section')
Inputs may be any that keep to these rules, and one draw needn't show every extreme that they name: `tile_rows`: in each layer, the 3 entries of every aligned group of 3 consecutive tiles (one tile column) name different tile rows.
All inputs are finite; a program needn't handle non-finite values.
Results may differ from a plain program's by a relative error of at most 0.025.
Values may be sent and summed in bfloat16 or wider, within the bound.
No kernel may reach another device: no remote copies, remote signals or barrier semaphores. Data moves between devices by JAX's collectives and lax.ppermute only.
A program may use at most 64 MiB of HBM per device.

v0:
```python
import jax
import jax.numpy as jnp
from jax import lax
from jax.sharding import PartitionSpec as P

NMB = 4


EPS = 1e-06


def from_behind(array, axis, by):
    peers = lax.axis_size(axis)
    pairs = [(i, i + by) for i in range(peers) if 0 <= i + by < peers]
    return lax.ppermute(array, axis, pairs)


def row_scale(h):
    hf = h.astype(jnp.float32)
    return (hf, lax.rsqrt(jnp.mean(hf * hf, axis=1, keepdims=True) + EPS))


def layer_forward(h, tile_set, rows, nb, kpc):
    count = h.shape[0]
    blk = tile_set.shape[-1]
    hf, scale = row_scale(h)
    low = (hf * scale).astype(jnp.bfloat16)
    picked = jnp.take(low.reshape(count, nb, blk), rows, axis=1).reshape(count, nb, kpc, blk)
    mixed = jnp.einsum(
        "mnkr,nkrc->mnc",
        picked,
        tile_set.reshape(nb, kpc, blk, blk),
        preferred_element_type=jnp.float32,
    ).reshape(count, nb * blk)
    act = jnp.tanh(mixed)
    out = (hf + act).astype(jnp.bfloat16)
    return (out, act)


def layer_backward(h, act, grad, tile_set, rows, nb, kpc):
    count = h.shape[0]
    blk = tile_set.shape[-1]
    hf, scale = row_scale(h)
    gradf = grad.astype(jnp.float32)
    dz = (gradf * (1.0 - act * act)).astype(jnp.bfloat16)
    back = jnp.einsum(
        "mnc,nkrc->mnkr",
        dz.reshape(count, nb, blk),
        tile_set.reshape(nb, kpc, blk, blk),
        preferred_element_type=jnp.float32,
    )
    onehot = (rows[:, None] == jnp.arange(nb, dtype=jnp.int32)[None, :]).astype(jnp.float32)
    spread = jnp.einsum(
        "mtr,tb->mbr", back.reshape(count, nb * kpc, blk), onehot, precision=lax.Precision.HIGHEST
    ).reshape(count, nb * blk)
    normed = hf * scale
    inner = jnp.mean(spread * normed, axis=1, keepdims=True)
    result = gradf + scale * (spread - normed * inner)
    return (dz, result.astype(jnp.bfloat16))


def local(inputs, tiles, tile_rows, out_grad):
    sections = lax.axis_size("section")
    section = lax.axis_index("section")
    tile_set = tiles[0]
    rows = tile_rows[0]
    blk = tiles.shape[-1]
    width = inputs.shape[1]
    nb = width // blk
    kpc = tiles.shape[1] // nb
    total = inputs.shape[0]
    groups = NMB
    group_rows = total // groups
    feed = inputs.reshape(groups, group_rows, width)
    seeds = out_grad.reshape(groups, group_rows, width)
    saved_h = jnp.zeros((groups, group_rows, width), jnp.bfloat16)
    saved_act = jnp.zeros((groups, group_rows, width), jnp.float32)
    blank = jnp.zeros((group_rows, width), jnp.bfloat16)

    def forward_step(step, carry):
        incoming, keep_h, keep_act = carry
        slot = step - section
        live = jnp.logical_and(slot >= 0, slot < groups)
        index = jnp.clip(slot, 0, groups - 1)
        start_h = jnp.where(section == 0, feed[index], incoming)

        def forward_work(state):
            store_h, store_act = state
            out, act = layer_forward(start_h, tile_set, rows, nb, kpc)
            store_h = lax.dynamic_update_index_in_dim(store_h, start_h, index, 0)
            store_act = lax.dynamic_update_index_in_dim(store_act, act, index, 0)
            return (out, store_h, store_act)

        def forward_skip(state):
            return (blank,) + state

        out, keep_h, keep_act = lax.cond(live, forward_work, forward_skip, (keep_h, keep_act))
        incoming = from_behind(out, "section", 1)
        return (incoming, keep_h, keep_act)

    unused, saved_h, saved_act = lax.fori_loop(
        0, sections + groups - 1, forward_step, (blank, saved_h, saved_act)
    )
    saved_dz = jnp.zeros((groups, group_rows, width), jnp.bfloat16)

    def backward_step(step, carry):
        incoming, keep_dz = carry
        slot = step - (sections - 1 - section)
        live = jnp.logical_and(slot >= 0, slot < groups)
        index = jnp.clip(slot, 0, groups - 1)
        grad_in = jnp.where(section == sections - 1, seeds[index], incoming)

        def backward_work(store_dz):
            dz, current = layer_backward(
                saved_h[index], saved_act[index], grad_in, tile_set, rows, nb, kpc
            )
            store_dz = lax.dynamic_update_index_in_dim(store_dz, dz, index, 0)
            return (current, store_dz)

        def backward_skip(store_dz):
            return (blank, store_dz)

        out, keep_dz = lax.cond(live, backward_work, backward_skip, keep_dz)
        incoming = from_behind(out, "section", -1)
        return (incoming, keep_dz)

    unused, saved_dz = lax.fori_loop(0, sections + groups - 1, backward_step, (blank, saved_dz))
    flat_h = saved_h.reshape(total, width)
    hf, scale = row_scale(flat_h)
    low = (hf * scale).astype(jnp.bfloat16)
    picked = jnp.take(low.reshape(total, nb, blk), rows, axis=1).reshape(total, nb, kpc, blk)
    dz_all = saved_dz.reshape(total, nb, blk)
    term = jnp.einsum("mnkr,mnc->rnkc", picked, dz_all, preferred_element_type=jnp.float32)
    term = term.reshape(blk, 1, nb * kpc, blk)
    return lax.psum_scatter(term, "dp", scatter_dimension=0, tiled=True)


def solution(mesh):
    return jax.shard_map(
        local,
        mesh=mesh,
        in_specs=(P("dp", None), P("section", None, None, None), P("section", None), P("dp", None)),
        out_specs=P("dp", "section", None, None),
        check_vma=False,
    )
```

profile of v0, /device:TPU:0, one launch (start us, length us, event | category | flops | bytes accessed | tf_op | source)
XLA Modules:
  0.0 282.2 jit_solution(3219409569776310578)
XLA Ops:
  10.3 1.3 broadcast_in_dim.60
  11.6 84.2 %while.38 = (s32[]{:T(128)}, bf16[32,3072]{1,0:T(8,128)(2,1)S(1)}, bf16[4,32,3072]{2,1,0:T(8,128)(2,1)}, f32[4,32,3072]{2,1,0:T(8,128)}, s32[]{:T(128)}, /*index...) while((s32[]{:T(128)}, bf16[32,3072]{1,0:T(8,128)(2,1)S(1)}, ...), condition=%wide.region_4.5_spmd, body=%wide.region_0.4_spmd.sunk | while | flops 76777136 | bytes 9837579 | solution.py:101
  11.6 5.2 %conditional.4 = (bf16[32,3072]{1,0:T(8,128)(2,1)}, bf16[4,32,3072]{2,1,0:T(8,128)(2,1)}, f32[4,32,3072]{2,1,0:T(8,128)}) conditional(s32[]{:T(128)} %convert_element_type.140, (bf16[4,32,3072]{2,1,0:T(8,128)(2,1)}, f32[4,32,3072]{2,1,0:T(8,128)}) %tuple.106, (pred[]{:T(512)}, s32[]{:T(128)}, bf16[4,32,3072]{2,1,0:T(8,128)(2,1)}, ...), branch_computations={%region_1.1_spmd, %region_2.3_spmd} | conditional | flops 76777128 | bytes 9050872 | solution.py:97
  11.8 1.7 bitcast_dynamic-update-slice_fusion.1
  18.1 5.3 %collective-permute-done = bf16[32,3072]{1,0:T(8,128)(2,1)S(1)} collective-permute-done((bf16[32,3072]{1,0:T(8,128)(2,1)}, bf16[32,3072]{1,0:T(8,128)(2,1)S(1)}, u32[]{:S(2)}, u32[]{:S(2)}) %collective-permute-start) | collective-permute-done | bytes 196640 | tf_op jit(solution)/shard_map/while/body/eval_jaxpr/ppermute | solution.py:15
  23.4 5.2 %conditional.4 = (bf16[32,3072]{1,0:T(8,128)(2,1)}, bf16[4,32,3072]{2,1,0:T(8,128)(2,1)}, f32[4,32,3072]{2,1,0:T(8,128)}) conditional(s32[]{:T(128)} %convert_element_type.140, (bf16[4,32,3072]{2,1,0:T(8,128)(2,1)}, f32[4,32,3072]{2,1,0:T(8,128)}) %tuple.106, (pred[]{:T(512)}, s32[]{:T(128)}, bf16[4,32,3072]{2,1,0:T(8,128)(2,1)}, ...), branch_computations={%region_1.1_spmd, %region_2.3_spmd} | conditional | flops 76777128 | bytes 9050872 | solution.py:97
  23.6 1.7 bitcast_dynamic-update-slice_fusion.1
  28.6 4.3 %collective-permute-start = (bf16[32,3072]{1,0:T(8,128)(2,1)}, bf16[32,3072]{1,0:T(8,128)(2,1)S(1)}, u32[]{:S(2)}, u32[]{:S(2)}) collective-permute-start(bf16[32,3072]{1,0:T(8,128)(2,1)} %get-tuple-element.762), channel_id=1, source_target_pairs={{0,1},{1,2},{2,3},{4,5},{5,6},{6,7},{8,9},{9,10},{10,11},{12,13},{... | collective-permute-start | bytes 589832 | tf_op jit(solution)/shard_map/while/body/eval_jaxpr/ppermute | solution.py:15
  32.9 4.5 %collective-permute-done = bf16[32,3072]{1,0:T(8,128)(2,1)S(1)} collective-permute-done((bf16[32,3072]{1,0:T(8,128)(2,1)}, bf16[32,3072]{1,0:T(8,128)(2,1)S(1)}, u32[]{:S(2)}, u32[]{:S(2)}) %collective-permute-start) | collective-permute-done | bytes 196640 | tf_op jit(solution)/shard_map/while/body/eval_jaxpr/ppermute | solution.py:15
  37.3 5.1 %conditional.4 = (bf16[32,3072]{1,0:T(8,128)(2,1)}, bf16[4,32,3072]{2,1,0:T(8,128)(2,1)}, f32[4,32,3072]{2,1,0:T(8,128)}) conditional(s32[]{:T(128)} %convert_element_type.140, (bf16[4,32,3072]{2,1,0:T(8,128)(2,1)}, f32[4,32,3072]{2,1,0:T(8,128)}) %tuple.106, (pred[]{:T(512)}, s32[]{:T(128)}, bf16[4,32,3072]{2,1,0:T(8,128)(2,1)}, ...), branch_computations={%region_1.1_spmd, %region_2.3_spmd} | conditional | flops 76777128 | bytes 9050872 | solution.py:97
  37.5 1.7 bitcast_dynamic-update-slice_fusion.1
  42.5 4.3 %collective-permute-start = (bf16[32,3072]{1,0:T(8,128)(2,1)}, bf16[32,3072]{1,0:T(8,128)(2,1)S(1)}, u32[]{:S(2)}, u32[]{:S(2)}) collective-permute-start(bf16[32,3072]{1,0:T(8,128)(2,1)} %get-tuple-element.762), channel_id=1, source_target_pairs={{0,1},{1,2},{2,3},{4,5},{5,6},{6,7},{8,9},{9,10},{10,11},{12,13},{... | collective-permute-start | bytes 589832 | tf_op jit(solution)/shard_map/while/body/eval_jaxpr/ppermute | solution.py:15
  46.8 3.6 %collective-permute-done = bf16[32,3072]{1,0:T(8,128)(2,1)S(1)} collective-permute-done((bf16[32,3072]{1,0:T(8,128)(2,1)}, bf16[32,3072]{1,0:T(8,128)(2,1)S(1)}, u32[]{:S(2)}, u32[]{:S(2)}) %collective-permute-start) | collective-permute-done | bytes 196640 | tf_op jit(solution)/shard_map/while/body/eval_jaxpr/ppermute | solution.py:15
  50.4 5.2 %conditional.4 = (bf16[32,3072]{1,0:T(8,128)(2,1)}, bf16[4,32,3072]{2,1,0:T(8,128)(2,1)}, f32[4,32,3072]{2,1,0:T(8,128)}) conditional(s32[]{:T(128)} %convert_element_type.140, (bf16[4,32,3072]{2,1,0:T(8,128)(2,1)}, f32[4,32,3072]{2,1,0:T(8,128)}) %tuple.106, (pred[]{:T(512)}, s32[]{:T(128)}, bf16[4,32,3072]{2,1,0:T(8,128)(2,1)}, ...), branch_computations={%region_1.1_spmd, %region_2.3_spmd} | conditional | flops 76777128 | bytes 9050872 | solution.py:97
  50.5 1.7 bitcast_dynamic-update-slice_fusion.1
  55.6 4.2 %collective-permute-start = (bf16[32,3072]{1,0:T(8,128)(2,1)}, bf16[32,3072]{1,0:T(8,128)(2,1)S(1)}, u32[]{:S(2)}, u32[]{:S(2)}) collective-permute-start(bf16[32,3072]{1,0:T(8,128)(2,1)} %get-tuple-element.762), channel_id=1, source_target_pairs={{0,1},{1,2},{2,3},{4,5},{5,6},{6,7},{8,9},{9,10},{10,11},{12,13},{... | collective-permute-start | bytes 589832 | tf_op jit(solution)/shard_map/while/body/eval_jaxpr/ppermute | solution.py:15
  59.8 3.5 %collective-permute-done = bf16[32,3072]{1,0:T(8,128)(2,1)S(1)} collective-permute-done((bf16[32,3072]{1,0:T(8,128)(2,1)}, bf16[32,3072]{1,0:T(8,128)(2,1)S(1)}, u32[]{:S(2)}, u32[]{:S(2)}) %collective-permute-start) | collective-permute-done | bytes 196640 | tf_op jit(solution)/shard_map/while/body/eval_jaxpr/ppermute | solution.py:15
  64.0 8.8 %collective-permute-start = (bf16[32,3072]{1,0:T(8,128)(2,1)}, bf16[32,3072]{1,0:T(8,128)(2,1)S(1)}, u32[]{:S(2)}, u32[]{:S(2)}) collective-permute-start(bf16[32,3072]{1,0:T(8,128)(2,1)} %get-tuple-element.762), channel_id=1, source_target_pairs={{0,1},{1,2},{2,3},{4,5},{5,6},{6,7},{8,9},{9,10},{10,11},{12,13},{... | collective-permute-start | bytes 589832 | tf_op jit(solution)/shard_map/while/body/eval_jaxpr/ppermute | solution.py:15
  72.8 3.5 %collective-permute-done = bf16[32,3072]{1,0:T(8,128)(2,1)S(1)} collective-permute-done((bf16[32,3072]{1,0:T(8,128)(2,1)}, bf16[32,3072]{1,0:T(8,128)(2,1)S(1)}, u32[]{:S(2)}, u32[]{:S(2)}) %collective-permute-start) | collective-permute-done | bytes 196640 | tf_op jit(solution)/shard_map/while/body/eval_jaxpr/ppermute | solution.py:15
  76.9 4.3 %collective-permute-start = (bf16[32,3072]{1,0:T(8,128)(2,1)}, bf16[32,3072]{1,0:T(8,128)(2,1)S(1)}, u32[]{:S(2)}, u32[]{:S(2)}) collective-permute-start(bf16[32,3072]{1,0:T(8,128)(2,1)} %get-tuple-element.762), channel_id=1, source_target_pairs={{0,1},{1,2},{2,3},{4,5},{5,6},{6,7},{8,9},{9,10},{10,11},{12,13},{... | collective-permute-start | bytes 589832 | tf_op jit(solution)/shard_map/while/body/eval_jaxpr/ppermute | solution.py:15
  81.2 3.5 %collective-permute-done = bf16[32,3072]{1,0:T(8,128)(2,1)S(1)} collective-permute-done((bf16[32,3072]{1,0:T(8,128)(2,1)}, bf16[32,3072]{1,0:T(8,128)(2,1)S(1)}, u32[]{:S(2)}, u32[]{:S(2)}) %collective-permute-start) | collective-permute-done | bytes 196640 | tf_op jit(solution)/shard_map/while/body/eval_jaxpr/ppermute | solution.py:15
  85.4 7.0 %collective-permute-start = (bf16[32,3072]{1,0:T(8,128)(2,1)}, bf16[32,3072]{1,0:T(8,128)(2,1)S(1)}, u32[]{:S(2)}, u32[]{:S(2)}) collective-permute-start(bf16[32,3072]{1,0:T(8,128)(2,1)} %get-tuple-element.762), channel_id=1, source_target_pairs={{0,1},{1,2},{2,3},{4,5},{5,6},{6,7},{8,9},{9,10},{10,11},{12,13},{... | collective-permute-start | bytes 589832 | tf_op jit(solution)/shard_map/while/body/eval_jaxpr/ppermute | solution.py:15
  92.4 3.5 %collective-permute-done = bf16[32,3072]{1,0:T(8,128)(2,1)S(1)} collective-permute-done((bf16[32,3072]{1,0:T(8,128)(2,1)}, bf16[32,3072]{1,0:T(8,128)(2,1)S(1)}, u32[]{:S(2)}, u32[]{:S(2)}) %collective-permute-start) | collective-permute-done | bytes 196640 | tf_op jit(solution)/shard_map/while/body/eval_jaxpr/ppermute | solution.py:15
  95.8 1.4 multiply_reduce_fusion
  98.3 108.1 %while.39 = (s32[]{:T(128)}, bf16[32,3072]{1,0:T(8,128)(2,1)S(1)}, bf16[4,32,3072]{2,1,0:T(8,128)(2,1)}, s32[]{:T(128)}, pred[]{:T(512)}, /*index=5*/bf16[4,32,3...) while((s32[]{:T(128)}, bf16[32,3072]{1,0:T(8,128)(2,1)S(1)}, ...), condition=%wide.region_10.11_spmd, body=%wide.region_5.10_spmd.sunk | while | flops 162596576 | bytes 10815724 | solution.py:127
  99.6 6.6 %collective-permute-done.1 = bf16[32,3072]{1,0:T(8,128)(2,1)S(1)} collective-permute-done((bf16[32,3072]{1,0:T(8,128)(2,1)S(1)}, bf16[32,3072]{1,0:T(8,128)(2,1)S(1)}, u32[]{:S(2)}, u32[]{:S(2)}) %collective-permute-start.1) | collective-permute-done | bytes 196640 | tf_op jit(solution)/shard_map/while/body/eval_jaxpr/ppermute | solution.py:15
  107.6 9.0 %collective-permute-done.1 = bf16[32,3072]{1,0:T(8,128)(2,1)S(1)} collective-permute-done((bf16[32,3072]{1,0:T(8,128)(2,1)S(1)}, bf16[32,3072]{1,0:T(8,128)(2,1)S(1)}, u32[]{:S(2)}, u32[]{:S(2)}) %collective-permute-start.1) | collective-permute-done | bytes 196640 | tf_op jit(solution)/shard_map/while/body/eval_jaxpr/ppermute | solution.py:15
  117.9 28.3 %collective-permute-done.1 = bf16[32,3072]{1,0:T(8,128)(2,1)S(1)} collective-permute-done((bf16[32,3072]{1,0:T(8,128)(2,1)S(1)}, bf16[32,3072]{1,0:T(8,128)(2,1)S(1)}, u32[]{:S(2)}, u32[]{:S(2)}) %collective-permute-start.1) | collective-permute-done | bytes 196640 | tf_op jit(solution)/shard_map/while/body/eval_jaxpr/ppermute | solution.py:15
  146.2 7.4 %conditional.5 = (bf16[32,3072]{1,0:T(8,128)(2,1)S(1)}, bf16[4,32,3072]{2,1,0:T(8,128)(2,1)}) conditional(s32[]{:T(128)} %convert_element_type.141, bf16[4,32,3072]{2,1,0:T(8,128)(2,1)} %get-tuple-element.838, (pred[]{:T(512)}, s32[]{:T(128)}, bf16[4,32,3072]{2,1,0:T(8,128)(2,1)S(1)}, bf16[32,3072]{1,0:T(8,128)(2,1)S(1)}, ...), branch_computations={%region_6.6_spmd, %region_7.9_spmd} | conditional | flops 162596576 | bytes 10029017 | solution.py:123
  148.2 1.8 bitcast_dynamic-update-slice_fusion
  151.0 1.5 fusion.11
  154.9 6.3 %collective-permute-done.1 = bf16[32,3072]{1,0:T(8,128)(2,1)S(1)} collective-permute-done((bf16[32,3072]{1,0:T(8,128)(2,1)S(1)}, bf16[32,3072]{1,0:T(8,128)(2,1)S(1)}, u32[]{:S(2)}, u32[]{:S(2)}) %collective-permute-start.1) | collective-permute-done | bytes 196640 | tf_op jit(solution)/shard_map/while/body/eval_jaxpr/ppermute | solution.py:15
  161.2 7.4 %conditional.5 = (bf16[32,3072]{1,0:T(8,128)(2,1)S(1)}, bf16[4,32,3072]{2,1,0:T(8,128)(2,1)}) conditional(s32[]{:T(128)} %convert_element_type.141, bf16[4,32,3072]{2,1,0:T(8,128)(2,1)} %get-tuple-element.838, (pred[]{:T(512)}, s32[]{:T(128)}, bf16[4,32,3072]{2,1,0:T(8,128)(2,1)S(1)}, bf16[32,3072]{1,0:T(8,128)(2,1)S(1)}, ...), branch_computations={%region_6.6_spmd, %region_7.9_spmd} | conditional | flops 162596576 | bytes 10029017 | solution.py:123
  163.2 1.8 bitcast_dynamic-update-slice_fusion
  166.0 1.5 fusion.11
  170.0 6.3 %collective-permute-done.1 = bf16[32,3072]{1,0:T(8,128)(2,1)S(1)} collective-permute-done((bf16[32,3072]{1,0:T(8,128)(2,1)S(1)}, bf16[32,3072]{1,0:T(8,128)(2,1)S(1)}, u32[]{:S(2)}, u32[]{:S(2)}) %collective-permute-start.1) | collective-permute-done | bytes 196640 | tf_op jit(solution)/shard_map/while/body/eval_jaxpr/ppermute | solution.py:15
  176.2 7.4 %conditional.5 = (bf16[32,3072]{1,0:T(8,128)(2,1)S(1)}, bf16[4,32,3072]{2,1,0:T(8,128)(2,1)}) conditional(s32[]{:T(128)} %convert_element_type.141, bf16[4,32,3072]{2,1,0:T(8,128)(2,1)} %get-tuple-element.838, (pred[]{:T(512)}, s32[]{:T(128)}, bf16[4,32,3072]{2,1,0:T(8,128)(2,1)S(1)}, bf16[32,3072]{1,0:T(8,128)(2,1)S(1)}, ...), branch_computations={%region_6.6_spmd, %region_7.9_spmd} | conditional | flops 162596576 | bytes 10029017 | solution.py:123
  178.3 1.8 bitcast_dynamic-update-slice_fusion
  181.1 1.5 fusion.11
  185.0 6.3 %collective-permute-done.1 = bf16[32,3072]{1,0:T(8,128)(2,1)S(1)} collective-permute-done((bf16[32,3072]{1,0:T(8,128)(2,1)S(1)}, bf16[32,3072]{1,0:T(8,128)(2,1)S(1)}, u32[]{:S(2)}, u32[]{:S(2)}) %collective-permute-start.1) | collective-permute-done | bytes 196640 | tf_op jit(solution)/shard_map/while/body/eval_jaxpr/ppermute | solution.py:15
  191.3 7.5 %conditional.5 = (bf16[32,3072]{1,0:T(8,128)(2,1)S(1)}, bf16[4,32,3072]{2,1,0:T(8,128)(2,1)}) conditional(s32[]{:T(128)} %convert_element_type.141, bf16[4,32,3072]{2,1,0:T(8,128)(2,1)} %get-tuple-element.838, (pred[]{:T(512)}, s32[]{:T(128)}, bf16[4,32,3072]{2,1,0:T(8,128)(2,1)S(1)}, bf16[32,3072]{1,0:T(8,128)(2,1)S(1)}, ...), branch_computations={%region_6.6_spmd, %region_7.9_spmd} | conditional | flops 162596576 | bytes 10029017 | solution.py:123
  193.4 1.8 bitcast_dynamic-update-slice_fusion
  196.2 1.5 fusion.11
  200.1 6.3 %collective-permute-done.1 = bf16[32,3072]{1,0:T(8,128)(2,1)S(1)} collective-permute-done((bf16[32,3072]{1,0:T(8,128)(2,1)S(1)}, bf16[32,3072]{1,0:T(8,128)(2,1)S(1)}, u32[]{:S(2)}, u32[]{:S(2)}) %collective-permute-start.1) | collective-permute-done | bytes 196640 | tf_op jit(solution)/shard_map/while/body/eval_jaxpr/ppermute | solution.py:15
  209.5 2.5 gather_fusion.1
  211.9 4.6 %fusion.26 = f32[24,128,3,128]{3,1,2,0:T(8,128)} fusion(bf16[128,24,3,128]{3,0,2,1:T(8,128)(2,1)} %bitcast.114, pred[24,3]{1,0:T(8,128)(4,1)S(1)} %compare_and_fusion.1, bf16[128,24,128,1]{2,1,0,3:T(8,128)(2,1)S(1)} %bitcast.117), kind=kOutput, calls=%fused_computation.49 | convolution fusion | flops 303169536 | bytes 7864392 | tf_op jit(solution)/shard_map/mnkr,mnc->rnkc/dot_general | solution.py:133
  216.5 6.1 %copy.24 = f32[128,1,72,128]{3,2,1,0:T(8,128)} copy(f32[128,1,72,128]{0,3,2,1:T(8,128)} %bitcast.113) | data formatting | bytes 9437184 | tf_op jit(solution)/shard_map/reshape | solution.py:134
  222.7 52.7 %reduce-scatter.2.cloned.1.call-done = f32[16,1,72,128]{3,2,1,0:T(8,128)} async-done(((f32[128,1,72,128]{3,2,1,0:T(8,128)}), f32[16,1,72,128]{3,2,1,0:T(8,128)}) %reduce-scatter.2.cloned.1.call-update) | async-done | bytes 589840 | tf_op jit(solution)/shard_map/reduce_scatter | solution.py:135
  (127 shorter events, 53.0 us)
Async XLA Ops:
  6.5 5.1 %copy-start.2 = (s32[1,72]{1,0:T(1,128)S(1)}, s32[1,72]{1,0:T(1,128)}, u32[]{:S(2)}) copy-start(s32[1,72]{1,0:T(1,128)} %param.14) | copy-start | bytes 868
  6.5 5.1 %copy-start = (bf16[1,72,128,128]{3,2,1,0:T(8,128)(2,1)S(1)}, bf16[1,72,128,128]{3,2,1,0:T(8,128)(2,1)}, u32[]{:S(2)}) copy-start(bf16[1,72,128,128]{3,2,1,0:T(8,128)(2,1)} %param.13) | copy-start | bytes 7077892
  6.5 268.9 %reduce-scatter.2.cloned.1.call-start = ((), (), s32[]{:S(2)}) async-start(), calls=%async_computation.1 | async-start | bytes 5308416 | tf_op jit(solution)/shard_map/reduce_scatter | solution.py:135
  16.8 6.6 %collective-permute-start = (bf16[32,3072]{1,0:T(8,128)(2,1)}, bf16[32,3072]{1,0:T(8,128)(2,1)S(1)}, u32[]{:S(2)}, u32[]{:S(2)}) collective-permute-start(bf16[32,3072]{1,0:T(8,128)(2,1)} %get-tuple-element.762), channel_id=1, source_target_pairs={{0,1},{1,2},{2,3},{4,5},{5,6},{6,7},{8,9},{9,10},{10,11},{12,13},{... | collective-permute-start | bytes 589832 | tf_op jit(solution)/shard_map/while/body/eval_jaxpr/ppermute | solution.py:15
  28.6 8.8 %collective-permute-start = (bf16[32,3072]{1,0:T(8,128)(2,1)}, bf16[32,3072]{1,0:T(8,128)(2,1)S(1)}, u32[]{:S(2)}, u32[]{:S(2)}) collective-permute-start(bf16[32,3072]{1,0:T(8,128)(2,1)} %get-tuple-element.762), channel_id=1, source_target_pairs={{0,1},{1,2},{2,3},{4,5},{5,6},{6,7},{8,9},{9,10},{10,11},{12,13},{... | collective-permute-start | bytes 589832 | tf_op jit(solution)/shard_map/while/body/eval_jaxpr/ppermute | solution.py:15
  42.5 7.9 %collective-permute-start = (bf16[32,3072]{1,0:T(8,128)(2,1)}, bf16[32,3072]{1,0:T(8,128)(2,1)S(1)}, u32[]{:S(2)}, u32[]{:S(2)}) collective-permute-start(bf16[32,3072]{1,0:T(8,128)(2,1)} %get-tuple-element.762), channel_id=1, source_target_pairs={{0,1},{1,2},{2,3},{4,5},{5,6},{6,7},{8,9},{9,10},{10,11},{12,13},{... | collective-permute-start | bytes 589832 | tf_op jit(solution)/shard_map/while/body/eval_jaxpr/ppermute | solution.py:15
  55.6 7.7 %collective-permute-start = (bf16[32,3072]{1,0:T(8,128)(2,1)}, bf16[32,3072]{1,0:T(8,128)(2,1)S(1)}, u32[]{:S(2)}, u32[]{:S(2)}) collective-permute-start(bf16[32,3072]{1,0:T(8,128)(2,1)} %get-tuple-element.762), channel_id=1, source_target_pairs={{0,1},{1,2},{2,3},{4,5},{5,6},{6,7},{8,9},{9,10},{10,11},{12,13},{... | collective-permute-start | bytes 589832 | tf_op jit(solution)/shard_map/while/body/eval_jaxpr/ppermute | solution.py:15
  64.0 12.3 %collective-permute-start = (bf16[32,3072]{1,0:T(8,128)(2,1)}, bf16[32,3072]{1,0:T(8,128)(2,1)S(1)}, u32[]{:S(2)}, u32[]{:S(2)}) collective-permute-start(bf16[32,3072]{1,0:T(8,128)(2,1)} %get-tuple-element.762), channel_id=1, source_target_pairs={{0,1},{1,2},{2,3},{4,5},{5,6},{6,7},{8,9},{9,10},{10,11},{12,13},{... | collective-permute-start | bytes 589832 | tf_op jit(solution)/shard_map/while/body/eval_jaxpr/ppermute | solution.py:15
  76.9 7.8 %collective-permute-start = (bf16[32,3072]{1,0:T(8,128)(2,1)}, bf16[32,3072]{1,0:T(8,128)(2,1)S(1)}, u32[]{:S(2)}, u32[]{:S(2)}) collective-permute-start(bf16[32,3072]{1,0:T(8,128)(2,1)} %get-tuple-element.762), channel_id=1, source_target_pairs={{0,1},{1,2},{2,3},{4,5},{5,6},{6,7},{8,9},{9,10},{10,11},{12,13},{... | collective-permute-start | bytes 589832 | tf_op jit(solution)/shard_map/while/body/eval_jaxpr/ppermute | solution.py:15
  85.4 10.4 %collective-permute-start = (bf16[32,3072]{1,0:T(8,128)(2,1)}, bf16[32,3072]{1,0:T(8,128)(2,1)S(1)}, u32[]{:S(2)}, u32[]{:S(2)}) collective-permute-start(bf16[32,3072]{1,0:T(8,128)(2,1)} %get-tuple-element.762), channel_id=1, source_target_pairs={{0,1},{1,2},{2,3},{4,5},{5,6},{6,7},{8,9},{9,10},{10,11},{12,13},{... | collective-permute-start | bytes 589832 | tf_op jit(solution)/shard_map/while/body/eval_jaxpr/ppermute | solution.py:15
  95.8 2.4 copy-start.1
  98.3 7.9 %collective-permute-start.1 = (bf16[32,3072]{1,0:T(8,128)(2,1)S(1)}, bf16[32,3072]{1,0:T(8,128)(2,1)S(1)}, u32[]{:S(2)}, u32[]{:S(2)}) collective-permute-start(bf16[32,3072]{1,0:T(8,128)(2,1)S(1)} %get-tuple-element.775), channel_id=1, source_target_pairs={{1,0},{2,1},{3,2},{5,4},{6,5},{7,6},{9,8},{10,9},{11,10},{13,12},{... | collective-permute-start | bytes 589832 | tf_op jit(solution)/shard_map/while/body/eval_jaxpr/ppermute | solution.py:15
  106.3 10.3 %collective-permute-start.1 = (bf16[32,3072]{1,0:T(8,128)(2,1)S(1)}, bf16[32,3072]{1,0:T(8,128)(2,1)S(1)}, u32[]{:S(2)}, u32[]{:S(2)}) collective-permute-start(bf16[32,3072]{1,0:T(8,128)(2,1)S(1)} %get-tuple-element.775), channel_id=1, source_target_pairs={{1,0},{2,1},{3,2},{5,4},{6,5},{7,6},{9,8},{10,9},{11,10},{13,12},{... | collective-permute-start | bytes 589832 | tf_op jit(solution)/shard_map/while/body/eval_jaxpr/ppermute | solution.py:15
  116.6 29.6 %collective-permute-start.1 = (bf16[32,3072]{1,0:T(8,128)(2,1)S(1)}, bf16[32,3072]{1,0:T(8,128)(2,1)S(1)}, u32[]{:S(2)}, u32[]{:S(2)}) collective-permute-start(bf16[32,3072]{1,0:T(8,128)(2,1)S(1)} %get-tuple-element.775), channel_id=1, source_target_pairs={{1,0},{2,1},{3,2},{5,4},{6,5},{7,6},{9,8},{10,9},{11,10},{13,12},{... | collective-permute-start | bytes 589832 | tf_op jit(solution)/shard_map/while/body/eval_jaxpr/ppermute | solution.py:15
  153.6 7.6 %collective-permute-start.1 = (bf16[32,3072]{1,0:T(8,128)(2,1)S(1)}, bf16[32,3072]{1,0:T(8,128)(2,1)S(1)}, u32[]{:S(2)}, u32[]{:S(2)}) collective-permute-start(bf16[32,3072]{1,0:T(8,128)(2,1)S(1)} %get-tuple-element.775), channel_id=1, source_target_pairs={{1,0},{2,1},{3,2},{5,4},{6,5},{7,6},{9,8},{10,9},{11,10},{13,12},{... | collective-permute-start | bytes 589832 | tf_op jit(solution)/shard_map/while/body/eval_jaxpr/ppermute | solution.py:15
  168.6 7.6 %collective-permute-start.1 = (bf16[32,3072]{1,0:T(8,128)(2,1)S(1)}, bf16[32,3072]{1,0:T(8,128)(2,1)S(1)}, u32[]{:S(2)}, u32[]{:S(2)}) collective-permute-start(bf16[32,3072]{1,0:T(8,128)(2,1)S(1)} %get-tuple-element.775), channel_id=1, source_target_pairs={{1,0},{2,1},{3,2},{5,4},{6,5},{7,6},{9,8},{10,9},{11,10},{13,12},{... | collective-permute-start | bytes 589832 | tf_op jit(solution)/shard_map/while/body/eval_jaxpr/ppermute | solution.py:15
  183.7 7.6 %collective-permute-start.1 = (bf16[32,3072]{1,0:T(8,128)(2,1)S(1)}, bf16[32,3072]{1,0:T(8,128)(2,1)S(1)}, u32[]{:S(2)}, u32[]{:S(2)}) collective-permute-start(bf16[32,3072]{1,0:T(8,128)(2,1)S(1)} %get-tuple-element.775), channel_id=1, source_target_pairs={{1,0},{2,1},{3,2},{5,4},{6,5},{7,6},{9,8},{10,9},{11,10},{13,12},{... | collective-permute-start | bytes 589832 | tf_op jit(solution)/shard_map/while/body/eval_jaxpr/ppermute | solution.py:15
  198.8 7.6 %collective-permute-start.1 = (bf16[32,3072]{1,0:T(8,128)(2,1)S(1)}, bf16[32,3072]{1,0:T(8,128)(2,1)S(1)}, u32[]{:S(2)}, u32[]{:S(2)}) collective-permute-start(bf16[32,3072]{1,0:T(8,128)(2,1)S(1)} %get-tuple-element.775), channel_id=1, source_target_pairs={{1,0},{2,1},{3,2},{5,4},{6,5},{7,6},{9,8},{10,9},{11,10},{13,12},{... | collective-permute-start | bytes 589832 | tf_op jit(solution)/shard_map/while/body/eval_jaxpr/ppermute | solution.py:15
Sparse Core Ops, SparseCore 0:
  222.8 52.5 reduce-scatter.1
where the time goes:
time: 283 us; the launch traced here: 282 us
  waiting for transfers between devices  149 us (53%)
  starting transfers between devices  43.1 us (15%)
  other arithmetic  34.5 us (12%)
  local copies, waits for them, and re-layouts  25 us (9%)
  matrix products  16.5 us (6%)
  between operations  13.5 us (5%)
    ppermute x14, waiting for transfers between devices, from_behind(): return lax.ppermute(array, axis, pairs)  96.3 us
    reduce_scatter x1, waiting for transfers between devices, local(): return lax.psum_scatter(term, 'dp', scatter_dimension=0, tiled=True)  52.7 us
    ppermute x14, starting transfers between devices, from_behind(): return lax.ppermute(array, axis, pairs)  43.1 us
    dynamic_update_slice x4, other arithmetic, backward_work(): store_dz = lax.dynamic_update_index_in_dim(store_dz, dz, index, 0)  7.06 us
    dynamic_update_slice x4, other arithmetic, forward_work(): store_h = lax.dynamic_update_index_in_dim(store_h, start_h, index, 0)  6.65 us
    reduce_sum x9, other arithmetic, row_scale(): return (hf, lax.rsqrt(jnp.mean(hf * hf, axis=1, keepdims=True) + EPS))  6.36 us
    reshape x1, local copies, waits for them, and re-layouts, local(): term = term.reshape(blk, 1, nb * kpc, blk)  6.08 us
    dot_general x4, matrix products, layer_backward(): jnp.einsum('mtr,tb->mbr', back.reshape(count, nb * kpc, blk), onehot, pre...  5.83 us
  transfers between devices with their start and end apart: 15, of which 15 were waited for; matrix products, arithmetic and copies ran while one was open for 0% of the time, Pallas kernels for 0%

commit v1 on v0

v1 whole, which is shorter than its diff:
```python
import functools

import jax
import jax.numpy as jnp
from jax import lax
from jax.experimental import pallas as pl
from jax.experimental.pallas import tpu as pltpu
from jax.sharding import PartitionSpec as P

NMB = 4
EPS = 1e-06
F32 = jnp.float32
BF16 = jnp.bfloat16
VM = pltpu.VMEM
ANY = pl.ANY
LIMIT = 24 * 1024 * 1024


def in_vmem(array):
    return pltpu.with_memory_space_constraint(array, pltpu.VMEM)


def call(body, outs, ins, scratch=(), aliases=None, flops=10**8, nbytes=3 * 10**6):
    arrays, in_specs = [], []
    for array, space in ins:
        arrays.append(in_vmem(array) if space is VM else array)
        in_specs.append(pl.BlockSpec(memory_space=space))
    out_shape, out_specs = [], []
    for shape, dtype, space in outs:
        out_shape.append(VM(shape, dtype) if space is VM else jax.ShapeDtypeStruct(shape, dtype))
        out_specs.append(pl.BlockSpec(memory_space=space))
    return pl.pallas_call(
        body,
        out_shape=out_shape,
        in_specs=in_specs,
        out_specs=out_specs,
        scratch_shapes=list(scratch),
        input_output_aliases=aliases or {},
        compiler_params=pltpu.CompilerParams(vmem_limit_bytes=LIMIT),
        cost_estimate=pl.CostEstimate(flops=flops, bytes_accessed=nbytes, transcendentals=0),
    )(*arrays)


def columns(n, blk):
    return slice(n * blk, (n + 1) * blk)


def init_body(tiles, tiles_v, keep_h, keep_d, keep_z, sem):
    copy = pltpu.make_async_copy(tiles.at[0], tiles_v, sem)
    copy.start()
    copy.wait()


def norm(hf):
    return lax.rsqrt(jnp.mean(hf * hf, axis=1, keepdims=True) + EPS)


def run_forward(rows, tiles, h, u3, put, nb, kpc, blk):
    hf = h[...].astype(F32)
    scale = norm(hf)
    for n in range(nb):
        u3[n] = (hf[:, columns(n, blk)] * scale).astype(BF16)
    for n in range(nb):
        x = jnp.concatenate([u3[rows[0, n * kpc + k]] for k in range(kpc)], axis=1)
        w = tiles[n * kpc : (n + 1) * kpc].reshape(kpc * blk, blk)
        a = jnp.tanh(jnp.dot(x, w, preferred_element_type=F32))
        put(n, hf[:, columns(n, blk)], a)


def run_backward(rows, tiles, h, dz, gradf, v3, put, nb, kpc, blk):
    v3[...] = jnp.zeros_like(v3)
    for n in range(nb):
        w = tiles[n * kpc : (n + 1) * kpc].reshape(kpc * blk, blk)
        back = lax.dot_general(
            dz[:, columns(n, blk)], w, (((1,), (1,)), ((), ())), preferred_element_type=F32
        )
        for k in range(kpc):
            r = rows[0, n * kpc + k]
            v3[r] = v3[r] + back[:, columns(k, blk)]
    hf = h[...].astype(F32)
    scale = norm(hf)
    width = nb * blk
    total = jnp.zeros((hf.shape[0], blk), F32)
    for n in range(nb):
        total = total + v3[n] * (hf[:, columns(n, blk)] * scale)
    inner = jnp.sum(total, axis=1, keepdims=True) * (1.0 / width)
    for n in range(nb):
        q = hf[:, columns(n, blk)] * scale
        put(n, gradf(n) + scale * (v3[n] - q * inner))


def forward_body(s, m, nb, kpc, blk, from_feed, rows, tiles, hin, kh_in, kd_in, hout, kh, kd, u3, obuf, sems):
    @pl.when(lax.axis_index("section") == s)
    def _():
        R = obuf.shape[0]
        src = hin.at[pl.ds(m * R, R)] if from_feed else hin
        load = pltpu.make_async_copy(src, kh.at[m], sems.at[0])
        load.start()
        load.wait()

        def put(n, hblk, a):
            obuf[:, columns(n, blk)] = (hblk + a).astype(BF16)
            kd[m, :, columns(n, blk)] = 1.0 - a * a

        run_forward(rows, tiles, kh.at[m], u3, put, nb, kpc, blk)
        store = pltpu.make_async_copy(obuf, hout, sems.at[1])
        store.start()
        store.wait()


def backward_steps(m, nb, kpc, blk, rows, tiles, g, kh, kd, kz, v3, obuf, gout, sem):
    for n in range(nb):
        c = columns(n, blk)
        kz[m, :, c] = (g[:, c].astype(F32) * kd[m, :, c]).astype(BF16)

    def put(n, block):
        obuf[:, columns(n, blk)] = block.astype(BF16)

    run_backward(
        rows, tiles, kh.at[m], kz.at[m], lambda n: g[:, columns(n, blk)].astype(F32), v3, put, nb, kpc, blk
    )
    store = pltpu.make_async_copy(obuf, gout, sem)
    store.start()
    store.wait()


def turn_body(s, m, nb, kpc, blk, from_feed, rows, tiles, hin, seeds, kh_in, kd_in, kz_in, gout, kh, kd, kz, u3, v3, g, obuf, sems):
    @pl.when(lax.axis_index("section") == s)
    def _():
        R = obuf.shape[0]
        src = hin.at[pl.ds(m * R, R)] if from_feed else hin
        load = pltpu.make_async_copy(src, kh.at[m], sems.at[0])
        load.start()
        seed = pltpu.make_async_copy(seeds.at[pl.ds(m * R, R)], g, sems.at[1])
        seed.start()
        load.wait()

        def put(n, hblk, a):
            kd[m, :, columns(n, blk)] = 1.0 - a * a

        run_forward(rows, tiles, kh.at[m], u3, put, nb, kpc, blk)
        seed.wait()
        backward_steps(m, nb, kpc, blk, rows, tiles, g, kh, kd, kz, v3, obuf, gout, sems.at[2])


def backward_body(s, m, nb, kpc, blk, rows, tiles, gin, kh, kd, kz_in, gout, kz, v3, g, obuf, sems):
    @pl.when(lax.axis_index("section") == s)
    def _():
        load = pltpu.make_async_copy(gin, g, sems.at[0])
        load.start()
        load.wait()
        backward_steps(m, nb, kpc, blk, rows, tiles, g, kh, kd, kz, v3, obuf, gout, sems.at[1])


def first_body(m, nb, blk, gin, kd, kz_in, kz, g, sems):
    @pl.when(lax.axis_index("section") == 0)
    def _():
        load = pltpu.make_async_copy(gin, g, sems.at[0])
        load.start()
        load.wait()
        for n in range(nb):
            c = columns(n, blk)
            kz[m, :, c] = (g[:, c].astype(F32) * kd[m, :, c]).astype(BF16)


def term_body(nb, kpc, blk, half, rows, kh, kz, keep, send, uT, zb, kbuf, sbuf, sems):
    M, R, E = kh.shape
    total = M * R
    hf = kh[...].reshape(total, E).astype(F32)
    scale = norm(hf)
    for n in range(nb):
        u = hf[:, columns(n, blk)] * scale
        uT[n] = u.astype(BF16).astype(F32).T.astype(BF16)
    me = lax.axis_index("dp") % 2
    parts = blk // half

    for n in range(nb):
        z = kz[:, :, columns(n, blk)].reshape(total, blk)
        for k in range(kpc):
            t = n * kpc + k
            term = jnp.dot(uT[rows[0, t]], z, preferred_element_type=F32).astype(BF16)
            for j in range(parts // 2):
                even = term[2 * j * half : (2 * j + 1) * half]
                odd = term[(2 * j + 1) * half : (2 * j + 2) * half]
                kbuf[j, t] = jnp.where(me == 0, even, odd)
                sbuf[j, t] = jnp.where(me == 0, odd, even)
    a = pltpu.make_async_copy(kbuf, keep, sems.at[0])
    b = pltpu.make_async_copy(sbuf, send, sems.at[1])
    a.start()
    b.start()
    a.wait()
    b.wait()


def pair_body(parts, keep, got, *refs):
    outs, (mine, abuf, bbuf, obuf, sems) = refs[:parts], refs[parts:]
    me = lax.axis_index("dp") // 2
    loads = [pltpu.make_async_copy(keep, abuf, sems.at[0]), pltpu.make_async_copy(got, bbuf, sems.at[1])]
    for c in loads:
        c.start()
    for c in loads:
        c.wait()
    stores = []
    for j in range(parts):
        other = me ^ j
        both = abuf[other].astype(F32) + bbuf[other].astype(F32)
        obuf[j] = both.astype(BF16)
        c = pltpu.make_async_copy(obuf.at[j], outs[j], sems.at[2 + j])
        c.start()
        stores.append(c)
    for c in stores:
        c.wait()


def final_body(parts, *refs):
    ins, (out, bufs, sems) = refs[:parts], refs[parts:]
    loads = [pltpu.make_async_copy(ins[j], bufs.at[j], sems.at[j]) for j in range(parts)]
    for c in loads:
        c.start()
    for c in loads:
        c.wait()
    nt = bufs.shape[1]
    for t in range(nt):
        total = bufs[0, t].astype(F32)
        for j in range(1, parts):
            total = total + bufs[j, t].astype(F32)
        out[:, 0, t, :] = total


def local(inputs, tiles, tile_rows, out_grad):
    sections = lax.axis_size("section")
    groups = lax.axis_size("dp")
    nt, blk = tiles.shape[1], tiles.shape[-1]
    E = inputs.shape[1]
    nb = E // blk
    kpc = nt // nb
    total = inputs.shape[0]
    M = NMB
    R = total // M
    SM = pltpu.SMEM
    dma = pltpu.SemaphoreType.DMA

    kh_s, kd_s, kz_s = ((M, R, E), BF16, VM), ((M, R, E), F32, VM), ((M, R, E), BF16, VM)
    tiles_v, kh, kd, kz = call(
        init_body, [((nt, blk, blk), BF16, VM), kh_s, kd_s, kz_s], [(tiles, ANY)], [dma], nbytes=5 * 10**6
    )
    u3 = pltpu.VMEM((nb, R, blk), BF16)
    v3 = pltpu.VMEM((nb, R, blk), F32)
    buf = pltpu.VMEM((R, E), BF16)
    last = sections - 1
    line = ((R, E), BF16, ANY)

    arrived = [inputs] * M
    for s in range(last):
        sent = []
        for m in range(M):
            out, kh, kd = call(
                functools.partial(forward_body, s, m, nb, kpc, blk, s == 0),
                [line, kh_s, kd_s],
                [(tile_rows, SM), (tiles_v, VM), (arrived[m], ANY), (kh, VM), (kd, VM)],
                [u3, buf, dma((2,))],
                {3: 1, 4: 2},
            )
            sent.append(lax.ppermute(out, "section", [(s, s + 1)]))
        arrived = sent
    back = []
    for m in range(M):
        out, kh, kd, kz = call(
            functools.partial(turn_body, last, m, nb, kpc, blk, last == 0),
            [line, kh_s, kd_s, kz_s],
            [(tile_rows, SM), (tiles_v, VM), (arrived[m], ANY), (out_grad, ANY), (kh, VM), (kd, VM), (kz, VM)],
            [u3, v3, buf, buf, dma((3,))],
            {4: 1, 5: 2, 6: 3},
        )
        if last > 0:
            back.append(lax.ppermute(out, "section", [(last, last - 1)]))
    for s in range(last - 1, 0, -1):
        sent = []
        for m in range(M):
            out, kz = call(
                functools.partial(backward_body, s, m, nb, kpc, blk),
                [line, kz_s],
                [(tile_rows, SM), (tiles_v, VM), (back[m], ANY), (kh, VM), (kd, VM), (kz, VM)],
                [v3, buf, buf, dma((2,))],
                {5: 1},
            )
            sent.append(lax.ppermute(out, "section", [(s, s - 1)]))
        back = sent
    for m in range(len(back)):
        (kz,) = call(
            functools.partial(first_body, m, nb, blk),
            [kz_s],
            [(back[m], ANY), (kd, VM), (kz, VM)],
            [buf, dma((1,))],
            {2: 0},
        )

    half = blk // groups
    if half % 16 == 0 and groups % 2 == 0:
        parts = groups // 2
        piece = (parts, nt, half, blk)
        keep, send = call(
            functools.partial(term_body, nb, kpc, blk, half),
            [(piece, BF16, ANY), (piece, BF16, ANY)],
            [(tile_rows, SM), (kh, VM), (kz, VM)],
            [pltpu.VMEM((nb, blk, total), BF16), pltpu.VMEM((1, 8, 128), BF16), pltpu.VMEM(piece, BF16), pltpu.VMEM(piece, BF16), dma((2,))],
        )
        got = lax.ppermute(send, "dp", [(i, i ^ 1) for i in range(groups)])
        one = (nt, half, blk)
        pieces = call(
            functools.partial(pair_body, parts),
            [(one, BF16, ANY)] * parts,
            [(keep, ANY), (got, ANY)],
            [pltpu.VMEM((1, 8, 128), BF16), pltpu.VMEM(piece, BF16), pltpu.VMEM(piece, BF16), pltpu.VMEM(piece, BF16), dma((2 + parts,))],
        )
        ready = [pieces[0]] + [
            lax.ppermute(pieces[j], "dp", [(i, i ^ (2 * j)) for i in range(groups)]) for j in range(1, parts)
        ]
        (out,) = call(
            functools.partial(final_body, parts),
            [((half, 1, nt, blk), F32, pltpu.VMEM)],
            [(r, ANY) for r in ready],
            [pltpu.VMEM((parts,) + one, BF16), dma((parts,))],
        )
        return out
    hf = kh.reshape(total, E).astype(F32)
    low = (hf * norm(hf)).astype(BF16)
    picked = jnp.take(low.reshape(total, nb, blk), tile_rows[0], axis=1).reshape(total, nb, kpc, blk)
    term = jnp.einsum("mnkr,mnc->rnkc", picked, kz.reshape(total, nb, blk), preferred_element_type=F32)
    return lax.psum_scatter(term.reshape(blk, 1, nt, blk), "dp", scatter_dimension=0, tiled=True)


def solution(mesh):
    return jax.shard_map(
        local,
        mesh=mesh,
        in_specs=(P("dp", None), P("section", None, None, None), P("section", None), P("dp", None)),
        out_specs=P("dp", "section", None, None),
        check_vma=False,
    )
```

time: 283 us -> 102 us (0.36)
  waiting for transfers between devices: 149 us -> 46.1 us
  other arithmetic: 34.5 us -> 0 us
  Pallas kernels: 0 us -> 24.5 us
  local copies, waits for them, and re-layouts: 25 us -> 3.06 us
  matrix products: 16.5 us -> 0 us
  starting transfers between devices: 43.1 us -> 27.2 us
  between operations: 13.5 us -> 0.63 us
    reduce_scatter x1 -> x0, waiting for transfers between devices: 52.7 us -> none  [local(): return lax.psum_scatter(term, 'dp', scatter_dimension=0, tiled=True)]
    ppermute x14 -> x28, waiting for transfers between devices: 96.3 us -> 46.1 us  [the longest x8 26.5 us: local(): sent.append(lax.ppermute(out, 'section', [(s, s - 1)]))]
    pallas_call x0 -> x32, Pallas kernels: none -> 24.5 us  [call(): pl.pallas_call(body, out_shape=out_shape, in_specs=in_specs, out_specs=ou...]
    dot_general x13 -> x0, matrix products: 16.5 us -> none  [the longest x4 5.83 us: layer_backward(): jnp.einsum('mtr,tb->mbr', back.reshape(count, nb * kpc, blk), onehot, pre...]
    ppermute x14 -> x28, starting transfers between devices: 43.1 us -> 27.2 us  [the longest x12 13 us: local(): sent.append(lax.ppermute(out, 'section', [(s, s + 1)]))]
    dynamic_update_slice x8 -> x0, other arithmetic: 13.7 us -> none  [the longest x4 7.06 us: backward_work(): store_dz = lax.dynamic_update_index_in_dim(store_dz, dz, index, 0)]
    convert_element_type x9 -> x0, other arithmetic: 7.82 us -> none  [the longest x4 4.57 us: layer_backward(): return (dz, result.astype(jnp.bfloat16))]
    reduce_sum x9 -> x0, other arithmetic: 6.36 us -> none  [row_scale(): return (hf, lax.rsqrt(jnp.mean(hf * hf, axis=1, keepdims=True) + EPS))]
  transfers between devices with their start and end apart: 15 -> 28, of which waited for: 15 -> 9; matrix products, arithmetic and copies ran while one was open for 0% -> 0% of each run, Pallas kernels for 0% -> 18%
where the time goes in v1:
time: 102 us; the launch traced here: 101 us
  waiting for transfers between devices  46.1 us (45%)
  starting transfers between devices  27.2 us (27%)
  Pallas kernels  24.5 us (24%)
  local copies, waits for them, and re-layouts  3.06 us (3%)
    ppermute x8, waiting for transfers between devices, local(): sent.append(lax.ppermute(out, 'section', [(s, s - 1)]))  26.5 us
    pallas_call x32, Pallas kernels, call(): pl.pallas_call(body, out_shape=out_shape, in_specs=in_specs, out_specs=ou...  24.5 us
    ppermute x3, waiting for transfers between devices, local(): lax.ppermute(pieces[j], 'dp', [(i, i ^ 2 * j) for i in range(groups)])  13.1 us
    ppermute x12, starting transfers between devices, local(): sent.append(lax.ppermute(out, 'section', [(s, s + 1)]))  13 us
    ppermute x8, starting transfers between devices, local(): sent.append(lax.ppermute(out, 'section', [(s, s - 1)]))  7.86 us
    ppermute x12, waiting for transfers between devices, local(): sent.append(lax.ppermute(out, 'section', [(s, s + 1)]))  3.64 us
    ppermute x3, starting transfers between devices, local(): lax.ppermute(pieces[j], 'dp', [(i, i ^ 2 * j) for i in range(groups)])  3.55 us
    unnamed x9, local copies, waits for them, and re-layouts  3.06 us
  transfers between devices with their start and end apart: 28, of which 9 were waited for; matrix products, arithmetic and copies ran while one was open for 0% of the time, Pallas kernels for 18%

profile of v1, /device:TPU:0, one launch (start us, length us, event | category | flops | bytes accessed | tf_op | source)
XLA Modules:
  0.0 101.4 jit_solution(5435780850980975915)
XLA Ops:
  0.0 1.7 %copy-done.2 = bf16[1,72,128,128]{3,2,1,0:T(8,128)(2,1)S(1)} copy-done((bf16[1,72,128,128]{3,2,1,0:T(8,128)(2,1)S(1)}, bf16[1,72,128,128]{3,2,1,0:T(8,128)(2,1)}, u32[]{:S(2)}) %copy-start.2) | copy-done | bytes 2359320
  2.4 1.8 %shard_map.47 = (bf16[32,3072]{1,0:T(8,128)(2,1)S(1)}, bf16[4,32,3072]{2,1,0:T(8,128)(2,1)S(1)}, f32[4,32,3072]{2,1,0:T(8,128)S(1)}) custom-call(s32[1,72]{1,0:T(1,128)S(1)} %copy-done.3, bf16[72,128,128]{2,1,0:T(8,128)(2,1)S(1)} %get-tuple-element.83.tiles, bf16[128,3072]{1,0:T(8,128)(2,1)S(1)} %copy-done.1, ...), custom_call_target="tpu_custom_call", output_to_operand_aliasing={{1}: (3, {}), {2}: (4, {})} | custom-call | flops 100000000 | bytes 3000000 | tf_op jit(solution)/shard_map/pallas_call | solution.py:32
  4.2 3.7 %collective-permute-start.3 = (bf16[32,3072]{1,0:T(8,128)(2,1)S(1)}, bf16[32,3072]{1,0:T(8,128)(2,1)S(1)}, u32[]{:S(2)}, u32[]{:S(2)}) collective-permute-start(bf16[32,3072]{1,0:T(8,128)(2,1)S(1)} %get-tuple-element.95), channel_id=1, source_target_pairs={{0,1},{4,5},{8,9},{12,13},{16,17},{20,21},{24,25},{28,29}} | collective-permute-start | bytes 589832 | tf_op jit(solution)/shard_map/ppermute | solution.py:264
  7.9 1.8 %shard_map.48 = (bf16[32,3072]{1,0:T(8,128)(2,1)S(1)}, bf16[4,32,3072]{2,1,0:T(8,128)(2,1)S(1)}, f32[4,32,3072]{2,1,0:T(8,128)S(1)}) custom-call(s32[1,72]{1,0:T(1,128)S(1)} %copy-done.3, bf16[72,128,128]{2,1,0:T(8,128)(2,1)S(1)} %get-tuple-element.83.tiles, bf16[128,3072]{1,0:T(8,128)(2,1)S(1)} %copy-done.1, ...), custom_call_target="tpu_custom_call", output_to_operand_aliasing={{1}: (3, {}), {2}: (4, {})} | custom-call | flops 100000000 | bytes 3000000 | tf_op jit(solution)/shard_map/pallas_call | solution.py:32
  9.8 1.3 %collective-permute-start.2 = (bf16[32,3072]{1,0:T(8,128)(2,1)S(1)}, bf16[32,3072]{1,0:T(8,128)(2,1)S(1)}, u32[]{:S(2)}, u32[]{:S(2)}) collective-permute-start(bf16[32,3072]{1,0:T(8,128)(2,1)S(1)} %get-tuple-element.94), channel_id=1, source_target_pairs={{0,1},{4,5},{8,9},{12,13},{16,17},{20,21},{24,25},{28,29}} | collective-permute-start | bytes 589832 | tf_op jit(solution)/shard_map/ppermute | solution.py:264
  11.1 1.8 %shard_map.49 = (bf16[32,3072]{1,0:T(8,128)(2,1)S(1)}, bf16[4,32,3072]{2,1,0:T(8,128)(2,1)S(1)}, f32[4,32,3072]{2,1,0:T(8,128)S(1)}) custom-call(s32[1,72]{1,0:T(1,128)S(1)} %copy-done.3, bf16[72,128,128]{2,1,0:T(8,128)(2,1)S(1)} %get-tuple-element.83.tiles, bf16[128,3072]{1,0:T(8,128)(2,1)S(1)} %copy-done.1, ...), custom_call_target="tpu_custom_call", output_to_operand_aliasing={{1}: (3, {}), {2}: (4, {})} | custom-call | flops 100000000 | bytes 3000000 | tf_op jit(solution)/shard_map/pallas_call | solution.py:32
  12.9 1.3 %collective-permute-start.1 = (bf16[32,3072]{1,0:T(8,128)(2,1)S(1)}, bf16[32,3072]{1,0:T(8,128)(2,1)S(1)}, u32[]{:S(2)}, u32[]{:S(2)}) collective-permute-start(bf16[32,3072]{1,0:T(8,128)(2,1)S(1)} %get-tuple-element.93), channel_id=1, source_target_pairs={{0,1},{4,5},{8,9},{12,13},{16,17},{20,21},{24,25},{28,29}} | collective-permute-start | bytes 589832 | tf_op jit(solution)/shard_map/ppermute | solution.py:264
  14.2 1.8 %shard_map.50 = (bf16[32,3072]{1,0:T(8,128)(2,1)S(1)}, bf16[4,32,3072]{2,1,0:T(8,128)(2,1)S(1)}, f32[4,32,3072]{2,1,0:T(8,128)S(1)}) custom-call(s32[1,72]{1,0:T(1,128)S(1)} %copy-done.3, bf16[72,128,128]{2,1,0:T(8,128)(2,1)S(1)} %get-tuple-element.83.tiles, bf16[128,3072]{1,0:T(8,128)(2,1)S(1)} %copy-done.1, ...), custom_call_target="tpu_custom_call", output_to_operand_aliasing={{1}: (3, {}), {2}: (4, {})} | custom-call | flops 100000000 | bytes 3000000 | tf_op jit(solution)/shard_map/pallas_call | solution.py:32
  16.0 1.3 %collective-permute-start = (bf16[32,3072]{1,0:T(8,128)(2,1)S(1)}, bf16[32,3072]{1,0:T(8,128)(2,1)S(1)}, u32[]{:S(2)}, u32[]{:S(2)}) collective-permute-start(bf16[32,3072]{1,0:T(8,128)(2,1)S(1)} %get-tuple-element.92), channel_id=1, source_target_pairs={{0,1},{4,5},{8,9},{12,13},{16,17},{20,21},{24,25},{28,29}} | collective-permute-start | bytes 589832 | tf_op jit(solution)/shard_map/ppermute | solution.py:264
  17.9 0.7 collective-permute-start.7
  19.2 0.7 collective-permute-start.6
  19.8 1.7 %collective-permute-done.1.hin = bf16[32,3072]{1,0:T(8,128)(2,1)S(1)} collective-permute-done((bf16[32,3072]{1,0:T(8,128)(2,1)S(1)}, bf16[32,3072]{1,0:T(8,128)(2,1)S(1)}, u32[]{:S(2)}, u32[]{:S(2)}) %collective-permute-start.1) | collective-permute-done | bytes 196640 | tf_op jit(solution)/shard_map/ppermute | solution.py:264
  22.1 0.7 collective-permute-start.5
  22.8 1.9 %collective-permute-done.hin = bf16[32,3072]{1,0:T(8,128)(2,1)S(1)} collective-permute-done((bf16[32,3072]{1,0:T(8,128)(2,1)S(1)}, bf16[32,3072]{1,0:T(8,128)(2,1)S(1)}, u32[]{:S(2)}, u32[]{:S(2)}) %collective-permute-start) | collective-permute-done | bytes 196640 | tf_op jit(solution)/shard_map/ppermute | solution.py:264
  25.3 0.7 collective-permute-start.4
  26.6 0.7 collective-permute-start.11
  27.8 0.7 collective-permute-start.10
  29.1 0.7 collective-permute-start.9
  30.4 0.7 collective-permute-start.8
  31.1 0.6 shard_map.59
  31.7 0.7 collective-permute-start.15
  32.4 0.6 shard_map.60
  33.0 0.7 collective-permute-start.14
  33.7 0.8 shard_map.61
  34.4 0.7 collective-permute-start.13
  35.1 0.6 shard_map.62
  35.7 0.7 collective-permute-start.12
  37.0 0.7 collective-permute-start.19
  38.3 0.7 collective-permute-start.18
  39.5 0.7 collective-permute-start.17
  40.8 0.7 collective-permute-start.16
  42.1 1.3 %collective-permute-start.23 = (bf16[32,3072]{1,0:T(8,128)(2,1)S(1)}, bf16[32,3072]{1,0:T(8,128)(2,1)S(1)}, u32[]{:S(2)}, u32[]{:S(2)}) collective-permute-start(bf16[32,3072]{1,0:T(8,128)(2,1)S(1)} %get-tuple-element.153), channel_id=1, source_target_pairs={{1,0},{5,4},{9,8},{13,12},{17,16},{21,20},{25,24},{29,28}} | collective-permute-start | bytes 589832 | tf_op jit(solution)/shard_map/ppermute | solution.py:287
  44.0 1.3 %collective-permute-start.22 = (bf16[32,3072]{1,0:T(8,128)(2,1)S(1)}, bf16[32,3072]{1,0:T(8,128)(2,1)S(1)}, u32[]{:S(2)}, u32[]{:S(2)}) collective-permute-start(bf16[32,3072]{1,0:T(8,128)(2,1)S(1)} %get-tuple-element.152), channel_id=1, source_target_pairs={{1,0},{5,4},{9,8},{13,12},{17,16},{21,20},{25,24},{29,28}} | collective-permute-start | bytes 589832 | tf_op jit(solution)/shard_map/ppermute | solution.py:287
  45.9 1.3 %collective-permute-start.21 = (bf16[32,3072]{1,0:T(8,128)(2,1)S(1)}, bf16[32,3072]{1,0:T(8,128)(2,1)S(1)}, u32[]{:S(2)}, u32[]{:S(2)}) collective-permute-start(bf16[32,3072]{1,0:T(8,128)(2,1)S(1)} %get-tuple-element.151), channel_id=1, source_target_pairs={{1,0},{5,4},{9,8},{13,12},{17,16},{21,20},{25,24},{29,28}} | collective-permute-start | bytes 589832 | tf_op jit(solution)/shard_map/ppermute | solution.py:287
  47.8 1.3 %collective-permute-start.20 = (bf16[32,3072]{1,0:T(8,128)(2,1)S(1)}, bf16[32,3072]{1,0:T(8,128)(2,1)S(1)}, u32[]{:S(2)}, u32[]{:S(2)}) collective-permute-start(bf16[32,3072]{1,0:T(8,128)(2,1)S(1)} %get-tuple-element.150), channel_id=1, source_target_pairs={{1,0},{5,4},{9,8},{13,12},{17,16},{21,20},{25,24},{29,28}} | collective-permute-start | bytes 589832 | tf_op jit(solution)/shard_map/ppermute | solution.py:287
  49.1 14.7 %collective-permute-done.23.gin = bf16[32,3072]{1,0:T(8,128)(2,1)S(1)} collective-permute-done((bf16[32,3072]{1,0:T(8,128)(2,1)S(1)}, bf16[32,3072]{1,0:T(8,128)(2,1)S(1)}, u32[]{:S(2)}, u32[]{:S(2)}) %collective-permute-start.23) | collective-permute-done | bytes 196640 | tf_op jit(solution)/shard_map/ppermute | solution.py:287
  64.1 3.9 %collective-permute-done.22.gin = bf16[32,3072]{1,0:T(8,128)(2,1)S(1)} collective-permute-done((bf16[32,3072]{1,0:T(8,128)(2,1)S(1)}, bf16[32,3072]{1,0:T(8,128)(2,1)S(1)}, u32[]{:S(2)}, u32[]{:S(2)}) %collective-permute-start.22) | collective-permute-done | bytes 196640 | tf_op jit(solution)/shard_map/ppermute | solution.py:287
  68.3 4.7 %collective-permute-done.21.gin = bf16[32,3072]{1,0:T(8,128)(2,1)S(1)} collective-permute-done((bf16[32,3072]{1,0:T(8,128)(2,1)S(1)}, bf16[32,3072]{1,0:T(8,128)(2,1)S(1)}, u32[]{:S(2)}, u32[]{:S(2)}) %collective-permute-start.21) | collective-permute-done | bytes 196640 | tf_op jit(solution)/shard_map/ppermute | solution.py:287
  73.3 3.1 %collective-permute-done.20.gin = bf16[32,3072]{1,0:T(8,128)(2,1)S(1)} collective-permute-done((bf16[32,3072]{1,0:T(8,128)(2,1)S(1)}, bf16[32,3072]{1,0:T(8,128)(2,1)S(1)}, u32[]{:S(2)}, u32[]{:S(2)}) %collective-permute-start.20) | collective-permute-done | bytes 196640 | tf_op jit(solution)/shard_map/ppermute | solution.py:287
  76.9 2.4 %shard_map.75 = (bf16[4,72,16,128]{3,2,1,0:T(8,128)(2,1)S(1)}, bf16[4,72,16,128]{3,2,1,0:T(8,128)(2,1)S(1)}) custom-call(s32[1,72]{1,0:T(1,128)S(1)} %copy-done.3, bf16[4,32,3072]{2,1,0:T(8,128)(2,1)S(1)} %get-tuple-element.132.kh, bf16[4,32,3072]{2,1,0:T(8,128)(2,1)S(1)} %shard_map.74.kz), custom_call_target="tpu_custom_call" | custom-call | flops 100000000 | bytes 3000000 | tf_op jit(solution)/shard_map/pallas_call | solution.py:32
  79.4 2.8 %collective-permute-done.24.got = bf16[4,72,16,128]{3,2,1,0:T(8,128)(2,1)S(1)} collective-permute-done((bf16[4,72,16,128]{3,2,1,0:T(8,128)(2,1)S(1)}, bf16[4,72,16,128]{3,2,1,0:T(8,128)(2,1)S(1)}, u32[]{:S(2)}, u32[]{:S(2)}) %collective-permute-start.24) | collective-permute-done | bytes 1179680 | tf_op jit(solution)/shard_map/ppermute | solution.py:308
  82.2 1.1 %shard_map.76 = (bf16[72,16,128]{2,1,0:T(8,128)(2,1)S(1)}, bf16[72,16,128]{2,1,0:T(8,128)(2,1)S(1)}, bf16[72,16,128]{2,1,0:T(8,128)(2,1)S(1)}, bf16[72,16,128]{2,1,0:T(8,128)(2,1)S(1)}) custom-call(bf16[4,72,16,128]{3,2,1,0:T(8,128)(2,1)S(1)} %get-tuple-element.155.keep, bf16[4,72,16,128]{3,2,1,0:T(8,128)(2,1)S(1)} %collective-permute-done.24.got), custom_call_target="tpu_custom_call" | custom-call | flops 100000000 | bytes 3000000 | tf_op jit(solution)/shard_map/pallas_call | solution.py:32
  83.3 1.6 %collective-permute-start.25 = (bf16[72,16,128]{2,1,0:T(8,128)(2,1)S(1)}, bf16[72,16,128]{2,1,0:T(8,128)(2,1)S(1)}, u32[]{:S(2)}, u32[]{:S(2)}) collective-permute-start(bf16[72,16,128]{2,1,0:T(8,128)(2,1)S(1)} %get-tuple-element.158), channel_id=1, source_target_pairs={{0,8},{4,12},{8,0},{12,4},{16,24},{20,28},{24,16},{28,20},{1,9},{5... | collective-permute-start | bytes 884744 | tf_op jit(solution)/shard_map/ppermute | solution.py:317
  84.9 1.5 %collective-permute-start.26 = (bf16[72,16,128]{2,1,0:T(8,128)(2,1)S(1)}, bf16[72,16,128]{2,1,0:T(8,128)(2,1)S(1)}, u32[]{:S(2)}, u32[]{:S(2)}) collective-permute-start(bf16[72,16,128]{2,1,0:T(8,128)(2,1)S(1)} %get-tuple-element.159), channel_id=1, source_target_pairs={{0,16},{4,20},{8,24},{12,28},{16,0},{20,4},{24,8},{28,12},{1,17},{... | collective-permute-start | bytes 884744 | tf_op jit(solution)/shard_map/ppermute | solution.py:317
  86.9 6.4 %collective-permute-done.25.refs_1_ = bf16[72,16,128]{2,1,0:T(8,128)(2,1)S(1)} collective-permute-done((bf16[72,16,128]{2,1,0:T(8,128)(2,1)S(1)}, bf16[72,16,128]{2,1,0:T(8,128)(2,1)S(1)}, u32[]{:S(2)}, u32[]{:S(2)}) %collective-permute-start.25) | collective-permute-done | bytes 294944 | tf_op jit(solution)/shard_map/ppermute | solution.py:317
  93.2 6.7 %collective-permute-done.26.refs_2_ = bf16[72,16,128]{2,1,0:T(8,128)(2,1)S(1)} collective-permute-done((bf16[72,16,128]{2,1,0:T(8,128)(2,1)S(1)}, bf16[72,16,128]{2,1,0:T(8,128)(2,1)S(1)}, u32[]{:S(2)}, u32[]{:S(2)}) %collective-permute-start.26) | collective-permute-done | bytes 294944 | tf_op jit(solution)/shard_map/ppermute | solution.py:317
  100.0 0.7 shard_map.77
  100.6 0.8 copy.101
  (49 shorter events, 11.7 us)
Async XLA Ops:
  0.0 1.9 %copy-start.1 = (bf16[128,3072]{1,0:T(8,128)(2,1)S(1)}, bf16[128,3072]{1,0:T(8,128)(2,1)}, u32[]{:S(2)}) copy-start(bf16[128,3072]{1,0:T(8,128)(2,1)} %hin.7) | copy-start | bytes 2359300
  0.0 1.7 %copy-start.2 = (bf16[1,72,128,128]{3,2,1,0:T(8,128)(2,1)S(1)}, bf16[1,72,128,128]{3,2,1,0:T(8,128)(2,1)}, u32[]{:S(2)}) copy-start(bf16[1,72,128,128]{3,2,1,0:T(8,128)(2,1)} %tiles.1) | copy-start | bytes 7077892
  1.7 0.7 copy-start.3
  4.2 13.1 %collective-permute-start.3 = (bf16[32,3072]{1,0:T(8,128)(2,1)S(1)}, bf16[32,3072]{1,0:T(8,128)(2,1)S(1)}, u32[]{:S(2)}, u32[]{:S(2)}) collective-permute-start(bf16[32,3072]{1,0:T(8,128)(2,1)S(1)} %get-tuple-element.95), channel_id=1, source_target_pairs={{0,1},{4,5},{8,9},{12,13},{16,17},{20,21},{24,25},{28,29}} | collective-permute-start | bytes 589832 | tf_op jit(solution)/shard_map/ppermute | solution.py:264
  9.8 8.8 %collective-permute-start.2 = (bf16[32,3072]{1,0:T(8,128)(2,1)S(1)}, bf16[32,3072]{1,0:T(8,128)(2,1)S(1)}, u32[]{:S(2)}, u32[]{:S(2)}) collective-permute-start(bf16[32,3072]{1,0:T(8,128)(2,1)S(1)} %get-tuple-element.94), channel_id=1, source_target_pairs={{0,1},{4,5},{8,9},{12,13},{16,17},{20,21},{24,25},{28,29}} | collective-permute-start | bytes 589832 | tf_op jit(solution)/shard_map/ppermute | solution.py:264
  12.9 8.7 %collective-permute-start.1 = (bf16[32,3072]{1,0:T(8,128)(2,1)S(1)}, bf16[32,3072]{1,0:T(8,128)(2,1)S(1)}, u32[]{:S(2)}, u32[]{:S(2)}) collective-permute-start(bf16[32,3072]{1,0:T(8,128)(2,1)S(1)} %get-tuple-element.93), channel_id=1, source_target_pairs={{0,1},{4,5},{8,9},{12,13},{16,17},{20,21},{24,25},{28,29}} | collective-permute-start | bytes 589832 | tf_op jit(solution)/shard_map/ppermute | solution.py:264
  16.0 8.7 %collective-permute-start = (bf16[32,3072]{1,0:T(8,128)(2,1)S(1)}, bf16[32,3072]{1,0:T(8,128)(2,1)S(1)}, u32[]{:S(2)}, u32[]{:S(2)}) collective-permute-start(bf16[32,3072]{1,0:T(8,128)(2,1)S(1)} %get-tuple-element.92), channel_id=1, source_target_pairs={{0,1},{4,5},{8,9},{12,13},{16,17},{20,21},{24,25},{28,29}} | collective-permute-start | bytes 589832 | tf_op jit(solution)/shard_map/ppermute | solution.py:264
  17.9 8.1 %collective-permute-start.7 = (bf16[32,3072]{1,0:T(8,128)(2,1)S(1)}, bf16[32,3072]{1,0:T(8,128)(2,1)S(1)}, u32[]{:S(2)}, u32[]{:S(2)}) collective-permute-start(bf16[32,3072]{1,0:T(8,128)(2,1)S(1)} %get-tuple-element.107), channel_id=1, source_target_pairs={{1,2},{5,6},{9,10},{13,14},{17,18},{21,22},{25,26},{29,30}} | collective-permute-start | bytes 589832 | tf_op jit(solution)/shard_map/ppermute | solution.py:264
  19.2 8.1 %collective-permute-start.6 = (bf16[32,3072]{1,0:T(8,128)(2,1)S(1)}, bf16[32,3072]{1,0:T(8,128)(2,1)S(1)}, u32[]{:S(2)}, u32[]{:S(2)}) collective-permute-start(bf16[32,3072]{1,0:T(8,128)(2,1)S(1)} %get-tuple-element.106), channel_id=1, source_target_pairs={{1,2},{5,6},{9,10},{13,14},{17,18},{21,22},{25,26},{29,30}} | collective-permute-start | bytes 589832 | tf_op jit(solution)/shard_map/ppermute | solution.py:264
  22.1 6.4 %collective-permute-start.5 = (bf16[32,3072]{1,0:T(8,128)(2,1)S(1)}, bf16[32,3072]{1,0:T(8,128)(2,1)S(1)}, u32[]{:S(2)}, u32[]{:S(2)}) collective-permute-start(bf16[32,3072]{1,0:T(8,128)(2,1)S(1)} %get-tuple-element.105), channel_id=1, source_target_pairs={{1,2},{5,6},{9,10},{13,14},{17,18},{21,22},{25,26},{29,30}} | collective-permute-start | bytes 589832 | tf_op jit(solution)/shard_map/ppermute | solution.py:264
  25.3 4.5 %collective-permute-start.4 = (bf16[32,3072]{1,0:T(8,128)(2,1)S(1)}, bf16[32,3072]{1,0:T(8,128)(2,1)S(1)}, u32[]{:S(2)}, u32[]{:S(2)}) collective-permute-start(bf16[32,3072]{1,0:T(8,128)(2,1)S(1)} %get-tuple-element.104), channel_id=1, source_target_pairs={{1,2},{5,6},{9,10},{13,14},{17,18},{21,22},{25,26},{29,30}} | collective-permute-start | bytes 589832 | tf_op jit(solution)/shard_map/ppermute | solution.py:264
  26.6 4.5 %collective-permute-start.11 = (bf16[32,3072]{1,0:T(8,128)(2,1)S(1)}, bf16[32,3072]{1,0:T(8,128)(2,1)S(1)}, u32[]{:S(2)}, u32[]{:S(2)}) collective-permute-start(bf16[32,3072]{1,0:T(8,128)(2,1)S(1)} %get-tuple-element.119), channel_id=1, source_target_pairs={{2,3},{6,7},{10,11},{14,15},{18,19},{22,23},{26,27},{30,31}} | collective-permute-start | bytes 589832 | tf_op jit(solution)/shard_map/ppermute | solution.py:264
  27.8 4.5 %collective-permute-start.10 = (bf16[32,3072]{1,0:T(8,128)(2,1)S(1)}, bf16[32,3072]{1,0:T(8,128)(2,1)S(1)}, u32[]{:S(2)}, u32[]{:S(2)}) collective-permute-start(bf16[32,3072]{1,0:T(8,128)(2,1)S(1)} %get-tuple-element.118), channel_id=1, source_target_pairs={{2,3},{6,7},{10,11},{14,15},{18,19},{22,23},{26,27},{30,31}} | collective-permute-start | bytes 589832 | tf_op jit(solution)/shard_map/ppermute | solution.py:264
  29.1 4.5 %collective-permute-start.9 = (bf16[32,3072]{1,0:T(8,128)(2,1)S(1)}, bf16[32,3072]{1,0:T(8,128)(2,1)S(1)}, u32[]{:S(2)}, u32[]{:S(2)}) collective-permute-start(bf16[32,3072]{1,0:T(8,128)(2,1)S(1)} %get-tuple-element.117), channel_id=1, source_target_pairs={{2,3},{6,7},{10,11},{14,15},{18,19},{22,23},{26,27},{30,31}} | collective-permute-start | bytes 589832 | tf_op jit(solution)/shard_map/ppermute | solution.py:264
  29.8 1.3 %copy-start = (bf16[128,3072]{1,0:T(8,128)(2,1)S(1)}, bf16[128,3072]{1,0:T(8,128)(2,1)}, u32[]{:S(2)}) copy-start(bf16[128,3072]{1,0:T(8,128)(2,1)} %seeds.7) | copy-start | bytes 2359300
  30.4 4.7 %collective-permute-start.8 = (bf16[32,3072]{1,0:T(8,128)(2,1)S(1)}, bf16[32,3072]{1,0:T(8,128)(2,1)S(1)}, u32[]{:S(2)}, u32[]{:S(2)}) collective-permute-start(bf16[32,3072]{1,0:T(8,128)(2,1)S(1)} %get-tuple-element.116), channel_id=1, source_target_pairs={{2,3},{6,7},{10,11},{14,15},{18,19},{22,23},{26,27},{30,31}} | collective-permute-start | bytes 589832 | tf_op jit(solution)/shard_map/ppermute | solution.py:264
  31.7 4.7 %collective-permute-start.15 = (bf16[32,3072]{1,0:T(8,128)(2,1)S(1)}, bf16[32,3072]{1,0:T(8,128)(2,1)S(1)}, u32[]{:S(2)}, u32[]{:S(2)}) collective-permute-start(bf16[32,3072]{1,0:T(8,128)(2,1)S(1)} %get-tuple-element.137), channel_id=1, source_target_pairs={{3,2},{7,6},{11,10},{15,14},{19,18},{23,22},{27,26},{31,30}} | collective-permute-start | bytes 589832 | tf_op jit(solution)/shard_map/ppermute | solution.py:276
  33.0 4.7 %collective-permute-start.14 = (bf16[32,3072]{1,0:T(8,128)(2,1)S(1)}, bf16[32,3072]{1,0:T(8,128)(2,1)S(1)}, u32[]{:S(2)}, u32[]{:S(2)}) collective-permute-start(bf16[32,3072]{1,0:T(8,128)(2,1)S(1)} %get-tuple-element.136), channel_id=1, source_target_pairs={{3,2},{7,6},{11,10},{15,14},{19,18},{23,22},{27,26},{31,30}} | collective-permute-start | bytes 589832 | tf_op jit(solution)/shard_map/ppermute | solution.py:276
  34.4 4.5 %collective-permute-start.13 = (bf16[32,3072]{1,0:T(8,128)(2,1)S(1)}, bf16[32,3072]{1,0:T(8,128)(2,1)S(1)}, u32[]{:S(2)}, u32[]{:S(2)}) collective-permute-start(bf16[32,3072]{1,0:T(8,128)(2,1)S(1)} %get-tuple-element.135), channel_id=1, source_target_pairs={{3,2},{7,6},{11,10},{15,14},{19,18},{23,22},{27,26},{31,30}} | collective-permute-start | bytes 589832 | tf_op jit(solution)/shard_map/ppermute | solution.py:276
  35.7 4.5 %collective-permute-start.12 = (bf16[32,3072]{1,0:T(8,128)(2,1)S(1)}, bf16[32,3072]{1,0:T(8,128)(2,1)S(1)}, u32[]{:S(2)}, u32[]{:S(2)}) collective-permute-start(bf16[32,3072]{1,0:T(8,128)(2,1)S(1)} %get-tuple-element.133), channel_id=1, source_target_pairs={{3,2},{7,6},{11,10},{15,14},{19,18},{23,22},{27,26},{31,30}} | collective-permute-start | bytes 589832 | tf_op jit(solution)/shard_map/ppermute | solution.py:276
  37.0 4.5 %collective-permute-start.19 = (bf16[32,3072]{1,0:T(8,128)(2,1)S(1)}, bf16[32,3072]{1,0:T(8,128)(2,1)S(1)}, u32[]{:S(2)}, u32[]{:S(2)}) collective-permute-start(bf16[32,3072]{1,0:T(8,128)(2,1)S(1)} %get-tuple-element.145), channel_id=1, source_target_pairs={{2,1},{6,5},{10,9},{14,13},{18,17},{22,21},{26,25},{30,29}} | collective-permute-start | bytes 589832 | tf_op jit(solution)/shard_map/ppermute | solution.py:287
  38.3 5.1 %collective-permute-start.18 = (bf16[32,3072]{1,0:T(8,128)(2,1)S(1)}, bf16[32,3072]{1,0:T(8,128)(2,1)S(1)}, u32[]{:S(2)}, u32[]{:S(2)}) collective-permute-start(bf16[32,3072]{1,0:T(8,128)(2,1)S(1)} %get-tuple-element.144), channel_id=1, source_target_pairs={{2,1},{6,5},{10,9},{14,13},{18,17},{22,21},{26,25},{30,29}} | collective-permute-start | bytes 589832 | tf_op jit(solution)/shard_map/ppermute | solution.py:287
  39.5 5.7 %collective-permute-start.17 = (bf16[32,3072]{1,0:T(8,128)(2,1)S(1)}, bf16[32,3072]{1,0:T(8,128)(2,1)S(1)}, u32[]{:S(2)}, u32[]{:S(2)}) collective-permute-start(bf16[32,3072]{1,0:T(8,128)(2,1)S(1)} %get-tuple-element.143), channel_id=1, source_target_pairs={{2,1},{6,5},{10,9},{14,13},{18,17},{22,21},{26,25},{30,29}} | collective-permute-start | bytes 589832 | tf_op jit(solution)/shard_map/ppermute | solution.py:287
  40.8 6.4 %collective-permute-start.16 = (bf16[32,3072]{1,0:T(8,128)(2,1)S(1)}, bf16[32,3072]{1,0:T(8,128)(2,1)S(1)}, u32[]{:S(2)}, u32[]{:S(2)}) collective-permute-start(bf16[32,3072]{1,0:T(8,128)(2,1)S(1)} %get-tuple-element.142), channel_id=1, source_target_pairs={{2,1},{6,5},{10,9},{14,13},{18,17},{22,21},{26,25},{30,29}} | collective-permute-start | bytes 589832 | tf_op jit(solution)/shard_map/ppermute | solution.py:287
  42.1 21.7 %collective-permute-start.23 = (bf16[32,3072]{1,0:T(8,128)(2,1)S(1)}, bf16[32,3072]{1,0:T(8,128)(2,1)S(1)}, u32[]{:S(2)}, u32[]{:S(2)}) collective-permute-start(bf16[32,3072]{1,0:T(8,128)(2,1)S(1)} %get-tuple-element.153), channel_id=1, source_target_pairs={{1,0},{5,4},{9,8},{13,12},{17,16},{21,20},{25,24},{29,28}} | collective-permute-start | bytes 589832 | tf_op jit(solution)/shard_map/ppermute | solution.py:287
  44.0 24.0 %collective-permute-start.22 = (bf16[32,3072]{1,0:T(8,128)(2,1)S(1)}, bf16[32,3072]{1,0:T(8,128)(2,1)S(1)}, u32[]{:S(2)}, u32[]{:S(2)}) collective-permute-start(bf16[32,3072]{1,0:T(8,128)(2,1)S(1)} %get-tuple-element.152), channel_id=1, source_target_pairs={{1,0},{5,4},{9,8},{13,12},{17,16},{21,20},{25,24},{29,28}} | collective-permute-start | bytes 589832 | tf_op jit(solution)/shard_map/ppermute | solution.py:287
  45.9 27.2 %collective-permute-start.21 = (bf16[32,3072]{1,0:T(8,128)(2,1)S(1)}, bf16[32,3072]{1,0:T(8,128)(2,1)S(1)}, u32[]{:S(2)}, u32[]{:S(2)}) collective-permute-start(bf16[32,3072]{1,0:T(8,128)(2,1)S(1)} %get-tuple-element.151), channel_id=1, source_target_pairs={{1,0},{5,4},{9,8},{13,12},{17,16},{21,20},{25,24},{29,28}} | collective-permute-start | bytes 589832 | tf_op jit(solution)/shard_map/ppermute | solution.py:287
  47.8 28.7 %collective-permute-start.20 = (bf16[32,3072]{1,0:T(8,128)(2,1)S(1)}, bf16[32,3072]{1,0:T(8,128)(2,1)S(1)}, u32[]{:S(2)}, u32[]{:S(2)}) collective-permute-start(bf16[32,3072]{1,0:T(8,128)(2,1)S(1)} %get-tuple-element.150), channel_id=1, source_target_pairs={{1,0},{5,4},{9,8},{13,12},{17,16},{21,20},{25,24},{29,28}} | collective-permute-start | bytes 589832 | tf_op jit(solution)/shard_map/ppermute | solution.py:287
  79.3 2.9 %collective-permute-start.24 = (bf16[4,72,16,128]{3,2,1,0:T(8,128)(2,1)S(1)}, bf16[4,72,16,128]{3,2,1,0:T(8,128)(2,1)S(1)}, u32[]{:S(2)}, u32[]{:S(2)}) collective-permute-start(bf16[4,72,16,128]{3,2,1,0:T(8,128)(2,1)S(1)} %get-tuple-element.156), channel_id=1, source_target_pairs={{0,4},{4,0},{8,12},{12,8},{16,20},{20,16},{24,28},{28,24},{1,5},{5... | collective-permute-start | bytes 3538952 | tf_op jit(solution)/shard_map/ppermute | solution.py:308
  83.3 9.9 %collective-permute-start.25 = (bf16[72,16,128]{2,1,0:T(8,128)(2,1)S(1)}, bf16[72,16,128]{2,1,0:T(8,128)(2,1)S(1)}, u32[]{:S(2)}, u32[]{:S(2)}) collective-permute-start(bf16[72,16,128]{2,1,0:T(8,128)(2,1)S(1)} %get-tuple-element.158), channel_id=1, source_target_pairs={{0,8},{4,12},{8,0},{12,4},{16,24},{20,28},{24,16},{28,20},{1,9},{5... | collective-permute-start | bytes 884744 | tf_op jit(solution)/shard_map/ppermute | solution.py:317
  84.9 15.1 %collective-permute-start.26 = (bf16[72,16,128]{2,1,0:T(8,128)(2,1)S(1)}, bf16[72,16,128]{2,1,0:T(8,128)(2,1)S(1)}, u32[]{:S(2)}, u32[]{:S(2)}) collective-permute-start(bf16[72,16,128]{2,1,0:T(8,128)(2,1)S(1)} %get-tuple-element.159), channel_id=1, source_target_pairs={{0,16},{4,20},{8,24},{12,28},{16,0},{20,4},{24,8},{28,12},{1,17},{... | collective-permute-start | bytes 884744 | tf_op jit(solution)/shard_map/ppermute | solution.py:317
  86.4 13.6 %collective-permute-start.27 = (bf16[72,16,128]{2,1,0:T(8,128)(2,1)S(1)}, bf16[72,16,128]{2,1,0:T(8,128)(2,1)S(1)}, u32[]{:S(2)}, u32[]{:S(2)}) collective-permute-start(bf16[72,16,128]{2,1,0:T(8,128)(2,1)S(1)} %get-tuple-element.160), channel_id=1, source_target_pairs={{0,24},{4,28},{8,16},{12,20},{16,8},{20,12},{24,0},{28,4},{1,25},{... | collective-permute-start | bytes 884744 | tf_op jit(solution)/shard_map/ppermute | solution.py:317

commit v2 on v1

v2 whole, which is shorter than its diff:
```python
import functools

import jax
import jax.numpy as jnp
from jax import lax
from jax.experimental import pallas as pl
from jax.experimental.pallas import tpu as pltpu
from jax.sharding import PartitionSpec as P

NMB = 4
EPS = 1e-06
F32 = jnp.float32
BF16 = jnp.bfloat16
VM = pltpu.VMEM
HBM = pltpu.HBM
ANY = pl.ANY
LIMIT = 20 * 1024 * 1024
CHUNKS = 4


def call(body, outs, ins, scratch=(), aliases=None, flops=10**8, nbytes=3 * 10**6):
    arrays, in_specs = [], []
    for array, space in ins:
        arrays.append(array if space is ANY else pltpu.with_memory_space_constraint(array, space))
        in_specs.append(pl.BlockSpec(memory_space=space))
    out_shape, out_specs = [], []
    for shape, dtype, space in outs:
        out_shape.append(jax.ShapeDtypeStruct(shape, dtype) if space is ANY else space(shape, dtype))
        out_specs.append(pl.BlockSpec(memory_space=space))
    return pl.pallas_call(
        body,
        out_shape=out_shape,
        in_specs=in_specs,
        out_specs=out_specs,
        scratch_shapes=list(scratch),
        input_output_aliases=aliases or {},
        compiler_params=pltpu.CompilerParams(vmem_limit_bytes=LIMIT),
        cost_estimate=pl.CostEstimate(flops=flops, bytes_accessed=nbytes, transcendentals=0),
    )(*arrays)


def columns(n, blk):
    return slice(n * blk, (n + 1) * blk)


def norm(hf):
    return lax.rsqrt(jnp.mean(hf * hf, axis=1, keepdims=True) + EPS)


def fetch_rows(rows_v, rows, sem):
    copy = pltpu.make_async_copy(rows_v, rows, sem)
    copy.start()
    return copy


def normalise(hf, u3, nb, blk):
    scale = norm(hf)
    for n in range(nb):
        u3[n] = (hf[:, columns(n, blk)] * scale).astype(BF16)
    return scale


def mix(n, rows, tiles, u3, kpc, blk):
    x = jnp.concatenate([u3[rows[0, n * kpc + k]] for k in range(kpc)], axis=1)
    w = tiles[n * kpc : (n + 1) * kpc].reshape(kpc * blk, blk)
    return jnp.tanh(jnp.dot(x, w, preferred_element_type=F32))


def start_body(nb, kpc, blk, tiles, rows_h, feed, tiles_v, rows_v, kh, kd, kz, hout, u3, rows, sems):
    M, R, E = kh.shape
    nt = tiles_v.shape[0]
    step = nt // CHUNKS
    first = lax.axis_index("section") == 0
    row_copies = [
        pltpu.make_async_copy(rows_h, rows_v, sems.at[CHUNKS]),
        pltpu.make_async_copy(rows_h, rows, sems.at[CHUNKS + 1]),
    ]
    feeds = [
        pltpu.make_async_copy(feed.at[pl.ds(m * R, R)], kh.at[m], sems.at[CHUNKS + 2 + m]) for m in range(M)
    ]
    loads = [
        pltpu.make_async_copy(tiles.at[0, pl.ds(c * step, step)], tiles_v.at[pl.ds(c * step, step)], sems.at[c])
        for c in range(CHUNKS)
    ]

    @pl.when(first)
    def _():
        feeds[0].start()

    for c in row_copies:
        c.start()
    for c in loads:
        c.start()

    @pl.when(first)
    def _():
        for m in range(1, M):
            feeds[m].start()
        feeds[0].wait()
        hf = kh[0].astype(F32)
        normalise(hf, u3, nb, blk)

    for c in row_copies:
        c.wait()
    for c in range(CHUNKS):
        loads[c].wait()

        @pl.when(first)
        def _():
            for n in range(c * nb // CHUNKS, (c + 1) * nb // CHUNKS):
                a = mix(n, rows, tiles_v, u3, kpc, blk)
                s = columns(n, blk)
                hout[:, s] = (kh[0, :, s].astype(F32) + a).astype(BF16)
                kd[0, :, s] = 1.0 - a * a

    @pl.when(first)
    def _():
        for m in range(1, M):
            feeds[m].wait()


def forward_body(s, m, nb, kpc, blk, *refs):
    if s == 0:
        rows_v, tiles, kh, kd_in, hout, kd, u3, rows, sem = refs
    else:
        rows_v, tiles, hin, kh_in, kd_in, hout, kh, kd, u3, rows, sem = refs

    @pl.when(lax.axis_index("section") == s)
    def _():
        copy = fetch_rows(rows_v, rows, sem)
        if s == 0:
            h = kh[m]
        else:
            h = hin[...]
            kh[m] = h
        hf = h.astype(F32)
        normalise(hf, u3, nb, blk)
        copy.wait()
        for n in range(nb):
            a = mix(n, rows, tiles, u3, kpc, blk)
            c = columns(n, blk)
            hout[:, c] = (hf[:, c] + a).astype(BF16)
            kd[m, :, c] = 1.0 - a * a


def spread(rows, tiles, dz, v3, nb, kpc, blk):
    v3[...] = jnp.zeros_like(v3)
    for n in range(nb):
        w = tiles[n * kpc : (n + 1) * kpc].reshape(kpc * blk, blk)
        back = lax.dot_general(dz(n), w, (((1,), (1,)), ((), ())), preferred_element_type=F32)
        for k in range(kpc):
            r = rows[0, n * kpc + k]
            v3[r] = v3[r] + back[:, columns(k, blk)]


def finish(h, g, v3, gout, nb, blk):
    hf = h[...].astype(F32)
    scale = norm(hf)
    total = jnp.zeros((hf.shape[0], blk), F32)
    for n in range(nb):
        total = total + v3[n] * (hf[:, columns(n, blk)] * scale)
    inner = jnp.sum(total, axis=1, keepdims=True) * (1.0 / (nb * blk))
    for n in range(nb):
        c = columns(n, blk)
        q = hf[:, c] * scale
        gout[:, c] = (g[:, c].astype(F32) + scale * (v3[n] - q * inner)).astype(BF16)


def turn_body(s, m, nb, kpc, blk, rows_v, tiles, hin, seeds, kh_in, kd_in, kz_in, gout, kh, kd, kz, u3, v3, rows, sem):
    @pl.when(lax.axis_index("section") == s)
    def _():
        copy = fetch_rows(rows_v, rows, sem)
        R = gout.shape[0]
        h = hin[...]
        kh[m] = h
        hf = h.astype(F32)
        normalise(hf, u3, nb, blk)
        g = seeds.at[pl.ds(m * R, R)]
        copy.wait()
        for n in range(nb):
            a = mix(n, rows, tiles, u3, kpc, blk)
            c = columns(n, blk)
            kz[m, :, c] = (g[:, c].astype(F32) * (1.0 - a * a)).astype(BF16)
        spread(rows, tiles, lambda n: kz[m, :, columns(n, blk)], v3, nb, kpc, blk)
        finish(kh.at[m], g, v3, gout, nb, blk)


def backward_body(s, m, nb, kpc, blk, rows_v, tiles, gin, kh, kd, kz_in, gout, kz, v3, rows, sem):
    @pl.when(lax.axis_index("section") == s)
    def _():
        copy = fetch_rows(rows_v, rows, sem)
        for n in range(nb):
            c = columns(n, blk)
            kz[m, :, c] = (gin[:, c].astype(F32) * kd[m, :, c]).astype(BF16)
        copy.wait()
        spread(rows, tiles, lambda n: kz[m, :, columns(n, blk)], v3, nb, kpc, blk)
        finish(kh.at[m], gin, v3, gout, nb, blk)


def first_body(m, gin, kd, kz_in, kz, zs):
    section = lax.axis_index("section")

    @pl.when(section == 0)
    def _():
        z = (gin[...].astype(F32) * kd[m]).astype(BF16)
        kz[m] = z
        zs[...] = z

    @pl.when(section != 0)
    def _():
        zs[...] = kz[m]


def turned_body(nb, blk, half, parts, kh, keep, send, uT):
    M, R, E = kh.shape
    hf = kh[...].reshape(M * R, E).astype(F32)
    scale = norm(hf)
    me = lax.axis_index("dp") % 2
    for n in range(nb):
        u = (hf[:, columns(n, blk)] * scale).astype(BF16).astype(F32)
        uT[n] = u.T.astype(BF16).reshape(parts, 2, half, M * R)
        for j in range(parts):
            keep[n, j] = uT[n, j, me]
            send[n, j] = uT[n, j, 1 - me]


def term_body(js, M, nb, kpc, blk, half, rows_v, keep, got, kz, *refs):
    zgot, outs, (rows, sem) = refs[:M], refs[M : M + len(js)], refs[M + len(js) :]
    copy = fetch_rows(rows_v, rows, sem)
    chip = lax.axis_index("dp") // 2
    copy.wait()
    for n in range(nb):
        c = columns(n, blk)
        z = jnp.concatenate([kz[m, :, c] for m in range(M)] + [zgot[m][:, c] for m in range(M)], axis=0)
        pieces = []
        for k in range(kpc):
            r = rows[0, n * kpc + k]
            for j in js:
                pieces.append(jnp.concatenate([keep[r, chip ^ j], got[r, chip ^ j]], axis=1))
        term = jnp.dot(jnp.concatenate(pieces, axis=0), z, preferred_element_type=F32)
        for k in range(kpc):
            for i in range(len(js)):
                at = (k * len(js) + i) * half
                outs[i][n * kpc + k] = term[at : at + half].astype(outs[i].dtype)


def final_body(parts, *refs):
    ins, (out, buf, sems) = refs[:parts], refs[parts:]
    nt = ins[0].shape[0]
    step = 24 if nt % 24 == 0 else nt
    stores = []
    for t in range(nt):
        total = ins[0][t].astype(F32)
        for j in range(1, parts):
            total = total + ins[j][t].astype(F32)
        buf[:, t, :] = total
        if (t + 1) % step == 0:
            at = pl.ds(t + 1 - step, step)
            c = pltpu.make_async_copy(buf.at[:, at], out.at[:, 0, at], sems.at[t // step])
            c.start()
            stores.append(c)
    for c in stores:
        c.wait()


def local(inputs, tiles, tile_rows, out_grad):
    sections = lax.axis_size("section")
    groups = lax.axis_size("dp")
    nt, blk = tiles.shape[1], tiles.shape[-1]
    E = inputs.shape[1]
    nb = E // blk
    kpc = nt // nb
    total = inputs.shape[0]
    M = NMB
    R = total // M
    dma = pltpu.SemaphoreType.DMA

    kh_s, kd_s, kz_s = ((M, R, E), BF16, VM), ((M, R, E), F32, VM), ((M, R, E), BF16, VM)
    u3 = pltpu.VMEM((nb, R, blk), BF16)
    v3 = pltpu.VMEM((nb, R, blk), F32)
    rows_s = pltpu.SMEM((1, nt), jnp.int32)
    line = ((R, E), BF16, VM)
    last = sections - 1

    tiles_v, rows, kh, kd, kz, out = call(
        functools.partial(start_body, nb, kpc, blk),
        [((nt, blk, blk), BF16, VM), ((1, nt), jnp.int32, VM), kh_s, kd_s, kz_s, line],
        [(tiles, HBM), (tile_rows, HBM), (inputs, HBM)],
        [u3, rows_s, dma((CHUNKS + 2 + M,))],
    )

    def hop(array, a, b):
        return lax.ppermute(array, "section", [(a, b)])

    arrived = [[] for s in range(sections)]
    back = []
    for s in range(last):
        for m in range(M):
            if s == 0 and m > 0:
                out, kd = call(
                    functools.partial(forward_body, s, m, nb, kpc, blk),
                    [line, kd_s],
                    [(rows, VM), (tiles_v, VM), (kh, VM), (kd, VM)],
                    [u3, rows_s, dma],
                    {3: 1},
                )
            elif s > 0:
                out, kh, kd = call(
                    functools.partial(forward_body, s, m, nb, kpc, blk),
                    [line, kh_s, kd_s],
                    [(rows, VM), (tiles_v, VM), (arrived[s][m], VM), (kh, VM), (kd, VM)],
                    [u3, rows_s, dma],
                    {3: 1, 4: 2},
                )
            arrived[s + 1].append(hop(out, s, s + 1))
            for turning in [m - 1] * (s == last - 1 and m > 0) + [m] * (s == last - 1 and m == M - 1):
                out, kh, kd, kz = call(
                    functools.partial(turn_body, last, turning, nb, kpc, blk),
                    [line, kh_s, kd_s, kz_s],
                    [(rows, VM), (tiles_v, VM), (arrived[last][turning], VM), (out_grad, VM)]
                    + [(kh, VM), (kd, VM), (kz, VM)],
                    [u3, v3, rows_s, dma],
                    {4: 1, 5: 2, 6: 3},
                )
                back.append(hop(out, last, last - 1))
    for s in range(last - 1, 0, -1):
        sent = []
        for m in range(M):
            out, kz = call(
                functools.partial(backward_body, s, m, nb, kpc, blk),
                [line, kz_s],
                [(rows, VM), (tiles_v, VM), (back[m], VM), (kh, VM), (kd, VM), (kz, VM)],
                [v3, rows_s, dma],
                {5: 1},
            )
            sent.append(hop(out, s, s - 1))
        back = sent

    half = blk // groups
    direct = half % 16 == 0 and groups % 2 == 0
    swap = [(i, i ^ 1) for i in range(groups)]
    if direct:
        parts = groups // 2
        turned = ((nb, parts, half, total), BF16, VM)
        keep, send = call(
            functools.partial(turned_body, nb, blk, half, parts),
            [turned, turned],
            [(kh, VM)],
            [pltpu.VMEM((nb, parts, 2, half, total), BF16)],
        )
        got = lax.ppermute(send, "dp", swap)
    zgot = []
    for m in range(M):
        kz, z = call(
            functools.partial(first_body, m), [kz_s, line], [(back[m], VM), (kd, VM), (kz, VM)], [], {2: 0}
        )
        if direct:
            zgot.append(lax.ppermute(z, "dp", swap))
    if direct:
        piece = (nt, half, blk)

        def term(js, dtypes):
            return call(
                functools.partial(term_body, js, M, nb, kpc, blk, half),
                [(piece, d, VM) for d in dtypes],
                [(rows, VM), (keep, VM), (got, VM), (kz, VM)] + [(z, VM) for z in zgot],
                [rows_s, dma],
            )

        *sends, mine = term(list(range(1, parts)) + [0], [BF16] * (parts - 1) + [F32])
        ready = [mine] + [
            lax.ppermute(sends[j - 1], "dp", [(i, i ^ (2 * j)) for i in range(groups)]) for j in range(1, parts)
        ]
        (out,) = call(
            functools.partial(final_body, parts),
            [((half, 1, nt, blk), F32, HBM)],
            [(r, VM) for r in ready],
            [pltpu.VMEM((half, nt, blk), F32), dma((max(1, nt // 24),))],
        )
        return out
    hf = kh.reshape(total, E).astype(F32)
    low = (hf * norm(hf)).astype(BF16)
    picked = jnp.take(low.reshape(total, nb, blk), tile_rows[0], axis=1).reshape(total, nb, kpc, blk)
    term = jnp.einsum("mnkr,mnc->rnkc", picked, kz.reshape(total, nb, blk), preferred_element_type=F32)
    return lax.psum_scatter(term.reshape(blk, 1, nt, blk), "dp", scatter_dimension=0, tiled=True)


def solution(mesh):
    return jax.shard_map(
        local,
        mesh=mesh,
        in_specs=(P("dp", None), P("section", None, None, None), P("section", None), P("dp", None)),
        out_specs=P("dp", "section", None, None),
        check_vma=False,
    )
```

time: 102 us -> 98 us (0.961)
  Pallas kernels: 24.5 us -> 9.36 us
  waiting for transfers between devices: 46.1 us -> 58.3 us
  local copies, waits for them, and re-layouts: 3.06 us -> 0.01 us
  starting transfers between devices: 27.2 us -> 29.2 us
    pallas_call x32 -> x31, Pallas kernels: 24.5 us -> 9.36 us  [call(): pl.pallas_call(body, out_shape=out_shape, in_specs=in_specs, out_specs=ou...]
    ppermute x28 -> x32, waiting for transfers between devices: 46.1 us -> 58.3 us  [the longest x24 43.9 us: hop(): return lax.ppermute(array, 'section', [(a, b)])]
    unnamed x9 -> x2, local copies, waits for them, and re-layouts: 3.06 us -> 0.01 us
    ppermute x28 -> x32, starting transfers between devices: 27.2 us -> 29.2 us  [the longest x24 24.4 us: hop(): return lax.ppermute(array, 'section', [(a, b)])]
  transfers between devices with their start and end apart: 28 -> 32, of which waited for: 9 -> 11; matrix products, arithmetic and copies ran while one was open for 0% -> 0% of each run, Pallas kernels for 18% -> 5%
where the time goes in v2:
time: 98 us; the launch traced here: 97.6 us
  waiting for transfers between devices  58.3 us (59%)
  starting transfers between devices  29.2 us (30%)
  Pallas kernels  9.36 us (10%)
    ppermute x24, waiting for transfers between devices, hop(): return lax.ppermute(array, 'section', [(a, b)])  43.9 us
    ppermute x24, starting transfers between devices, hop(): return lax.ppermute(array, 'section', [(a, b)])  24.4 us
    ppermute x3, waiting for transfers between devices, local(): lax.ppermute(sends[j - 1], 'dp', [(i, i ^ 2 * j) for i in range(groups)])  13.2 us
    pallas_call x31, Pallas kernels, call(): pl.pallas_call(body, out_shape=out_shape, in_specs=in_specs, out_specs=ou...  9.36 us
    ppermute x3, starting transfers between devices, local(): lax.ppermute(sends[j - 1], 'dp', [(i, i ^ 2 * j) for i in range(groups)])  3.55 us
  transfers between devices with their start and end apart: 32, of which 11 were waited for; matrix products, arithmetic and copies ran while one was open for 0% of the time, Pallas kernels for 5%

profile of v2, /device:TPU:0, one launch (start us, length us, event | category | flops | bytes accessed | tf_op | source)
XLA Modules:
  0.0 97.6 jit_solution(9430187490167558521)
XLA Ops:
  0.0 2.2 %shard_map.46 = (bf16[72,128,128]{2,1,0:T(8,128)(2,1)S(1)}, s32[1,72]{1,0:T(1,128)S(1)}, bf16[4,32,3072]{2,1,0:T(8,128)(2,1)S(1)}, f32[4,32,3072]{2,1,0:T(8,128)...) custom-call(bf16[1,72,128,128]{3,2,1,0:T(8,128)(2,1)} %tiles.1, s32[1,72]{1,0:T(1,128)} %rows_h.1, ...), custom_call_target="tpu_custom_call" | custom-call | flops 100000000 | bytes 3000000 | tf_op jit(solution)/shard_map/pallas_call | solution.py:30
  2.2 4.4 %collective-permute-start.3 = (bf16[32,3072]{1,0:T(8,128)(2,1)S(1)}, bf16[32,3072]{1,0:T(8,128)(2,1)S(1)}, u32[]{:S(2)}, u32[]{:S(2)}) collective-permute-start(bf16[32,3072]{1,0:T(8,128)(2,1)S(1)} %get-tuple-element.96), channel_id=1, source_target_pairs={{0,1},{4,5},{8,9},{12,13},{16,17},{20,21},{24,25},{28,29}} | collective-permute-start | bytes 589832 | tf_op jit(solution)/shard_map/ppermute | solution.py:293
  6.7 1.1 %shard_map.47 = (bf16[32,3072]{1,0:T(8,128)(2,1)S(1)}, f32[4,32,3072]{2,1,0:T(8,128)S(1)}) custom-call(s32[1,72]{1,0:T(1,128)S(1)} %get-tuple-element.87.refs_0_.rows_v, bf16[72,128,128]{2,1,0:T(8,128)(2,1)S(1)} %get-tuple-element.88.refs_1_.tiles, bf16[4,32,3072]{2,1,0:T(8,128)(2,1)S(1)} %get-tuple-element.89.refs_2_.refs_3_, ...), custom_call_target="tpu_custom_call", output_to_operand_aliasing={{1}: (3, {})} | custom-call | flops 100000000 | bytes 3000000 | tf_op jit(solution)/shard_map/pallas_call | solution.py:30
  7.8 1.3 %collective-permute-start.2 = (bf16[32,3072]{1,0:T(8,128)(2,1)S(1)}, bf16[32,3072]{1,0:T(8,128)(2,1)S(1)}, u32[]{:S(2)}, u32[]{:S(2)}) collective-permute-start(bf16[32,3072]{1,0:T(8,128)(2,1)S(1)} %get-tuple-element.95), channel_id=1, source_target_pairs={{0,1},{4,5},{8,9},{12,13},{16,17},{20,21},{24,25},{28,29}} | collective-permute-start | bytes 589832 | tf_op jit(solution)/shard_map/ppermute | solution.py:293
  9.1 1.1 %shard_map.48 = (bf16[32,3072]{1,0:T(8,128)(2,1)S(1)}, f32[4,32,3072]{2,1,0:T(8,128)S(1)}) custom-call(s32[1,72]{1,0:T(1,128)S(1)} %get-tuple-element.87.refs_0_.rows_v, bf16[72,128,128]{2,1,0:T(8,128)(2,1)S(1)} %get-tuple-element.88.refs_1_.tiles, bf16[4,32,3072]{2,1,0:T(8,128)(2,1)S(1)} %get-tuple-element.89.refs_2_.refs_3_, ...), custom_call_target="tpu_custom_call", output_to_operand_aliasing={{1}: (3, {})} | custom-call | flops 100000000 | bytes 3000000 | tf_op jit(solution)/shard_map/pallas_call | solution.py:30
  10.2 1.3 %collective-permute-start.1 = (bf16[32,3072]{1,0:T(8,128)(2,1)S(1)}, bf16[32,3072]{1,0:T(8,128)(2,1)S(1)}, u32[]{:S(2)}, u32[]{:S(2)}) collective-permute-start(bf16[32,3072]{1,0:T(8,128)(2,1)S(1)} %get-tuple-element.94), channel_id=1, source_target_pairs={{0,1},{4,5},{8,9},{12,13},{16,17},{20,21},{24,25},{28,29}} | collective-permute-start | bytes 589832 | tf_op jit(solution)/shard_map/ppermute | solution.py:293
  11.5 1.1 %shard_map.49 = (bf16[32,3072]{1,0:T(8,128)(2,1)S(1)}, f32[4,32,3072]{2,1,0:T(8,128)S(1)}) custom-call(s32[1,72]{1,0:T(1,128)S(1)} %get-tuple-element.87.refs_0_.rows_v, bf16[72,128,128]{2,1,0:T(8,128)(2,1)S(1)} %get-tuple-element.88.refs_1_.tiles, bf16[4,32,3072]{2,1,0:T(8,128)(2,1)S(1)} %get-tuple-element.89.refs_2_.refs_3_, ...), custom_call_target="tpu_custom_call", output_to_operand_aliasing={{1}: (3, {})} | custom-call | flops 100000000 | bytes 3000000 | tf_op jit(solution)/shard_map/pallas_call | solution.py:30
  12.6 1.3 %collective-permute-start = (bf16[32,3072]{1,0:T(8,128)(2,1)S(1)}, bf16[32,3072]{1,0:T(8,128)(2,1)S(1)}, u32[]{:S(2)}, u32[]{:S(2)}) collective-permute-start(bf16[32,3072]{1,0:T(8,128)(2,1)S(1)} %get-tuple-element.93), channel_id=1, source_target_pairs={{0,1},{4,5},{8,9},{12,13},{16,17},{20,21},{24,25},{28,29}} | collective-permute-start | bytes 589832 | tf_op jit(solution)/shard_map/ppermute | solution.py:293
  14.0 0.7 collective-permute-start.6
  14.6 1.5 %collective-permute-done.2.refs_2_ = bf16[32,3072]{1,0:T(8,128)(2,1)S(1)} collective-permute-done((bf16[32,3072]{1,0:T(8,128)(2,1)S(1)}, bf16[32,3072]{1,0:T(8,128)(2,1)S(1)}, u32[]{:S(2)}, u32[]{:S(2)}) %collective-permute-start.2) | collective-permute-done | bytes 196640 | tf_op jit(solution)/shard_map/ppermute | solution.py:293
  16.2 0.7 collective-permute-start.5
  16.8 3.5 %collective-permute-done.1.refs_2_ = bf16[32,3072]{1,0:T(8,128)(2,1)S(1)} collective-permute-done((bf16[32,3072]{1,0:T(8,128)(2,1)S(1)}, bf16[32,3072]{1,0:T(8,128)(2,1)S(1)}, u32[]{:S(2)}, u32[]{:S(2)}) %collective-permute-start.1) | collective-permute-done | bytes 196640 | tf_op jit(solution)/shard_map/ppermute | solution.py:293
  20.4 3.0 %collective-permute-done.refs_2_ = bf16[32,3072]{1,0:T(8,128)(2,1)S(1)} collective-permute-done((bf16[32,3072]{1,0:T(8,128)(2,1)S(1)}, bf16[32,3072]{1,0:T(8,128)(2,1)S(1)}, u32[]{:S(2)}, u32[]{:S(2)}) %collective-permute-start) | collective-permute-done | bytes 196640 | tf_op jit(solution)/shard_map/ppermute | solution.py:293
  23.5 0.7 collective-permute-start.9
  24.2 0.7 collective-permute-start.8
  24.9 0.8 collective-permute-start.7
  25.7 0.7 collective-permute-start.4
  26.5 0.7 collective-permute-start.11
  27.3 0.7 collective-permute-start.10
  27.9 0.7 collective-permute-start.16
  28.6 0.7 collective-permute-start.15
  29.3 0.2 shard_map.60
  29.5 0.7 collective-permute-start.14
  30.2 0.7 collective-permute-start.13
  31.0 0.7 collective-permute-start.20
  31.7 0.7 collective-permute-start.19
  32.4 0.7 collective-permute-start.18
  33.1 0.7 collective-permute-start.17
  33.9 1.3 %collective-permute-start.24 = (bf16[32,3072]{1,0:T(8,128)(2,1)S(1)}, bf16[32,3072]{1,0:T(8,128)(2,1)S(1)}, u32[]{:S(2)}, u32[]{:S(2)}) collective-permute-start(bf16[32,3072]{1,0:T(8,128)(2,1)S(1)} %get-tuple-element.155), channel_id=1, source_target_pairs={{1,0},{5,4},{9,8},{13,12},{17,16},{21,20},{25,24},{29,28}} | collective-permute-start | bytes 589832 | tf_op jit(solution)/shard_map/ppermute | solution.py:293
  35.2 1.3 %collective-permute-start.23 = (bf16[32,3072]{1,0:T(8,128)(2,1)S(1)}, bf16[32,3072]{1,0:T(8,128)(2,1)S(1)}, u32[]{:S(2)}, u32[]{:S(2)}) collective-permute-start(bf16[32,3072]{1,0:T(8,128)(2,1)S(1)} %get-tuple-element.154), channel_id=1, source_target_pairs={{1,0},{5,4},{9,8},{13,12},{17,16},{21,20},{25,24},{29,28}} | collective-permute-start | bytes 589832 | tf_op jit(solution)/shard_map/ppermute | solution.py:293
  36.5 1.3 %collective-permute-start.22 = (bf16[32,3072]{1,0:T(8,128)(2,1)S(1)}, bf16[32,3072]{1,0:T(8,128)(2,1)S(1)}, u32[]{:S(2)}, u32[]{:S(2)}) collective-permute-start(bf16[32,3072]{1,0:T(8,128)(2,1)S(1)} %get-tuple-element.153), channel_id=1, source_target_pairs={{1,0},{5,4},{9,8},{13,12},{17,16},{21,20},{25,24},{29,28}} | collective-permute-start | bytes 589832 | tf_op jit(solution)/shard_map/ppermute | solution.py:293
  37.9 1.3 %collective-permute-start.21 = (bf16[32,3072]{1,0:T(8,128)(2,1)S(1)}, bf16[32,3072]{1,0:T(8,128)(2,1)S(1)}, u32[]{:S(2)}, u32[]{:S(2)}) collective-permute-start(bf16[32,3072]{1,0:T(8,128)(2,1)S(1)} %get-tuple-element.152), channel_id=1, source_target_pairs={{1,0},{5,4},{9,8},{13,12},{17,16},{21,20},{25,24},{29,28}} | collective-permute-start | bytes 589832 | tf_op jit(solution)/shard_map/ppermute | solution.py:293
  39.2 0.6 shard_map.62
  39.9 25.4 %collective-permute-done.24.gin = bf16[32,3072]{1,0:T(8,128)(2,1)S(1)} collective-permute-done((bf16[32,3072]{1,0:T(8,128)(2,1)S(1)}, bf16[32,3072]{1,0:T(8,128)(2,1)S(1)}, u32[]{:S(2)}, u32[]{:S(2)}) %collective-permute-start.24) | collective-permute-done | bytes 196640 | tf_op jit(solution)/shard_map/ppermute | solution.py:293
  65.3 3.8 %collective-permute-done.23.gin = bf16[32,3072]{1,0:T(8,128)(2,1)S(1)} collective-permute-done((bf16[32,3072]{1,0:T(8,128)(2,1)S(1)}, bf16[32,3072]{1,0:T(8,128)(2,1)S(1)}, u32[]{:S(2)}, u32[]{:S(2)}) %collective-permute-start.23) | collective-permute-done | bytes 196640 | tf_op jit(solution)/shard_map/ppermute | solution.py:293
  69.3 0.5 collective-permute-start.25
  69.8 3.9 %collective-permute-done.22.gin = bf16[32,3072]{1,0:T(8,128)(2,1)S(1)} collective-permute-done((bf16[32,3072]{1,0:T(8,128)(2,1)S(1)}, bf16[32,3072]{1,0:T(8,128)(2,1)S(1)}, u32[]{:S(2)}, u32[]{:S(2)}) %collective-permute-start.22) | collective-permute-done | bytes 196640 | tf_op jit(solution)/shard_map/ppermute | solution.py:293
  73.7 2.7 %collective-permute-done.21.gin = bf16[32,3072]{1,0:T(8,128)(2,1)S(1)} collective-permute-done((bf16[32,3072]{1,0:T(8,128)(2,1)S(1)}, bf16[32,3072]{1,0:T(8,128)(2,1)S(1)}, u32[]{:S(2)}, u32[]{:S(2)}) %collective-permute-start.21) | collective-permute-done | bytes 196640 | tf_op jit(solution)/shard_map/ppermute | solution.py:293
  76.5 0.5 collective-permute-start.27
  77.0 0.9 collective-permute-done.28.refs_3_
  77.9 0.3 collective-permute-done.27.refs_2_
  78.2 1.3 %shard_map.75 = (bf16[72,16,128]{2,1,0:T(8,128)(2,1)S(1)}, bf16[72,16,128]{2,1,0:T(8,128)(2,1)S(1)}, bf16[72,16,128]{2,1,0:T(8,128)(2,1)S(1)}, f32[72,16,128]{2,1,0:T(8,128)S(1)}) custom-call(s32[1,72]{1,0:T(1,128)S(1)} %get-tuple-element.87.refs_0_.rows_v, bf16[24,4,16,128]{3,2,1,0:T(8,128)(2,1)S(1)} %get-tuple-element.133.keep, ...), custom_call_target="tpu_custom_call" | custom-call | flops 100000000 | bytes 3000000 | tf_op jit(solution)/shard_map/pallas_call | solution.py:30
  79.6 1.6 %collective-permute-start.29 = (bf16[72,16,128]{2,1,0:T(8,128)(2,1)S(1)}, bf16[72,16,128]{2,1,0:T(8,128)(2,1)S(1)}, u32[]{:S(2)}, u32[]{:S(2)}) collective-permute-start(bf16[72,16,128]{2,1,0:T(8,128)(2,1)S(1)} %get-tuple-element.166), channel_id=1, source_target_pairs={{0,8},{4,12},{8,0},{12,4},{16,24},{20,28},{24,16},{28,20},{1,9},{5... | collective-permute-start | bytes 884744 | tf_op jit(solution)/shard_map/ppermute | solution.py:372
  81.1 1.5 %collective-permute-start.30 = (bf16[72,16,128]{2,1,0:T(8,128)(2,1)S(1)}, bf16[72,16,128]{2,1,0:T(8,128)(2,1)S(1)}, u32[]{:S(2)}, u32[]{:S(2)}) collective-permute-start(bf16[72,16,128]{2,1,0:T(8,128)(2,1)S(1)} %get-tuple-element.167), channel_id=1, source_target_pairs={{0,16},{4,20},{8,24},{12,28},{16,0},{20,4},{24,8},{28,12},{1,17},{... | collective-permute-start | bytes 884744 | tf_op jit(solution)/shard_map/ppermute | solution.py:372
  82.6 0.5 collective-permute-start.31
  83.1 6.3 %collective-permute-done.29.refs_1_ = bf16[72,16,128]{2,1,0:T(8,128)(2,1)S(1)} collective-permute-done((bf16[72,16,128]{2,1,0:T(8,128)(2,1)S(1)}, bf16[72,16,128]{2,1,0:T(8,128)(2,1)S(1)}, u32[]{:S(2)}, u32[]{:S(2)}) %collective-permute-start.29) | collective-permute-done | bytes 294944 | tf_op jit(solution)/shard_map/ppermute | solution.py:372
  89.5 6.8 %collective-permute-done.30.refs_2_ = bf16[72,16,128]{2,1,0:T(8,128)(2,1)S(1)} collective-permute-done((bf16[72,16,128]{2,1,0:T(8,128)(2,1)S(1)}, bf16[72,16,128]{2,1,0:T(8,128)(2,1)S(1)}, u32[]{:S(2)}, u32[]{:S(2)}) %collective-permute-start.30) | collective-permute-done | bytes 294944 | tf_op jit(solution)/shard_map/ppermute | solution.py:372
  96.3 1.1 %shard_map.76 = f32[16,1,72,128]{3,2,1,0:T(8,128)} custom-call(f32[72,16,128]{2,1,0:T(8,128)S(1)} %get-tuple-element.165.refs_0_, bf16[72,16,128]{2,1,0:T(8,128)(2,1)S(1)} %collective-permute-done.29.refs_1_, bf16[72,16,128]{2,1,0:T(8,128)(2,1)S(1)} %collective-permute-done.30.refs_2_, bf16[72,16,128]{2,1,0:T(8,128)(2,1)S(1)} %collective-permute-done.31.refs_3_), custom_call_target="tpu_custom_call" | custom-call | flops 100000000 | bytes 3000000 | tf_op jit(solution)/shard_map/pallas_call | solution.py:30
  (49 shorter events, 0.8 us)
Async XLA Ops:
  2.2 11.7 %collective-permute-start.3 = (bf16[32,3072]{1,0:T(8,128)(2,1)S(1)}, bf16[32,3072]{1,0:T(8,128)(2,1)S(1)}, u32[]{:S(2)}, u32[]{:S(2)}) collective-permute-start(bf16[32,3072]{1,0:T(8,128)(2,1)S(1)} %get-tuple-element.96), channel_id=1, source_target_pairs={{0,1},{4,5},{8,9},{12,13},{16,17},{20,21},{24,25},{28,29}} | collective-permute-start | bytes 589832 | tf_op jit(solution)/shard_map/ppermute | solution.py:293
  7.8 8.4 %collective-permute-start.2 = (bf16[32,3072]{1,0:T(8,128)(2,1)S(1)}, bf16[32,3072]{1,0:T(8,128)(2,1)S(1)}, u32[]{:S(2)}, u32[]{:S(2)}) collective-permute-start(bf16[32,3072]{1,0:T(8,128)(2,1)S(1)} %get-tuple-element.95), channel_id=1, source_target_pairs={{0,1},{4,5},{8,9},{12,13},{16,17},{20,21},{24,25},{28,29}} | collective-permute-start | bytes 589832 | tf_op jit(solution)/shard_map/ppermute | solution.py:293
  10.2 10.2 %collective-permute-start.1 = (bf16[32,3072]{1,0:T(8,128)(2,1)S(1)}, bf16[32,3072]{1,0:T(8,128)(2,1)S(1)}, u32[]{:S(2)}, u32[]{:S(2)}) collective-permute-start(bf16[32,3072]{1,0:T(8,128)(2,1)S(1)} %get-tuple-element.94), channel_id=1, source_target_pairs={{0,1},{4,5},{8,9},{12,13},{16,17},{20,21},{24,25},{28,29}} | collective-permute-start | bytes 589832 | tf_op jit(solution)/shard_map/ppermute | solution.py:293
  12.6 10.8 %collective-permute-start = (bf16[32,3072]{1,0:T(8,128)(2,1)S(1)}, bf16[32,3072]{1,0:T(8,128)(2,1)S(1)}, u32[]{:S(2)}, u32[]{:S(2)}) collective-permute-start(bf16[32,3072]{1,0:T(8,128)(2,1)S(1)} %get-tuple-element.93), channel_id=1, source_target_pairs={{0,1},{4,5},{8,9},{12,13},{16,17},{20,21},{24,25},{28,29}} | collective-permute-start | bytes 589832 | tf_op jit(solution)/shard_map/ppermute | solution.py:293
  14.0 9.5 %collective-permute-start.6 = (bf16[32,3072]{1,0:T(8,128)(2,1)S(1)}, bf16[32,3072]{1,0:T(8,128)(2,1)S(1)}, u32[]{:S(2)}, u32[]{:S(2)}) collective-permute-start(bf16[32,3072]{1,0:T(8,128)(2,1)S(1)} %get-tuple-element.106), channel_id=1, source_target_pairs={{1,2},{5,6},{9,10},{13,14},{17,18},{21,22},{25,26},{29,30}} | collective-permute-start | bytes 589832 | tf_op jit(solution)/shard_map/ppermute | solution.py:293
  16.2 8.7 %collective-permute-start.5 = (bf16[32,3072]{1,0:T(8,128)(2,1)S(1)}, bf16[32,3072]{1,0:T(8,128)(2,1)S(1)}, u32[]{:S(2)}, u32[]{:S(2)}) collective-permute-start(bf16[32,3072]{1,0:T(8,128)(2,1)S(1)} %get-tuple-element.105), channel_id=1, source_target_pairs={{1,2},{5,6},{9,10},{13,14},{17,18},{21,22},{25,26},{29,30}} | collective-permute-start | bytes 589832 | tf_op jit(solution)/shard_map/ppermute | solution.py:293
  23.5 2.9 %collective-permute-start.9 = (bf16[32,3072]{1,0:T(8,128)(2,1)S(1)}, bf16[32,3072]{1,0:T(8,128)(2,1)S(1)}, u32[]{:S(2)}, u32[]{:S(2)}) collective-permute-start(bf16[32,3072]{1,0:T(8,128)(2,1)S(1)} %get-tuple-element.113), channel_id=1, source_target_pairs={{2,3},{6,7},{10,11},{14,15},{18,19},{22,23},{26,27},{30,31}} | collective-permute-start | bytes 589832 | tf_op jit(solution)/shard_map/ppermute | solution.py:293
  24.2 2.3 %collective-permute-start.8 = (bf16[32,3072]{1,0:T(8,128)(2,1)S(1)}, bf16[32,3072]{1,0:T(8,128)(2,1)S(1)}, u32[]{:S(2)}, u32[]{:S(2)}) collective-permute-start(bf16[32,3072]{1,0:T(8,128)(2,1)S(1)} %get-tuple-element.112), channel_id=1, source_target_pairs={{1,2},{5,6},{9,10},{13,14},{17,18},{21,22},{25,26},{29,30}} | collective-permute-start | bytes 589832 | tf_op jit(solution)/shard_map/ppermute | solution.py:293
  24.9 1.5 %copy-start = (bf16[128,3072]{1,0:T(8,128)(2,1)S(1)}, bf16[128,3072]{1,0:T(8,128)(2,1)}, u32[]{:S(2)}) copy-start(bf16[128,3072]{1,0:T(8,128)(2,1)} %seeds.7) | copy-start | bytes 2359300
  24.9 2.3 %collective-permute-start.7 = (bf16[32,3072]{1,0:T(8,128)(2,1)S(1)}, bf16[32,3072]{1,0:T(8,128)(2,1)S(1)}, u32[]{:S(2)}, u32[]{:S(2)}) collective-permute-start(bf16[32,3072]{1,0:T(8,128)(2,1)S(1)} %get-tuple-element.111), channel_id=1, source_target_pairs={{2,3},{6,7},{10,11},{14,15},{18,19},{22,23},{26,27},{30,31}} | collective-permute-start | bytes 589832 | tf_op jit(solution)/shard_map/ppermute | solution.py:293
  25.7 1.5 %collective-permute-start.4 = (bf16[32,3072]{1,0:T(8,128)(2,1)S(1)}, bf16[32,3072]{1,0:T(8,128)(2,1)S(1)}, u32[]{:S(2)}, u32[]{:S(2)}) collective-permute-start(bf16[32,3072]{1,0:T(8,128)(2,1)S(1)} %get-tuple-element.104), channel_id=1, source_target_pairs={{1,2},{5,6},{9,10},{13,14},{17,18},{21,22},{25,26},{29,30}} | collective-permute-start | bytes 589832 | tf_op jit(solution)/shard_map/ppermute | solution.py:293
  26.5 2.8 %collective-permute-start.11 = (bf16[32,3072]{1,0:T(8,128)(2,1)S(1)}, bf16[32,3072]{1,0:T(8,128)(2,1)S(1)}, u32[]{:S(2)}, u32[]{:S(2)}) collective-permute-start(bf16[32,3072]{1,0:T(8,128)(2,1)S(1)} %get-tuple-element.125), channel_id=1, source_target_pairs={{2,3},{6,7},{10,11},{14,15},{18,19},{22,23},{26,27},{30,31}} | collective-permute-start | bytes 589832 | tf_op jit(solution)/shard_map/ppermute | solution.py:293
  27.3 2.9 %collective-permute-start.10 = (bf16[32,3072]{1,0:T(8,128)(2,1)S(1)}, bf16[32,3072]{1,0:T(8,128)(2,1)S(1)}, u32[]{:S(2)}, u32[]{:S(2)}) collective-permute-start(bf16[32,3072]{1,0:T(8,128)(2,1)S(1)} %get-tuple-element.124), channel_id=1, source_target_pairs={{2,3},{6,7},{10,11},{14,15},{18,19},{22,23},{26,27},{30,31}} | collective-permute-start | bytes 589832 | tf_op jit(solution)/shard_map/ppermute | solution.py:293
  27.9 3.0 %collective-permute-start.16 = (bf16[32,3072]{1,0:T(8,128)(2,1)S(1)}, bf16[32,3072]{1,0:T(8,128)(2,1)S(1)}, u32[]{:S(2)}, u32[]{:S(2)}) collective-permute-start(bf16[32,3072]{1,0:T(8,128)(2,1)S(1)} %get-tuple-element.139), channel_id=1, source_target_pairs={{3,2},{7,6},{11,10},{15,14},{19,18},{23,22},{27,26},{31,30}} | collective-permute-start | bytes 589832 | tf_op jit(solution)/shard_map/ppermute | solution.py:293
  28.6 3.0 %collective-permute-start.15 = (bf16[32,3072]{1,0:T(8,128)(2,1)S(1)}, bf16[32,3072]{1,0:T(8,128)(2,1)S(1)}, u32[]{:S(2)}, u32[]{:S(2)}) collective-permute-start(bf16[32,3072]{1,0:T(8,128)(2,1)S(1)} %get-tuple-element.138), channel_id=1, source_target_pairs={{3,2},{7,6},{11,10},{15,14},{19,18},{23,22},{27,26},{31,30}} | collective-permute-start | bytes 589832 | tf_op jit(solution)/shard_map/ppermute | solution.py:293
  29.5 2.9 %collective-permute-start.14 = (bf16[32,3072]{1,0:T(8,128)(2,1)S(1)}, bf16[32,3072]{1,0:T(8,128)(2,1)S(1)}, u32[]{:S(2)}, u32[]{:S(2)}) collective-permute-start(bf16[32,3072]{1,0:T(8,128)(2,1)S(1)} %get-tuple-element.137), channel_id=1, source_target_pairs={{3,2},{7,6},{11,10},{15,14},{19,18},{23,22},{27,26},{31,30}} | collective-permute-start | bytes 589832 | tf_op jit(solution)/shard_map/ppermute | solution.py:293
  30.2 2.9 %collective-permute-start.13 = (bf16[32,3072]{1,0:T(8,128)(2,1)S(1)}, bf16[32,3072]{1,0:T(8,128)(2,1)S(1)}, u32[]{:S(2)}, u32[]{:S(2)}) collective-permute-start(bf16[32,3072]{1,0:T(8,128)(2,1)S(1)} %get-tuple-element.135), channel_id=1, source_target_pairs={{3,2},{7,6},{11,10},{15,14},{19,18},{23,22},{27,26},{31,30}} | collective-permute-start | bytes 589832 | tf_op jit(solution)/shard_map/ppermute | solution.py:293
  31.0 2.9 %collective-permute-start.20 = (bf16[32,3072]{1,0:T(8,128)(2,1)S(1)}, bf16[32,3072]{1,0:T(8,128)(2,1)S(1)}, u32[]{:S(2)}, u32[]{:S(2)}) collective-permute-start(bf16[32,3072]{1,0:T(8,128)(2,1)S(1)} %get-tuple-element.147), channel_id=1, source_target_pairs={{2,1},{6,5},{10,9},{14,13},{18,17},{22,21},{26,25},{30,29}} | collective-permute-start | bytes 589832 | tf_op jit(solution)/shard_map/ppermute | solution.py:293
  31.7 3.5 %collective-permute-start.19 = (bf16[32,3072]{1,0:T(8,128)(2,1)S(1)}, bf16[32,3072]{1,0:T(8,128)(2,1)S(1)}, u32[]{:S(2)}, u32[]{:S(2)}) collective-permute-start(bf16[32,3072]{1,0:T(8,128)(2,1)S(1)} %get-tuple-element.146), channel_id=1, source_target_pairs={{2,1},{6,5},{10,9},{14,13},{18,17},{22,21},{26,25},{30,29}} | collective-permute-start | bytes 589832 | tf_op jit(solution)/shard_map/ppermute | solution.py:293
  32.4 4.1 %collective-permute-start.18 = (bf16[32,3072]{1,0:T(8,128)(2,1)S(1)}, bf16[32,3072]{1,0:T(8,128)(2,1)S(1)}, u32[]{:S(2)}, u32[]{:S(2)}) collective-permute-start(bf16[32,3072]{1,0:T(8,128)(2,1)S(1)} %get-tuple-element.145), channel_id=1, source_target_pairs={{2,1},{6,5},{10,9},{14,13},{18,17},{22,21},{26,25},{30,29}} | collective-permute-start | bytes 589832 | tf_op jit(solution)/shard_map/ppermute | solution.py:293
  33.1 4.7 %collective-permute-start.17 = (bf16[32,3072]{1,0:T(8,128)(2,1)S(1)}, bf16[32,3072]{1,0:T(8,128)(2,1)S(1)}, u32[]{:S(2)}, u32[]{:S(2)}) collective-permute-start(bf16[32,3072]{1,0:T(8,128)(2,1)S(1)} %get-tuple-element.144), channel_id=1, source_target_pairs={{2,1},{6,5},{10,9},{14,13},{18,17},{22,21},{26,25},{30,29}} | collective-permute-start | bytes 589832 | tf_op jit(solution)/shard_map/ppermute | solution.py:293
  33.9 31.4 %collective-permute-start.24 = (bf16[32,3072]{1,0:T(8,128)(2,1)S(1)}, bf16[32,3072]{1,0:T(8,128)(2,1)S(1)}, u32[]{:S(2)}, u32[]{:S(2)}) collective-permute-start(bf16[32,3072]{1,0:T(8,128)(2,1)S(1)} %get-tuple-element.155), channel_id=1, source_target_pairs={{1,0},{5,4},{9,8},{13,12},{17,16},{21,20},{25,24},{29,28}} | collective-permute-start | bytes 589832 | tf_op jit(solution)/shard_map/ppermute | solution.py:293
  35.2 33.9 %collective-permute-start.23 = (bf16[32,3072]{1,0:T(8,128)(2,1)S(1)}, bf16[32,3072]{1,0:T(8,128)(2,1)S(1)}, u32[]{:S(2)}, u32[]{:S(2)}) collective-permute-start(bf16[32,3072]{1,0:T(8,128)(2,1)S(1)} %get-tuple-element.154), channel_id=1, source_target_pairs={{1,0},{5,4},{9,8},{13,12},{17,16},{21,20},{25,24},{29,28}} | collective-permute-start | bytes 589832 | tf_op jit(solution)/shard_map/ppermute | solution.py:293
  36.5 37.1 %collective-permute-start.22 = (bf16[32,3072]{1,0:T(8,128)(2,1)S(1)}, bf16[32,3072]{1,0:T(8,128)(2,1)S(1)}, u32[]{:S(2)}, u32[]{:S(2)}) collective-permute-start(bf16[32,3072]{1,0:T(8,128)(2,1)S(1)} %get-tuple-element.153), channel_id=1, source_target_pairs={{1,0},{5,4},{9,8},{13,12},{17,16},{21,20},{25,24},{29,28}} | collective-permute-start | bytes 589832 | tf_op jit(solution)/shard_map/ppermute | solution.py:293
  37.9 38.5 %collective-permute-start.21 = (bf16[32,3072]{1,0:T(8,128)(2,1)S(1)}, bf16[32,3072]{1,0:T(8,128)(2,1)S(1)}, u32[]{:S(2)}, u32[]{:S(2)}) collective-permute-start(bf16[32,3072]{1,0:T(8,128)(2,1)S(1)} %get-tuple-element.152), channel_id=1, source_target_pairs={{1,0},{5,4},{9,8},{13,12},{17,16},{21,20},{25,24},{29,28}} | collective-permute-start | bytes 589832 | tf_op jit(solution)/shard_map/ppermute | solution.py:293
  39.8 37.2 %collective-permute-start.12 = (bf16[24,4,16,128]{3,2,1,0:T(8,128)(2,1)S(1)}, bf16[24,4,16,128]{3,2,1,0:T(8,128)(2,1)S(1)}, u32[]{:S(2)}, u32[]{:S(2)}) collective-permute-start(bf16[24,4,16,128]{3,2,1,0:T(8,128)(2,1)S(1)} %get-tuple-element.134), channel_id=1, source_target_pairs={{0,4},{4,0},{8,12},{12,8},{16,20},{20,16},{24,28},{28,24},{1,5},{5... | collective-permute-start | bytes 1179656 | tf_op jit(solution)/shard_map/ppermute | solution.py:351
  69.2 7.8 %collective-permute-start.26 = (bf16[32,3072]{1,0:T(8,128)(2,1)S(1)}, bf16[32,3072]{1,0:T(8,128)(2,1)S(1)}, u32[]{:S(2)}, u32[]{:S(2)}) collective-permute-start(bf16[32,3072]{1,0:T(8,128)(2,1)S(1)} %get-tuple-element.162), channel_id=1, source_target_pairs={{0,4},{4,0},{8,12},{12,8},{16,20},{20,16},{24,28},{28,24},{1,5},{5... | collective-permute-start | bytes 589832 | tf_op jit(solution)/shard_map/ppermute | solution.py:358
  69.3 7.8 %collective-permute-start.25 = (bf16[32,3072]{1,0:T(8,128)(2,1)S(1)}, bf16[32,3072]{1,0:T(8,128)(2,1)S(1)}, u32[]{:S(2)}, u32[]{:S(2)}) collective-permute-start(bf16[32,3072]{1,0:T(8,128)(2,1)S(1)} %get-tuple-element.161), channel_id=1, source_target_pairs={{0,4},{4,0},{8,12},{12,8},{16,20},{20,16},{24,28},{28,24},{1,5},{5... | collective-permute-start | bytes 589832 | tf_op jit(solution)/shard_map/ppermute | solution.py:358
  76.4 1.5 %collective-permute-start.28 = (bf16[32,3072]{1,0:T(8,128)(2,1)S(1)}, bf16[32,3072]{1,0:T(8,128)(2,1)S(1)}, u32[]{:S(2)}, u32[]{:S(2)}) collective-permute-start(bf16[32,3072]{1,0:T(8,128)(2,1)S(1)} %get-tuple-element.164), channel_id=1, source_target_pairs={{0,4},{4,0},{8,12},{12,8},{16,20},{20,16},{24,28},{28,24},{1,5},{5... | collective-permute-start | bytes 589832 | tf_op jit(solution)/shard_map/ppermute | solution.py:358
  76.5 1.7 %collective-permute-start.27 = (bf16[32,3072]{1,0:T(8,128)(2,1)S(1)}, bf16[32,3072]{1,0:T(8,128)(2,1)S(1)}, u32[]{:S(2)}, u32[]{:S(2)}) collective-permute-start(bf16[32,3072]{1,0:T(8,128)(2,1)S(1)} %get-tuple-element.163), channel_id=1, source_target_pairs={{0,4},{4,0},{8,12},{12,8},{16,20},{20,16},{24,28},{28,24},{1,5},{5... | collective-permute-start | bytes 589832 | tf_op jit(solution)/shard_map/ppermute | solution.py:358
  79.6 9.9 %collective-permute-start.29 = (bf16[72,16,128]{2,1,0:T(8,128)(2,1)S(1)}, bf16[72,16,128]{2,1,0:T(8,128)(2,1)S(1)}, u32[]{:S(2)}, u32[]{:S(2)}) collective-permute-start(bf16[72,16,128]{2,1,0:T(8,128)(2,1)S(1)} %get-tuple-element.166), channel_id=1, source_target_pairs={{0,8},{4,12},{8,0},{12,4},{16,24},{20,28},{24,16},{28,20},{1,9},{5... | collective-permute-start | bytes 884744 | tf_op jit(solution)/shard_map/ppermute | solution.py:372
  81.1 15.2 %collective-permute-start.30 = (bf16[72,16,128]{2,1,0:T(8,128)(2,1)S(1)}, bf16[72,16,128]{2,1,0:T(8,128)(2,1)S(1)}, u32[]{:S(2)}, u32[]{:S(2)}) collective-permute-start(bf16[72,16,128]{2,1,0:T(8,128)(2,1)S(1)} %get-tuple-element.167), channel_id=1, source_target_pairs={{0,16},{4,20},{8,24},{12,28},{16,0},{20,4},{24,8},{28,12},{1,17},{... | collective-permute-start | bytes 884744 | tf_op jit(solution)/shard_map/ppermute | solution.py:372
  82.6 13.7 %collective-permute-start.31 = (bf16[72,16,128]{2,1,0:T(8,128)(2,1)S(1)}, bf16[72,16,128]{2,1,0:T(8,128)(2,1)S(1)}, u32[]{:S(2)}, u32[]{:S(2)}) collective-permute-start(bf16[72,16,128]{2,1,0:T(8,128)(2,1)S(1)} %get-tuple-element.168), channel_id=1, source_target_pairs={{0,24},{4,28},{8,16},{12,20},{16,8},{20,12},{24,0},{28,4},{1,25},{... | collective-permute-start | bytes 884744 | tf_op jit(solution)/shard_map/ppermute | solution.py:372

commit v3 on v2

--- a/solution.py
+++ b/solution.py
@@ -16,6 +16,7 @@
 ANY = pl.ANY
 LIMIT = 20 * 1024 * 1024
 CHUNKS = 4
+MEET = 1
 
 
 def call(body, outs, ins, scratch=(), aliases=None, flops=10**8, nbytes=3 * 10**6):
@@ -66,81 +67,82 @@
     return jnp.tanh(jnp.dot(x, w, preferred_element_type=F32))
 
 
-def start_body(nb, kpc, blk, tiles, rows_h, feed, tiles_v, rows_v, kh, kd, kz, hout, u3, rows, sems):
-    M, R, E = kh.shape
-    nt = tiles_v.shape[0]
-    step = nt // CHUNKS
-    first = lax.axis_index("section") == 0
-    row_copies = [
-        pltpu.make_async_copy(rows_h, rows_v, sems.at[CHUNKS]),
-        pltpu.make_async_copy(rows_h, rows, sems.at[CHUNKS + 1]),
-    ]
-    feeds = [
-        pltpu.make_async_copy(feed.at[pl.ds(m * R, R)], kh.at[m], sems.at[CHUNKS + 2 + m]) for m in range(M)
-    ]
-    loads = [
+def tile_loads(tiles, tiles_v, sems):
+    step = tiles_v.shape[0] // CHUNKS
+    return [
         pltpu.make_async_copy(tiles.at[0, pl.ds(c * step, step)], tiles_v.at[pl.ds(c * step, step)], sems.at[c])
         for c in range(CHUNKS)
     ]
 
-    @pl.when(first)
-    def _():
-        feeds[0].start()
-
-    for c in row_copies:
-        c.start()
-    for c in loads:
-        c.start()
-
-    @pl.when(first)
-    def _():
-        for m in range(1, M):
-            feeds[m].start()
+
+def load_body(tiles, rows_h, tiles_in, rows_in, tiles_v, rows_v, sems):
+    @pl.when(lax.axis_index("section") != 0)
+    def _():
+        copies = [pltpu.make_async_copy(rows_h, rows_v, sems.at[CHUNKS])] + tile_loads(tiles, tiles_v, sems)
+        for c in copies:
+            c.start()
+        for c in copies:
+            c.wait()
+
+
+def start_body(nb, kpc, blk, tiles, rows_h, feed, tiles_v, rows_v, kh, kd, kz, hout, u3, rows, sems):
+    M, R, E = kh.shape
+
+    @pl.when(lax.axis_index("section") == 0)
+    def _():
+        feeds = [
+            pltpu.make_async_copy(feed.at[pl.ds(m * R, R)], kh.at[m], sems.at[CHUNKS + 2 + m]) for m in range(M)
+        ]
+        row_copies = [
+            pltpu.make_async_copy(rows_h, rows_v, sems.at[CHUNKS]),
+            pltpu.make_async_copy(rows_h, rows, sems.at[CHUNKS + 1]),
+        ]
+        loads = tile_loads(tiles, tiles_v, sems)
+        for c in feeds[:1] + row_copies + loads + feeds[1:]:
+            c.start()
         feeds[0].wait()
         hf = kh[0].astype(F32)
         normalise(hf, u3, nb, blk)
-
-    for c in row_copies:
-        c.wait()
-    for c in range(CHUNKS):
-        loads[c].wait()
-
-        @pl.when(first)
-        def _():
+        for c in row_copies:
+            c.wait()
+        for c in range(CHUNKS):
+            loads[c].wait()
             for n in range(c * nb // CHUNKS, (c + 1) * nb // CHUNKS):
                 a = mix(n, rows, tiles_v, u3, kpc, blk)
                 s = columns(n, blk)
-                hout[:, s] = (kh[0, :, s].astype(F32) + a).astype(BF16)
+                hout[:, s] = (hf[:, s] + a).astype(BF16)
                 kd[0, :, s] = 1.0 - a * a
-
-    @pl.when(first)
-    def _():
-        for m in range(1, M):
-            feeds[m].wait()
+        for c in feeds[1:]:
+            c.wait()
+
+
+def forward_work(m, nb, kpc, blk, rows_v, tiles, hin, hout, kh, kd, u3, rows, sem):
+    copy = fetch_rows(rows_v, rows, sem)
+    if hin is None:
+        h = kh[m]
+    else:
+        h = hin[...]
+        kh[m] = h
+    hf = h.astype(F32)
+    normalise(hf, u3, nb, blk)
+    copy.wait()
+    for n in range(nb):
+        a = mix(n, rows, tiles, u3, kpc, blk)
+        c = columns(n, blk)
+        hout[:, c] = (hf[:, c] + a).astype(BF16)
+        kd[m, :, c] = 1.0 - a * a
 
 
 def forward_body(s, m, nb, kpc, blk, *refs):
     if s == 0:
         rows_v, tiles, kh, kd_in, hout, kd, u3, rows, sem = refs
+        hin = None
     else:
         rows_v, tiles, hin, kh_in, kd_in, hout, kh, kd, u3, rows, sem = refs
 
     @pl.when(lax.axis_index("section") == s)
     def _():
-        copy = fetch_rows(rows_v, rows, sem)
-        if s == 0:
-            h = kh[m]
-        else:
-            h = hin[...]
-            kh[m] = h
-        hf = h.astype(F32)
-        normalise(hf, u3, nb, blk)
-        copy.wait()
-        for n in range(nb):
-            a = mix(n, rows, tiles, u3, kpc, blk)
-            c = columns(n, blk)
-            hout[:, c] = (hf[:, c] + a).astype(BF16)
-            kd[m, :, c] = 1.0 - a * a
+        forward_work(m, nb, kpc, blk, rows_v, tiles, hin, hout, kh, kd, u3, rows, sem)
 
 
 def spread(rows, tiles, dz, v3, nb, kpc, blk):
@@ -166,26 +168,44 @@
         gout[:, c] = (g[:, c].astype(F32) + scale * (v3[n] - q * inner)).astype(BF16)
 
 
+def turn_work(m, nb, kpc, blk, rows_v, tiles, hin, seeds, gout, kh, kz, u3, v3, rows, sem):
+    copy = fetch_rows(rows_v, rows, sem)
+    R = gout.shape[0]
+    h = hin[...]
+    kh[m] = h
+    hf = h.astype(F32)
+    normalise(hf, u3, nb, blk)
+    g = seeds.at[pl.ds(m * R, R)]
+    copy.wait()
+    for n in range(nb):
+        a = mix(n, rows, tiles, u3, kpc, blk)
+        c = columns(n, blk)
+        kz[m, :, c] = (g[:, c].astype(F32) * (1.0 - a * a)).astype(BF16)
+    spread(rows, tiles, lambda n: kz[m, :, columns(n, blk)], v3, nb, kpc, blk)
+    finish(kh.at[m], g, v3, gout, nb, blk)
+
+
 def turn_body(s, m, nb, kpc, blk, rows_v, tiles, hin, seeds, kh_in, kd_in, kz_in, gout, kh, kd, kz, u3, v3, rows, sem):
     @pl.when(lax.axis_index("section") == s)
     def _():
-        copy = fetch_rows(rows_v, rows, sem)
-        R = gout.shape[0]
-        h = hin[...]
-        kh[m] = h
-        hf = h.astype(F32)
-        normalise(hf, u3, nb, blk)
-        g = seeds.at[pl.ds(m * R, R)]
-        copy.wait()
-        for n in range(nb):
-            a = mix(n, rows, tiles, u3, kpc, blk)
-            c = columns(n, blk)
-            kz[m, :, c] = (g[:, c].astype(F32) * (1.0 - a * a)).astype(BF16)
-        spread(rows, tiles, lambda n: kz[m, :, columns(n, blk)], v3, nb, kpc, blk)
-        finish(kh.at[m], g, v3, gout, nb, blk)
-
-
-def backward_body(s, m, nb, kpc, blk, rows_v, tiles, gin, kh, kd, kz_in, gout, kz, v3, rows, sem):
+        turn_work(m, nb, kpc, blk, rows_v, tiles, hin, seeds, gout, kh, kz, u3, v3, rows, sem)
+
+
+def meet_body(s, a, b, nb, kpc, blk, rows_v, tiles, hin_a, hin_b, seeds, kh_in, kd_in, kz_in, *refs):
+    out, kh, kd, kz, u3, v3, rows, sem = refs
+
+    @pl.when(lax.axis_index("section") == s - 1)
+    def _():
+        forward_work(a, nb, kpc, blk, rows_v, tiles, None if s == 1 else hin_a, out, kh, kd, u3, rows, sem)
+
+    @pl.when(lax.axis_index("section") == s)
+    def _():
+        turn_work(b, nb, kpc, blk, rows_v, tiles, hin_b, seeds, out, kh, kz, u3, v3, rows, sem)
+
+
+def backward_body(s, m, nb, kpc, blk, rows_v, tiles, gin, kh, kd, kz_in, *refs):
+    gout, kz, v3, rows, sem = refs[-5:]
+
     @pl.when(lax.axis_index("section") == s)
     def _():
         copy = fetch_rows(rows_v, rows, sem)
@@ -197,21 +217,18 @@
         finish(kh.at[m], gin, v3, gout, nb, blk)
 
 
-def first_body(m, gin, kd, kz_in, kz, zs):
-    section = lax.axis_index("section")
-
-    @pl.when(section == 0)
-    def _():
-        z = (gin[...].astype(F32) * kd[m]).astype(BF16)
-        kz[m] = z
-        zs[...] = z
-
-    @pl.when(section != 0)
-    def _():
-        zs[...] = kz[m]
-
-
-def turned_body(nb, blk, half, parts, kh, keep, send, uT):
+def first_body(m, gin, kd, kz_in, *refs):
+    kz, *zs = refs[-2:] if refs[1:] else refs
+
+    @pl.when(lax.axis_index("section") == 0)
+    def _():
+        kz[m] = (gin[...].astype(F32) * kd[m]).astype(BF16)
+
+    for ref in zs:
+        ref[...] = kz[...]
+
+
+def turned_body(nb, blk, half, parts, kh, kd_in, keep, send, kd, uT):
     M, R, E = kh.shape
     hf = kh[...].reshape(M * R, E).astype(F32)
     scale = norm(hf)
@@ -225,13 +242,13 @@
 
 
 def term_body(js, M, nb, kpc, blk, half, rows_v, keep, got, kz, *refs):
-    zgot, outs, (rows, sem) = refs[:M], refs[M : M + len(js)], refs[M + len(js) :]
+    zgot, *outs, rows, sem = refs
     copy = fetch_rows(rows_v, rows, sem)
     chip = lax.axis_index("dp") // 2
     copy.wait()
     for n in range(nb):
         c = columns(n, blk)
-        z = jnp.concatenate([kz[m, :, c] for m in range(M)] + [zgot[m][:, c] for m in range(M)], axis=0)
+        z = jnp.concatenate([kz[m, :, c] for m in range(M)] + [zgot[m, :, c] for m in range(M)], axis=0)
         pieces = []
         for k in range(kpc):
             r = rows[0, n * kpc + k]
@@ -292,78 +309,135 @@
     def hop(array, a, b):
         return lax.ppermute(array, "section", [(a, b)])
 
-    arrived = [[] for s in range(sections)]
-    back = []
-    for s in range(last):
-        for m in range(M):
-            if s == 0 and m > 0:
-                out, kd = call(
-                    functools.partial(forward_body, s, m, nb, kpc, blk),
-                    [line, kd_s],
-                    [(rows, VM), (tiles_v, VM), (kh, VM), (kd, VM)],
-                    [u3, rows_s, dma],
-                    {3: 1},
-                )
-            elif s > 0:
-                out, kh, kd = call(
-                    functools.partial(forward_body, s, m, nb, kpc, blk),
-                    [line, kh_s, kd_s],
-                    [(rows, VM), (tiles_v, VM), (arrived[s][m], VM), (kh, VM), (kd, VM)],
-                    [u3, rows_s, dma],
-                    {3: 1, 4: 2},
-                )
-            arrived[s + 1].append(hop(out, s, s + 1))
-            for turning in [m - 1] * (s == last - 1 and m > 0) + [m] * (s == last - 1 and m == M - 1):
-                out, kh, kd, kz = call(
-                    functools.partial(turn_body, last, turning, nb, kpc, blk),
-                    [line, kh_s, kd_s, kz_s],
-                    [(rows, VM), (tiles_v, VM), (arrived[last][turning], VM), (out_grad, VM)]
-                    + [(kh, VM), (kd, VM), (kz, VM)],
-                    [u3, v3, rows_s, dma],
-                    {4: 1, 5: 2, 6: 3},
-                )
-                back.append(hop(out, last, last - 1))
-    for s in range(last - 1, 0, -1):
-        sent = []
-        for m in range(M):
-            out, kz = call(
-                functools.partial(backward_body, s, m, nb, kpc, blk),
-                [line, kz_s],
-                [(rows, VM), (tiles_v, VM), (back[m], VM), (kh, VM), (kd, VM), (kz, VM)],
-                [v3, rows_s, dma],
-                {5: 1},
+    def forward(s, m):
+        nonlocal kh, kd
+        if s == 0:
+            out, kd = call(
+                functools.partial(forward_body, s, m, nb, kpc, blk),
+                [line, kd_s],
+                [(rows, VM), (tiles_v, VM), (kh, VM), (kd, VM)],
+                [u3, rows_s, dma],
+                {3: 1},
             )
-            sent.append(hop(out, s, s - 1))
-        back = sent
+        else:
+            out, kh, kd = call(
+                functools.partial(forward_body, s, m, nb, kpc, blk),
+                [line, kh_s, kd_s],
+                [(rows, VM), (tiles_v, VM), (held[m], VM), (kh, VM), (kd, VM)],
+                [u3, rows_s, dma],
+                {3: 1, 4: 2},
+            )
+        held[m] = hop(out, s, s + 1)
+
+    def turn(s, m):
+        nonlocal kh, kd, kz
+        out, kh, kd, kz = call(
+            functools.partial(turn_body, s, m, nb, kpc, blk),
+            [line, kh_s, kd_s, kz_s],
+            [(rows, VM), (tiles_v, VM), (held[m], VM), (out_grad, VM), (kh, VM), (kd, VM), (kz, VM)],
+            [u3, v3, rows_s, dma],
+            {4: 1, 5: 2, 6: 3},
+        )
+        held[m] = hop(out, s, s - 1)
+
+    def backward(s, m, tied=()):
+        nonlocal kz
+        out, kz = call(
+            functools.partial(backward_body, s, m, nb, kpc, blk),
+            [line, kz_s],
+            [(rows, VM), (tiles_v, VM), (held[m], VM), (kh, VM), (kd, VM), (kz, VM)] + [(x, VM) for x in tied],
+            [v3, rows_s, dma],
+            {5: 1},
+        )
+        held[m] = hop(out, s, s - 1)
+
+    def load(s, m):
+        nonlocal tiles_v, rows
+        tiles_v, rows = call(
+            load_body,
+            [((nt, blk, blk), BF16, VM), ((1, nt), jnp.int32, VM)],
+            [(tiles, HBM), (tile_rows, HBM), (tiles_v, VM), (rows, VM)],
+            [dma((CHUNKS + 1,))],
+            {2: 0, 3: 1},
+        )
 
     half = blk // groups
     direct = half % 16 == 0 and groups % 2 == 0
     swap = [(i, i ^ 1) for i in range(groups)]
+    swapped = {}
+
+    def turned():
+        nonlocal kd
+        parts = groups // 2
+        shape = ((nb, parts, half, total), BF16, VM)
+        swapped["keep"], send, kd = call(
+            functools.partial(turned_body, nb, blk, half, parts),
+            [shape, shape, kd_s],
+            [(kh, VM), (kd, VM)],
+            [pltpu.VMEM((nb, parts, 2, half, total), BF16)],
+            {1: 2},
+        )
+        swapped["got"] = lax.ppermute(send, "dp", swap)
+
+    def meet(a, b):
+        nonlocal kh, kd, kz
+        out, kh, kd, kz = call(
+            functools.partial(meet_body, last, a, b, nb, kpc, blk),
+            [line, kh_s, kd_s, kz_s],
+            [(rows, VM), (tiles_v, VM), (held[a], VM), (held[b], VM), (out_grad, VM), (kh, VM), (kd, VM), (kz, VM)],
+            [u3, v3, rows_s, dma],
+            {5: 1, 6: 2, 7: 3},
+        )
+        held[a] = held[b] = lax.ppermute(out, "section", [(last - 1, last), (last, last - 1)])
+
+    held = [hop(out, 0, 1)] + [None] * (M - 1)
+
+    def step(m, at):
+        nonlocal kz
+        if at < last:
+            forward(at, m)
+        elif at == last:
+            turn(at, m)
+        elif at < 2 * last:
+            backward(2 * last - at, m)
+        else:
+            ends = direct and m == M - 1
+            if ends:
+                turned()
+            kz, *z = call(
+                functools.partial(first_body, m),
+                [kz_s] * (1 + ends),
+                [(held[m], VM), (kd, VM), (kz, VM)] + ([(swapped["keep"], VM)] if ends else []),
+                [],
+                {2: 0},
+            )
+            if ends:
+                swapped["z"] = lax.ppermute(z[0], "dp", swap)
+
+    plan = [(m, 0) for m in range(1, M - 1)]
+    for at in range(1, 2 * last + 1):
+        plan += [(0, at), (M - 1, at - 1)] + [(m, at) for m in range(1, M - 1)]
+    plan.append((M - 1, 2 * last))
+    pairs = {(0, last): (M - 2, last - 1), (1, last): (M - 1, last - 1)} if MEET else {}
+    for i, (m, at) in enumerate(plan):
+        if (m, at) in pairs.values():
+            continue
+        if (m, at) in pairs:
+            meet(pairs[m, at][0], m)
+        else:
+            step(m, at)
+        if i == 0:
+            load(0, 0)
+
     if direct:
         parts = groups // 2
-        turned = ((nb, parts, half, total), BF16, VM)
-        keep, send = call(
-            functools.partial(turned_body, nb, blk, half, parts),
-            [turned, turned],
-            [(kh, VM)],
-            [pltpu.VMEM((nb, parts, 2, half, total), BF16)],
-        )
-        got = lax.ppermute(send, "dp", swap)
-    zgot = []
-    for m in range(M):
-        kz, z = call(
-            functools.partial(first_body, m), [kz_s, line], [(back[m], VM), (kd, VM), (kz, VM)], [], {2: 0}
-        )
-        if direct:
-            zgot.append(lax.ppermute(z, "dp", swap))
-    if direct:
         piece = (nt, half, blk)
 
         def term(js, dtypes):
             return call(
                 functools.partial(term_body, js, M, nb, kpc, blk, half),
                 [(piece, d, VM) for d in dtypes],
-                [(rows, VM), (keep, VM), (got, VM), (kz, VM)] + [(z, VM) for z in zgot],
+                [(rows, VM), (swapped["keep"], VM), (swapped["got"], VM), (kz, VM), (swapped["z"], VM)],
                 [rows_s, dma],
             )
 

time: 98 us -> 90.5 us (0.923)
  waiting for transfers between devices: 58.3 us -> 50.3 us
    ppermute x24 -> x20, waiting for transfers between devices: 43.9 us -> 36 us  [hop(): return lax.ppermute(array, 'section', [(a, b)])]
    ppermute x3, waiting for transfers between devices: 13.2 us -> 12 us  [local(): lax.ppermute(sends[j - 1], 'dp', [(i, i ^ 2 * j) for i in range(groups)])]
    ppermute x5 -> x4, waiting for transfers between devices: 1.21 us -> 2.34 us  [the longest x1 2.34 us: turned(): swapped['got'] = lax.ppermute(send, 'dp', swap)]
    ppermute x24 -> x20, starting transfers between devices: 24.4 us -> 23.8 us  [hop(): return lax.ppermute(array, 'section', [(a, b)])]
    pallas_call x31 -> x30, Pallas kernels: 9.36 us -> 9.46 us  [call(): pl.pallas_call(body, out_shape=out_shape, in_specs=in_specs, out_specs=ou...]
  transfers between devices with their start and end apart: 32 -> 27, of which waited for: 11 -> 10; matrix products, arithmetic and copies ran while one was open for 0% -> 0% of each run, Pallas kernels for 5% -> 5%
where the time goes in v3:
time: 90.5 us; the launch traced here: 90 us
  waiting for transfers between devices  50.3 us (56%)
  starting transfers between devices  29.3 us (32%)
  Pallas kernels  9.46 us (10%)
    ppermute x20, waiting for transfers between devices, hop(): return lax.ppermute(array, 'section', [(a, b)])  36 us
    ppermute x20, starting transfers between devices, hop(): return lax.ppermute(array, 'section', [(a, b)])  23.8 us
    ppermute x3, waiting for transfers between devices, local(): lax.ppermute(sends[j - 1], 'dp', [(i, i ^ 2 * j) for i in range(groups)])  12 us
    pallas_call x30, Pallas kernels, call(): pl.pallas_call(body, out_shape=out_shape, in_specs=in_specs, out_specs=ou...  9.46 us
    ppermute x3, starting transfers between devices, local(): lax.ppermute(sends[j - 1], 'dp', [(i, i ^ 2 * j) for i in range(groups)])  3.55 us
    ppermute x1, waiting for transfers between devices, turned(): swapped['got'] = lax.ppermute(send, 'dp', swap)  2.34 us
  transfers between devices with their start and end apart: 27, of which 10 were waited for; matrix products, arithmetic and copies ran while one was open for 0% of the time, Pallas kernels for 5%

profile of v3, /device:TPU:0, one launch (start us, length us, event | category | flops | bytes accessed | tf_op | source)
XLA Modules:
  0.0 90.0 jit_solution(8752261420812798416)
XLA Ops:
  0.0 2.2 %shard_map.46 = (bf16[72,128,128]{2,1,0:T(8,128)(2,1)S(1)}, s32[1,72]{1,0:T(1,128)S(1)}, bf16[4,32,3072]{2,1,0:T(8,128)(2,1)S(1)}, f32[4,32,3072]{2,1,0:T(8,128)...) custom-call(bf16[1,72,128,128]{3,2,1,0:T(8,128)(2,1)} %tiles.3, s32[1,72]{1,0:T(1,128)} %rows_h.3, ...), custom_call_target="tpu_custom_call" | custom-call | flops 100000000 | bytes 3000000 | tf_op jit(solution)/shard_map/pallas_call | solution.py:31
  2.2 2.8 %collective-permute-start = (bf16[32,3072]{1,0:T(8,128)(2,1)S(1)}, bf16[32,3072]{1,0:T(8,128)(2,1)S(1)}, u32[]{:S(2)}, u32[]{:S(2)}) collective-permute-start(bf16[32,3072]{1,0:T(8,128)(2,1)S(1)} %get-tuple-element.82), channel_id=1, source_target_pairs={{0,1},{4,5},{8,9},{12,13},{16,17},{20,21},{24,25},{28,29}} | collective-permute-start | bytes 589832 | tf_op jit(solution)/shard_map/ppermute | solution.py:310
  5.0 1.1 %shard_map.48 = (bf16[32,3072]{1,0:T(8,128)(2,1)S(1)}, f32[4,32,3072]{2,1,0:T(8,128)S(1)}) custom-call(s32[1,72]{1,0:T(1,128)S(1)} %get-tuple-element.79.rows_in.refs_0_, bf16[72,128,128]{2,1,0:T(8,128)(2,1)S(1)} %get-tuple-element.78.tiles_in.refs_1_, bf16[4,32,3072]{2,1,0:T(8,128)(2,1)S(1)} %get-tuple-element.83.refs_2_.refs_3_, ...), custom_call_target="tpu_custom_call", output_to_operand_aliasing={{1}: (3, {})} | custom-call | flops 100000000 | bytes 3000000 | tf_op jit(solution)/shard_map/pallas_call | solution.py:31
  6.2 1.3 %collective-permute-start.4 = (bf16[32,3072]{1,0:T(8,128)(2,1)S(1)}, bf16[32,3072]{1,0:T(8,128)(2,1)S(1)}, u32[]{:S(2)}, u32[]{:S(2)}) collective-permute-start(bf16[32,3072]{1,0:T(8,128)(2,1)S(1)} %get-tuple-element.92), channel_id=1, source_target_pairs={{0,1},{4,5},{8,9},{12,13},{16,17},{20,21},{24,25},{28,29}} | collective-permute-start | bytes 589832 | tf_op jit(solution)/shard_map/ppermute | solution.py:310
  7.5 0.1 shard_map.47
  7.5 1.1 %shard_map.49 = (bf16[32,3072]{1,0:T(8,128)(2,1)S(1)}, f32[4,32,3072]{2,1,0:T(8,128)S(1)}) custom-call(s32[1,72]{1,0:T(1,128)S(1)} %get-tuple-element.80.refs_0_.rows_v, bf16[72,128,128]{2,1,0:T(8,128)(2,1)S(1)} %get-tuple-element.81.refs_1_.tiles, bf16[4,32,3072]{2,1,0:T(8,128)(2,1)S(1)} %get-tuple-element.83.refs_2_.refs_3_, ...), custom_call_target="tpu_custom_call", output_to_operand_aliasing={{1}: (3, {})} | custom-call | flops 100000000 | bytes 3000000 | tf_op jit(solution)/shard_map/pallas_call | solution.py:31
  8.7 1.3 %collective-permute-start.3 = (bf16[32,3072]{1,0:T(8,128)(2,1)S(1)}, bf16[32,3072]{1,0:T(8,128)(2,1)S(1)}, u32[]{:S(2)}, u32[]{:S(2)}) collective-permute-start(bf16[32,3072]{1,0:T(8,128)(2,1)S(1)} %get-tuple-element.91), channel_id=1, source_target_pairs={{0,1},{4,5},{8,9},{12,13},{16,17},{20,21},{24,25},{28,29}} | collective-permute-start | bytes 589832 | tf_op jit(solution)/shard_map/ppermute | solution.py:310
  10.0 0.4 collective-permute-done.refs_2_
  10.3 0.7 collective-permute-start.2
  11.0 1.1 %shard_map.51 = (bf16[32,3072]{1,0:T(8,128)(2,1)S(1)}, f32[4,32,3072]{2,1,0:T(8,128)S(1)}) custom-call(s32[1,72]{1,0:T(1,128)S(1)} %get-tuple-element.80.refs_0_.rows_v, bf16[72,128,128]{2,1,0:T(8,128)(2,1)S(1)} %get-tuple-element.81.refs_1_.tiles, bf16[4,32,3072]{2,1,0:T(8,128)(2,1)S(1)} %get-tuple-element.87.refs_2_.refs_3_, ...), custom_call_target="tpu_custom_call", output_to_operand_aliasing={{1}: (3, {})} | custom-call | flops 100000000 | bytes 3000000 | tf_op jit(solution)/shard_map/pallas_call | solution.py:31
  12.1 5.0 %collective-permute-start.1 = (bf16[32,3072]{1,0:T(8,128)(2,1)S(1)}, bf16[32,3072]{1,0:T(8,128)(2,1)S(1)}, u32[]{:S(2)}, u32[]{:S(2)}) collective-permute-start(bf16[32,3072]{1,0:T(8,128)(2,1)S(1)} %get-tuple-element.89), channel_id=1, source_target_pairs={{0,1},{4,5},{8,9},{12,13},{16,17},{20,21},{24,25},{28,29}} | collective-permute-start | bytes 589832 | tf_op jit(solution)/shard_map/ppermute | solution.py:310
  17.2 0.7 collective-permute-start.6
  17.9 0.9 collective-permute-done.3.refs_2_
  18.8 0.7 collective-permute-start.8
  19.5 0.7 collective-permute-start.9
  20.2 1.6 %collective-permute-done.1.refs_2_ = bf16[32,3072]{1,0:T(8,128)(2,1)S(1)} collective-permute-done((bf16[32,3072]{1,0:T(8,128)(2,1)S(1)}, bf16[32,3072]{1,0:T(8,128)(2,1)S(1)}, u32[]{:S(2)}, u32[]{:S(2)}) %collective-permute-start.1) | collective-permute-done | bytes 196640 | tf_op jit(solution)/shard_map/ppermute | solution.py:310
  21.8 0.7 collective-permute-start.5
  22.6 0.8 collective-permute-start.7
  23.4 0.3 copy-done
  23.7 0.7 collective-permute-start.11
  24.4 0.7 collective-permute-start.10
  25.1 0.2 shard_map.59
  25.3 0.7 collective-permute-start.15
  26.0 0.7 collective-permute-start.14
  26.8 0.7 collective-permute-start.13
  27.5 0.7 collective-permute-start.19
  28.2 0.7 collective-permute-start.18
  28.9 1.3 %collective-permute-start.17 = (bf16[32,3072]{1,0:T(8,128)(2,1)S(1)}, bf16[32,3072]{1,0:T(8,128)(2,1)S(1)}, u32[]{:S(2)}, u32[]{:S(2)}) collective-permute-start(bf16[32,3072]{1,0:T(8,128)(2,1)S(1)} %get-tuple-element.134), channel_id=1, source_target_pairs={{1,0},{5,4},{9,8},{13,12},{17,16},{21,20},{25,24},{29,28}} | collective-permute-start | bytes 589832 | tf_op jit(solution)/shard_map/ppermute | solution.py:310
  30.3 0.7 collective-permute-start.16
  31.0 1.3 %collective-permute-start.22 = (bf16[32,3072]{1,0:T(8,128)(2,1)S(1)}, bf16[32,3072]{1,0:T(8,128)(2,1)S(1)}, u32[]{:S(2)}, u32[]{:S(2)}) collective-permute-start(bf16[32,3072]{1,0:T(8,128)(2,1)S(1)} %get-tuple-element.143), channel_id=1, source_target_pairs={{1,0},{5,4},{9,8},{13,12},{17,16},{21,20},{25,24},{29,28}} | collective-permute-start | bytes 589832 | tf_op jit(solution)/shard_map/ppermute | solution.py:310
  32.3 1.3 %collective-permute-start.21 = (bf16[32,3072]{1,0:T(8,128)(2,1)S(1)}, bf16[32,3072]{1,0:T(8,128)(2,1)S(1)}, u32[]{:S(2)}, u32[]{:S(2)}) collective-permute-start(bf16[32,3072]{1,0:T(8,128)(2,1)S(1)} %get-tuple-element.142), channel_id=1, source_target_pairs={{1,0},{5,4},{9,8},{13,12},{17,16},{21,20},{25,24},{29,28}} | collective-permute-start | bytes 589832 | tf_op jit(solution)/shard_map/ppermute | solution.py:310
  33.6 25.2 %collective-permute-done.17.gin = bf16[32,3072]{1,0:T(8,128)(2,1)S(1)} collective-permute-done((bf16[32,3072]{1,0:T(8,128)(2,1)S(1)}, bf16[32,3072]{1,0:T(8,128)(2,1)S(1)}, u32[]{:S(2)}, u32[]{:S(2)}) %collective-permute-start.17) | collective-permute-done | bytes 196640 | tf_op jit(solution)/shard_map/ppermute | solution.py:310
  58.9 1.3 %collective-permute-start.20 = (bf16[32,3072]{1,0:T(8,128)(2,1)S(1)}, bf16[32,3072]{1,0:T(8,128)(2,1)S(1)}, u32[]{:S(2)}, u32[]{:S(2)}) collective-permute-start(bf16[32,3072]{1,0:T(8,128)(2,1)S(1)} %get-tuple-element.140), channel_id=1, source_target_pairs={{1,0},{5,4},{9,8},{13,12},{17,16},{21,20},{25,24},{29,28}} | collective-permute-start | bytes 589832 | tf_op jit(solution)/shard_map/ppermute | solution.py:310
  60.2 3.2 %collective-permute-done.22.gin = bf16[32,3072]{1,0:T(8,128)(2,1)S(1)} collective-permute-done((bf16[32,3072]{1,0:T(8,128)(2,1)S(1)}, bf16[32,3072]{1,0:T(8,128)(2,1)S(1)}, u32[]{:S(2)}, u32[]{:S(2)}) %collective-permute-start.22) | collective-permute-done | bytes 196640 | tf_op jit(solution)/shard_map/ppermute | solution.py:310
  63.4 3.3 %collective-permute-done.21.gin = bf16[32,3072]{1,0:T(8,128)(2,1)S(1)} collective-permute-done((bf16[32,3072]{1,0:T(8,128)(2,1)S(1)}, bf16[32,3072]{1,0:T(8,128)(2,1)S(1)}, u32[]{:S(2)}, u32[]{:S(2)}) %collective-permute-start.21) | collective-permute-done | bytes 196640 | tf_op jit(solution)/shard_map/ppermute | solution.py:310
  66.8 0.6 shard_map.62
  67.4 1.4 %collective-permute-done.20.gin = bf16[32,3072]{1,0:T(8,128)(2,1)S(1)} collective-permute-done((bf16[32,3072]{1,0:T(8,128)(2,1)S(1)}, bf16[32,3072]{1,0:T(8,128)(2,1)S(1)}, u32[]{:S(2)}, u32[]{:S(2)}) %collective-permute-start.20) | collective-permute-done | bytes 196640 | tf_op jit(solution)/shard_map/ppermute | solution.py:310
  68.8 0.1 shard_map.73
  68.9 0.1 collective-permute-start.23
  69.0 0.5 collective-permute-start.12
  69.5 2.3 %collective-permute-done.12.got = bf16[24,4,16,128]{3,2,1,0:T(8,128)(2,1)S(1)} collective-permute-done((bf16[24,4,16,128]{3,2,1,0:T(8,128)(2,1)S(1)}, bf16[24,4,16,128]{3,2,1,0:T(8,128)(2,1)S(1)}, u32[]{:S(2)}, u32[]{:S(2)}) %collective-permute-start.12) | collective-permute-done | bytes 393248 | tf_op jit(solution)/shard_map/ppermute | solution.py:380
  71.8 1.3 %shard_map.74 = (bf16[72,16,128]{2,1,0:T(8,128)(2,1)S(1)}, bf16[72,16,128]{2,1,0:T(8,128)(2,1)S(1)}, bf16[72,16,128]{2,1,0:T(8,128)(2,1)S(1)}, f32[72,16,128]{2,1,0:T(8,128)S(1)}) custom-call(s32[1,72]{1,0:T(1,128)S(1)} %get-tuple-element.80.refs_0_.rows_v, bf16[24,4,16,128]{3,2,1,0:T(8,128)(2,1)S(1)} %get-tuple-element.124.refs_0_.keep, ...), custom_call_target="tpu_custom_call" | custom-call | flops 100000000 | bytes 3000000 | tf_op jit(solution)/shard_map/pallas_call | solution.py:31
  73.2 0.5 collective-permute-start.24
  73.7 1.5 %collective-permute-start.25 = (bf16[72,16,128]{2,1,0:T(8,128)(2,1)S(1)}, bf16[72,16,128]{2,1,0:T(8,128)(2,1)S(1)}, u32[]{:S(2)}, u32[]{:S(2)}) collective-permute-start(bf16[72,16,128]{2,1,0:T(8,128)(2,1)S(1)} %get-tuple-element.149), channel_id=1, source_target_pairs={{0,16},{4,20},{8,24},{12,28},{16,0},{20,4},{24,8},{28,12},{1,17},{... | collective-permute-start | bytes 884744 | tf_op jit(solution)/shard_map/ppermute | solution.py:446
  75.2 1.5 %collective-permute-start.26 = (bf16[72,16,128]{2,1,0:T(8,128)(2,1)S(1)}, bf16[72,16,128]{2,1,0:T(8,128)(2,1)S(1)}, u32[]{:S(2)}, u32[]{:S(2)}) collective-permute-start(bf16[72,16,128]{2,1,0:T(8,128)(2,1)S(1)} %get-tuple-element.150), channel_id=1, source_target_pairs={{0,24},{4,28},{8,16},{12,20},{16,8},{20,12},{24,0},{28,4},{1,25},{... | collective-permute-start | bytes 884744 | tf_op jit(solution)/shard_map/ppermute | solution.py:446
  76.7 6.4 %collective-permute-done.24.refs_1_ = bf16[72,16,128]{2,1,0:T(8,128)(2,1)S(1)} collective-permute-done((bf16[72,16,128]{2,1,0:T(8,128)(2,1)S(1)}, bf16[72,16,128]{2,1,0:T(8,128)(2,1)S(1)}, u32[]{:S(2)}, u32[]{:S(2)}) %collective-permute-start.24) | collective-permute-done | bytes 294944 | tf_op jit(solution)/shard_map/ppermute | solution.py:446
  83.1 5.7 %collective-permute-done.25.refs_2_ = bf16[72,16,128]{2,1,0:T(8,128)(2,1)S(1)} collective-permute-done((bf16[72,16,128]{2,1,0:T(8,128)(2,1)S(1)}, bf16[72,16,128]{2,1,0:T(8,128)(2,1)S(1)}, u32[]{:S(2)}, u32[]{:S(2)}) %collective-permute-start.25) | collective-permute-done | bytes 294944 | tf_op jit(solution)/shard_map/ppermute | solution.py:446
  88.8 1.1 %shard_map.75 = f32[16,1,72,128]{3,2,1,0:T(8,128)} custom-call(f32[72,16,128]{2,1,0:T(8,128)S(1)} %get-tuple-element.147.refs_0_, bf16[72,16,128]{2,1,0:T(8,128)(2,1)S(1)} %collective-permute-done.24.refs_1_, bf16[72,16,128]{2,1,0:T(8,128)(2,1)S(1)} %collective-permute-done.25.refs_2_, bf16[72,16,128]{2,1,0:T(8,128)(2,1)S(1)} %collective-permute-done.26.refs_3_), custom_call_target="tpu_custom_call" | custom-call | flops 100000000 | bytes 3000000 | tf_op jit(solution)/shard_map/pallas_call | solution.py:31
  (38 shorter events, 0.6 us)
Async XLA Ops:
  2.2 8.1 %collective-permute-start = (bf16[32,3072]{1,0:T(8,128)(2,1)S(1)}, bf16[32,3072]{1,0:T(8,128)(2,1)S(1)}, u32[]{:S(2)}, u32[]{:S(2)}) collective-permute-start(bf16[32,3072]{1,0:T(8,128)(2,1)S(1)} %get-tuple-element.82), channel_id=1, source_target_pairs={{0,1},{4,5},{8,9},{12,13},{16,17},{20,21},{24,25},{28,29}} | collective-permute-start | bytes 589832 | tf_op jit(solution)/shard_map/ppermute | solution.py:310
  6.2 11.0 %collective-permute-start.4 = (bf16[32,3072]{1,0:T(8,128)(2,1)S(1)}, bf16[32,3072]{1,0:T(8,128)(2,1)S(1)}, u32[]{:S(2)}, u32[]{:S(2)}) collective-permute-start(bf16[32,3072]{1,0:T(8,128)(2,1)S(1)} %get-tuple-element.92), channel_id=1, source_target_pairs={{0,1},{4,5},{8,9},{12,13},{16,17},{20,21},{24,25},{28,29}} | collective-permute-start | bytes 589832 | tf_op jit(solution)/shard_map/ppermute | solution.py:310
  8.7 10.1 %collective-permute-start.3 = (bf16[32,3072]{1,0:T(8,128)(2,1)S(1)}, bf16[32,3072]{1,0:T(8,128)(2,1)S(1)}, u32[]{:S(2)}, u32[]{:S(2)}) collective-permute-start(bf16[32,3072]{1,0:T(8,128)(2,1)S(1)} %get-tuple-element.91), channel_id=1, source_target_pairs={{0,1},{4,5},{8,9},{12,13},{16,17},{20,21},{24,25},{28,29}} | collective-permute-start | bytes 589832 | tf_op jit(solution)/shard_map/ppermute | solution.py:310
  10.3 9.1 %collective-permute-start.2 = (bf16[32,3072]{1,0:T(8,128)(2,1)S(1)}, bf16[32,3072]{1,0:T(8,128)(2,1)S(1)}, u32[]{:S(2)}, u32[]{:S(2)}) collective-permute-start(bf16[32,3072]{1,0:T(8,128)(2,1)S(1)} %get-tuple-element.90), channel_id=1, source_target_pairs={{1,2},{5,6},{9,10},{13,14},{17,18},{21,22},{25,26},{29,30}} | collective-permute-start | bytes 589832 | tf_op jit(solution)/shard_map/ppermute | solution.py:310
  12.1 9.7 %collective-permute-start.1 = (bf16[32,3072]{1,0:T(8,128)(2,1)S(1)}, bf16[32,3072]{1,0:T(8,128)(2,1)S(1)}, u32[]{:S(2)}, u32[]{:S(2)}) collective-permute-start(bf16[32,3072]{1,0:T(8,128)(2,1)S(1)} %get-tuple-element.89), channel_id=1, source_target_pairs={{0,1},{4,5},{8,9},{12,13},{16,17},{20,21},{24,25},{28,29}} | collective-permute-start | bytes 589832 | tf_op jit(solution)/shard_map/ppermute | solution.py:310
  17.2 5.3 %collective-permute-start.6 = (bf16[32,3072]{1,0:T(8,128)(2,1)S(1)}, bf16[32,3072]{1,0:T(8,128)(2,1)S(1)}, u32[]{:S(2)}, u32[]{:S(2)}) collective-permute-start(bf16[32,3072]{1,0:T(8,128)(2,1)S(1)} %get-tuple-element.101), channel_id=1, source_target_pairs={{1,2},{5,6},{9,10},{13,14},{17,18},{21,22},{25,26},{29,30}} | collective-permute-start | bytes 589832 | tf_op jit(solution)/shard_map/ppermute | solution.py:310
  18.8 4.6 %collective-permute-start.8 = (bf16[32,3072]{1,0:T(8,128)(2,1)S(1)}, bf16[32,3072]{1,0:T(8,128)(2,1)S(1)}, u32[]{:S(2)}, u32[]{:S(2)}) collective-permute-start(bf16[32,3072]{1,0:T(8,128)(2,1)S(1)} %get-tuple-element.105), channel_id=1, source_target_pairs={{1,2},{5,6},{9,10},{13,14},{17,18},{21,22},{25,26},{29,30}} | collective-permute-start | bytes 589832 | tf_op jit(solution)/shard_map/ppermute | solution.py:310
  19.5 3.9 %collective-permute-start.9 = (bf16[32,3072]{1,0:T(8,128)(2,1)S(1)}, bf16[32,3072]{1,0:T(8,128)(2,1)S(1)}, u32[]{:S(2)}, u32[]{:S(2)}) collective-permute-start(bf16[32,3072]{1,0:T(8,128)(2,1)S(1)} %get-tuple-element.106), channel_id=1, source_target_pairs={{2,3},{6,7},{10,11},{14,15},{18,19},{22,23},{26,27},{30,31}} | collective-permute-start | bytes 589832 | tf_op jit(solution)/shard_map/ppermute | solution.py:310
  21.8 2.5 %collective-permute-start.5 = (bf16[32,3072]{1,0:T(8,128)(2,1)S(1)}, bf16[32,3072]{1,0:T(8,128)(2,1)S(1)}, u32[]{:S(2)}, u32[]{:S(2)}) collective-permute-start(bf16[32,3072]{1,0:T(8,128)(2,1)S(1)} %get-tuple-element.100), channel_id=1, source_target_pairs={{1,2},{5,6},{9,10},{13,14},{17,18},{21,22},{25,26},{29,30}} | collective-permute-start | bytes 589832 | tf_op jit(solution)/shard_map/ppermute | solution.py:310
  22.5 1.1 %copy-start = (bf16[128,3072]{1,0:T(8,128)(2,1)S(1)}, bf16[128,3072]{1,0:T(8,128)(2,1)}, u32[]{:S(2)}) copy-start(bf16[128,3072]{1,0:T(8,128)(2,1)} %seeds.7) | copy-start | bytes 2359300
  22.6 1.8 %collective-permute-start.7 = (bf16[32,3072]{1,0:T(8,128)(2,1)S(1)}, bf16[32,3072]{1,0:T(8,128)(2,1)S(1)}, u32[]{:S(2)}, u32[]{:S(2)}) collective-permute-start(bf16[32,3072]{1,0:T(8,128)(2,1)S(1)} %get-tuple-element.104), channel_id=1, source_target_pairs={{2,3},{6,7},{10,11},{14,15},{18,19},{22,23},{26,27},{30,31}} | collective-permute-start | bytes 589832 | tf_op jit(solution)/shard_map/ppermute | solution.py:310
  23.7 1.4 %collective-permute-start.11 = (bf16[32,3072]{1,0:T(8,128)(2,1)S(1)}, bf16[32,3072]{1,0:T(8,128)(2,1)S(1)}, u32[]{:S(2)}, u32[]{:S(2)}) collective-permute-start(bf16[32,3072]{1,0:T(8,128)(2,1)S(1)} %get-tuple-element.114), channel_id=1, source_target_pairs={{2,3},{3,2},{6,7},{7,6},{10,11},{11,10},{14,15},{15,14},{18,19},{1... | collective-permute-start | bytes 589832 | tf_op jit(solution)/shard_map/ppermute | solution.py:391
  24.4 2.3 %collective-permute-start.10 = (bf16[32,3072]{1,0:T(8,128)(2,1)S(1)}, bf16[32,3072]{1,0:T(8,128)(2,1)S(1)}, u32[]{:S(2)}, u32[]{:S(2)}) collective-permute-start(bf16[32,3072]{1,0:T(8,128)(2,1)S(1)} %get-tuple-element.113), channel_id=1, source_target_pairs={{2,3},{3,2},{6,7},{7,6},{10,11},{11,10},{14,15},{15,14},{18,19},{1... | collective-permute-start | bytes 589832 | tf_op jit(solution)/shard_map/ppermute | solution.py:391
  25.3 2.8 %collective-permute-start.15 = (bf16[32,3072]{1,0:T(8,128)(2,1)S(1)}, bf16[32,3072]{1,0:T(8,128)(2,1)S(1)}, u32[]{:S(2)}, u32[]{:S(2)}) collective-permute-start(bf16[32,3072]{1,0:T(8,128)(2,1)S(1)} %get-tuple-element.128), channel_id=1, source_target_pairs={{3,2},{7,6},{11,10},{15,14},{19,18},{23,22},{27,26},{31,30}} | collective-permute-start | bytes 589832 | tf_op jit(solution)/shard_map/ppermute | solution.py:310
  26.0 2.8 %collective-permute-start.14 = (bf16[32,3072]{1,0:T(8,128)(2,1)S(1)}, bf16[32,3072]{1,0:T(8,128)(2,1)S(1)}, u32[]{:S(2)}, u32[]{:S(2)}) collective-permute-start(bf16[32,3072]{1,0:T(8,128)(2,1)S(1)} %get-tuple-element.127), channel_id=1, source_target_pairs={{2,1},{6,5},{10,9},{14,13},{18,17},{22,21},{26,25},{30,29}} | collective-permute-start | bytes 589832 | tf_op jit(solution)/shard_map/ppermute | solution.py:310
  26.8 3.5 %collective-permute-start.13 = (bf16[32,3072]{1,0:T(8,128)(2,1)S(1)}, bf16[32,3072]{1,0:T(8,128)(2,1)S(1)}, u32[]{:S(2)}, u32[]{:S(2)}) collective-permute-start(bf16[32,3072]{1,0:T(8,128)(2,1)S(1)} %get-tuple-element.126), channel_id=1, source_target_pairs={{3,2},{7,6},{11,10},{15,14},{19,18},{23,22},{27,26},{31,30}} | collective-permute-start | bytes 589832 | tf_op jit(solution)/shard_map/ppermute | solution.py:310
  27.5 3.5 %collective-permute-start.19 = (bf16[32,3072]{1,0:T(8,128)(2,1)S(1)}, bf16[32,3072]{1,0:T(8,128)(2,1)S(1)}, u32[]{:S(2)}, u32[]{:S(2)}) collective-permute-start(bf16[32,3072]{1,0:T(8,128)(2,1)S(1)} %get-tuple-element.136), channel_id=1, source_target_pairs={{2,1},{6,5},{10,9},{14,13},{18,17},{22,21},{26,25},{30,29}} | collective-permute-start | bytes 589832 | tf_op jit(solution)/shard_map/ppermute | solution.py:310
  28.2 4.1 %collective-permute-start.18 = (bf16[32,3072]{1,0:T(8,128)(2,1)S(1)}, bf16[32,3072]{1,0:T(8,128)(2,1)S(1)}, u32[]{:S(2)}, u32[]{:S(2)}) collective-permute-start(bf16[32,3072]{1,0:T(8,128)(2,1)S(1)} %get-tuple-element.135), channel_id=1, source_target_pairs={{2,1},{6,5},{10,9},{14,13},{18,17},{22,21},{26,25},{30,29}} | collective-permute-start | bytes 589832 | tf_op jit(solution)/shard_map/ppermute | solution.py:310
  28.9 29.9 %collective-permute-start.17 = (bf16[32,3072]{1,0:T(8,128)(2,1)S(1)}, bf16[32,3072]{1,0:T(8,128)(2,1)S(1)}, u32[]{:S(2)}, u32[]{:S(2)}) collective-permute-start(bf16[32,3072]{1,0:T(8,128)(2,1)S(1)} %get-tuple-element.134), channel_id=1, source_target_pairs={{1,0},{5,4},{9,8},{13,12},{17,16},{21,20},{25,24},{29,28}} | collective-permute-start | bytes 589832 | tf_op jit(solution)/shard_map/ppermute | solution.py:310
  30.3 28.6 %collective-permute-start.16 = (bf16[32,3072]{1,0:T(8,128)(2,1)S(1)}, bf16[32,3072]{1,0:T(8,128)(2,1)S(1)}, u32[]{:S(2)}, u32[]{:S(2)}) collective-permute-start(bf16[32,3072]{1,0:T(8,128)(2,1)S(1)} %get-tuple-element.133), channel_id=1, source_target_pairs={{2,1},{6,5},{10,9},{14,13},{18,17},{22,21},{26,25},{30,29}} | collective-permute-start | bytes 589832 | tf_op jit(solution)/shard_map/ppermute | solution.py:310
  31.0 32.4 %collective-permute-start.22 = (bf16[32,3072]{1,0:T(8,128)(2,1)S(1)}, bf16[32,3072]{1,0:T(8,128)(2,1)S(1)}, u32[]{:S(2)}, u32[]{:S(2)}) collective-permute-start(bf16[32,3072]{1,0:T(8,128)(2,1)S(1)} %get-tuple-element.143), channel_id=1, source_target_pairs={{1,0},{5,4},{9,8},{13,12},{17,16},{21,20},{25,24},{29,28}} | collective-permute-start | bytes 589832 | tf_op jit(solution)/shard_map/ppermute | solution.py:310
  32.3 34.4 %collective-permute-start.21 = (bf16[32,3072]{1,0:T(8,128)(2,1)S(1)}, bf16[32,3072]{1,0:T(8,128)(2,1)S(1)}, u32[]{:S(2)}, u32[]{:S(2)}) collective-permute-start(bf16[32,3072]{1,0:T(8,128)(2,1)S(1)} %get-tuple-element.142), channel_id=1, source_target_pairs={{1,0},{5,4},{9,8},{13,12},{17,16},{21,20},{25,24},{29,28}} | collective-permute-start | bytes 589832 | tf_op jit(solution)/shard_map/ppermute | solution.py:310
  58.9 9.9 %collective-permute-start.20 = (bf16[32,3072]{1,0:T(8,128)(2,1)S(1)}, bf16[32,3072]{1,0:T(8,128)(2,1)S(1)}, u32[]{:S(2)}, u32[]{:S(2)}) collective-permute-start(bf16[32,3072]{1,0:T(8,128)(2,1)S(1)} %get-tuple-element.140), channel_id=1, source_target_pairs={{1,0},{5,4},{9,8},{13,12},{17,16},{21,20},{25,24},{29,28}} | collective-permute-start | bytes 589832 | tf_op jit(solution)/shard_map/ppermute | solution.py:310
  68.9 2.9 %collective-permute-start.23 = (bf16[4,32,3072]{2,1,0:T(8,128)(2,1)S(1)}, bf16[4,32,3072]{2,1,0:T(8,128)(2,1)S(1)}, u32[]{:S(2)}, u32[]{:S(2)}) collective-permute-start(bf16[4,32,3072]{2,1,0:T(8,128)(2,1)S(1)} %get-tuple-element.146), channel_id=1, source_target_pairs={{0,4},{4,0},{8,12},{12,8},{16,20},{20,16},{24,28},{28,24},{1,5},{5... | collective-permute-start | bytes 2359304 | tf_op jit(solution)/shard_map/ppermute | solution.py:415
  69.0 2.8 %collective-permute-start.12 = (bf16[24,4,16,128]{3,2,1,0:T(8,128)(2,1)S(1)}, bf16[24,4,16,128]{3,2,1,0:T(8,128)(2,1)S(1)}, u32[]{:S(2)}, u32[]{:S(2)}) collective-permute-start(bf16[24,4,16,128]{3,2,1,0:T(8,128)(2,1)S(1)} %get-tuple-element.125), channel_id=1, source_target_pairs={{0,4},{4,0},{8,12},{12,8},{16,20},{20,16},{24,28},{28,24},{1,5},{5... | collective-permute-start | bytes 1179656 | tf_op jit(solution)/shard_map/ppermute | solution.py:380
  73.2 9.9 %collective-permute-start.24 = (bf16[72,16,128]{2,1,0:T(8,128)(2,1)S(1)}, bf16[72,16,128]{2,1,0:T(8,128)(2,1)S(1)}, u32[]{:S(2)}, u32[]{:S(2)}) collective-permute-start(bf16[72,16,128]{2,1,0:T(8,128)(2,1)S(1)} %get-tuple-element.148), channel_id=1, source_target_pairs={{0,8},{4,12},{8,0},{12,4},{16,24},{20,28},{24,16},{28,20},{1,9},{5... | collective-permute-start | bytes 884744 | tf_op jit(solution)/shard_map/ppermute | solution.py:446
  73.7 15.1 %collective-permute-start.25 = (bf16[72,16,128]{2,1,0:T(8,128)(2,1)S(1)}, bf16[72,16,128]{2,1,0:T(8,128)(2,1)S(1)}, u32[]{:S(2)}, u32[]{:S(2)}) collective-permute-start(bf16[72,16,128]{2,1,0:T(8,128)(2,1)S(1)} %get-tuple-element.149), channel_id=1, source_target_pairs={{0,16},{4,20},{8,24},{12,28},{16,0},{20,4},{24,8},{28,12},{1,17},{... | collective-permute-start | bytes 884744 | tf_op jit(solution)/shard_map/ppermute | solution.py:446
  75.2 13.6 %collective-permute-start.26 = (bf16[72,16,128]{2,1,0:T(8,128)(2,1)S(1)}, bf16[72,16,128]{2,1,0:T(8,128)(2,1)S(1)}, u32[]{:S(2)}, u32[]{:S(2)}) collective-permute-start(bf16[72,16,128]{2,1,0:T(8,128)(2,1)S(1)} %get-tuple-element.150), channel_id=1, source_target_pairs={{0,24},{4,28},{8,16},{12,20},{16,8},{20,12},{24,0},{28,4},{1,25},{... | collective-permute-start | bytes 884744 | tf_op jit(solution)/shard_map/ppermute | solution.py:446

commit v4 on v3

--- a/solution.py
+++ b/solution.py
@@ -13,6 +13,7 @@
 BF16 = jnp.bfloat16
 VM = pltpu.VMEM
 HBM = pltpu.HBM
+SM = pltpu.SMEM
 ANY = pl.ANY
 LIMIT = 20 * 1024 * 1024
 CHUNKS = 4
@@ -22,7 +23,7 @@
 def call(body, outs, ins, scratch=(), aliases=None, flops=10**8, nbytes=3 * 10**6):
     arrays, in_specs = [], []
     for array, space in ins:
-        arrays.append(array if space is ANY else pltpu.with_memory_space_constraint(array, space))
+        arrays.append(array if space in (ANY, SM) else pltpu.with_memory_space_constraint(array, space))
         in_specs.append(pl.BlockSpec(memory_space=space))
     out_shape, out_specs = [], []
     for shape, dtype, space in outs:
@@ -48,12 +49,6 @@
     return lax.rsqrt(jnp.mean(hf * hf, axis=1, keepdims=True) + EPS)
 
 
-def fetch_rows(rows_v, rows, sem):
-    copy = pltpu.make_async_copy(rows_v, rows, sem)
-    copy.start()
-    return copy
-
-
 def normalise(hf, u3, nb, blk):
     scale = norm(hf)
     for n in range(nb):
@@ -75,28 +70,30 @@
     ]
 
 
-def load_body(tiles, rows_h, tiles_in, rows_in, tiles_v, rows_v, sems):
+def load_body(tiles, rows_h, tiles_in, tiles_v, rows, sems):
+    row_copy = pltpu.make_async_copy(rows_h, rows, sems.at[CHUNKS])
+    row_copy.start()
+
     @pl.when(lax.axis_index("section") != 0)
     def _():
-        copies = [pltpu.make_async_copy(rows_h, rows_v, sems.at[CHUNKS])] + tile_loads(tiles, tiles_v, sems)
+        copies = tile_loads(tiles, tiles_v, sems)
         for c in copies:
             c.start()
         for c in copies:
             c.wait()
 
-
-def start_body(nb, kpc, blk, tiles, rows_h, feed, tiles_v, rows_v, kh, kd, kz, hout, u3, rows, sems):
+    row_copy.wait()
+
+
+def start_body(nb, kpc, blk, tiles, rows_h, feed, tiles_v, rows, kh, kd, kz, hout, u3, sems):
     M, R, E = kh.shape
 
     @pl.when(lax.axis_index("section") == 0)
     def _():
         feeds = [
-            pltpu.make_async_copy(feed.at[pl.ds(m * R, R)], kh.at[m], sems.at[CHUNKS + 2 + m]) for m in range(M)
+            pltpu.make_async_copy(feed.at[pl.ds(m * R, R)], kh.at[m], sems.at[CHUNKS + 1 + m]) for m in range(M)
         ]
-        row_copies = [
-            pltpu.make_async_copy(rows_h, rows_v, sems.at[CHUNKS]),
-            pltpu.make_async_copy(rows_h, rows, sems.at[CHUNKS + 1]),
-        ]
+        row_copies = [pltpu.make_async_copy(rows_h, rows, sems.at[CHUNKS])]
         loads = tile_loads(tiles, tiles_v, sems)
         for c in feeds[:1] + row_copies + loads + feeds[1:]:
             c.start()
@@ -116,8 +113,7 @@
             c.wait()
 
 
-def forward_work(m, nb, kpc, blk, rows_v, tiles, hin, hout, kh, kd, u3, rows, sem):
-    copy = fetch_rows(rows_v, rows, sem)
+def forward_work(m, nb, kpc, blk, rows, tiles, hin, hout, kh, kd, u3):
     if hin is None:
         h = kh[m]
     else:
@@ -125,7 +121,6 @@
         kh[m] = h
     hf = h.astype(F32)
     normalise(hf, u3, nb, blk)
-    copy.wait()
     for n in range(nb):
         a = mix(n, rows, tiles, u3, kpc, blk)
         c = columns(n, blk)
@@ -135,14 +130,14 @@
 
 def forward_body(s, m, nb, kpc, blk, *refs):
     if s == 0:
-        rows_v, tiles, kh, kd_in, hout, kd, u3, rows, sem = refs
+        rows, tiles, kh, kd_in, hout, kd, u3 = refs
         hin = None
     else:
-        rows_v, tiles, hin, kh_in, kd_in, hout, kh, kd, u3, rows, sem = refs
+        rows, tiles, hin, kh_in, kd_in, hout, kh, kd, u3 = refs
 
     @pl.when(lax.axis_index("section") == s)
     def _():
-        forward_work(m, nb, kpc, blk, rows_v, tiles, hin, hout, kh, kd, u3, rows, sem)
+        forward_work(m, nb, kpc, blk, rows, tiles, hin, hout, kh, kd, u3)
 
 
 def spread(rows, tiles, dz, v3, nb, kpc, blk):
@@ -168,15 +163,13 @@
         gout[:, c] = (g[:, c].astype(F32) + scale * (v3[n] - q * inner)).astype(BF16)
 
 
-def turn_work(m, nb, kpc, blk, rows_v, tiles, hin, seeds, gout, kh, kz, u3, v3, rows, sem):
-    copy = fetch_rows(rows_v, rows, sem)
+def turn_work(m, nb, kpc, blk, rows, tiles, hin, seeds, gout, kh, kz, u3, v3):
     R = gout.shape[0]
     h = hin[...]
     kh[m] = h
     hf = h.astype(F32)
     normalise(hf, u3, nb, blk)
     g = seeds.at[pl.ds(m * R, R)]
-    copy.wait()
     for n in range(nb):
         a = mix(n, rows, tiles, u3, kpc, blk)
         c = columns(n, blk)
@@ -185,34 +178,32 @@
     finish(kh.at[m], g, v3, gout, nb, blk)
 
 
-def turn_body(s, m, nb, kpc, blk, rows_v, tiles, hin, seeds, kh_in, kd_in, kz_in, gout, kh, kd, kz, u3, v3, rows, sem):
+def turn_body(s, m, nb, kpc, blk, rows, tiles, hin, seeds, kh_in, kd_in, kz_in, gout, kh, kd, kz, u3, v3):
     @pl.when(lax.axis_index("section") == s)
     def _():
-        turn_work(m, nb, kpc, blk, rows_v, tiles, hin, seeds, gout, kh, kz, u3, v3, rows, sem)
-
-
-def meet_body(s, a, b, nb, kpc, blk, rows_v, tiles, hin_a, hin_b, seeds, kh_in, kd_in, kz_in, *refs):
-    out, kh, kd, kz, u3, v3, rows, sem = refs
+        turn_work(m, nb, kpc, blk, rows, tiles, hin, seeds, gout, kh, kz, u3, v3)
+
+
+def meet_body(s, a, b, nb, kpc, blk, rows, tiles, hin_a, hin_b, seeds, kh_in, kd_in, kz_in, *refs):
+    out, kh, kd, kz, u3, v3 = refs
 
     @pl.when(lax.axis_index("section") == s - 1)
     def _():
-        forward_work(a, nb, kpc, blk, rows_v, tiles, None if s == 1 else hin_a, out, kh, kd, u3, rows, sem)
+        forward_work(a, nb, kpc, blk, rows, tiles, None if s == 1 else hin_a, out, kh, kd, u3)
 
     @pl.when(lax.axis_index("section") == s)
     def _():
-        turn_work(b, nb, kpc, blk, rows_v, tiles, hin_b, seeds, out, kh, kz, u3, v3, rows, sem)
-
-
-def backward_body(s, m, nb, kpc, blk, rows_v, tiles, gin, kh, kd, kz_in, *refs):
-    gout, kz, v3, rows, sem = refs[-5:]
+        turn_work(b, nb, kpc, blk, rows, tiles, hin_b, seeds, out, kh, kz, u3, v3)
+
+
+def backward_body(s, m, nb, kpc, blk, rows, tiles, gin, kh, kd, kz_in, *refs):
+    gout, kz, v3 = refs[-3:]
 
     @pl.when(lax.axis_index("section") == s)
     def _():
-        copy = fetch_rows(rows_v, rows, sem)
         for n in range(nb):
             c = columns(n, blk)
             kz[m, :, c] = (gin[:, c].astype(F32) * kd[m, :, c]).astype(BF16)
-        copy.wait()
         spread(rows, tiles, lambda n: kz[m, :, columns(n, blk)], v3, nb, kpc, blk)
         finish(kh.at[m], gin, v3, gout, nb, blk)
 
@@ -241,39 +232,42 @@
             send[n, j] = uT[n, j, 1 - me]
 
 
-def term_body(js, M, nb, kpc, blk, half, rows_v, keep, got, kz, *refs):
-    zgot, *outs, rows, sem = refs
-    copy = fetch_rows(rows_v, rows, sem)
+def term_body(jobs, M, nb, kpc, blk, half, rows, keep, got, kz, zgot, *refs):
+    outs = refs
     chip = lax.axis_index("dp") // 2
-    copy.wait()
     for n in range(nb):
         c = columns(n, blk)
+        todo = [(out, i, j, n - lo) for out, (js, lo, hi) in zip(outs, jobs) if lo <= n < hi for i, j in enumerate(js)]
+        if not todo:
+            continue
         z = jnp.concatenate([kz[m, :, c] for m in range(M)] + [zgot[m, :, c] for m in range(M)], axis=0)
         pieces = []
         for k in range(kpc):
             r = rows[0, n * kpc + k]
-            for j in js:
+            for _, _, j, _ in todo:
                 pieces.append(jnp.concatenate([keep[r, chip ^ j], got[r, chip ^ j]], axis=1))
         term = jnp.dot(jnp.concatenate(pieces, axis=0), z, preferred_element_type=F32)
         for k in range(kpc):
-            for i in range(len(js)):
-                at = (k * len(js) + i) * half
-                outs[i][n * kpc + k] = term[at : at + half].astype(outs[i].dtype)
-
-
-def final_body(parts, *refs):
-    ins, (out, buf, sems) = refs[:parts], refs[parts:]
-    nt = ins[0].shape[0]
-    step = 24 if nt % 24 == 0 else nt
+            for p, (out, i, _, at) in enumerate(todo):
+                row = (k * len(todo) + p) * half
+                out[i, at * kpc + k] = term[row : row + half].astype(out.dtype)
+
+
+def relay_body(mine, got, out):
+    out[...] = (mine[0] + got[1].astype(F32)).astype(BF16)
+
+
+def final_body(mine, a1, a2, b1, b2, out, buf, sems):
+    nt = mine.shape[1]
+    cut = nt // 2
+    step = cut // 3 if cut % 24 == 0 else cut
     stores = []
     for t in range(nt):
-        total = ins[0][t].astype(F32)
-        for j in range(1, parts):
-            total = total + ins[j][t].astype(F32)
-        buf[:, t, :] = total
+        one, two, at = (a1, a2, t) if t < cut else (b1, b2, t - cut)
+        buf[:, t, :] = mine[0, t] + (one[0, at].astype(F32) + two[at].astype(F32))
         if (t + 1) % step == 0:
-            at = pl.ds(t + 1 - step, step)
-            c = pltpu.make_async_copy(buf.at[:, at], out.at[:, 0, at], sems.at[t // step])
+            part = pl.ds(t + 1 - step, step)
+            c = pltpu.make_async_copy(buf.at[:, part], out.at[:, 0, part], sems.at[t // step])
             c.start()
             stores.append(c)
     for c in stores:
@@ -295,15 +289,14 @@
     kh_s, kd_s, kz_s = ((M, R, E), BF16, VM), ((M, R, E), F32, VM), ((M, R, E), BF16, VM)
     u3 = pltpu.VMEM((nb, R, blk), BF16)
     v3 = pltpu.VMEM((nb, R, blk), F32)
-    rows_s = pltpu.SMEM((1, nt), jnp.int32)
     line = ((R, E), BF16, VM)
     last = sections - 1
 
     tiles_v, rows, kh, kd, kz, out = call(
         functools.partial(start_body, nb, kpc, blk),
-        [((nt, blk, blk), BF16, VM), ((1, nt), jnp.int32, VM), kh_s, kd_s, kz_s, line],
+        [((nt, blk, blk), BF16, VM), ((1, nt), jnp.int32, SM), kh_s, kd_s, kz_s, line],
         [(tiles, HBM), (tile_rows, HBM), (inputs, HBM)],
-        [u3, rows_s, dma((CHUNKS + 2 + M,))],
+        [u3, dma((CHUNKS + 1 + M,))],
     )
 
     def hop(array, a, b):
@@ -315,16 +308,16 @@
             out, kd = call(
                 functools.partial(forward_body, s, m, nb, kpc, blk),
                 [line, kd_s],
-                [(rows, VM), (tiles_v, VM), (kh, VM), (kd, VM)],
-                [u3, rows_s, dma],
+                [(rows, SM), (tiles_v, VM), (kh, VM), (kd, VM)],
+                [u3],
                 {3: 1},
             )
         else:
             out, kh, kd = call(
                 functools.partial(forward_body, s, m, nb, kpc, blk),
                 [line, kh_s, kd_s],
-                [(rows, VM), (tiles_v, VM), (held[m], VM), (kh, VM), (kd, VM)],
-                [u3, rows_s, dma],
+                [(rows, SM), (tiles_v, VM), (held[m], VM), (kh, VM), (kd, VM)],
+                [u3],
                 {3: 1, 4: 2},
             )
         held[m] = hop(out, s, s + 1)
@@ -334,8 +327,8 @@
         out, kh, kd, kz = call(
             functools.partial(turn_body, s, m, nb, kpc, blk),
             [line, kh_s, kd_s, kz_s],
-            [(rows, VM), (tiles_v, VM), (held[m], VM), (out_grad, VM), (kh, VM), (kd, VM), (kz, VM)],
-            [u3, v3, rows_s, dma],
+            [(rows, SM), (tiles_v, VM), (held[m], VM), (out_grad, VM), (kh, VM), (kd, VM), (kz, VM)],
+            [u3, v3],
             {4: 1, 5: 2, 6: 3},
         )
         held[m] = hop(out, s, s - 1)
@@ -345,8 +338,8 @@
         out, kz = call(
             functools.partial(backward_body, s, m, nb, kpc, blk),
             [line, kz_s],
-            [(rows, VM), (tiles_v, VM), (held[m], VM), (kh, VM), (kd, VM), (kz, VM)] + [(x, VM) for x in tied],
-            [v3, rows_s, dma],
+            [(rows, SM), (tiles_v, VM), (held[m], VM), (kh, VM), (kd, VM), (kz, VM)] + [(x, VM) for x in tied],
+            [v3],
             {5: 1},
         )
         held[m] = hop(out, s, s - 1)
@@ -355,14 +348,14 @@
         nonlocal tiles_v, rows
         tiles_v, rows = call(
             load_body,
-            [((nt, blk, blk), BF16, VM), ((1, nt), jnp.int32, VM)],
-            [(tiles, HBM), (tile_rows, HBM), (tiles_v, VM), (rows, VM)],
+            [((nt, blk, blk), BF16, VM), ((1, nt), jnp.int32, SM)],
+            [(tiles, HBM), (tile_rows, HBM), (tiles_v, VM)],
             [dma((CHUNKS + 1,))],
-            {2: 0, 3: 1},
+            {2: 0},
         )
 
     half = blk // groups
-    direct = half % 16 == 0 and groups % 2 == 0
+    direct = half % 16 == 0 and groups == 8 and nb % 2 == 0 and last > 0
     swap = [(i, i ^ 1) for i in range(groups)]
     swapped = {}
 
@@ -384,8 +377,8 @@
         out, kh, kd, kz = call(
             functools.partial(meet_body, last, a, b, nb, kpc, blk),
             [line, kh_s, kd_s, kz_s],
-            [(rows, VM), (tiles_v, VM), (held[a], VM), (held[b], VM), (out_grad, VM), (kh, VM), (kd, VM), (kz, VM)],
-            [u3, v3, rows_s, dma],
+            [(rows, SM), (tiles_v, VM), (held[a], VM), (held[b], VM), (out_grad, VM), (kh, VM), (kd, VM), (kz, VM)],
+            [u3, v3],
             {5: 1, 6: 2, 7: 3},
         )
         held[a] = held[b] = lax.ppermute(out, "section", [(last - 1, last), (last, last - 1)])
@@ -430,26 +423,33 @@
             load(0, 0)
 
     if direct:
-        parts = groups // 2
-        piece = (nt, half, blk)
-
-        def term(js, dtypes):
+        mid, cut = nb // 2, nt // 2
+
+        def term(jobs, dtype):
             return call(
-                functools.partial(term_body, js, M, nb, kpc, blk, half),
-                [(piece, d, VM) for d in dtypes],
-                [(rows, VM), (swapped["keep"], VM), (swapped["got"], VM), (kz, VM), (swapped["z"], VM)],
-                [rows_s, dma],
+                functools.partial(term_body, jobs, M, nb, kpc, blk, half),
+                [((len(js), (hi - lo) * kpc, half, blk), dtype, VM) for js, lo, hi in jobs],
+                [(rows, SM), (swapped["keep"], VM), (swapped["got"], VM), (kz, VM), (swapped["z"], VM)],
+                [],
             )
 
-        *sends, mine = term(list(range(1, parts)) + [0], [BF16] * (parts - 1) + [F32])
-        ready = [mine] + [
-            lax.ppermute(sends[j - 1], "dp", [(i, i ^ (2 * j)) for i in range(groups)]) for j in range(1, parts)
-        ]
+        def across(array, j):
+            return lax.ppermute(array, "dp", [(i, i ^ (2 * j)) for i in range(groups)])
+
+        def relay(mine, got):
+            (out,) = call(relay_body, [((cut, half, blk), BF16, VM)], [(mine, VM), (got, VM)])
+            return out
+
+        send_a, send_b = term([((1, 3), 0, mid), ((2, 3), mid, nb)], BF16)
+        got_a, got_b = across(send_a, 1), across(send_b, 2)
+        mine, next_a, next_b = term([((0,), 0, nb), ((2,), 0, mid), ((1,), mid, nb)], F32)
+        last_a = across(relay(next_a, got_a), 2)
+        last_b = across(relay(next_b, got_b), 1)
         (out,) = call(
-            functools.partial(final_body, parts),
+            final_body,
             [((half, 1, nt, blk), F32, HBM)],
-            [(r, VM) for r in ready],
-            [pltpu.VMEM((half, nt, blk), F32), dma((max(1, nt // 24),))],
+            [(mine, VM), (got_a, VM), (last_a, VM), (got_b, VM), (last_b, VM)],
+            [pltpu.VMEM((half, nt, blk), F32), dma((6,))],
         )
         return out
     hf = kh.reshape(total, E).astype(F32)

time: 90.5 us -> 86.5 us (0.956)
  waiting for transfers between devices: 50.3 us -> 47.2 us
  Pallas kernels: 9.46 us -> 8.33 us
    ppermute x3 -> x4, waiting for transfers between devices: 12 us -> 10.4 us  [across(): return lax.ppermute(array, 'dp', [(i, i ^ 2 * j) for i in range(groups)])]
    ppermute x20, waiting for transfers between devices: 36 us -> 34.5 us  [hop(): return lax.ppermute(array, 'section', [(a, b)])]
    pallas_call x30 -> x33, Pallas kernels: 9.46 us -> 8.33 us  [call(): pl.pallas_call(body, out_shape=out_shape, in_specs=in_specs, out_specs=ou...]
    ppermute x3 -> x4, starting transfers between devices: 3.55 us -> 3.79 us  [across(): return lax.ppermute(array, 'dp', [(i, i ^ 2 * j) for i in range(groups)])]
  transfers between devices with their start and end apart: 27 -> 28, of which waited for: 10 -> 11; matrix products, arithmetic and copies ran while one was open for 0% -> 0% of each run, Pallas kernels for 5% -> 5%
where the time goes in v4:
time: 86.5 us; the launch traced here: 86 us
  waiting for transfers between devices  47.2 us (55%)
  starting transfers between devices  29.5 us (34%)
  Pallas kernels  8.33 us (10%)
    ppermute x20, waiting for transfers between devices, hop(): return lax.ppermute(array, 'section', [(a, b)])  34.5 us
    ppermute x20, starting transfers between devices, hop(): return lax.ppermute(array, 'section', [(a, b)])  23.8 us
    ppermute x4, waiting for transfers between devices, across(): return lax.ppermute(array, 'dp', [(i, i ^ 2 * j) for i in range(groups)])  10.4 us
    pallas_call x33, Pallas kernels, call(): pl.pallas_call(body, out_shape=out_shape, in_specs=in_specs, out_specs=ou...  8.33 us
    ppermute x4, starting transfers between devices, across(): return lax.ppermute(array, 'dp', [(i, i ^ 2 * j) for i in range(groups)])  3.79 us
    ppermute x1, waiting for transfers between devices, turned(): swapped['got'] = lax.ppermute(send, 'dp', swap)  2.34 us
  transfers between devices with their start and end apart: 28, of which 11 were waited for; matrix products, arithmetic and copies ran while one was open for 0% of the time, Pallas kernels for 5%

profile of v4, /device:TPU:0, one launch (start us, length us, event | category | flops | bytes accessed | tf_op | source)
XLA Modules:
  0.0 86.0 jit_solution(5030833958161823071)
XLA Ops:
  0.0 2.2 %shard_map.46 = (bf16[72,128,128]{2,1,0:T(8,128)(2,1)S(1)}, s32[1,72]{1,0:T(1,128)S(4)}, bf16[4,32,3072]{2,1,0:T(8,128)(2,1)S(1)}, f32[4,32,3072]{2,1,0:T(8,128)...) custom-call(bf16[1,72,128,128]{3,2,1,0:T(8,128)(2,1)} %tiles.3, s32[1,72]{1,0:T(1,128)} %rows_h.3, ...), custom_call_target="tpu_custom_call" | custom-call | flops 100000000 | bytes 3000000 | tf_op jit(solution)/shard_map/pallas_call | solution.py:32
  2.2 2.8 %collective-permute-start = (bf16[32,3072]{1,0:T(8,128)(2,1)S(1)}, bf16[32,3072]{1,0:T(8,128)(2,1)S(1)}, u32[]{:S(2)}, u32[]{:S(2)}) collective-permute-start(bf16[32,3072]{1,0:T(8,128)(2,1)S(1)} %get-tuple-element.82), channel_id=1, source_target_pairs={{0,1},{4,5},{8,9},{12,13},{16,17},{20,21},{24,25},{28,29}} | collective-permute-start | bytes 589832 | tf_op jit(solution)/shard_map/ppermute | solution.py:303
  5.0 0.7 shard_map.48
  5.7 1.3 %collective-permute-start.4 = (bf16[32,3072]{1,0:T(8,128)(2,1)S(1)}, bf16[32,3072]{1,0:T(8,128)(2,1)S(1)}, u32[]{:S(2)}, u32[]{:S(2)}) collective-permute-start(bf16[32,3072]{1,0:T(8,128)(2,1)S(1)} %get-tuple-element.93), channel_id=1, source_target_pairs={{0,1},{4,5},{8,9},{12,13},{16,17},{20,21},{24,25},{28,29}} | collective-permute-start | bytes 589832 | tf_op jit(solution)/shard_map/ppermute | solution.py:303
  7.0 0.7 shard_map.47
  7.8 0.7 shard_map.49
  8.4 1.3 %collective-permute-start.3 = (bf16[32,3072]{1,0:T(8,128)(2,1)S(1)}, bf16[32,3072]{1,0:T(8,128)(2,1)S(1)}, u32[]{:S(2)}, u32[]{:S(2)}) collective-permute-start(bf16[32,3072]{1,0:T(8,128)(2,1)S(1)} %get-tuple-element.92), channel_id=1, source_target_pairs={{0,1},{4,5},{8,9},{12,13},{16,17},{20,21},{24,25},{28,29}} | collective-permute-start | bytes 589832 | tf_op jit(solution)/shard_map/ppermute | solution.py:303
  9.8 0.6 collective-permute-done.refs_2_
  10.3 0.7 collective-permute-start.2
  11.0 0.7 shard_map.51
  11.7 5.0 %collective-permute-start.1 = (bf16[32,3072]{1,0:T(8,128)(2,1)S(1)}, bf16[32,3072]{1,0:T(8,128)(2,1)S(1)}, u32[]{:S(2)}, u32[]{:S(2)}) collective-permute-start(bf16[32,3072]{1,0:T(8,128)(2,1)S(1)} %get-tuple-element.90), channel_id=1, source_target_pairs={{0,1},{4,5},{8,9},{12,13},{16,17},{20,21},{24,25},{28,29}} | collective-permute-start | bytes 589832 | tf_op jit(solution)/shard_map/ppermute | solution.py:303
  16.8 0.7 collective-permute-start.6
  17.4 1.3 %collective-permute-done.3.refs_2_ = bf16[32,3072]{1,0:T(8,128)(2,1)S(1)} collective-permute-done((bf16[32,3072]{1,0:T(8,128)(2,1)S(1)}, bf16[32,3072]{1,0:T(8,128)(2,1)S(1)}, u32[]{:S(2)}, u32[]{:S(2)}) %collective-permute-start.3) | collective-permute-done | bytes 196640 | tf_op jit(solution)/shard_map/ppermute | solution.py:303
  18.7 0.7 collective-permute-start.8
  19.4 0.7 collective-permute-start.9
  20.1 1.7 %collective-permute-done.1.refs_2_ = bf16[32,3072]{1,0:T(8,128)(2,1)S(1)} collective-permute-done((bf16[32,3072]{1,0:T(8,128)(2,1)S(1)}, bf16[32,3072]{1,0:T(8,128)(2,1)S(1)}, u32[]{:S(2)}, u32[]{:S(2)}) %collective-permute-start.1) | collective-permute-done | bytes 196640 | tf_op jit(solution)/shard_map/ppermute | solution.py:303
  21.8 0.7 collective-permute-start.5
  22.5 0.8 collective-permute-start.7
  23.4 0.3 copy-done
  23.6 0.7 collective-permute-start.11
  24.3 0.7 collective-permute-start.10
  25.2 0.7 collective-permute-start.15
  25.9 0.7 collective-permute-start.14
  26.7 0.7 collective-permute-start.13
  27.4 0.7 collective-permute-start.19
  28.1 0.7 collective-permute-start.18
  28.8 1.3 %collective-permute-start.17 = (bf16[32,3072]{1,0:T(8,128)(2,1)S(1)}, bf16[32,3072]{1,0:T(8,128)(2,1)S(1)}, u32[]{:S(2)}, u32[]{:S(2)}) collective-permute-start(bf16[32,3072]{1,0:T(8,128)(2,1)S(1)} %get-tuple-element.135), channel_id=1, source_target_pairs={{1,0},{5,4},{9,8},{13,12},{17,16},{21,20},{25,24},{29,28}} | collective-permute-start | bytes 589832 | tf_op jit(solution)/shard_map/ppermute | solution.py:303
  30.1 0.7 collective-permute-start.16
  30.8 1.3 %collective-permute-start.22 = (bf16[32,3072]{1,0:T(8,128)(2,1)S(1)}, bf16[32,3072]{1,0:T(8,128)(2,1)S(1)}, u32[]{:S(2)}, u32[]{:S(2)}) collective-permute-start(bf16[32,3072]{1,0:T(8,128)(2,1)S(1)} %get-tuple-element.144), channel_id=1, source_target_pairs={{1,0},{5,4},{9,8},{13,12},{17,16},{21,20},{25,24},{29,28}} | collective-permute-start | bytes 589832 | tf_op jit(solution)/shard_map/ppermute | solution.py:303
  32.2 1.3 %collective-permute-start.21 = (bf16[32,3072]{1,0:T(8,128)(2,1)S(1)}, bf16[32,3072]{1,0:T(8,128)(2,1)S(1)}, u32[]{:S(2)}, u32[]{:S(2)}) collective-permute-start(bf16[32,3072]{1,0:T(8,128)(2,1)S(1)} %get-tuple-element.143), channel_id=1, source_target_pairs={{1,0},{5,4},{9,8},{13,12},{17,16},{21,20},{25,24},{29,28}} | collective-permute-start | bytes 589832 | tf_op jit(solution)/shard_map/ppermute | solution.py:303
  33.5 23.1 %collective-permute-done.17.gin = bf16[32,3072]{1,0:T(8,128)(2,1)S(1)} collective-permute-done((bf16[32,3072]{1,0:T(8,128)(2,1)S(1)}, bf16[32,3072]{1,0:T(8,128)(2,1)S(1)}, u32[]{:S(2)}, u32[]{:S(2)}) %collective-permute-start.17) | collective-permute-done | bytes 196640 | tf_op jit(solution)/shard_map/ppermute | solution.py:303
  56.6 1.3 %collective-permute-start.20 = (bf16[32,3072]{1,0:T(8,128)(2,1)S(1)}, bf16[32,3072]{1,0:T(8,128)(2,1)S(1)}, u32[]{:S(2)}, u32[]{:S(2)}) collective-permute-start(bf16[32,3072]{1,0:T(8,128)(2,1)S(1)} %get-tuple-element.141), channel_id=1, source_target_pairs={{1,0},{5,4},{9,8},{13,12},{17,16},{21,20},{25,24},{29,28}} | collective-permute-start | bytes 589832 | tf_op jit(solution)/shard_map/ppermute | solution.py:303
  57.9 2.7 %collective-permute-done.22.gin = bf16[32,3072]{1,0:T(8,128)(2,1)S(1)} collective-permute-done((bf16[32,3072]{1,0:T(8,128)(2,1)S(1)}, bf16[32,3072]{1,0:T(8,128)(2,1)S(1)}, u32[]{:S(2)}, u32[]{:S(2)}) %collective-permute-start.22) | collective-permute-done | bytes 196640 | tf_op jit(solution)/shard_map/ppermute | solution.py:303
  60.7 3.6 %collective-permute-done.21.gin = bf16[32,3072]{1,0:T(8,128)(2,1)S(1)} collective-permute-done((bf16[32,3072]{1,0:T(8,128)(2,1)S(1)}, bf16[32,3072]{1,0:T(8,128)(2,1)S(1)}, u32[]{:S(2)}, u32[]{:S(2)}) %collective-permute-start.21) | collective-permute-done | bytes 196640 | tf_op jit(solution)/shard_map/ppermute | solution.py:303
  64.4 0.6 shard_map.62
  65.0 1.4 %collective-permute-done.20.gin = bf16[32,3072]{1,0:T(8,128)(2,1)S(1)} collective-permute-done((bf16[32,3072]{1,0:T(8,128)(2,1)S(1)}, bf16[32,3072]{1,0:T(8,128)(2,1)S(1)}, u32[]{:S(2)}, u32[]{:S(2)}) %collective-permute-start.20) | collective-permute-done | bytes 196640 | tf_op jit(solution)/shard_map/ppermute | solution.py:303
  66.6 0.5 collective-permute-start.12
  67.1 2.3 %collective-permute-done.12.got = bf16[24,4,16,128]{3,2,1,0:T(8,128)(2,1)S(1)} collective-permute-done((bf16[24,4,16,128]{3,2,1,0:T(8,128)(2,1)S(1)}, bf16[24,4,16,128]{3,2,1,0:T(8,128)(2,1)S(1)}, u32[]{:S(2)}, u32[]{:S(2)}) %collective-permute-start.12) | collective-permute-done | bytes 393248 | tf_op jit(solution)/shard_map/ppermute | solution.py:373
  69.5 0.5 shard_map.75
  70.0 0.4 collective-permute-start.24
  70.3 1.5 %collective-permute-start.26 = (bf16[2,36,16,128]{3,2,1,0:T(8,128)(2,1)S(1)}, bf16[2,36,16,128]{3,2,1,0:T(8,128)(2,1)S(1)}, u32[]{:S(2)}, u32[]{:S(2)}) collective-permute-start(bf16[2,36,16,128]{3,2,1,0:T(8,128)(2,1)S(1)} %get-tuple-element.151), channel_id=1, source_target_pairs={{0,16},{4,20},{8,24},{12,28},{16,0},{20,4},{24,8},{28,12},{1,17},{... | collective-permute-start | bytes 884744 | tf_op jit(solution)/shard_map/ppermute | solution.py:437
  71.8 0.5 shard_map.74
  72.3 6.8 %collective-permute-done.24.got.a1 = bf16[2,36,16,128]{3,2,1,0:T(8,128)(2,1)S(1)} collective-permute-done((bf16[2,36,16,128]{3,2,1,0:T(8,128)(2,1)S(1)}, bf16[2,36,16,128]{3,2,1,0:T(8,128)(2,1)S(1)}, u32[]{:S(2)}, u32[]{:S(2)}) %collective-permute-start.24) | collective-permute-done | bytes 294944 | tf_op jit(solution)/shard_map/ppermute | solution.py:437
  79.1 0.4 collective-permute-start.25
  79.5 1.6 %collective-permute-start.27 = (bf16[36,16,128]{2,1,0:T(8,128)(2,1)S(1)}, bf16[36,16,128]{2,1,0:T(8,128)(2,1)S(1)}, u32[]{:S(2)}, u32[]{:S(2)}) collective-permute-start(bf16[36,16,128]{2,1,0:T(8,128)(2,1)S(1)} %shard_map.77), channel_id=1, source_target_pairs={{0,8},{4,12},{8,0},{12,4},{16,24},{20,28},{24,16},{28,20},{1,9},{5... | collective-permute-start | bytes 442376 | tf_op jit(solution)/shard_map/ppermute | solution.py:437
  81.1 3.2 %collective-permute-done.25.a2 = bf16[36,16,128]{2,1,0:T(8,128)(2,1)S(1)} collective-permute-done((bf16[36,16,128]{2,1,0:T(8,128)(2,1)S(1)}, bf16[36,16,128]{2,1,0:T(8,128)(2,1)S(1)}, u32[]{:S(2)}, u32[]{:S(2)}) %collective-permute-start.25) | collective-permute-done | bytes 147488 | tf_op jit(solution)/shard_map/ppermute | solution.py:437
  84.3 0.4 collective-permute-done.27.b2
  84.7 1.1 %shard_map.78 = f32[16,1,72,128]{3,2,1,0:T(8,128)} custom-call(f32[1,72,16,128]{3,2,1,0:T(8,128)S(1)} %get-tuple-element.148.mine, bf16[2,36,16,128]{3,2,1,0:T(8,128)(2,1)S(1)} %collective-permute-done.24.got.a1, bf16[36,16,128]{2,1,0:T(8,128)(2,1)S(1)} %collective-permute-done.25.a2, bf16[2,36,16,128]{3,2,1,0:T(8,128)(2,1)S(1)} %collective-permute-done.26.got.b1, ...), custom_call_target="tpu_custom_call" | custom-call | flops 100000000 | bytes 3000000 | tf_op jit(solution)/shard_map/pallas_call | solution.py:32
  (43 shorter events, 0.8 us)
Async XLA Ops:
  2.2 8.1 %collective-permute-start = (bf16[32,3072]{1,0:T(8,128)(2,1)S(1)}, bf16[32,3072]{1,0:T(8,128)(2,1)S(1)}, u32[]{:S(2)}, u32[]{:S(2)}) collective-permute-start(bf16[32,3072]{1,0:T(8,128)(2,1)S(1)} %get-tuple-element.82), channel_id=1, source_target_pairs={{0,1},{4,5},{8,9},{12,13},{16,17},{20,21},{24,25},{28,29}} | collective-permute-start | bytes 589832 | tf_op jit(solution)/shard_map/ppermute | solution.py:303
  5.7 11.0 %collective-permute-start.4 = (bf16[32,3072]{1,0:T(8,128)(2,1)S(1)}, bf16[32,3072]{1,0:T(8,128)(2,1)S(1)}, u32[]{:S(2)}, u32[]{:S(2)}) collective-permute-start(bf16[32,3072]{1,0:T(8,128)(2,1)S(1)} %get-tuple-element.93), channel_id=1, source_target_pairs={{0,1},{4,5},{8,9},{12,13},{16,17},{20,21},{24,25},{28,29}} | collective-permute-start | bytes 589832 | tf_op jit(solution)/shard_map/ppermute | solution.py:303
  8.4 10.3 %collective-permute-start.3 = (bf16[32,3072]{1,0:T(8,128)(2,1)S(1)}, bf16[32,3072]{1,0:T(8,128)(2,1)S(1)}, u32[]{:S(2)}, u32[]{:S(2)}) collective-permute-start(bf16[32,3072]{1,0:T(8,128)(2,1)S(1)} %get-tuple-element.92), channel_id=1, source_target_pairs={{0,1},{4,5},{8,9},{12,13},{16,17},{20,21},{24,25},{28,29}} | collective-permute-start | bytes 589832 | tf_op jit(solution)/shard_map/ppermute | solution.py:303
  10.3 9.1 %collective-permute-start.2 = (bf16[32,3072]{1,0:T(8,128)(2,1)S(1)}, bf16[32,3072]{1,0:T(8,128)(2,1)S(1)}, u32[]{:S(2)}, u32[]{:S(2)}) collective-permute-start(bf16[32,3072]{1,0:T(8,128)(2,1)S(1)} %get-tuple-element.91), channel_id=1, source_target_pairs={{1,2},{5,6},{9,10},{13,14},{17,18},{21,22},{25,26},{29,30}} | collective-permute-start | bytes 589832 | tf_op jit(solution)/shard_map/ppermute | solution.py:303
  11.7 10.1 %collective-permute-start.1 = (bf16[32,3072]{1,0:T(8,128)(2,1)S(1)}, bf16[32,3072]{1,0:T(8,128)(2,1)S(1)}, u32[]{:S(2)}, u32[]{:S(2)}) collective-permute-start(bf16[32,3072]{1,0:T(8,128)(2,1)S(1)} %get-tuple-element.90), channel_id=1, source_target_pairs={{0,1},{4,5},{8,9},{12,13},{16,17},{20,21},{24,25},{28,29}} | collective-permute-start | bytes 589832 | tf_op jit(solution)/shard_map/ppermute | solution.py:303
  16.8 5.7 %collective-permute-start.6 = (bf16[32,3072]{1,0:T(8,128)(2,1)S(1)}, bf16[32,3072]{1,0:T(8,128)(2,1)S(1)}, u32[]{:S(2)}, u32[]{:S(2)}) collective-permute-start(bf16[32,3072]{1,0:T(8,128)(2,1)S(1)} %get-tuple-element.102), channel_id=1, source_target_pairs={{1,2},{5,6},{9,10},{13,14},{17,18},{21,22},{25,26},{29,30}} | collective-permute-start | bytes 589832 | tf_op jit(solution)/shard_map/ppermute | solution.py:303
  18.7 4.6 %collective-permute-start.8 = (bf16[32,3072]{1,0:T(8,128)(2,1)S(1)}, bf16[32,3072]{1,0:T(8,128)(2,1)S(1)}, u32[]{:S(2)}, u32[]{:S(2)}) collective-permute-start(bf16[32,3072]{1,0:T(8,128)(2,1)S(1)} %get-tuple-element.106), channel_id=1, source_target_pairs={{1,2},{5,6},{9,10},{13,14},{17,18},{21,22},{25,26},{29,30}} | collective-permute-start | bytes 589832 | tf_op jit(solution)/shard_map/ppermute | solution.py:303
  19.4 3.9 %collective-permute-start.9 = (bf16[32,3072]{1,0:T(8,128)(2,1)S(1)}, bf16[32,3072]{1,0:T(8,128)(2,1)S(1)}, u32[]{:S(2)}, u32[]{:S(2)}) collective-permute-start(bf16[32,3072]{1,0:T(8,128)(2,1)S(1)} %get-tuple-element.107), channel_id=1, source_target_pairs={{2,3},{6,7},{10,11},{14,15},{18,19},{22,23},{26,27},{30,31}} | collective-permute-start | bytes 589832 | tf_op jit(solution)/shard_map/ppermute | solution.py:303
  21.8 2.5 %collective-permute-start.5 = (bf16[32,3072]{1,0:T(8,128)(2,1)S(1)}, bf16[32,3072]{1,0:T(8,128)(2,1)S(1)}, u32[]{:S(2)}, u32[]{:S(2)}) collective-permute-start(bf16[32,3072]{1,0:T(8,128)(2,1)S(1)} %get-tuple-element.101), channel_id=1, source_target_pairs={{1,2},{5,6},{9,10},{13,14},{17,18},{21,22},{25,26},{29,30}} | collective-permute-start | bytes 589832 | tf_op jit(solution)/shard_map/ppermute | solution.py:303
  22.5 1.1 %copy-start = (bf16[128,3072]{1,0:T(8,128)(2,1)S(1)}, bf16[128,3072]{1,0:T(8,128)(2,1)}, u32[]{:S(2)}) copy-start(bf16[128,3072]{1,0:T(8,128)(2,1)} %seeds.7) | copy-start | bytes 2359300
  22.5 1.8 %collective-permute-start.7 = (bf16[32,3072]{1,0:T(8,128)(2,1)S(1)}, bf16[32,3072]{1,0:T(8,128)(2,1)S(1)}, u32[]{:S(2)}, u32[]{:S(2)}) collective-permute-start(bf16[32,3072]{1,0:T(8,128)(2,1)S(1)} %get-tuple-element.105), channel_id=1, source_target_pairs={{2,3},{6,7},{10,11},{14,15},{18,19},{22,23},{26,27},{30,31}} | collective-permute-start | bytes 589832 | tf_op jit(solution)/shard_map/ppermute | solution.py:303
  23.6 1.4 %collective-permute-start.11 = (bf16[32,3072]{1,0:T(8,128)(2,1)S(1)}, bf16[32,3072]{1,0:T(8,128)(2,1)S(1)}, u32[]{:S(2)}, u32[]{:S(2)}) collective-permute-start(bf16[32,3072]{1,0:T(8,128)(2,1)S(1)} %get-tuple-element.115), channel_id=1, source_target_pairs={{2,3},{3,2},{6,7},{7,6},{10,11},{11,10},{14,15},{15,14},{18,19},{1... | collective-permute-start | bytes 589832 | tf_op jit(solution)/shard_map/ppermute | solution.py:384
  24.3 2.3 %collective-permute-start.10 = (bf16[32,3072]{1,0:T(8,128)(2,1)S(1)}, bf16[32,3072]{1,0:T(8,128)(2,1)S(1)}, u32[]{:S(2)}, u32[]{:S(2)}) collective-permute-start(bf16[32,3072]{1,0:T(8,128)(2,1)S(1)} %get-tuple-element.114), channel_id=1, source_target_pairs={{2,3},{3,2},{6,7},{7,6},{10,11},{11,10},{14,15},{15,14},{18,19},{1... | collective-permute-start | bytes 589832 | tf_op jit(solution)/shard_map/ppermute | solution.py:384
  25.2 2.8 %collective-permute-start.15 = (bf16[32,3072]{1,0:T(8,128)(2,1)S(1)}, bf16[32,3072]{1,0:T(8,128)(2,1)S(1)}, u32[]{:S(2)}, u32[]{:S(2)}) collective-permute-start(bf16[32,3072]{1,0:T(8,128)(2,1)S(1)} %get-tuple-element.129), channel_id=1, source_target_pairs={{3,2},{7,6},{11,10},{15,14},{19,18},{23,22},{27,26},{31,30}} | collective-permute-start | bytes 589832 | tf_op jit(solution)/shard_map/ppermute | solution.py:303
  25.9 2.8 %collective-permute-start.14 = (bf16[32,3072]{1,0:T(8,128)(2,1)S(1)}, bf16[32,3072]{1,0:T(8,128)(2,1)S(1)}, u32[]{:S(2)}, u32[]{:S(2)}) collective-permute-start(bf16[32,3072]{1,0:T(8,128)(2,1)S(1)} %get-tuple-element.128), channel_id=1, source_target_pairs={{2,1},{6,5},{10,9},{14,13},{18,17},{22,21},{26,25},{30,29}} | collective-permute-start | bytes 589832 | tf_op jit(solution)/shard_map/ppermute | solution.py:303
  26.7 3.4 %collective-permute-start.13 = (bf16[32,3072]{1,0:T(8,128)(2,1)S(1)}, bf16[32,3072]{1,0:T(8,128)(2,1)S(1)}, u32[]{:S(2)}, u32[]{:S(2)}) collective-permute-start(bf16[32,3072]{1,0:T(8,128)(2,1)S(1)} %get-tuple-element.127), channel_id=1, source_target_pairs={{3,2},{7,6},{11,10},{15,14},{19,18},{23,22},{27,26},{31,30}} | collective-permute-start | bytes 589832 | tf_op jit(solution)/shard_map/ppermute | solution.py:303
  27.4 3.4 %collective-permute-start.19 = (bf16[32,3072]{1,0:T(8,128)(2,1)S(1)}, bf16[32,3072]{1,0:T(8,128)(2,1)S(1)}, u32[]{:S(2)}, u32[]{:S(2)}) collective-permute-start(bf16[32,3072]{1,0:T(8,128)(2,1)S(1)} %get-tuple-element.137), channel_id=1, source_target_pairs={{2,1},{6,5},{10,9},{14,13},{18,17},{22,21},{26,25},{30,29}} | collective-permute-start | bytes 589832 | tf_op jit(solution)/shard_map/ppermute | solution.py:303
  28.1 4.1 %collective-permute-start.18 = (bf16[32,3072]{1,0:T(8,128)(2,1)S(1)}, bf16[32,3072]{1,0:T(8,128)(2,1)S(1)}, u32[]{:S(2)}, u32[]{:S(2)}) collective-permute-start(bf16[32,3072]{1,0:T(8,128)(2,1)S(1)} %get-tuple-element.136), channel_id=1, source_target_pairs={{2,1},{6,5},{10,9},{14,13},{18,17},{22,21},{26,25},{30,29}} | collective-permute-start | bytes 589832 | tf_op jit(solution)/shard_map/ppermute | solution.py:303
  28.8 27.8 %collective-permute-start.17 = (bf16[32,3072]{1,0:T(8,128)(2,1)S(1)}, bf16[32,3072]{1,0:T(8,128)(2,1)S(1)}, u32[]{:S(2)}, u32[]{:S(2)}) collective-permute-start(bf16[32,3072]{1,0:T(8,128)(2,1)S(1)} %get-tuple-element.135), channel_id=1, source_target_pairs={{1,0},{5,4},{9,8},{13,12},{17,16},{21,20},{25,24},{29,28}} | collective-permute-start | bytes 589832 | tf_op jit(solution)/shard_map/ppermute | solution.py:303
  30.1 26.5 %collective-permute-start.16 = (bf16[32,3072]{1,0:T(8,128)(2,1)S(1)}, bf16[32,3072]{1,0:T(8,128)(2,1)S(1)}, u32[]{:S(2)}, u32[]{:S(2)}) collective-permute-start(bf16[32,3072]{1,0:T(8,128)(2,1)S(1)} %get-tuple-element.134), channel_id=1, source_target_pairs={{2,1},{6,5},{10,9},{14,13},{18,17},{22,21},{26,25},{30,29}} | collective-permute-start | bytes 589832 | tf_op jit(solution)/shard_map/ppermute | solution.py:303
  30.8 29.8 %collective-permute-start.22 = (bf16[32,3072]{1,0:T(8,128)(2,1)S(1)}, bf16[32,3072]{1,0:T(8,128)(2,1)S(1)}, u32[]{:S(2)}, u32[]{:S(2)}) collective-permute-start(bf16[32,3072]{1,0:T(8,128)(2,1)S(1)} %get-tuple-element.144), channel_id=1, source_target_pairs={{1,0},{5,4},{9,8},{13,12},{17,16},{21,20},{25,24},{29,28}} | collective-permute-start | bytes 589832 | tf_op jit(solution)/shard_map/ppermute | solution.py:303
  32.2 32.2 %collective-permute-start.21 = (bf16[32,3072]{1,0:T(8,128)(2,1)S(1)}, bf16[32,3072]{1,0:T(8,128)(2,1)S(1)}, u32[]{:S(2)}, u32[]{:S(2)}) collective-permute-start(bf16[32,3072]{1,0:T(8,128)(2,1)S(1)} %get-tuple-element.143), channel_id=1, source_target_pairs={{1,0},{5,4},{9,8},{13,12},{17,16},{21,20},{25,24},{29,28}} | collective-permute-start | bytes 589832 | tf_op jit(solution)/shard_map/ppermute | solution.py:303
  56.6 9.8 %collective-permute-start.20 = (bf16[32,3072]{1,0:T(8,128)(2,1)S(1)}, bf16[32,3072]{1,0:T(8,128)(2,1)S(1)}, u32[]{:S(2)}, u32[]{:S(2)}) collective-permute-start(bf16[32,3072]{1,0:T(8,128)(2,1)S(1)} %get-tuple-element.141), channel_id=1, source_target_pairs={{1,0},{5,4},{9,8},{13,12},{17,16},{21,20},{25,24},{29,28}} | collective-permute-start | bytes 589832 | tf_op jit(solution)/shard_map/ppermute | solution.py:303
  66.5 2.9 %collective-permute-start.23 = (bf16[4,32,3072]{2,1,0:T(8,128)(2,1)S(1)}, bf16[4,32,3072]{2,1,0:T(8,128)(2,1)S(1)}, u32[]{:S(2)}, u32[]{:S(2)}) collective-permute-start(bf16[4,32,3072]{2,1,0:T(8,128)(2,1)S(1)} %get-tuple-element.147), channel_id=1, source_target_pairs={{0,4},{4,0},{8,12},{12,8},{16,20},{20,16},{24,28},{28,24},{1,5},{5... | collective-permute-start | bytes 2359304 | tf_op jit(solution)/shard_map/ppermute | solution.py:408
  66.6 2.8 %collective-permute-start.12 = (bf16[24,4,16,128]{3,2,1,0:T(8,128)(2,1)S(1)}, bf16[24,4,16,128]{3,2,1,0:T(8,128)(2,1)S(1)}, u32[]{:S(2)}, u32[]{:S(2)}) collective-permute-start(bf16[24,4,16,128]{3,2,1,0:T(8,128)(2,1)S(1)} %get-tuple-element.126), channel_id=1, source_target_pairs={{0,4},{4,0},{8,12},{12,8},{16,20},{20,16},{24,28},{28,24},{1,5},{5... | collective-permute-start | bytes 1179656 | tf_op jit(solution)/shard_map/ppermute | solution.py:373
  70.0 9.1 %collective-permute-start.24 = (bf16[2,36,16,128]{3,2,1,0:T(8,128)(2,1)S(1)}, bf16[2,36,16,128]{3,2,1,0:T(8,128)(2,1)S(1)}, u32[]{:S(2)}, u32[]{:S(2)}) collective-permute-start(bf16[2,36,16,128]{3,2,1,0:T(8,128)(2,1)S(1)} %get-tuple-element.149), channel_id=1, source_target_pairs={{0,8},{4,12},{8,0},{12,4},{16,24},{20,28},{24,16},{28,20},{1,9},{5... | collective-permute-start | bytes 884744 | tf_op jit(solution)/shard_map/ppermute | solution.py:437
  70.3 9.2 %collective-permute-start.26 = (bf16[2,36,16,128]{3,2,1,0:T(8,128)(2,1)S(1)}, bf16[2,36,16,128]{3,2,1,0:T(8,128)(2,1)S(1)}, u32[]{:S(2)}, u32[]{:S(2)}) collective-permute-start(bf16[2,36,16,128]{3,2,1,0:T(8,128)(2,1)S(1)} %get-tuple-element.151), channel_id=1, source_target_pairs={{0,16},{4,20},{8,24},{12,28},{16,0},{20,4},{24,8},{28,12},{1,17},{... | collective-permute-start | bytes 884744 | tf_op jit(solution)/shard_map/ppermute | solution.py:437
  79.1 5.2 %collective-permute-start.25 = (bf16[36,16,128]{2,1,0:T(8,128)(2,1)S(1)}, bf16[36,16,128]{2,1,0:T(8,128)(2,1)S(1)}, u32[]{:S(2)}, u32[]{:S(2)}) collective-permute-start(bf16[36,16,128]{2,1,0:T(8,128)(2,1)S(1)} %shard_map.76), channel_id=1, source_target_pairs={{0,16},{4,20},{8,24},{12,28},{16,0},{20,4},{24,8},{28,12},{1,17},{... | collective-permute-start | bytes 442376 | tf_op jit(solution)/shard_map/ppermute | solution.py:437
  79.5 5.2 %collective-permute-start.27 = (bf16[36,16,128]{2,1,0:T(8,128)(2,1)S(1)}, bf16[36,16,128]{2,1,0:T(8,128)(2,1)S(1)}, u32[]{:S(2)}, u32[]{:S(2)}) collective-permute-start(bf16[36,16,128]{2,1,0:T(8,128)(2,1)S(1)} %shard_map.77), channel_id=1, source_target_pairs={{0,8},{4,12},{8,0},{12,4},{16,24},{20,28},{24,16},{28,20},{1,9},{5... | collective-permute-start | bytes 442376 | tf_op jit(solution)/shard_map/ppermute | solution.py:437

commit v5 on v4

--- a/solution.py
+++ b/solution.py
@@ -18,6 +18,9 @@
 LIMIT = 20 * 1024 * 1024
 CHUNKS = 4
 MEET = 1
+PIECES = 4
+COST_LAST = 10**10
+PARTS = 3
 
 
 def call(body, outs, ins, scratch=(), aliases=None, flops=10**8, nbytes=3 * 10**6):
@@ -216,10 +219,10 @@
         kz[m] = (gin[...].astype(F32) * kd[m]).astype(BF16)
 
     for ref in zs:
-        ref[...] = kz[...]
-
-
-def turned_body(nb, blk, half, parts, kh, kd_in, keep, send, kd, uT):
+        ref[...] = kz[m]
+
+
+def turned_body(nb, blk, half, parts, kh, kd_in, kz, keep, send, early, kd, uT):
     M, R, E = kh.shape
     hf = kh[...].reshape(M * R, E).astype(F32)
     scale = norm(hf)
@@ -230,9 +233,10 @@
         for j in range(parts):
             keep[n, j] = uT[n, j, me]
             send[n, j] = uT[n, j, 1 - me]
-
-
-def term_body(jobs, M, nb, kpc, blk, half, rows, keep, got, kz, zgot, *refs):
+    early[...] = kz[: M - 1]
+
+
+def term_body(jobs, M, nb, kpc, blk, half, rows, keep, got, kz, zearly, zlast, *refs):
     outs = refs
     chip = lax.axis_index("dp") // 2
     for n in range(nb):
@@ -240,7 +244,7 @@
         todo = [(out, i, j, n - lo) for out, (js, lo, hi) in zip(outs, jobs) if lo <= n < hi for i, j in enumerate(js)]
         if not todo:
             continue
-        z = jnp.concatenate([kz[m, :, c] for m in range(M)] + [zgot[m, :, c] for m in range(M)], axis=0)
+        z = jnp.concatenate([kz[m, :, c] for m in range(M)] + [zearly[m, :, c] for m in range(M - 1)] + [zlast[:, c]], axis=0)
         pieces = []
         for k in range(kpc):
             r = rows[0, n * kpc + k]
@@ -257,19 +261,26 @@
     out[...] = (mine[0] + got[1].astype(F32)).astype(BF16)
 
 
-def final_body(mine, a1, a2, b1, b2, out, buf, sems):
-    nt = mine.shape[1]
-    cut = nt // 2
-    step = cut // 3 if cut % 24 == 0 else cut
+def final_body(ends, mine, *refs):
+    firsts, seconds = refs[: len(ends)], refs[len(ends) : 2 * len(ends)]
+    out, flat, buf, sems = refs[2 * len(ends) :]
+    half, nt, blk = buf.shape
+    parts = sems.shape[0]
+    step = nt // parts
     stores = []
-    for t in range(nt):
-        one, two, at = (a1, a2, t) if t < cut else (b1, b2, t - cut)
-        buf[:, t, :] = mine[0, t] + (one[0, at].astype(F32) + two[at].astype(F32))
-        if (t + 1) % step == 0:
-            part = pl.ds(t + 1 - step, step)
-            c = pltpu.make_async_copy(buf.at[:, part], out.at[:, 0, part], sems.at[t // step])
-            c.start()
-            stores.append(c)
+    for p in range(parts):
+        for t in range(p * step, (p + 1) * step):
+            piece = [t < end for end in ends].index(True)
+            at = t - ([0] + ends)[piece]
+            both = firsts[piece][0, at].astype(F32) + seconds[piece][at].astype(F32)
+            flat[t * half : (t + 1) * half] = mine[0, t] + both
+        for g in range(p * step, (p + 1) * step, 8):
+            for r in range(half):
+                buf[r, g : g + 8, :] = flat[pl.ds(g * half + r, 8, stride=half), :]
+        part = pl.ds(p * step, step)
+        c = pltpu.make_async_copy(buf.at[:, part], out.at[:, 0, part], sems.at[p])
+        c.start()
+        stores.append(c)
     for c in stores:
         c.wait()
 
@@ -355,7 +366,7 @@
         )
 
     half = blk // groups
-    direct = half % 16 == 0 and groups == 8 and nb % 2 == 0 and last > 0
+    direct = half % 16 == 0 and groups == 8 and nt % 24 == 0 and nb % PIECES == 0 and last > 0
     swap = [(i, i ^ 1) for i in range(groups)]
     swapped = {}
 
@@ -363,14 +374,15 @@
         nonlocal kd
         parts = groups // 2
         shape = ((nb, parts, half, total), BF16, VM)
-        swapped["keep"], send, kd = call(
+        swapped["keep"], send, early, kd = call(
             functools.partial(turned_body, nb, blk, half, parts),
-            [shape, shape, kd_s],
-            [(kh, VM), (kd, VM)],
+            [shape, shape, ((M - 1, R, E), BF16, VM), kd_s],
+            [(kh, VM), (kd, VM), (kz, VM)],
             [pltpu.VMEM((nb, parts, 2, half, total), BF16)],
-            {1: 2},
+            {1: 3},
         )
         swapped["got"] = lax.ppermute(send, "dp", swap)
+        swapped["early"] = lax.ppermute(early, "dp", swap)
 
     def meet(a, b):
         nonlocal kh, kd, kz
@@ -399,10 +411,11 @@
                 turned()
             kz, *z = call(
                 functools.partial(first_body, m),
-                [kz_s] * (1 + ends),
+                [kz_s] + [line] * ends,
                 [(held[m], VM), (kd, VM), (kz, VM)] + ([(swapped["keep"], VM)] if ends else []),
                 [],
                 {2: 0},
+                *([COST_LAST, COST_LAST // 100] if ends else []),
             )
             if ends:
                 swapped["z"] = lax.ppermute(z[0], "dp", swap)
@@ -423,13 +436,13 @@
             load(0, 0)
 
     if direct:
-        mid, cut = nb // 2, nt // 2
 
         def term(jobs, dtype):
             return call(
                 functools.partial(term_body, jobs, M, nb, kpc, blk, half),
                 [((len(js), (hi - lo) * kpc, half, blk), dtype, VM) for js, lo, hi in jobs],
-                [(rows, SM), (swapped["keep"], VM), (swapped["got"], VM), (kz, VM), (swapped["z"], VM)],
+                [(rows, SM), (swapped["keep"], VM), (swapped["got"], VM), (kz, VM)]
+                + [(swapped["early"], VM), (swapped["z"], VM)],
                 [],
             )
 
@@ -437,19 +450,20 @@
             return lax.ppermute(array, "dp", [(i, i ^ (2 * j)) for i in range(groups)])
 
         def relay(mine, got):
-            (out,) = call(relay_body, [((cut, half, blk), BF16, VM)], [(mine, VM), (got, VM)])
+            (out,) = call(relay_body, [(mine.shape[1:], BF16, VM)], [(mine, VM), (got, VM)])
             return out
 
-        send_a, send_b = term([((1, 3), 0, mid), ((2, 3), mid, nb)], BF16)
-        got_a, got_b = across(send_a, 1), across(send_b, 2)
-        mine, next_a, next_b = term([((0,), 0, nb), ((2,), 0, mid), ((1,), mid, nb)], F32)
-        last_a = across(relay(next_a, got_a), 2)
-        last_b = across(relay(next_b, got_b), 1)
+        cut = nb // PIECES
+        routes = [(1 + p % 2, p * cut, (p + 1) * cut) for p in range(PIECES)]
+        sends = term([((j, 3), lo, hi) for j, lo, hi in routes], BF16)
+        firsts = [across(send, j) for send, (j, lo, hi) in zip(sends, routes)]
+        mine, *after = term([((0,), 0, nb)] + [((3 - j,), lo, hi) for j, lo, hi in routes], F32)
+        seconds = [across(relay(mid, got), 3 - j) for mid, got, (j, lo, hi) in zip(after, firsts, routes)]
         (out,) = call(
-            final_body,
+            functools.partial(final_body, [hi * kpc for j, lo, hi in routes]),
             [((half, 1, nt, blk), F32, HBM)],
-            [(mine, VM), (got_a, VM), (last_a, VM), (got_b, VM), (last_b, VM)],
-            [pltpu.VMEM((half, nt, blk), F32), dma((6,))],
+            [(mine, VM)] + [(x, VM) for x in firsts + seconds],
+            [pltpu.VMEM((nt * half, blk), F32), pltpu.VMEM((half, nt, blk), F32), dma((PARTS,))],
         )
         return out
     hf = kh.reshape(total, E).astype(F32)

time: 86.5 us -> 84.6 us (0.978)
  waiting for transfers between devices: 47.2 us -> 41 us
  starting transfers between devices: 29.5 us -> 34 us
    ppermute x4 -> x8, waiting for transfers between devices: 10.4 us -> 5.72 us  [across(): return lax.ppermute(array, 'dp', [(i, i ^ 2 * j) for i in range(groups)])]
    ppermute x4 -> x8, starting transfers between devices: 3.79 us -> 8.17 us  [across(): return lax.ppermute(array, 'dp', [(i, i ^ 2 * j) for i in range(groups)])]
    ppermute x1, waiting for transfers between devices: 2.34 us -> 0.01 us  [turned(): swapped['got'] = lax.ppermute(send, 'dp', swap)]
    ppermute x1, waiting for transfers between devices: 0.01 us -> 1.43 us  [step(): swapped['z'] = lax.ppermute(z[0], 'dp', swap)]
    pallas_call x33 -> x35, Pallas kernels: 8.33 us -> 8.16 us  [call(): pl.pallas_call(body, out_shape=out_shape, in_specs=in_specs, out_specs=ou...]
  transfers between devices with their start and end apart: 28 -> 33, of which waited for: 11 -> 13; matrix products, arithmetic and copies ran while one was open for 0% -> 0% of each run, Pallas kernels for 5% -> 5%
where the time goes in v5:
time: 84.6 us; the launch traced here: 84.1 us
  waiting for transfers between devices  41 us (48%)
  starting transfers between devices  34 us (40%)
  Pallas kernels  8.16 us (10%)
    ppermute x20, waiting for transfers between devices, hop(): return lax.ppermute(array, 'section', [(a, b)])  33.9 us
    ppermute x20, starting transfers between devices, hop(): return lax.ppermute(array, 'section', [(a, b)])  23.8 us
    ppermute x8, starting transfers between devices, across(): return lax.ppermute(array, 'dp', [(i, i ^ 2 * j) for i in range(groups)])  8.17 us
    pallas_call x35, Pallas kernels, call(): pl.pallas_call(body, out_shape=out_shape, in_specs=in_specs, out_specs=ou...  8.16 us
    ppermute x8, waiting for transfers between devices, across(): return lax.ppermute(array, 'dp', [(i, i ^ 2 * j) for i in range(groups)])  5.72 us
  transfers between devices with their start and end apart: 33, of which 13 were waited for; matrix products, arithmetic and copies ran while one was open for 0% of the time, Pallas kernels for 5%

profile of v5, /device:TPU:0, one launch (start us, length us, event | category | flops | bytes accessed | tf_op | source)
XLA Modules:
  0.0 84.1 jit_solution(3978478856651055175)
XLA Ops:
  0.0 2.2 %shard_map.46 = (bf16[72,128,128]{2,1,0:T(8,128)(2,1)S(1)}, s32[1,72]{1,0:T(1,128)S(4)}, bf16[4,32,3072]{2,1,0:T(8,128)(2,1)S(1)}, f32[4,32,3072]{2,1,0:T(8,128)...) custom-call(bf16[1,72,128,128]{3,2,1,0:T(8,128)(2,1)} %tiles.3, s32[1,72]{1,0:T(1,128)} %rows_h.3, ...), custom_call_target="tpu_custom_call" | custom-call | flops 100000000 | bytes 3000000 | tf_op jit(solution)/shard_map/pallas_call | solution.py:35
  2.2 2.8 %collective-permute-start = (bf16[32,3072]{1,0:T(8,128)(2,1)S(1)}, bf16[32,3072]{1,0:T(8,128)(2,1)S(1)}, u32[]{:S(2)}, u32[]{:S(2)}) collective-permute-start(bf16[32,3072]{1,0:T(8,128)(2,1)S(1)} %get-tuple-element.87), channel_id=1, source_target_pairs={{0,1},{4,5},{8,9},{12,13},{16,17},{20,21},{24,25},{28,29}} | collective-permute-start | bytes 589832 | tf_op jit(solution)/shard_map/ppermute | solution.py:314
  5.0 0.7 shard_map.48
  5.7 1.3 %collective-permute-start.4 = (bf16[32,3072]{1,0:T(8,128)(2,1)S(1)}, bf16[32,3072]{1,0:T(8,128)(2,1)S(1)}, u32[]{:S(2)}, u32[]{:S(2)}) collective-permute-start(bf16[32,3072]{1,0:T(8,128)(2,1)S(1)} %get-tuple-element.98), channel_id=1, source_target_pairs={{0,1},{4,5},{8,9},{12,13},{16,17},{20,21},{24,25},{28,29}} | collective-permute-start | bytes 589832 | tf_op jit(solution)/shard_map/ppermute | solution.py:314
  7.0 0.7 shard_map.47
  7.8 0.7 shard_map.49
  8.4 1.3 %collective-permute-start.3 = (bf16[32,3072]{1,0:T(8,128)(2,1)S(1)}, bf16[32,3072]{1,0:T(8,128)(2,1)S(1)}, u32[]{:S(2)}, u32[]{:S(2)}) collective-permute-start(bf16[32,3072]{1,0:T(8,128)(2,1)S(1)} %get-tuple-element.97), channel_id=1, source_target_pairs={{0,1},{4,5},{8,9},{12,13},{16,17},{20,21},{24,25},{28,29}} | collective-permute-start | bytes 589832 | tf_op jit(solution)/shard_map/ppermute | solution.py:314
  9.8 0.6 collective-permute-done.refs_2_
  10.3 0.7 collective-permute-start.2
  11.0 0.7 shard_map.51
  11.7 5.1 %collective-permute-start.1 = (bf16[32,3072]{1,0:T(8,128)(2,1)S(1)}, bf16[32,3072]{1,0:T(8,128)(2,1)S(1)}, u32[]{:S(2)}, u32[]{:S(2)}) collective-permute-start(bf16[32,3072]{1,0:T(8,128)(2,1)S(1)} %get-tuple-element.95), channel_id=1, source_target_pairs={{0,1},{4,5},{8,9},{12,13},{16,17},{20,21},{24,25},{28,29}} | collective-permute-start | bytes 589832 | tf_op jit(solution)/shard_map/ppermute | solution.py:314
  16.8 0.7 collective-permute-start.6
  17.5 1.3 %collective-permute-done.3.refs_2_ = bf16[32,3072]{1,0:T(8,128)(2,1)S(1)} collective-permute-done((bf16[32,3072]{1,0:T(8,128)(2,1)S(1)}, bf16[32,3072]{1,0:T(8,128)(2,1)S(1)}, u32[]{:S(2)}, u32[]{:S(2)}) %collective-permute-start.3) | collective-permute-done | bytes 196640 | tf_op jit(solution)/shard_map/ppermute | solution.py:314
  18.7 0.7 collective-permute-start.8
  19.4 0.7 collective-permute-start.9
  20.1 1.7 %collective-permute-done.1.refs_2_ = bf16[32,3072]{1,0:T(8,128)(2,1)S(1)} collective-permute-done((bf16[32,3072]{1,0:T(8,128)(2,1)S(1)}, bf16[32,3072]{1,0:T(8,128)(2,1)S(1)}, u32[]{:S(2)}, u32[]{:S(2)}) %collective-permute-start.1) | collective-permute-done | bytes 196640 | tf_op jit(solution)/shard_map/ppermute | solution.py:314
  21.8 0.7 collective-permute-start.5
  22.5 0.8 collective-permute-start.7
  23.6 0.7 collective-permute-start.11
  24.3 0.7 collective-permute-start.10
  25.2 0.7 collective-permute-start.12
  25.9 0.7 collective-permute-start.16
  26.7 0.7 collective-permute-start.15
  27.4 0.7 collective-permute-start.14
  28.1 0.7 collective-permute-start.13
  28.8 1.3 %collective-permute-start.20 = (bf16[32,3072]{1,0:T(8,128)(2,1)S(1)}, bf16[32,3072]{1,0:T(8,128)(2,1)S(1)}, u32[]{:S(2)}, u32[]{:S(2)}) collective-permute-start(bf16[32,3072]{1,0:T(8,128)(2,1)S(1)} %get-tuple-element.144), channel_id=1, source_target_pairs={{1,0},{5,4},{9,8},{13,12},{17,16},{21,20},{25,24},{29,28}} | collective-permute-start | bytes 589832 | tf_op jit(solution)/shard_map/ppermute | solution.py:314
  30.1 0.7 collective-permute-start.19
  30.8 1.3 %collective-permute-start.18 = (bf16[32,3072]{1,0:T(8,128)(2,1)S(1)}, bf16[32,3072]{1,0:T(8,128)(2,1)S(1)}, u32[]{:S(2)}, u32[]{:S(2)}) collective-permute-start(bf16[32,3072]{1,0:T(8,128)(2,1)S(1)} %get-tuple-element.142), channel_id=1, source_target_pairs={{1,0},{5,4},{9,8},{13,12},{17,16},{21,20},{25,24},{29,28}} | collective-permute-start | bytes 589832 | tf_op jit(solution)/shard_map/ppermute | solution.py:314
  32.2 1.3 %collective-permute-start.17 = (bf16[32,3072]{1,0:T(8,128)(2,1)S(1)}, bf16[32,3072]{1,0:T(8,128)(2,1)S(1)}, u32[]{:S(2)}, u32[]{:S(2)}) collective-permute-start(bf16[32,3072]{1,0:T(8,128)(2,1)S(1)} %get-tuple-element.141), channel_id=1, source_target_pairs={{1,0},{5,4},{9,8},{13,12},{17,16},{21,20},{25,24},{29,28}} | collective-permute-start | bytes 589832 | tf_op jit(solution)/shard_map/ppermute | solution.py:314
  33.5 23.1 %collective-permute-done.20.gin = bf16[32,3072]{1,0:T(8,128)(2,1)S(1)} collective-permute-done((bf16[32,3072]{1,0:T(8,128)(2,1)S(1)}, bf16[32,3072]{1,0:T(8,128)(2,1)S(1)}, u32[]{:S(2)}, u32[]{:S(2)}) %collective-permute-start.20) | collective-permute-done | bytes 196640 | tf_op jit(solution)/shard_map/ppermute | solution.py:314
  56.6 1.3 %collective-permute-start.22 = (bf16[32,3072]{1,0:T(8,128)(2,1)S(1)}, bf16[32,3072]{1,0:T(8,128)(2,1)S(1)}, u32[]{:S(2)}, u32[]{:S(2)}) collective-permute-start(bf16[32,3072]{1,0:T(8,128)(2,1)S(1)} %get-tuple-element.149), channel_id=1, source_target_pairs={{1,0},{5,4},{9,8},{13,12},{17,16},{21,20},{25,24},{29,28}} | collective-permute-start | bytes 589832 | tf_op jit(solution)/shard_map/ppermute | solution.py:314
  57.9 2.7 %collective-permute-done.18.gin = bf16[32,3072]{1,0:T(8,128)(2,1)S(1)} collective-permute-done((bf16[32,3072]{1,0:T(8,128)(2,1)S(1)}, bf16[32,3072]{1,0:T(8,128)(2,1)S(1)}, u32[]{:S(2)}, u32[]{:S(2)}) %collective-permute-start.18) | collective-permute-done | bytes 196640 | tf_op jit(solution)/shard_map/ppermute | solution.py:314
  60.7 3.6 %collective-permute-done.17.gin = bf16[32,3072]{1,0:T(8,128)(2,1)S(1)} collective-permute-done((bf16[32,3072]{1,0:T(8,128)(2,1)S(1)}, bf16[32,3072]{1,0:T(8,128)(2,1)S(1)}, u32[]{:S(2)}, u32[]{:S(2)}) %collective-permute-start.17) | collective-permute-done | bytes 196640 | tf_op jit(solution)/shard_map/ppermute | solution.py:314
  64.4 0.6 shard_map.72
  65.1 0.5 collective-permute-start.23
  65.6 0.8 collective-permute-done.22.gin
  66.6 1.4 %collective-permute-done.24.zlast = bf16[32,3072]{1,0:T(8,128)(2,1)S(1)} collective-permute-done((bf16[32,3072]{1,0:T(8,128)(2,1)S(1)}, bf16[32,3072]{1,0:T(8,128)(2,1)S(1)}, u32[]{:S(2)}, u32[]{:S(2)}) %collective-permute-start.24) | collective-permute-done | bytes 196640 | tf_op jit(solution)/shard_map/ppermute | solution.py:421
  68.0 0.5 shard_map.75
  68.9 1.5 %collective-permute-start.26 = (bf16[2,18,16,128]{3,2,1,0:T(8,128)(2,1)S(1)}, bf16[2,18,16,128]{3,2,1,0:T(8,128)(2,1)S(1)}, u32[]{:S(2)}, u32[]{:S(2)}) collective-permute-start(bf16[2,18,16,128]{3,2,1,0:T(8,128)(2,1)S(1)} %get-tuple-element.156), channel_id=1, source_target_pairs={{0,16},{4,20},{8,24},{12,28},{16,0},{20,4},{24,8},{28,12},{1,17},{... | collective-permute-start | bytes 442376 | tf_op jit(solution)/shard_map/ppermute | solution.py:450
  70.4 0.6 collective-permute-start.27
  71.0 1.7 %collective-permute-start.28 = (bf16[2,18,16,128]{3,2,1,0:T(8,128)(2,1)S(1)}, bf16[2,18,16,128]{3,2,1,0:T(8,128)(2,1)S(1)}, u32[]{:S(2)}, u32[]{:S(2)}) collective-permute-start(bf16[2,18,16,128]{3,2,1,0:T(8,128)(2,1)S(1)} %get-tuple-element.158), channel_id=1, source_target_pairs={{0,16},{4,20},{8,24},{12,28},{16,0},{20,4},{24,8},{28,12},{1,17},{... | collective-permute-start | bytes 442376 | tf_op jit(solution)/shard_map/ppermute | solution.py:450
  72.7 0.5 shard_map.74
  73.1 2.2 %collective-permute-done.25.got.refs_0_ = bf16[2,18,16,128]{3,2,1,0:T(8,128)(2,1)S(1)} collective-permute-done((bf16[2,18,16,128]{3,2,1,0:T(8,128)(2,1)S(1)}, bf16[2,18,16,128]{3,2,1,0:T(8,128)(2,1)S(1)}, u32[]{:S(2)}, u32[]{:S(2)}) %collective-permute-start.25) | collective-permute-done | bytes 147488 | tf_op jit(solution)/shard_map/ppermute | solution.py:450
  75.7 1.7 %collective-permute-start.30 = (bf16[18,16,128]{2,1,0:T(8,128)(2,1)S(1)}, bf16[18,16,128]{2,1,0:T(8,128)(2,1)S(1)}, u32[]{:S(2)}, u32[]{:S(2)}) collective-permute-start(bf16[18,16,128]{2,1,0:T(8,128)(2,1)S(1)} %shard_map.77), channel_id=1, source_target_pairs={{0,8},{4,12},{8,0},{12,4},{16,24},{20,28},{24,16},{28,20},{1,9},{5... | collective-permute-start | bytes 221192 | tf_op jit(solution)/shard_map/ppermute | solution.py:450
  77.4 1.0 %collective-permute-done.27.got.refs_2_ = bf16[2,18,16,128]{3,2,1,0:T(8,128)(2,1)S(1)} collective-permute-done((bf16[2,18,16,128]{3,2,1,0:T(8,128)(2,1)S(1)}, bf16[2,18,16,128]{3,2,1,0:T(8,128)(2,1)S(1)}, u32[]{:S(2)}, u32[]{:S(2)}) %collective-permute-start.27) | collective-permute-done | bytes 147488 | tf_op jit(solution)/shard_map/ppermute | solution.py:450
  78.6 1.9 %collective-permute-start.32 = (bf16[18,16,128]{2,1,0:T(8,128)(2,1)S(1)}, bf16[18,16,128]{2,1,0:T(8,128)(2,1)S(1)}, u32[]{:S(2)}, u32[]{:S(2)}) collective-permute-start(bf16[18,16,128]{2,1,0:T(8,128)(2,1)S(1)} %shard_map.79), channel_id=1, source_target_pairs={{0,8},{4,12},{8,0},{12,4},{16,24},{20,28},{24,16},{28,20},{1,9},{5... | collective-permute-start | bytes 221192 | tf_op jit(solution)/shard_map/ppermute | solution.py:450
  80.6 2.3 %collective-permute-done.31.refs_6_ = bf16[18,16,128]{2,1,0:T(8,128)(2,1)S(1)} collective-permute-done((bf16[18,16,128]{2,1,0:T(8,128)(2,1)S(1)}, bf16[18,16,128]{2,1,0:T(8,128)(2,1)S(1)}, u32[]{:S(2)}, u32[]{:S(2)}) %collective-permute-start.31) | collective-permute-done | bytes 73760 | tf_op jit(solution)/shard_map/ppermute | solution.py:450
  83.0 1.0 %shard_map.80 = f32[16,1,72,128]{3,2,1,0:T(8,128)} custom-call(f32[1,72,16,128]{3,2,1,0:T(8,128)S(1)} %get-tuple-element.154.mine, bf16[2,18,16,128]{3,2,1,0:T(8,128)(2,1)S(1)} %collective-permute-done.25.got.refs_0_, bf16[2,18,16,128]{3,2,1,0:T(8,128)(2,1)S(1)} %collective-permute-done.26.got.refs_1_, ...), custom_call_target="tpu_custom_call" | custom-call | flops 100000000 | bytes 3000000 | tf_op jit(solution)/shard_map/pallas_call | solution.py:35
  (55 shorter events, 2.2 us)
Async XLA Ops:
  2.2 8.1 %collective-permute-start = (bf16[32,3072]{1,0:T(8,128)(2,1)S(1)}, bf16[32,3072]{1,0:T(8,128)(2,1)S(1)}, u32[]{:S(2)}, u32[]{:S(2)}) collective-permute-start(bf16[32,3072]{1,0:T(8,128)(2,1)S(1)} %get-tuple-element.87), channel_id=1, source_target_pairs={{0,1},{4,5},{8,9},{12,13},{16,17},{20,21},{24,25},{28,29}} | collective-permute-start | bytes 589832 | tf_op jit(solution)/shard_map/ppermute | solution.py:314
  5.7 11.0 %collective-permute-start.4 = (bf16[32,3072]{1,0:T(8,128)(2,1)S(1)}, bf16[32,3072]{1,0:T(8,128)(2,1)S(1)}, u32[]{:S(2)}, u32[]{:S(2)}) collective-permute-start(bf16[32,3072]{1,0:T(8,128)(2,1)S(1)} %get-tuple-element.98), channel_id=1, source_target_pairs={{0,1},{4,5},{8,9},{12,13},{16,17},{20,21},{24,25},{28,29}} | collective-permute-start | bytes 589832 | tf_op jit(solution)/shard_map/ppermute | solution.py:314
  8.4 10.3 %collective-permute-start.3 = (bf16[32,3072]{1,0:T(8,128)(2,1)S(1)}, bf16[32,3072]{1,0:T(8,128)(2,1)S(1)}, u32[]{:S(2)}, u32[]{:S(2)}) collective-permute-start(bf16[32,3072]{1,0:T(8,128)(2,1)S(1)} %get-tuple-element.97), channel_id=1, source_target_pairs={{0,1},{4,5},{8,9},{12,13},{16,17},{20,21},{24,25},{28,29}} | collective-permute-start | bytes 589832 | tf_op jit(solution)/shard_map/ppermute | solution.py:314
  10.3 9.1 %collective-permute-start.2 = (bf16[32,3072]{1,0:T(8,128)(2,1)S(1)}, bf16[32,3072]{1,0:T(8,128)(2,1)S(1)}, u32[]{:S(2)}, u32[]{:S(2)}) collective-permute-start(bf16[32,3072]{1,0:T(8,128)(2,1)S(1)} %get-tuple-element.96), channel_id=1, source_target_pairs={{1,2},{5,6},{9,10},{13,14},{17,18},{21,22},{25,26},{29,30}} | collective-permute-start | bytes 589832 | tf_op jit(solution)/shard_map/ppermute | solution.py:314
  11.7 10.1 %collective-permute-start.1 = (bf16[32,3072]{1,0:T(8,128)(2,1)S(1)}, bf16[32,3072]{1,0:T(8,128)(2,1)S(1)}, u32[]{:S(2)}, u32[]{:S(2)}) collective-permute-start(bf16[32,3072]{1,0:T(8,128)(2,1)S(1)} %get-tuple-element.95), channel_id=1, source_target_pairs={{0,1},{4,5},{8,9},{12,13},{16,17},{20,21},{24,25},{28,29}} | collective-permute-start | bytes 589832 | tf_op jit(solution)/shard_map/ppermute | solution.py:314
  16.8 5.7 %collective-permute-start.6 = (bf16[32,3072]{1,0:T(8,128)(2,1)S(1)}, bf16[32,3072]{1,0:T(8,128)(2,1)S(1)}, u32[]{:S(2)}, u32[]{:S(2)}) collective-permute-start(bf16[32,3072]{1,0:T(8,128)(2,1)S(1)} %get-tuple-element.107), channel_id=1, source_target_pairs={{1,2},{5,6},{9,10},{13,14},{17,18},{21,22},{25,26},{29,30}} | collective-permute-start | bytes 589832 | tf_op jit(solution)/shard_map/ppermute | solution.py:314
  18.7 4.6 %collective-permute-start.8 = (bf16[32,3072]{1,0:T(8,128)(2,1)S(1)}, bf16[32,3072]{1,0:T(8,128)(2,1)S(1)}, u32[]{:S(2)}, u32[]{:S(2)}) collective-permute-start(bf16[32,3072]{1,0:T(8,128)(2,1)S(1)} %get-tuple-element.111), channel_id=1, source_target_pairs={{1,2},{5,6},{9,10},{13,14},{17,18},{21,22},{25,26},{29,30}} | collective-permute-start | bytes 589832 | tf_op jit(solution)/shard_map/ppermute | solution.py:314
  19.4 3.9 %collective-permute-start.9 = (bf16[32,3072]{1,0:T(8,128)(2,1)S(1)}, bf16[32,3072]{1,0:T(8,128)(2,1)S(1)}, u32[]{:S(2)}, u32[]{:S(2)}) collective-permute-start(bf16[32,3072]{1,0:T(8,128)(2,1)S(1)} %get-tuple-element.112), channel_id=1, source_target_pairs={{2,3},{6,7},{10,11},{14,15},{18,19},{22,23},{26,27},{30,31}} | collective-permute-start | bytes 589832 | tf_op jit(solution)/shard_map/ppermute | solution.py:314
  21.8 2.5 %collective-permute-start.5 = (bf16[32,3072]{1,0:T(8,128)(2,1)S(1)}, bf16[32,3072]{1,0:T(8,128)(2,1)S(1)}, u32[]{:S(2)}, u32[]{:S(2)}) collective-permute-start(bf16[32,3072]{1,0:T(8,128)(2,1)S(1)} %get-tuple-element.106), channel_id=1, source_target_pairs={{1,2},{5,6},{9,10},{13,14},{17,18},{21,22},{25,26},{29,30}} | collective-permute-start | bytes 589832 | tf_op jit(solution)/shard_map/ppermute | solution.py:314
  22.5 1.1 %copy-start = (bf16[128,3072]{1,0:T(8,128)(2,1)S(1)}, bf16[128,3072]{1,0:T(8,128)(2,1)}, u32[]{:S(2)}) copy-start(bf16[128,3072]{1,0:T(8,128)(2,1)} %seeds.7) | copy-start | bytes 2359300
  22.5 1.8 %collective-permute-start.7 = (bf16[32,3072]{1,0:T(8,128)(2,1)S(1)}, bf16[32,3072]{1,0:T(8,128)(2,1)S(1)}, u32[]{:S(2)}, u32[]{:S(2)}) collective-permute-start(bf16[32,3072]{1,0:T(8,128)(2,1)S(1)} %get-tuple-element.110), channel_id=1, source_target_pairs={{2,3},{6,7},{10,11},{14,15},{18,19},{22,23},{26,27},{30,31}} | collective-permute-start | bytes 589832 | tf_op jit(solution)/shard_map/ppermute | solution.py:314
  23.6 1.4 %collective-permute-start.11 = (bf16[32,3072]{1,0:T(8,128)(2,1)S(1)}, bf16[32,3072]{1,0:T(8,128)(2,1)S(1)}, u32[]{:S(2)}, u32[]{:S(2)}) collective-permute-start(bf16[32,3072]{1,0:T(8,128)(2,1)S(1)} %get-tuple-element.120), channel_id=1, source_target_pairs={{2,3},{3,2},{6,7},{7,6},{10,11},{11,10},{14,15},{15,14},{18,19},{1... | collective-permute-start | bytes 589832 | tf_op jit(solution)/shard_map/ppermute | solution.py:396
  24.3 2.3 %collective-permute-start.10 = (bf16[32,3072]{1,0:T(8,128)(2,1)S(1)}, bf16[32,3072]{1,0:T(8,128)(2,1)S(1)}, u32[]{:S(2)}, u32[]{:S(2)}) collective-permute-start(bf16[32,3072]{1,0:T(8,128)(2,1)S(1)} %get-tuple-element.119), channel_id=1, source_target_pairs={{2,3},{3,2},{6,7},{7,6},{10,11},{11,10},{14,15},{15,14},{18,19},{1... | collective-permute-start | bytes 589832 | tf_op jit(solution)/shard_map/ppermute | solution.py:396
  25.2 2.8 %collective-permute-start.12 = (bf16[32,3072]{1,0:T(8,128)(2,1)S(1)}, bf16[32,3072]{1,0:T(8,128)(2,1)S(1)}, u32[]{:S(2)}, u32[]{:S(2)}) collective-permute-start(bf16[32,3072]{1,0:T(8,128)(2,1)S(1)} %get-tuple-element.130), channel_id=1, source_target_pairs={{3,2},{7,6},{11,10},{15,14},{19,18},{23,22},{27,26},{31,30}} | collective-permute-start | bytes 589832 | tf_op jit(solution)/shard_map/ppermute | solution.py:314
  25.9 2.8 %collective-permute-start.16 = (bf16[32,3072]{1,0:T(8,128)(2,1)S(1)}, bf16[32,3072]{1,0:T(8,128)(2,1)S(1)}, u32[]{:S(2)}, u32[]{:S(2)}) collective-permute-start(bf16[32,3072]{1,0:T(8,128)(2,1)S(1)} %get-tuple-element.136), channel_id=1, source_target_pairs={{2,1},{6,5},{10,9},{14,13},{18,17},{22,21},{26,25},{30,29}} | collective-permute-start | bytes 589832 | tf_op jit(solution)/shard_map/ppermute | solution.py:314
  26.7 3.4 %collective-permute-start.15 = (bf16[32,3072]{1,0:T(8,128)(2,1)S(1)}, bf16[32,3072]{1,0:T(8,128)(2,1)S(1)}, u32[]{:S(2)}, u32[]{:S(2)}) collective-permute-start(bf16[32,3072]{1,0:T(8,128)(2,1)S(1)} %get-tuple-element.135), channel_id=1, source_target_pairs={{3,2},{7,6},{11,10},{15,14},{19,18},{23,22},{27,26},{31,30}} | collective-permute-start | bytes 589832 | tf_op jit(solution)/shard_map/ppermute | solution.py:314
  27.4 3.4 %collective-permute-start.14 = (bf16[32,3072]{1,0:T(8,128)(2,1)S(1)}, bf16[32,3072]{1,0:T(8,128)(2,1)S(1)}, u32[]{:S(2)}, u32[]{:S(2)}) collective-permute-start(bf16[32,3072]{1,0:T(8,128)(2,1)S(1)} %get-tuple-element.134), channel_id=1, source_target_pairs={{2,1},{6,5},{10,9},{14,13},{18,17},{22,21},{26,25},{30,29}} | collective-permute-start | bytes 589832 | tf_op jit(solution)/shard_map/ppermute | solution.py:314
  28.1 4.1 %collective-permute-start.13 = (bf16[32,3072]{1,0:T(8,128)(2,1)S(1)}, bf16[32,3072]{1,0:T(8,128)(2,1)S(1)}, u32[]{:S(2)}, u32[]{:S(2)}) collective-permute-start(bf16[32,3072]{1,0:T(8,128)(2,1)S(1)} %get-tuple-element.133), channel_id=1, source_target_pairs={{2,1},{6,5},{10,9},{14,13},{18,17},{22,21},{26,25},{30,29}} | collective-permute-start | bytes 589832 | tf_op jit(solution)/shard_map/ppermute | solution.py:314
  28.8 27.8 %collective-permute-start.20 = (bf16[32,3072]{1,0:T(8,128)(2,1)S(1)}, bf16[32,3072]{1,0:T(8,128)(2,1)S(1)}, u32[]{:S(2)}, u32[]{:S(2)}) collective-permute-start(bf16[32,3072]{1,0:T(8,128)(2,1)S(1)} %get-tuple-element.144), channel_id=1, source_target_pairs={{1,0},{5,4},{9,8},{13,12},{17,16},{21,20},{25,24},{29,28}} | collective-permute-start | bytes 589832 | tf_op jit(solution)/shard_map/ppermute | solution.py:314
  30.1 26.5 %collective-permute-start.19 = (bf16[32,3072]{1,0:T(8,128)(2,1)S(1)}, bf16[32,3072]{1,0:T(8,128)(2,1)S(1)}, u32[]{:S(2)}, u32[]{:S(2)}) collective-permute-start(bf16[32,3072]{1,0:T(8,128)(2,1)S(1)} %get-tuple-element.143), channel_id=1, source_target_pairs={{2,1},{6,5},{10,9},{14,13},{18,17},{22,21},{26,25},{30,29}} | collective-permute-start | bytes 589832 | tf_op jit(solution)/shard_map/ppermute | solution.py:314
  30.8 29.8 %collective-permute-start.18 = (bf16[32,3072]{1,0:T(8,128)(2,1)S(1)}, bf16[32,3072]{1,0:T(8,128)(2,1)S(1)}, u32[]{:S(2)}, u32[]{:S(2)}) collective-permute-start(bf16[32,3072]{1,0:T(8,128)(2,1)S(1)} %get-tuple-element.142), channel_id=1, source_target_pairs={{1,0},{5,4},{9,8},{13,12},{17,16},{21,20},{25,24},{29,28}} | collective-permute-start | bytes 589832 | tf_op jit(solution)/shard_map/ppermute | solution.py:314
  32.2 32.2 %collective-permute-start.17 = (bf16[32,3072]{1,0:T(8,128)(2,1)S(1)}, bf16[32,3072]{1,0:T(8,128)(2,1)S(1)}, u32[]{:S(2)}, u32[]{:S(2)}) collective-permute-start(bf16[32,3072]{1,0:T(8,128)(2,1)S(1)} %get-tuple-element.141), channel_id=1, source_target_pairs={{1,0},{5,4},{9,8},{13,12},{17,16},{21,20},{25,24},{29,28}} | collective-permute-start | bytes 589832 | tf_op jit(solution)/shard_map/ppermute | solution.py:314
  56.6 9.8 %collective-permute-start.22 = (bf16[32,3072]{1,0:T(8,128)(2,1)S(1)}, bf16[32,3072]{1,0:T(8,128)(2,1)S(1)}, u32[]{:S(2)}, u32[]{:S(2)}) collective-permute-start(bf16[32,3072]{1,0:T(8,128)(2,1)S(1)} %get-tuple-element.149), channel_id=1, source_target_pairs={{1,0},{5,4},{9,8},{13,12},{17,16},{21,20},{25,24},{29,28}} | collective-permute-start | bytes 589832 | tf_op jit(solution)/shard_map/ppermute | solution.py:314
  65.0 3.0 %collective-permute-start.21 = (bf16[24,4,16,128]{3,2,1,0:T(8,128)(2,1)S(1)}, bf16[24,4,16,128]{3,2,1,0:T(8,128)(2,1)S(1)}, u32[]{:S(2)}, u32[]{:S(2)}) collective-permute-start(bf16[24,4,16,128]{3,2,1,0:T(8,128)(2,1)S(1)} %get-tuple-element.148), channel_id=1, source_target_pairs={{0,4},{4,0},{8,12},{12,8},{16,20},{20,16},{24,28},{28,24},{1,5},{5... | collective-permute-start | bytes 1179656 | tf_op jit(solution)/shard_map/ppermute | solution.py:384
  65.1 2.9 %collective-permute-start.23 = (bf16[3,32,3072]{2,1,0:T(8,128)(2,1)S(1)}, bf16[3,32,3072]{2,1,0:T(8,128)(2,1)S(1)}, u32[]{:S(2)}, u32[]{:S(2)}) collective-permute-start(bf16[3,32,3072]{2,1,0:T(8,128)(2,1)S(1)} %get-tuple-element.152), channel_id=1, source_target_pairs={{0,4},{4,0},{8,12},{12,8},{16,20},{20,16},{24,28},{28,24},{1,5},{5... | collective-permute-start | bytes 1769480 | tf_op jit(solution)/shard_map/ppermute | solution.py:385
  66.5 1.5 %collective-permute-start.24 = (bf16[32,3072]{1,0:T(8,128)(2,1)S(1)}, bf16[32,3072]{1,0:T(8,128)(2,1)S(1)}, u32[]{:S(2)}, u32[]{:S(2)}) collective-permute-start(bf16[32,3072]{1,0:T(8,128)(2,1)S(1)} %get-tuple-element.153), channel_id=1, source_target_pairs={{0,4},{4,0},{8,12},{12,8},{16,20},{20,16},{24,28},{28,24},{1,5},{5... | collective-permute-start | bytes 589832 | tf_op jit(solution)/shard_map/ppermute | solution.py:421
  68.5 6.8 %collective-permute-start.25 = (bf16[2,18,16,128]{3,2,1,0:T(8,128)(2,1)S(1)}, bf16[2,18,16,128]{3,2,1,0:T(8,128)(2,1)S(1)}, u32[]{:S(2)}, u32[]{:S(2)}) collective-permute-start(bf16[2,18,16,128]{3,2,1,0:T(8,128)(2,1)S(1)} %get-tuple-element.155), channel_id=1, source_target_pairs={{0,8},{4,12},{8,0},{12,4},{16,24},{20,28},{24,16},{28,20},{1,9},{5... | collective-permute-start | bytes 442376 | tf_op jit(solution)/shard_map/ppermute | solution.py:450
  68.9 6.8 %collective-permute-start.26 = (bf16[2,18,16,128]{3,2,1,0:T(8,128)(2,1)S(1)}, bf16[2,18,16,128]{3,2,1,0:T(8,128)(2,1)S(1)}, u32[]{:S(2)}, u32[]{:S(2)}) collective-permute-start(bf16[2,18,16,128]{3,2,1,0:T(8,128)(2,1)S(1)} %get-tuple-element.156), channel_id=1, source_target_pairs={{0,16},{4,20},{8,24},{12,28},{16,0},{20,4},{24,8},{28,12},{1,17},{... | collective-permute-start | bytes 442376 | tf_op jit(solution)/shard_map/ppermute | solution.py:450
  70.4 8.0 %collective-permute-start.27 = (bf16[2,18,16,128]{3,2,1,0:T(8,128)(2,1)S(1)}, bf16[2,18,16,128]{3,2,1,0:T(8,128)(2,1)S(1)}, u32[]{:S(2)}, u32[]{:S(2)}) collective-permute-start(bf16[2,18,16,128]{3,2,1,0:T(8,128)(2,1)S(1)} %get-tuple-element.157), channel_id=1, source_target_pairs={{0,8},{4,12},{8,0},{12,4},{16,24},{20,28},{24,16},{28,20},{1,9},{5... | collective-permute-start | bytes 442376 | tf_op jit(solution)/shard_map/ppermute | solution.py:450
  71.0 7.6 %collective-permute-start.28 = (bf16[2,18,16,128]{3,2,1,0:T(8,128)(2,1)S(1)}, bf16[2,18,16,128]{3,2,1,0:T(8,128)(2,1)S(1)}, u32[]{:S(2)}, u32[]{:S(2)}) collective-permute-start(bf16[2,18,16,128]{3,2,1,0:T(8,128)(2,1)S(1)} %get-tuple-element.158), channel_id=1, source_target_pairs={{0,16},{4,20},{8,24},{12,28},{16,0},{20,4},{24,8},{28,12},{1,17},{... | collective-permute-start | bytes 442376 | tf_op jit(solution)/shard_map/ppermute | solution.py:450
  75.3 5.2 %collective-permute-start.29 = (bf16[18,16,128]{2,1,0:T(8,128)(2,1)S(1)}, bf16[18,16,128]{2,1,0:T(8,128)(2,1)S(1)}, u32[]{:S(2)}, u32[]{:S(2)}) collective-permute-start(bf16[18,16,128]{2,1,0:T(8,128)(2,1)S(1)} %shard_map.76), channel_id=1, source_target_pairs={{0,16},{4,20},{8,24},{12,28},{16,0},{20,4},{24,8},{28,12},{1,17},{... | collective-permute-start | bytes 221192 | tf_op jit(solution)/shard_map/ppermute | solution.py:450
  75.7 4.9 %collective-permute-start.30 = (bf16[18,16,128]{2,1,0:T(8,128)(2,1)S(1)}, bf16[18,16,128]{2,1,0:T(8,128)(2,1)S(1)}, u32[]{:S(2)}, u32[]{:S(2)}) collective-permute-start(bf16[18,16,128]{2,1,0:T(8,128)(2,1)S(1)} %shard_map.77), channel_id=1, source_target_pairs={{0,8},{4,12},{8,0},{12,4},{16,24},{20,28},{24,16},{28,20},{1,9},{5... | collective-permute-start | bytes 221192 | tf_op jit(solution)/shard_map/ppermute | solution.py:450
  78.5 4.4 %collective-permute-start.31 = (bf16[18,16,128]{2,1,0:T(8,128)(2,1)S(1)}, bf16[18,16,128]{2,1,0:T(8,128)(2,1)S(1)}, u32[]{:S(2)}, u32[]{:S(2)}) collective-permute-start(bf16[18,16,128]{2,1,0:T(8,128)(2,1)S(1)} %shard_map.78), channel_id=1, source_target_pairs={{0,16},{4,20},{8,24},{12,28},{16,0},{20,4},{24,8},{28,12},{1,17},{... | collective-permute-start | bytes 221192 | tf_op jit(solution)/shard_map/ppermute | solution.py:450
  78.6 4.4 %collective-permute-start.32 = (bf16[18,16,128]{2,1,0:T(8,128)(2,1)S(1)}, bf16[18,16,128]{2,1,0:T(8,128)(2,1)S(1)}, u32[]{:S(2)}, u32[]{:S(2)}) collective-permute-start(bf16[18,16,128]{2,1,0:T(8,128)(2,1)S(1)} %shard_map.79), channel_id=1, source_target_pairs={{0,8},{4,12},{8,0},{12,4},{16,24},{20,28},{24,16},{28,20},{1,9},{5... | collective-permute-start | bytes 221192 | tf_op jit(solution)/shard_map/ppermute | solution.py:450

commit v6 on v5

--- a/solution.py
+++ b/solution.py
@@ -73,17 +73,20 @@
     ]
 
 
-def load_body(tiles, rows_h, tiles_in, tiles_v, rows, sems):
+def load_body(tiles, rows_h, tiles_in, tiles_v, tiles_t, rows, sems):
     row_copy = pltpu.make_async_copy(rows_h, rows, sems.at[CHUNKS])
     row_copy.start()
 
     @pl.when(lax.axis_index("section") != 0)
     def _():
         copies = tile_loads(tiles, tiles_v, sems)
+        step = tiles_v.shape[0] // CHUNKS
         for c in copies:
             c.start()
-        for c in copies:
+        for i, c in enumerate(copies):
             c.wait()
+            for t in range(i * step, (i + 1) * step):
+                tiles_t[t] = tiles_v[t].T
 
     row_copy.wait()
 
@@ -143,11 +146,11 @@
         forward_work(m, nb, kpc, blk, rows, tiles, hin, hout, kh, kd, u3)
 
 
-def spread(rows, tiles, dz, v3, nb, kpc, blk):
+def spread(rows, tiles_t, dz, v3, nb, kpc, blk):
     v3[...] = jnp.zeros_like(v3)
     for n in range(nb):
-        w = tiles[n * kpc : (n + 1) * kpc].reshape(kpc * blk, blk)
-        back = lax.dot_general(dz(n), w, (((1,), (1,)), ((), ())), preferred_element_type=F32)
+        w = jnp.concatenate([tiles_t[n * kpc + k] for k in range(kpc)], axis=1)
+        back = jnp.dot(dz(n), w, preferred_element_type=F32)
         for k in range(kpc):
             r = rows[0, n * kpc + k]
             v3[r] = v3[r] + back[:, columns(k, blk)]
@@ -166,7 +169,7 @@
         gout[:, c] = (g[:, c].astype(F32) + scale * (v3[n] - q * inner)).astype(BF16)
 
 
-def turn_work(m, nb, kpc, blk, rows, tiles, hin, seeds, gout, kh, kz, u3, v3):
+def turn_work(m, nb, kpc, blk, rows, tiles, tiles_t, hin, seeds, gout, kh, kz, u3, v3):
     R = gout.shape[0]
     h = hin[...]
     kh[m] = h
@@ -177,17 +180,17 @@
         a = mix(n, rows, tiles, u3, kpc, blk)
         c = columns(n, blk)
         kz[m, :, c] = (g[:, c].astype(F32) * (1.0 - a * a)).astype(BF16)
-    spread(rows, tiles, lambda n: kz[m, :, columns(n, blk)], v3, nb, kpc, blk)
+    spread(rows, tiles_t, lambda n: kz[m, :, columns(n, blk)], v3, nb, kpc, blk)
     finish(kh.at[m], g, v3, gout, nb, blk)
 
 
-def turn_body(s, m, nb, kpc, blk, rows, tiles, hin, seeds, kh_in, kd_in, kz_in, gout, kh, kd, kz, u3, v3):
+def turn_body(s, m, nb, kpc, blk, rows, tiles, tiles_t, hin, seeds, kh_in, kd_in, kz_in, gout, kh, kd, kz, u3, v3):
     @pl.when(lax.axis_index("section") == s)
     def _():
-        turn_work(m, nb, kpc, blk, rows, tiles, hin, seeds, gout, kh, kz, u3, v3)
-
-
-def meet_body(s, a, b, nb, kpc, blk, rows, tiles, hin_a, hin_b, seeds, kh_in, kd_in, kz_in, *refs):
+        turn_work(m, nb, kpc, blk, rows, tiles, tiles_t, hin, seeds, gout, kh, kz, u3, v3)
+
+
+def meet_body(s, a, b, nb, kpc, blk, rows, tiles, tiles_t, hin_a, hin_b, seeds, kh_in, kd_in, kz_in, *refs):
     out, kh, kd, kz, u3, v3 = refs
 
     @pl.when(lax.axis_index("section") == s - 1)
@@ -196,10 +199,10 @@
 
     @pl.when(lax.axis_index("section") == s)
     def _():
-        turn_work(b, nb, kpc, blk, rows, tiles, hin_b, seeds, out, kh, kz, u3, v3)
-
-
-def backward_body(s, m, nb, kpc, blk, rows, tiles, gin, kh, kd, kz_in, *refs):
+        turn_work(b, nb, kpc, blk, rows, tiles, tiles_t, hin_b, seeds, out, kh, kz, u3, v3)
+
+
+def backward_body(s, m, nb, kpc, blk, rows, tiles_t, gin, kh, kd, kz_in, *refs):
     gout, kz, v3 = refs[-3:]
 
     @pl.when(lax.axis_index("section") == s)
@@ -207,7 +210,7 @@
         for n in range(nb):
             c = columns(n, blk)
             kz[m, :, c] = (gin[:, c].astype(F32) * kd[m, :, c]).astype(BF16)
-        spread(rows, tiles, lambda n: kz[m, :, columns(n, blk)], v3, nb, kpc, blk)
+        spread(rows, tiles_t, lambda n: kz[m, :, columns(n, blk)], v3, nb, kpc, blk)
         finish(kh.at[m], gin, v3, gout, nb, blk)
 
 
@@ -338,9 +341,9 @@
         out, kh, kd, kz = call(
             functools.partial(turn_body, s, m, nb, kpc, blk),
             [line, kh_s, kd_s, kz_s],
-            [(rows, SM), (tiles_v, VM), (held[m], VM), (out_grad, VM), (kh, VM), (kd, VM), (kz, VM)],
+            [(rows, SM), (tiles_v, VM), (tiles_t, VM), (held[m], VM), (out_grad, VM), (kh, VM), (kd, VM), (kz, VM)],
             [u3, v3],
-            {4: 1, 5: 2, 6: 3},
+            {5: 1, 6: 2, 7: 3},
         )
         held[m] = hop(out, s, s - 1)
 
@@ -349,17 +352,19 @@
         out, kz = call(
             functools.partial(backward_body, s, m, nb, kpc, blk),
             [line, kz_s],
-            [(rows, SM), (tiles_v, VM), (held[m], VM), (kh, VM), (kd, VM), (kz, VM)] + [(x, VM) for x in tied],
+            [(rows, SM), (tiles_t, VM), (held[m], VM), (kh, VM), (kd, VM), (kz, VM)] + [(x, VM) for x in tied],
             [v3],
             {5: 1},
         )
         held[m] = hop(out, s, s - 1)
 
+    tiles_t = None
+
     def load(s, m):
-        nonlocal tiles_v, rows
-        tiles_v, rows = call(
+        nonlocal tiles_v, tiles_t, rows
+        tiles_v, tiles_t, rows = call(
             load_body,
-            [((nt, blk, blk), BF16, VM), ((1, nt), jnp.int32, SM)],
+            [((nt, blk, blk), BF16, VM), ((nt, blk, blk), BF16, VM), ((1, nt), jnp.int32, SM)],
             [(tiles, HBM), (tile_rows, HBM), (tiles_v, VM)],
             [dma((CHUNKS + 1,))],
             {2: 0},
@@ -389,9 +394,10 @@
         out, kh, kd, kz = call(
             functools.partial(meet_body, last, a, b, nb, kpc, blk),
             [line, kh_s, kd_s, kz_s],
-            [(rows, SM), (tiles_v, VM), (held[a], VM), (held[b], VM), (out_grad, VM), (kh, VM), (kd, VM), (kz, VM)],
+            [(rows, SM), (tiles_v, VM), (tiles_t, VM), (held[a], VM), (held[b], VM), (out_grad, VM)]
+            + [(kh, VM), (kd, VM), (kz, VM)],
             [u3, v3],
-            {5: 1, 6: 2, 7: 3},
+            {6: 1, 7: 2, 8: 3},
         )
         held[a] = held[b] = lax.ppermute(out, "section", [(last - 1, last), (last, last - 1)])
 

time: 84.6 us -> 83.4 us (0.986)
  waiting for transfers between devices: 41 us -> 39.9 us
    ppermute x20, waiting for transfers between devices: 33.9 us -> 32.8 us  [hop(): return lax.ppermute(array, 'section', [(a, b)])]
where the time goes in v6:
time: 83.4 us; the launch traced here: 83 us
  waiting for transfers between devices  39.9 us (48%)
  starting transfers between devices  34 us (41%)
  Pallas kernels  8.15 us (10%)
    ppermute x20, waiting for transfers between devices, hop(): return lax.ppermute(array, 'section', [(a, b)])  32.8 us
    ppermute x20, starting transfers between devices, hop(): return lax.ppermute(array, 'section', [(a, b)])  23.8 us
    ppermute x8, starting transfers between devices, across(): return lax.ppermute(array, 'dp', [(i, i ^ 2 * j) for i in range(groups)])  8.17 us
    pallas_call x35, Pallas kernels, call(): pl.pallas_call(body, out_shape=out_shape, in_specs=in_specs, out_specs=ou...  8.15 us
    ppermute x8, waiting for transfers between devices, across(): return lax.ppermute(array, 'dp', [(i, i ^ 2 * j) for i in range(groups)])  5.72 us
  transfers between devices with their start and end apart: 33, of which 13 were waited for; matrix products, arithmetic and copies ran while one was open for 0% of the time, Pallas kernels for 5%

profile of v6, /device:TPU:0, one launch (start us, length us, event | category | flops | bytes accessed | tf_op | source)
XLA Modules:
  0.0 83.0 jit_solution(5328969358194051260)
XLA Ops:
  0.0 2.2 %shard_map.46 = (bf16[72,128,128]{2,1,0:T(8,128)(2,1)S(1)}, s32[1,72]{1,0:T(1,128)S(4)}, bf16[4,32,3072]{2,1,0:T(8,128)(2,1)S(1)}, f32[4,32,3072]{2,1,0:T(8,128)...) custom-call(bf16[1,72,128,128]{3,2,1,0:T(8,128)(2,1)} %tiles.3, s32[1,72]{1,0:T(1,128)} %rows_h.3, ...), custom_call_target="tpu_custom_call" | custom-call | flops 100000000 | bytes 3000000 | tf_op jit(solution)/shard_map/pallas_call | solution.py:35
  2.2 2.8 %collective-permute-start = (bf16[32,3072]{1,0:T(8,128)(2,1)S(1)}, bf16[32,3072]{1,0:T(8,128)(2,1)S(1)}, u32[]{:S(2)}, u32[]{:S(2)}) collective-permute-start(bf16[32,3072]{1,0:T(8,128)(2,1)S(1)} %get-tuple-element.89), channel_id=1, source_target_pairs={{0,1},{4,5},{8,9},{12,13},{16,17},{20,21},{24,25},{28,29}} | collective-permute-start | bytes 589832 | tf_op jit(solution)/shard_map/ppermute | solution.py:317
  5.0 0.7 shard_map.48
  5.7 1.3 %collective-permute-start.4 = (bf16[32,3072]{1,0:T(8,128)(2,1)S(1)}, bf16[32,3072]{1,0:T(8,128)(2,1)S(1)}, u32[]{:S(2)}, u32[]{:S(2)}) collective-permute-start(bf16[32,3072]{1,0:T(8,128)(2,1)S(1)} %get-tuple-element.100), channel_id=1, source_target_pairs={{0,1},{4,5},{8,9},{12,13},{16,17},{20,21},{24,25},{28,29}} | collective-permute-start | bytes 589832 | tf_op jit(solution)/shard_map/ppermute | solution.py:317
  7.0 0.7 shard_map.47
  7.8 0.7 shard_map.49
  8.4 1.3 %collective-permute-start.3 = (bf16[32,3072]{1,0:T(8,128)(2,1)S(1)}, bf16[32,3072]{1,0:T(8,128)(2,1)S(1)}, u32[]{:S(2)}, u32[]{:S(2)}) collective-permute-start(bf16[32,3072]{1,0:T(8,128)(2,1)S(1)} %get-tuple-element.99), channel_id=1, source_target_pairs={{0,1},{4,5},{8,9},{12,13},{16,17},{20,21},{24,25},{28,29}} | collective-permute-start | bytes 589832 | tf_op jit(solution)/shard_map/ppermute | solution.py:317
  9.8 0.6 collective-permute-done.refs_2_
  10.3 0.7 collective-permute-start.2
  11.0 0.7 shard_map.51
  11.7 5.1 %collective-permute-start.1 = (bf16[32,3072]{1,0:T(8,128)(2,1)S(1)}, bf16[32,3072]{1,0:T(8,128)(2,1)S(1)}, u32[]{:S(2)}, u32[]{:S(2)}) collective-permute-start(bf16[32,3072]{1,0:T(8,128)(2,1)S(1)} %get-tuple-element.97), channel_id=1, source_target_pairs={{0,1},{4,5},{8,9},{12,13},{16,17},{20,21},{24,25},{28,29}} | collective-permute-start | bytes 589832 | tf_op jit(solution)/shard_map/ppermute | solution.py:317
  16.8 0.7 collective-permute-start.6
  17.5 1.3 %collective-permute-done.3.refs_2_ = bf16[32,3072]{1,0:T(8,128)(2,1)S(1)} collective-permute-done((bf16[32,3072]{1,0:T(8,128)(2,1)S(1)}, bf16[32,3072]{1,0:T(8,128)(2,1)S(1)}, u32[]{:S(2)}, u32[]{:S(2)}) %collective-permute-start.3) | collective-permute-done | bytes 196640 | tf_op jit(solution)/shard_map/ppermute | solution.py:317
  18.7 0.7 collective-permute-start.8
  19.4 0.7 collective-permute-start.9
  20.1 1.7 %collective-permute-done.1.refs_2_ = bf16[32,3072]{1,0:T(8,128)(2,1)S(1)} collective-permute-done((bf16[32,3072]{1,0:T(8,128)(2,1)S(1)}, bf16[32,3072]{1,0:T(8,128)(2,1)S(1)}, u32[]{:S(2)}, u32[]{:S(2)}) %collective-permute-start.1) | collective-permute-done | bytes 196640 | tf_op jit(solution)/shard_map/ppermute | solution.py:317
  21.8 0.7 collective-permute-start.5
  22.5 0.8 collective-permute-start.7
  23.6 0.7 collective-permute-start.11
  24.3 0.7 collective-permute-start.10
  25.2 0.7 collective-permute-start.12
  25.9 0.7 collective-permute-start.16
  26.7 0.7 collective-permute-start.15
  27.4 0.7 collective-permute-start.14
  28.1 0.7 collective-permute-start.13
  28.8 1.3 %collective-permute-start.20 = (bf16[32,3072]{1,0:T(8,128)(2,1)S(1)}, bf16[32,3072]{1,0:T(8,128)(2,1)S(1)}, u32[]{:S(2)}, u32[]{:S(2)}) collective-permute-start(bf16[32,3072]{1,0:T(8,128)(2,1)S(1)} %get-tuple-element.146), channel_id=1, source_target_pairs={{1,0},{5,4},{9,8},{13,12},{17,16},{21,20},{25,24},{29,28}} | collective-permute-start | bytes 589832 | tf_op jit(solution)/shard_map/ppermute | solution.py:317
  30.1 0.7 collective-permute-start.19
  30.8 1.3 %collective-permute-start.18 = (bf16[32,3072]{1,0:T(8,128)(2,1)S(1)}, bf16[32,3072]{1,0:T(8,128)(2,1)S(1)}, u32[]{:S(2)}, u32[]{:S(2)}) collective-permute-start(bf16[32,3072]{1,0:T(8,128)(2,1)S(1)} %get-tuple-element.144), channel_id=1, source_target_pairs={{1,0},{5,4},{9,8},{13,12},{17,16},{21,20},{25,24},{29,28}} | collective-permute-start | bytes 589832 | tf_op jit(solution)/shard_map/ppermute | solution.py:317
  32.2 1.3 %collective-permute-start.17 = (bf16[32,3072]{1,0:T(8,128)(2,1)S(1)}, bf16[32,3072]{1,0:T(8,128)(2,1)S(1)}, u32[]{:S(2)}, u32[]{:S(2)}) collective-permute-start(bf16[32,3072]{1,0:T(8,128)(2,1)S(1)} %get-tuple-element.143), channel_id=1, source_target_pairs={{1,0},{5,4},{9,8},{13,12},{17,16},{21,20},{25,24},{29,28}} | collective-permute-start | bytes 589832 | tf_op jit(solution)/shard_map/ppermute | solution.py:317
  33.5 21.3 %collective-permute-done.20.gin = bf16[32,3072]{1,0:T(8,128)(2,1)S(1)} collective-permute-done((bf16[32,3072]{1,0:T(8,128)(2,1)S(1)}, bf16[32,3072]{1,0:T(8,128)(2,1)S(1)}, u32[]{:S(2)}, u32[]{:S(2)}) %collective-permute-start.20) | collective-permute-done | bytes 196640 | tf_op jit(solution)/shard_map/ppermute | solution.py:317
  54.8 1.3 %collective-permute-start.22 = (bf16[32,3072]{1,0:T(8,128)(2,1)S(1)}, bf16[32,3072]{1,0:T(8,128)(2,1)S(1)}, u32[]{:S(2)}, u32[]{:S(2)}) collective-permute-start(bf16[32,3072]{1,0:T(8,128)(2,1)S(1)} %get-tuple-element.151), channel_id=1, source_target_pairs={{1,0},{5,4},{9,8},{13,12},{17,16},{21,20},{25,24},{29,28}} | collective-permute-start | bytes 589832 | tf_op jit(solution)/shard_map/ppermute | solution.py:317
  56.1 2.8 %collective-permute-done.18.gin = bf16[32,3072]{1,0:T(8,128)(2,1)S(1)} collective-permute-done((bf16[32,3072]{1,0:T(8,128)(2,1)S(1)}, bf16[32,3072]{1,0:T(8,128)(2,1)S(1)}, u32[]{:S(2)}, u32[]{:S(2)}) %collective-permute-start.18) | collective-permute-done | bytes 196640 | tf_op jit(solution)/shard_map/ppermute | solution.py:317
  58.9 4.4 %collective-permute-done.17.gin = bf16[32,3072]{1,0:T(8,128)(2,1)S(1)} collective-permute-done((bf16[32,3072]{1,0:T(8,128)(2,1)S(1)}, bf16[32,3072]{1,0:T(8,128)(2,1)S(1)}, u32[]{:S(2)}, u32[]{:S(2)}) %collective-permute-start.17) | collective-permute-done | bytes 196640 | tf_op jit(solution)/shard_map/ppermute | solution.py:317
  63.3 0.6 shard_map.72
  64.0 0.5 collective-permute-start.23
  64.5 0.8 %collective-permute-done.22.gin = bf16[32,3072]{1,0:T(8,128)(2,1)S(1)} collective-permute-done((bf16[32,3072]{1,0:T(8,128)(2,1)S(1)}, bf16[32,3072]{1,0:T(8,128)(2,1)S(1)}, u32[]{:S(2)}, u32[]{:S(2)}) %collective-permute-start.22) | collective-permute-done | bytes 196640 | tf_op jit(solution)/shard_map/ppermute | solution.py:317
  65.5 1.4 %collective-permute-done.24.zlast = bf16[32,3072]{1,0:T(8,128)(2,1)S(1)} collective-permute-done((bf16[32,3072]{1,0:T(8,128)(2,1)S(1)}, bf16[32,3072]{1,0:T(8,128)(2,1)S(1)}, u32[]{:S(2)}, u32[]{:S(2)}) %collective-permute-start.24) | collective-permute-done | bytes 196640 | tf_op jit(solution)/shard_map/ppermute | solution.py:427
  66.9 0.5 shard_map.75
  67.8 1.5 %collective-permute-start.26 = (bf16[2,18,16,128]{3,2,1,0:T(8,128)(2,1)S(1)}, bf16[2,18,16,128]{3,2,1,0:T(8,128)(2,1)S(1)}, u32[]{:S(2)}, u32[]{:S(2)}) collective-permute-start(bf16[2,18,16,128]{3,2,1,0:T(8,128)(2,1)S(1)} %get-tuple-element.158), channel_id=1, source_target_pairs={{0,16},{4,20},{8,24},{12,28},{16,0},{20,4},{24,8},{28,12},{1,17},{... | collective-permute-start | bytes 442376 | tf_op jit(solution)/shard_map/ppermute | solution.py:456
  69.3 0.6 collective-permute-start.27
  69.9 1.7 %collective-permute-start.28 = (bf16[2,18,16,128]{3,2,1,0:T(8,128)(2,1)S(1)}, bf16[2,18,16,128]{3,2,1,0:T(8,128)(2,1)S(1)}, u32[]{:S(2)}, u32[]{:S(2)}) collective-permute-start(bf16[2,18,16,128]{3,2,1,0:T(8,128)(2,1)S(1)} %get-tuple-element.160), channel_id=1, source_target_pairs={{0,16},{4,20},{8,24},{12,28},{16,0},{20,4},{24,8},{28,12},{1,17},{... | collective-permute-start | bytes 442376 | tf_op jit(solution)/shard_map/ppermute | solution.py:456
  71.5 0.5 shard_map.74
  72.0 2.2 %collective-permute-done.25.got.refs_0_ = bf16[2,18,16,128]{3,2,1,0:T(8,128)(2,1)S(1)} collective-permute-done((bf16[2,18,16,128]{3,2,1,0:T(8,128)(2,1)S(1)}, bf16[2,18,16,128]{3,2,1,0:T(8,128)(2,1)S(1)}, u32[]{:S(2)}, u32[]{:S(2)}) %collective-permute-start.25) | collective-permute-done | bytes 147488 | tf_op jit(solution)/shard_map/ppermute | solution.py:456
  74.7 1.7 %collective-permute-start.30 = (bf16[18,16,128]{2,1,0:T(8,128)(2,1)S(1)}, bf16[18,16,128]{2,1,0:T(8,128)(2,1)S(1)}, u32[]{:S(2)}, u32[]{:S(2)}) collective-permute-start(bf16[18,16,128]{2,1,0:T(8,128)(2,1)S(1)} %shard_map.77), channel_id=1, source_target_pairs={{0,8},{4,12},{8,0},{12,4},{16,24},{20,28},{24,16},{28,20},{1,9},{5... | collective-permute-start | bytes 221192 | tf_op jit(solution)/shard_map/ppermute | solution.py:456
  76.3 1.0 %collective-permute-done.27.got.refs_2_ = bf16[2,18,16,128]{3,2,1,0:T(8,128)(2,1)S(1)} collective-permute-done((bf16[2,18,16,128]{3,2,1,0:T(8,128)(2,1)S(1)}, bf16[2,18,16,128]{3,2,1,0:T(8,128)(2,1)S(1)}, u32[]{:S(2)}, u32[]{:S(2)}) %collective-permute-start.27) | collective-permute-done | bytes 147488 | tf_op jit(solution)/shard_map/ppermute | solution.py:456
  77.5 1.9 %collective-permute-start.32 = (bf16[18,16,128]{2,1,0:T(8,128)(2,1)S(1)}, bf16[18,16,128]{2,1,0:T(8,128)(2,1)S(1)}, u32[]{:S(2)}, u32[]{:S(2)}) collective-permute-start(bf16[18,16,128]{2,1,0:T(8,128)(2,1)S(1)} %shard_map.79), channel_id=1, source_target_pairs={{0,8},{4,12},{8,0},{12,4},{16,24},{20,28},{24,16},{28,20},{1,9},{5... | collective-permute-start | bytes 221192 | tf_op jit(solution)/shard_map/ppermute | solution.py:456
  79.5 2.2 %collective-permute-done.31.refs_6_ = bf16[18,16,128]{2,1,0:T(8,128)(2,1)S(1)} collective-permute-done((bf16[18,16,128]{2,1,0:T(8,128)(2,1)S(1)}, bf16[18,16,128]{2,1,0:T(8,128)(2,1)S(1)}, u32[]{:S(2)}, u32[]{:S(2)}) %collective-permute-start.31) | collective-permute-done | bytes 73760 | tf_op jit(solution)/shard_map/ppermute | solution.py:456
  81.9 1.0 %shard_map.80 = f32[16,1,72,128]{3,2,1,0:T(8,128)} custom-call(f32[1,72,16,128]{3,2,1,0:T(8,128)S(1)} %get-tuple-element.156.mine, bf16[2,18,16,128]{3,2,1,0:T(8,128)(2,1)S(1)} %collective-permute-done.25.got.refs_0_, bf16[2,18,16,128]{3,2,1,0:T(8,128)(2,1)S(1)} %collective-permute-done.26.got.refs_1_, ...), custom_call_target="tpu_custom_call" | custom-call | flops 100000000 | bytes 3000000 | tf_op jit(solution)/shard_map/pallas_call | solution.py:35
  (55 shorter events, 2.3 us)
Async XLA Ops:
  2.2 8.1 %collective-permute-start = (bf16[32,3072]{1,0:T(8,128)(2,1)S(1)}, bf16[32,3072]{1,0:T(8,128)(2,1)S(1)}, u32[]{:S(2)}, u32[]{:S(2)}) collective-permute-start(bf16[32,3072]{1,0:T(8,128)(2,1)S(1)} %get-tuple-element.89), channel_id=1, source_target_pairs={{0,1},{4,5},{8,9},{12,13},{16,17},{20,21},{24,25},{28,29}} | collective-permute-start | bytes 589832 | tf_op jit(solution)/shard_map/ppermute | solution.py:317
  5.7 11.0 %collective-permute-start.4 = (bf16[32,3072]{1,0:T(8,128)(2,1)S(1)}, bf16[32,3072]{1,0:T(8,128)(2,1)S(1)}, u32[]{:S(2)}, u32[]{:S(2)}) collective-permute-start(bf16[32,3072]{1,0:T(8,128)(2,1)S(1)} %get-tuple-element.100), channel_id=1, source_target_pairs={{0,1},{4,5},{8,9},{12,13},{16,17},{20,21},{24,25},{28,29}} | collective-permute-start | bytes 589832 | tf_op jit(solution)/shard_map/ppermute | solution.py:317
  8.4 10.3 %collective-permute-start.3 = (bf16[32,3072]{1,0:T(8,128)(2,1)S(1)}, bf16[32,3072]{1,0:T(8,128)(2,1)S(1)}, u32[]{:S(2)}, u32[]{:S(2)}) collective-permute-start(bf16[32,3072]{1,0:T(8,128)(2,1)S(1)} %get-tuple-element.99), channel_id=1, source_target_pairs={{0,1},{4,5},{8,9},{12,13},{16,17},{20,21},{24,25},{28,29}} | collective-permute-start | bytes 589832 | tf_op jit(solution)/shard_map/ppermute | solution.py:317
  10.3 9.1 %collective-permute-start.2 = (bf16[32,3072]{1,0:T(8,128)(2,1)S(1)}, bf16[32,3072]{1,0:T(8,128)(2,1)S(1)}, u32[]{:S(2)}, u32[]{:S(2)}) collective-permute-start(bf16[32,3072]{1,0:T(8,128)(2,1)S(1)} %get-tuple-element.98), channel_id=1, source_target_pairs={{1,2},{5,6},{9,10},{13,14},{17,18},{21,22},{25,26},{29,30}} | collective-permute-start | bytes 589832 | tf_op jit(solution)/shard_map/ppermute | solution.py:317
  11.7 10.1 %collective-permute-start.1 = (bf16[32,3072]{1,0:T(8,128)(2,1)S(1)}, bf16[32,3072]{1,0:T(8,128)(2,1)S(1)}, u32[]{:S(2)}, u32[]{:S(2)}) collective-permute-start(bf16[32,3072]{1,0:T(8,128)(2,1)S(1)} %get-tuple-element.97), channel_id=1, source_target_pairs={{0,1},{4,5},{8,9},{12,13},{16,17},{20,21},{24,25},{28,29}} | collective-permute-start | bytes 589832 | tf_op jit(solution)/shard_map/ppermute | solution.py:317
  16.8 5.7 %collective-permute-start.6 = (bf16[32,3072]{1,0:T(8,128)(2,1)S(1)}, bf16[32,3072]{1,0:T(8,128)(2,1)S(1)}, u32[]{:S(2)}, u32[]{:S(2)}) collective-permute-start(bf16[32,3072]{1,0:T(8,128)(2,1)S(1)} %get-tuple-element.109), channel_id=1, source_target_pairs={{1,2},{5,6},{9,10},{13,14},{17,18},{21,22},{25,26},{29,30}} | collective-permute-start | bytes 589832 | tf_op jit(solution)/shard_map/ppermute | solution.py:317
  18.7 4.6 %collective-permute-start.8 = (bf16[32,3072]{1,0:T(8,128)(2,1)S(1)}, bf16[32,3072]{1,0:T(8,128)(2,1)S(1)}, u32[]{:S(2)}, u32[]{:S(2)}) collective-permute-start(bf16[32,3072]{1,0:T(8,128)(2,1)S(1)} %get-tuple-element.113), channel_id=1, source_target_pairs={{1,2},{5,6},{9,10},{13,14},{17,18},{21,22},{25,26},{29,30}} | collective-permute-start | bytes 589832 | tf_op jit(solution)/shard_map/ppermute | solution.py:317
  19.4 3.9 %collective-permute-start.9 = (bf16[32,3072]{1,0:T(8,128)(2,1)S(1)}, bf16[32,3072]{1,0:T(8,128)(2,1)S(1)}, u32[]{:S(2)}, u32[]{:S(2)}) collective-permute-start(bf16[32,3072]{1,0:T(8,128)(2,1)S(1)} %get-tuple-element.114), channel_id=1, source_target_pairs={{2,3},{6,7},{10,11},{14,15},{18,19},{22,23},{26,27},{30,31}} | collective-permute-start | bytes 589832 | tf_op jit(solution)/shard_map/ppermute | solution.py:317
  21.8 2.5 %collective-permute-start.5 = (bf16[32,3072]{1,0:T(8,128)(2,1)S(1)}, bf16[32,3072]{1,0:T(8,128)(2,1)S(1)}, u32[]{:S(2)}, u32[]{:S(2)}) collective-permute-start(bf16[32,3072]{1,0:T(8,128)(2,1)S(1)} %get-tuple-element.108), channel_id=1, source_target_pairs={{1,2},{5,6},{9,10},{13,14},{17,18},{21,22},{25,26},{29,30}} | collective-permute-start | bytes 589832 | tf_op jit(solution)/shard_map/ppermute | solution.py:317
  22.5 1.1 %copy-start = (bf16[128,3072]{1,0:T(8,128)(2,1)S(1)}, bf16[128,3072]{1,0:T(8,128)(2,1)}, u32[]{:S(2)}) copy-start(bf16[128,3072]{1,0:T(8,128)(2,1)} %seeds.7) | copy-start | bytes 2359300
  22.5 1.8 %collective-permute-start.7 = (bf16[32,3072]{1,0:T(8,128)(2,1)S(1)}, bf16[32,3072]{1,0:T(8,128)(2,1)S(1)}, u32[]{:S(2)}, u32[]{:S(2)}) collective-permute-start(bf16[32,3072]{1,0:T(8,128)(2,1)S(1)} %get-tuple-element.112), channel_id=1, source_target_pairs={{2,3},{6,7},{10,11},{14,15},{18,19},{22,23},{26,27},{30,31}} | collective-permute-start | bytes 589832 | tf_op jit(solution)/shard_map/ppermute | solution.py:317
  23.6 1.4 %collective-permute-start.11 = (bf16[32,3072]{1,0:T(8,128)(2,1)S(1)}, bf16[32,3072]{1,0:T(8,128)(2,1)S(1)}, u32[]{:S(2)}, u32[]{:S(2)}) collective-permute-start(bf16[32,3072]{1,0:T(8,128)(2,1)S(1)} %get-tuple-element.122), channel_id=1, source_target_pairs={{2,3},{3,2},{6,7},{7,6},{10,11},{11,10},{14,15},{15,14},{18,19},{1... | collective-permute-start | bytes 589832 | tf_op jit(solution)/shard_map/ppermute | solution.py:402
  24.3 2.3 %collective-permute-start.10 = (bf16[32,3072]{1,0:T(8,128)(2,1)S(1)}, bf16[32,3072]{1,0:T(8,128)(2,1)S(1)}, u32[]{:S(2)}, u32[]{:S(2)}) collective-permute-start(bf16[32,3072]{1,0:T(8,128)(2,1)S(1)} %get-tuple-element.121), channel_id=1, source_target_pairs={{2,3},{3,2},{6,7},{7,6},{10,11},{11,10},{14,15},{15,14},{18,19},{1... | collective-permute-start | bytes 589832 | tf_op jit(solution)/shard_map/ppermute | solution.py:402
  25.2 2.8 %collective-permute-start.12 = (bf16[32,3072]{1,0:T(8,128)(2,1)S(1)}, bf16[32,3072]{1,0:T(8,128)(2,1)S(1)}, u32[]{:S(2)}, u32[]{:S(2)}) collective-permute-start(bf16[32,3072]{1,0:T(8,128)(2,1)S(1)} %get-tuple-element.132), channel_id=1, source_target_pairs={{3,2},{7,6},{11,10},{15,14},{19,18},{23,22},{27,26},{31,30}} | collective-permute-start | bytes 589832 | tf_op jit(solution)/shard_map/ppermute | solution.py:317
  25.9 2.8 %collective-permute-start.16 = (bf16[32,3072]{1,0:T(8,128)(2,1)S(1)}, bf16[32,3072]{1,0:T(8,128)(2,1)S(1)}, u32[]{:S(2)}, u32[]{:S(2)}) collective-permute-start(bf16[32,3072]{1,0:T(8,128)(2,1)S(1)} %get-tuple-element.138), channel_id=1, source_target_pairs={{2,1},{6,5},{10,9},{14,13},{18,17},{22,21},{26,25},{30,29}} | collective-permute-start | bytes 589832 | tf_op jit(solution)/shard_map/ppermute | solution.py:317
  26.7 3.4 %collective-permute-start.15 = (bf16[32,3072]{1,0:T(8,128)(2,1)S(1)}, bf16[32,3072]{1,0:T(8,128)(2,1)S(1)}, u32[]{:S(2)}, u32[]{:S(2)}) collective-permute-start(bf16[32,3072]{1,0:T(8,128)(2,1)S(1)} %get-tuple-element.137), channel_id=1, source_target_pairs={{3,2},{7,6},{11,10},{15,14},{19,18},{23,22},{27,26},{31,30}} | collective-permute-start | bytes 589832 | tf_op jit(solution)/shard_map/ppermute | solution.py:317
  27.4 3.4 %collective-permute-start.14 = (bf16[32,3072]{1,0:T(8,128)(2,1)S(1)}, bf16[32,3072]{1,0:T(8,128)(2,1)S(1)}, u32[]{:S(2)}, u32[]{:S(2)}) collective-permute-start(bf16[32,3072]{1,0:T(8,128)(2,1)S(1)} %get-tuple-element.136), channel_id=1, source_target_pairs={{2,1},{6,5},{10,9},{14,13},{18,17},{22,21},{26,25},{30,29}} | collective-permute-start | bytes 589832 | tf_op jit(solution)/shard_map/ppermute | solution.py:317
  28.1 4.1 %collective-permute-start.13 = (bf16[32,3072]{1,0:T(8,128)(2,1)S(1)}, bf16[32,3072]{1,0:T(8,128)(2,1)S(1)}, u32[]{:S(2)}, u32[]{:S(2)}) collective-permute-start(bf16[32,3072]{1,0:T(8,128)(2,1)S(1)} %get-tuple-element.135), channel_id=1, source_target_pairs={{2,1},{6,5},{10,9},{14,13},{18,17},{22,21},{26,25},{30,29}} | collective-permute-start | bytes 589832 | tf_op jit(solution)/shard_map/ppermute | solution.py:317
  28.8 25.9 %collective-permute-start.20 = (bf16[32,3072]{1,0:T(8,128)(2,1)S(1)}, bf16[32,3072]{1,0:T(8,128)(2,1)S(1)}, u32[]{:S(2)}, u32[]{:S(2)}) collective-permute-start(bf16[32,3072]{1,0:T(8,128)(2,1)S(1)} %get-tuple-element.146), channel_id=1, source_target_pairs={{1,0},{5,4},{9,8},{13,12},{17,16},{21,20},{25,24},{29,28}} | collective-permute-start | bytes 589832 | tf_op jit(solution)/shard_map/ppermute | solution.py:317
  30.1 24.6 %collective-permute-start.19 = (bf16[32,3072]{1,0:T(8,128)(2,1)S(1)}, bf16[32,3072]{1,0:T(8,128)(2,1)S(1)}, u32[]{:S(2)}, u32[]{:S(2)}) collective-permute-start(bf16[32,3072]{1,0:T(8,128)(2,1)S(1)} %get-tuple-element.145), channel_id=1, source_target_pairs={{2,1},{6,5},{10,9},{14,13},{18,17},{22,21},{26,25},{30,29}} | collective-permute-start | bytes 589832 | tf_op jit(solution)/shard_map/ppermute | solution.py:317
  30.8 28.0 %collective-permute-start.18 = (bf16[32,3072]{1,0:T(8,128)(2,1)S(1)}, bf16[32,3072]{1,0:T(8,128)(2,1)S(1)}, u32[]{:S(2)}, u32[]{:S(2)}) collective-permute-start(bf16[32,3072]{1,0:T(8,128)(2,1)S(1)} %get-tuple-element.144), channel_id=1, source_target_pairs={{1,0},{5,4},{9,8},{13,12},{17,16},{21,20},{25,24},{29,28}} | collective-permute-start | bytes 589832 | tf_op jit(solution)/shard_map/ppermute | solution.py:317
  32.2 31.1 %collective-permute-start.17 = (bf16[32,3072]{1,0:T(8,128)(2,1)S(1)}, bf16[32,3072]{1,0:T(8,128)(2,1)S(1)}, u32[]{:S(2)}, u32[]{:S(2)}) collective-permute-start(bf16[32,3072]{1,0:T(8,128)(2,1)S(1)} %get-tuple-element.143), channel_id=1, source_target_pairs={{1,0},{5,4},{9,8},{13,12},{17,16},{21,20},{25,24},{29,28}} | collective-permute-start | bytes 589832 | tf_op jit(solution)/shard_map/ppermute | solution.py:317
  54.8 10.6 %collective-permute-start.22 = (bf16[32,3072]{1,0:T(8,128)(2,1)S(1)}, bf16[32,3072]{1,0:T(8,128)(2,1)S(1)}, u32[]{:S(2)}, u32[]{:S(2)}) collective-permute-start(bf16[32,3072]{1,0:T(8,128)(2,1)S(1)} %get-tuple-element.151), channel_id=1, source_target_pairs={{1,0},{5,4},{9,8},{13,12},{17,16},{21,20},{25,24},{29,28}} | collective-permute-start | bytes 589832 | tf_op jit(solution)/shard_map/ppermute | solution.py:317
  63.9 3.0 %collective-permute-start.21 = (bf16[24,4,16,128]{3,2,1,0:T(8,128)(2,1)S(1)}, bf16[24,4,16,128]{3,2,1,0:T(8,128)(2,1)S(1)}, u32[]{:S(2)}, u32[]{:S(2)}) collective-permute-start(bf16[24,4,16,128]{3,2,1,0:T(8,128)(2,1)S(1)} %get-tuple-element.150), channel_id=1, source_target_pairs={{0,4},{4,0},{8,12},{12,8},{16,20},{20,16},{24,28},{28,24},{1,5},{5... | collective-permute-start | bytes 1179656 | tf_op jit(solution)/shard_map/ppermute | solution.py:389
  64.0 2.9 %collective-permute-start.23 = (bf16[3,32,3072]{2,1,0:T(8,128)(2,1)S(1)}, bf16[3,32,3072]{2,1,0:T(8,128)(2,1)S(1)}, u32[]{:S(2)}, u32[]{:S(2)}) collective-permute-start(bf16[3,32,3072]{2,1,0:T(8,128)(2,1)S(1)} %get-tuple-element.154), channel_id=1, source_target_pairs={{0,4},{4,0},{8,12},{12,8},{16,20},{20,16},{24,28},{28,24},{1,5},{5... | collective-permute-start | bytes 1769480 | tf_op jit(solution)/shard_map/ppermute | solution.py:390
  65.4 1.5 %collective-permute-start.24 = (bf16[32,3072]{1,0:T(8,128)(2,1)S(1)}, bf16[32,3072]{1,0:T(8,128)(2,1)S(1)}, u32[]{:S(2)}, u32[]{:S(2)}) collective-permute-start(bf16[32,3072]{1,0:T(8,128)(2,1)S(1)} %get-tuple-element.155), channel_id=1, source_target_pairs={{0,4},{4,0},{8,12},{12,8},{16,20},{20,16},{24,28},{28,24},{1,5},{5... | collective-permute-start | bytes 589832 | tf_op jit(solution)/shard_map/ppermute | solution.py:427
  67.4 6.8 %collective-permute-start.25 = (bf16[2,18,16,128]{3,2,1,0:T(8,128)(2,1)S(1)}, bf16[2,18,16,128]{3,2,1,0:T(8,128)(2,1)S(1)}, u32[]{:S(2)}, u32[]{:S(2)}) collective-permute-start(bf16[2,18,16,128]{3,2,1,0:T(8,128)(2,1)S(1)} %get-tuple-element.157), channel_id=1, source_target_pairs={{0,8},{4,12},{8,0},{12,4},{16,24},{20,28},{24,16},{28,20},{1,9},{5... | collective-permute-start | bytes 442376 | tf_op jit(solution)/shard_map/ppermute | solution.py:456
  67.8 6.8 %collective-permute-start.26 = (bf16[2,18,16,128]{3,2,1,0:T(8,128)(2,1)S(1)}, bf16[2,18,16,128]{3,2,1,0:T(8,128)(2,1)S(1)}, u32[]{:S(2)}, u32[]{:S(2)}) collective-permute-start(bf16[2,18,16,128]{3,2,1,0:T(8,128)(2,1)S(1)} %get-tuple-element.158), channel_id=1, source_target_pairs={{0,16},{4,20},{8,24},{12,28},{16,0},{20,4},{24,8},{28,12},{1,17},{... | collective-permute-start | bytes 442376 | tf_op jit(solution)/shard_map/ppermute | solution.py:456
  69.3 8.0 %collective-permute-start.27 = (bf16[2,18,16,128]{3,2,1,0:T(8,128)(2,1)S(1)}, bf16[2,18,16,128]{3,2,1,0:T(8,128)(2,1)S(1)}, u32[]{:S(2)}, u32[]{:S(2)}) collective-permute-start(bf16[2,18,16,128]{3,2,1,0:T(8,128)(2,1)S(1)} %get-tuple-element.159), channel_id=1, source_target_pairs={{0,8},{4,12},{8,0},{12,4},{16,24},{20,28},{24,16},{28,20},{1,9},{5... | collective-permute-start | bytes 442376 | tf_op jit(solution)/shard_map/ppermute | solution.py:456
  69.9 7.6 %collective-permute-start.28 = (bf16[2,18,16,128]{3,2,1,0:T(8,128)(2,1)S(1)}, bf16[2,18,16,128]{3,2,1,0:T(8,128)(2,1)S(1)}, u32[]{:S(2)}, u32[]{:S(2)}) collective-permute-start(bf16[2,18,16,128]{3,2,1,0:T(8,128)(2,1)S(1)} %get-tuple-element.160), channel_id=1, source_target_pairs={{0,16},{4,20},{8,24},{12,28},{16,0},{20,4},{24,8},{28,12},{1,17},{... | collective-permute-start | bytes 442376 | tf_op jit(solution)/shard_map/ppermute | solution.py:456
  74.2 5.1 %collective-permute-start.29 = (bf16[18,16,128]{2,1,0:T(8,128)(2,1)S(1)}, bf16[18,16,128]{2,1,0:T(8,128)(2,1)S(1)}, u32[]{:S(2)}, u32[]{:S(2)}) collective-permute-start(bf16[18,16,128]{2,1,0:T(8,128)(2,1)S(1)} %shard_map.76), channel_id=1, source_target_pairs={{0,16},{4,20},{8,24},{12,28},{16,0},{20,4},{24,8},{28,12},{1,17},{... | collective-permute-start | bytes 221192 | tf_op jit(solution)/shard_map/ppermute | solution.py:456
  74.7 4.9 %collective-permute-start.30 = (bf16[18,16,128]{2,1,0:T(8,128)(2,1)S(1)}, bf16[18,16,128]{2,1,0:T(8,128)(2,1)S(1)}, u32[]{:S(2)}, u32[]{:S(2)}) collective-permute-start(bf16[18,16,128]{2,1,0:T(8,128)(2,1)S(1)} %shard_map.77), channel_id=1, source_target_pairs={{0,8},{4,12},{8,0},{12,4},{16,24},{20,28},{24,16},{28,20},{1,9},{5... | collective-permute-start | bytes 221192 | tf_op jit(solution)/shard_map/ppermute | solution.py:456
  77.4 4.4 %collective-permute-start.31 = (bf16[18,16,128]{2,1,0:T(8,128)(2,1)S(1)}, bf16[18,16,128]{2,1,0:T(8,128)(2,1)S(1)}, u32[]{:S(2)}, u32[]{:S(2)}) collective-permute-start(bf16[18,16,128]{2,1,0:T(8,128)(2,1)S(1)} %shard_map.78), channel_id=1, source_target_pairs={{0,16},{4,20},{8,24},{12,28},{16,0},{20,4},{24,8},{28,12},{1,17},{... | collective-permute-start | bytes 221192 | tf_op jit(solution)/shard_map/ppermute | solution.py:456
  77.5 4.4 %collective-permute-start.32 = (bf16[18,16,128]{2,1,0:T(8,128)(2,1)S(1)}, bf16[18,16,128]{2,1,0:T(8,128)(2,1)S(1)}, u32[]{:S(2)}, u32[]{:S(2)}) collective-permute-start(bf16[18,16,128]{2,1,0:T(8,128)(2,1)S(1)} %shard_map.79), channel_id=1, source_target_pairs={{0,8},{4,12},{8,0},{12,4},{16,24},{20,28},{24,16},{28,20},{1,9},{5... | collective-permute-start | bytes 221192 | tf_op jit(solution)/shard_map/ppermute | solution.py:456

commit v7 on v6

--- a/solution.py
+++ b/solution.py
@@ -19,6 +19,7 @@
 CHUNKS = 4
 MEET = 1
 PIECES = 4
+ROUTES = (1, 2)
 COST_LAST = 10**10
 PARTS = 3
 
@@ -460,7 +461,7 @@
             return out
 
         cut = nb // PIECES
-        routes = [(1 + p % 2, p * cut, (p + 1) * cut) for p in range(PIECES)]
+        routes = [(ROUTES[p % len(ROUTES)], p * cut, (p + 1) * cut) for p in range(PIECES)]
         sends = term([((j, 3), lo, hi) for j, lo, hi in routes], BF16)
         firsts = [across(send, j) for send, (j, lo, hi) in zip(sends, routes)]
         mine, *after = term([((0,), 0, nb)] + [((3 - j,), lo, hi) for j, lo, hi in routes], F32)
@@ -469,7 +470,7 @@
             functools.partial(final_body, [hi * kpc for j, lo, hi in routes]),
             [((half, 1, nt, blk), F32, HBM)],
             [(mine, VM)] + [(x, VM) for x in firsts + seconds],
-            [pltpu.VMEM((nt * half, blk), F32), pltpu.VMEM((half, nt, blk), F32), dma((PARTS,))],
+            [pltpu.VMEM(((nt + 8) * half, blk), F32), pltpu.VMEM((half, nt, blk), F32), dma((PARTS,))],
         )
         return out
     hf = kh.reshape(total, E).astype(F32)

time: 83.4 us -> 83.4 us (level)
  no operation moved by 1% of the time
where the time goes in v7:
time: 83.4 us; the launch traced here: 83 us
  waiting for transfers between devices  39.9 us (48%)
  starting transfers between devices  34 us (41%)
  Pallas kernels  8.16 us (10%)
    ppermute x20, waiting for transfers between devices, hop(): return lax.ppermute(array, 'section', [(a, b)])  32.7 us
    ppermute x20, starting transfers between devices, hop(): return lax.ppermute(array, 'section', [(a, b)])  23.8 us
    ppermute x8, starting transfers between devices, across(): return lax.ppermute(array, 'dp', [(i, i ^ 2 * j) for i in range(groups)])  8.19 us
    pallas_call x35, Pallas kernels, call(): pl.pallas_call(body, out_shape=out_shape, in_specs=in_specs, out_specs=ou...  8.16 us
    ppermute x8, waiting for transfers between devices, across(): return lax.ppermute(array, 'dp', [(i, i ^ 2 * j) for i in range(groups)])  5.68 us
  transfers between devices with their start and end apart: 33, of which 13 were waited for; matrix products, arithmetic and copies ran while one was open for 0% of the time, Pallas kernels for 5%

profile of v7, /device:TPU:0, one launch (start us, length us, event | category | flops | bytes accessed | tf_op | source)
XLA Modules:
  0.0 83.0 jit_solution(9833553363178903769)
XLA Ops:
  0.0 2.2 %shard_map.46 = (bf16[72,128,128]{2,1,0:T(8,128)(2,1)S(1)}, s32[1,72]{1,0:T(1,128)S(4)}, bf16[4,32,3072]{2,1,0:T(8,128)(2,1)S(1)}, f32[4,32,3072]{2,1,0:T(8,128)...) custom-call(bf16[1,72,128,128]{3,2,1,0:T(8,128)(2,1)} %tiles.3, s32[1,72]{1,0:T(1,128)} %rows_h.3, ...), custom_call_target="tpu_custom_call" | custom-call | flops 100000000 | bytes 3000000 | tf_op jit(solution)/shard_map/pallas_call | solution.py:36
  2.2 2.8 %collective-permute-start = (bf16[32,3072]{1,0:T(8,128)(2,1)S(1)}, bf16[32,3072]{1,0:T(8,128)(2,1)S(1)}, u32[]{:S(2)}, u32[]{:S(2)}) collective-permute-start(bf16[32,3072]{1,0:T(8,128)(2,1)S(1)} %get-tuple-element.89), channel_id=1, source_target_pairs={{0,1},{4,5},{8,9},{12,13},{16,17},{20,21},{24,25},{28,29}} | collective-permute-start | bytes 589832 | tf_op jit(solution)/shard_map/ppermute | solution.py:318
  5.0 0.7 shard_map.48
  5.7 1.3 %collective-permute-start.4 = (bf16[32,3072]{1,0:T(8,128)(2,1)S(1)}, bf16[32,3072]{1,0:T(8,128)(2,1)S(1)}, u32[]{:S(2)}, u32[]{:S(2)}) collective-permute-start(bf16[32,3072]{1,0:T(8,128)(2,1)S(1)} %get-tuple-element.100), channel_id=1, source_target_pairs={{0,1},{4,5},{8,9},{12,13},{16,17},{20,21},{24,25},{28,29}} | collective-permute-start | bytes 589832 | tf_op jit(solution)/shard_map/ppermute | solution.py:318
  7.0 0.7 shard_map.47
  7.8 0.7 shard_map.49
  8.5 1.3 %collective-permute-start.3 = (bf16[32,3072]{1,0:T(8,128)(2,1)S(1)}, bf16[32,3072]{1,0:T(8,128)(2,1)S(1)}, u32[]{:S(2)}, u32[]{:S(2)}) collective-permute-start(bf16[32,3072]{1,0:T(8,128)(2,1)S(1)} %get-tuple-element.99), channel_id=1, source_target_pairs={{0,1},{4,5},{8,9},{12,13},{16,17},{20,21},{24,25},{28,29}} | collective-permute-start | bytes 589832 | tf_op jit(solution)/shard_map/ppermute | solution.py:318
  9.8 0.6 collective-permute-done.refs_2_
  10.3 0.7 collective-permute-start.2
  11.0 0.7 shard_map.51
  11.7 5.1 %collective-permute-start.1 = (bf16[32,3072]{1,0:T(8,128)(2,1)S(1)}, bf16[32,3072]{1,0:T(8,128)(2,1)S(1)}, u32[]{:S(2)}, u32[]{:S(2)}) collective-permute-start(bf16[32,3072]{1,0:T(8,128)(2,1)S(1)} %get-tuple-element.97), channel_id=1, source_target_pairs={{0,1},{4,5},{8,9},{12,13},{16,17},{20,21},{24,25},{28,29}} | collective-permute-start | bytes 589832 | tf_op jit(solution)/shard_map/ppermute | solution.py:318
  16.8 0.7 collective-permute-start.6
  17.5 1.3 %collective-permute-done.3.refs_2_ = bf16[32,3072]{1,0:T(8,128)(2,1)S(1)} collective-permute-done((bf16[32,3072]{1,0:T(8,128)(2,1)S(1)}, bf16[32,3072]{1,0:T(8,128)(2,1)S(1)}, u32[]{:S(2)}, u32[]{:S(2)}) %collective-permute-start.3) | collective-permute-done | bytes 196640 | tf_op jit(solution)/shard_map/ppermute | solution.py:318
  18.7 0.7 collective-permute-start.8
  19.4 0.7 collective-permute-start.9
  20.1 1.7 %collective-permute-done.1.refs_2_ = bf16[32,3072]{1,0:T(8,128)(2,1)S(1)} collective-permute-done((bf16[32,3072]{1,0:T(8,128)(2,1)S(1)}, bf16[32,3072]{1,0:T(8,128)(2,1)S(1)}, u32[]{:S(2)}, u32[]{:S(2)}) %collective-permute-start.1) | collective-permute-done | bytes 196640 | tf_op jit(solution)/shard_map/ppermute | solution.py:318
  21.8 0.7 collective-permute-start.5
  22.5 0.8 collective-permute-start.7
  23.6 0.7 collective-permute-start.11
  24.3 0.7 collective-permute-start.10
  25.2 0.7 collective-permute-start.12
  25.9 0.7 collective-permute-start.16
  26.7 0.7 collective-permute-start.15
  27.4 0.7 collective-permute-start.14
  28.1 0.7 collective-permute-start.13
  28.8 1.3 %collective-permute-start.20 = (bf16[32,3072]{1,0:T(8,128)(2,1)S(1)}, bf16[32,3072]{1,0:T(8,128)(2,1)S(1)}, u32[]{:S(2)}, u32[]{:S(2)}) collective-permute-start(bf16[32,3072]{1,0:T(8,128)(2,1)S(1)} %get-tuple-element.146), channel_id=1, source_target_pairs={{1,0},{5,4},{9,8},{13,12},{17,16},{21,20},{25,24},{29,28}} | collective-permute-start | bytes 589832 | tf_op jit(solution)/shard_map/ppermute | solution.py:318
  30.1 0.7 collective-permute-start.19
  30.8 1.3 %collective-permute-start.18 = (bf16[32,3072]{1,0:T(8,128)(2,1)S(1)}, bf16[32,3072]{1,0:T(8,128)(2,1)S(1)}, u32[]{:S(2)}, u32[]{:S(2)}) collective-permute-start(bf16[32,3072]{1,0:T(8,128)(2,1)S(1)} %get-tuple-element.144), channel_id=1, source_target_pairs={{1,0},{5,4},{9,8},{13,12},{17,16},{21,20},{25,24},{29,28}} | collective-permute-start | bytes 589832 | tf_op jit(solution)/shard_map/ppermute | solution.py:318
  32.2 1.3 %collective-permute-start.17 = (bf16[32,3072]{1,0:T(8,128)(2,1)S(1)}, bf16[32,3072]{1,0:T(8,128)(2,1)S(1)}, u32[]{:S(2)}, u32[]{:S(2)}) collective-permute-start(bf16[32,3072]{1,0:T(8,128)(2,1)S(1)} %get-tuple-element.143), channel_id=1, source_target_pairs={{1,0},{5,4},{9,8},{13,12},{17,16},{21,20},{25,24},{29,28}} | collective-permute-start | bytes 589832 | tf_op jit(solution)/shard_map/ppermute | solution.py:318
  33.5 21.2 %collective-permute-done.20.gin = bf16[32,3072]{1,0:T(8,128)(2,1)S(1)} collective-permute-done((bf16[32,3072]{1,0:T(8,128)(2,1)S(1)}, bf16[32,3072]{1,0:T(8,128)(2,1)S(1)}, u32[]{:S(2)}, u32[]{:S(2)}) %collective-permute-start.20) | collective-permute-done | bytes 196640 | tf_op jit(solution)/shard_map/ppermute | solution.py:318
  54.8 1.3 %collective-permute-start.22 = (bf16[32,3072]{1,0:T(8,128)(2,1)S(1)}, bf16[32,3072]{1,0:T(8,128)(2,1)S(1)}, u32[]{:S(2)}, u32[]{:S(2)}) collective-permute-start(bf16[32,3072]{1,0:T(8,128)(2,1)S(1)} %get-tuple-element.151), channel_id=1, source_target_pairs={{1,0},{5,4},{9,8},{13,12},{17,16},{21,20},{25,24},{29,28}} | collective-permute-start | bytes 589832 | tf_op jit(solution)/shard_map/ppermute | solution.py:318
  56.1 2.8 %collective-permute-done.18.gin = bf16[32,3072]{1,0:T(8,128)(2,1)S(1)} collective-permute-done((bf16[32,3072]{1,0:T(8,128)(2,1)S(1)}, bf16[32,3072]{1,0:T(8,128)(2,1)S(1)}, u32[]{:S(2)}, u32[]{:S(2)}) %collective-permute-start.18) | collective-permute-done | bytes 196640 | tf_op jit(solution)/shard_map/ppermute | solution.py:318
  58.9 4.3 %collective-permute-done.17.gin = bf16[32,3072]{1,0:T(8,128)(2,1)S(1)} collective-permute-done((bf16[32,3072]{1,0:T(8,128)(2,1)S(1)}, bf16[32,3072]{1,0:T(8,128)(2,1)S(1)}, u32[]{:S(2)}, u32[]{:S(2)}) %collective-permute-start.17) | collective-permute-done | bytes 196640 | tf_op jit(solution)/shard_map/ppermute | solution.py:318
  63.3 0.6 shard_map.72
  64.0 0.5 collective-permute-start.23
  64.5 0.8 %collective-permute-done.22.gin = bf16[32,3072]{1,0:T(8,128)(2,1)S(1)} collective-permute-done((bf16[32,3072]{1,0:T(8,128)(2,1)S(1)}, bf16[32,3072]{1,0:T(8,128)(2,1)S(1)}, u32[]{:S(2)}, u32[]{:S(2)}) %collective-permute-start.22) | collective-permute-done | bytes 196640 | tf_op jit(solution)/shard_map/ppermute | solution.py:318
  65.5 1.4 %collective-permute-done.24.zlast = bf16[32,3072]{1,0:T(8,128)(2,1)S(1)} collective-permute-done((bf16[32,3072]{1,0:T(8,128)(2,1)S(1)}, bf16[32,3072]{1,0:T(8,128)(2,1)S(1)}, u32[]{:S(2)}, u32[]{:S(2)}) %collective-permute-start.24) | collective-permute-done | bytes 196640 | tf_op jit(solution)/shard_map/ppermute | solution.py:428
  66.9 0.5 shard_map.75
  67.8 1.5 %collective-permute-start.26 = (bf16[2,18,16,128]{3,2,1,0:T(8,128)(2,1)S(1)}, bf16[2,18,16,128]{3,2,1,0:T(8,128)(2,1)S(1)}, u32[]{:S(2)}, u32[]{:S(2)}) collective-permute-start(bf16[2,18,16,128]{3,2,1,0:T(8,128)(2,1)S(1)} %get-tuple-element.158), channel_id=1, source_target_pairs={{0,16},{4,20},{8,24},{12,28},{16,0},{20,4},{24,8},{28,12},{1,17},{... | collective-permute-start | bytes 442376 | tf_op jit(solution)/shard_map/ppermute | solution.py:457
  69.3 0.5 collective-permute-start.27
  69.9 1.7 %collective-permute-start.28 = (bf16[2,18,16,128]{3,2,1,0:T(8,128)(2,1)S(1)}, bf16[2,18,16,128]{3,2,1,0:T(8,128)(2,1)S(1)}, u32[]{:S(2)}, u32[]{:S(2)}) collective-permute-start(bf16[2,18,16,128]{3,2,1,0:T(8,128)(2,1)S(1)} %get-tuple-element.160), channel_id=1, source_target_pairs={{0,16},{4,20},{8,24},{12,28},{16,0},{20,4},{24,8},{28,12},{1,17},{... | collective-permute-start | bytes 442376 | tf_op jit(solution)/shard_map/ppermute | solution.py:457
  71.5 0.5 shard_map.74
  72.0 2.2 %collective-permute-done.25.got.refs_0_ = bf16[2,18,16,128]{3,2,1,0:T(8,128)(2,1)S(1)} collective-permute-done((bf16[2,18,16,128]{3,2,1,0:T(8,128)(2,1)S(1)}, bf16[2,18,16,128]{3,2,1,0:T(8,128)(2,1)S(1)}, u32[]{:S(2)}, u32[]{:S(2)}) %collective-permute-start.25) | collective-permute-done | bytes 147488 | tf_op jit(solution)/shard_map/ppermute | solution.py:457
  74.7 1.7 %collective-permute-start.30 = (bf16[18,16,128]{2,1,0:T(8,128)(2,1)S(1)}, bf16[18,16,128]{2,1,0:T(8,128)(2,1)S(1)}, u32[]{:S(2)}, u32[]{:S(2)}) collective-permute-start(bf16[18,16,128]{2,1,0:T(8,128)(2,1)S(1)} %shard_map.77), channel_id=1, source_target_pairs={{0,8},{4,12},{8,0},{12,4},{16,24},{20,28},{24,16},{28,20},{1,9},{5... | collective-permute-start | bytes 221192 | tf_op jit(solution)/shard_map/ppermute | solution.py:457
  76.3 1.0 %collective-permute-done.27.got.refs_2_ = bf16[2,18,16,128]{3,2,1,0:T(8,128)(2,1)S(1)} collective-permute-done((bf16[2,18,16,128]{3,2,1,0:T(8,128)(2,1)S(1)}, bf16[2,18,16,128]{3,2,1,0:T(8,128)(2,1)S(1)}, u32[]{:S(2)}, u32[]{:S(2)}) %collective-permute-start.27) | collective-permute-done | bytes 147488 | tf_op jit(solution)/shard_map/ppermute | solution.py:457
  77.5 1.9 %collective-permute-start.32 = (bf16[18,16,128]{2,1,0:T(8,128)(2,1)S(1)}, bf16[18,16,128]{2,1,0:T(8,128)(2,1)S(1)}, u32[]{:S(2)}, u32[]{:S(2)}) collective-permute-start(bf16[18,16,128]{2,1,0:T(8,128)(2,1)S(1)} %shard_map.79), channel_id=1, source_target_pairs={{0,8},{4,12},{8,0},{12,4},{16,24},{20,28},{24,16},{28,20},{1,9},{5... | collective-permute-start | bytes 221192 | tf_op jit(solution)/shard_map/ppermute | solution.py:457
  79.5 2.2 %collective-permute-done.31.refs_6_ = bf16[18,16,128]{2,1,0:T(8,128)(2,1)S(1)} collective-permute-done((bf16[18,16,128]{2,1,0:T(8,128)(2,1)S(1)}, bf16[18,16,128]{2,1,0:T(8,128)(2,1)S(1)}, u32[]{:S(2)}, u32[]{:S(2)}) %collective-permute-start.31) | collective-permute-done | bytes 73760 | tf_op jit(solution)/shard_map/ppermute | solution.py:457
  81.9 1.0 %shard_map.80 = f32[16,1,72,128]{3,2,1,0:T(8,128)} custom-call(f32[1,72,16,128]{3,2,1,0:T(8,128)S(1)} %get-tuple-element.156.mine, bf16[2,18,16,128]{3,2,1,0:T(8,128)(2,1)S(1)} %collective-permute-done.25.got.refs_0_, bf16[2,18,16,128]{3,2,1,0:T(8,128)(2,1)S(1)} %collective-permute-done.26.got.refs_1_, ...), custom_call_target="tpu_custom_call" | custom-call | flops 100000000 | bytes 3000000 | tf_op jit(solution)/shard_map/pallas_call | solution.py:36
  (55 shorter events, 2.3 us)
Async XLA Ops:
  2.2 8.1 %collective-permute-start = (bf16[32,3072]{1,0:T(8,128)(2,1)S(1)}, bf16[32,3072]{1,0:T(8,128)(2,1)S(1)}, u32[]{:S(2)}, u32[]{:S(2)}) collective-permute-start(bf16[32,3072]{1,0:T(8,128)(2,1)S(1)} %get-tuple-element.89), channel_id=1, source_target_pairs={{0,1},{4,5},{8,9},{12,13},{16,17},{20,21},{24,25},{28,29}} | collective-permute-start | bytes 589832 | tf_op jit(solution)/shard_map/ppermute | solution.py:318
  5.7 11.0 %collective-permute-start.4 = (bf16[32,3072]{1,0:T(8,128)(2,1)S(1)}, bf16[32,3072]{1,0:T(8,128)(2,1)S(1)}, u32[]{:S(2)}, u32[]{:S(2)}) collective-permute-start(bf16[32,3072]{1,0:T(8,128)(2,1)S(1)} %get-tuple-element.100), channel_id=1, source_target_pairs={{0,1},{4,5},{8,9},{12,13},{16,17},{20,21},{24,25},{28,29}} | collective-permute-start | bytes 589832 | tf_op jit(solution)/shard_map/ppermute | solution.py:318
  8.5 10.3 %collective-permute-start.3 = (bf16[32,3072]{1,0:T(8,128)(2,1)S(1)}, bf16[32,3072]{1,0:T(8,128)(2,1)S(1)}, u32[]{:S(2)}, u32[]{:S(2)}) collective-permute-start(bf16[32,3072]{1,0:T(8,128)(2,1)S(1)} %get-tuple-element.99), channel_id=1, source_target_pairs={{0,1},{4,5},{8,9},{12,13},{16,17},{20,21},{24,25},{28,29}} | collective-permute-start | bytes 589832 | tf_op jit(solution)/shard_map/ppermute | solution.py:318
  10.3 9.1 %collective-permute-start.2 = (bf16[32,3072]{1,0:T(8,128)(2,1)S(1)}, bf16[32,3072]{1,0:T(8,128)(2,1)S(1)}, u32[]{:S(2)}, u32[]{:S(2)}) collective-permute-start(bf16[32,3072]{1,0:T(8,128)(2,1)S(1)} %get-tuple-element.98), channel_id=1, source_target_pairs={{1,2},{5,6},{9,10},{13,14},{17,18},{21,22},{25,26},{29,30}} | collective-permute-start | bytes 589832 | tf_op jit(solution)/shard_map/ppermute | solution.py:318
  11.7 10.1 %collective-permute-start.1 = (bf16[32,3072]{1,0:T(8,128)(2,1)S(1)}, bf16[32,3072]{1,0:T(8,128)(2,1)S(1)}, u32[]{:S(2)}, u32[]{:S(2)}) collective-permute-start(bf16[32,3072]{1,0:T(8,128)(2,1)S(1)} %get-tuple-element.97), channel_id=1, source_target_pairs={{0,1},{4,5},{8,9},{12,13},{16,17},{20,21},{24,25},{28,29}} | collective-permute-start | bytes 589832 | tf_op jit(solution)/shard_map/ppermute | solution.py:318
  16.8 5.7 %collective-permute-start.6 = (bf16[32,3072]{1,0:T(8,128)(2,1)S(1)}, bf16[32,3072]{1,0:T(8,128)(2,1)S(1)}, u32[]{:S(2)}, u32[]{:S(2)}) collective-permute-start(bf16[32,3072]{1,0:T(8,128)(2,1)S(1)} %get-tuple-element.109), channel_id=1, source_target_pairs={{1,2},{5,6},{9,10},{13,14},{17,18},{21,22},{25,26},{29,30}} | collective-permute-start | bytes 589832 | tf_op jit(solution)/shard_map/ppermute | solution.py:318
  18.7 4.6 %collective-permute-start.8 = (bf16[32,3072]{1,0:T(8,128)(2,1)S(1)}, bf16[32,3072]{1,0:T(8,128)(2,1)S(1)}, u32[]{:S(2)}, u32[]{:S(2)}) collective-permute-start(bf16[32,3072]{1,0:T(8,128)(2,1)S(1)} %get-tuple-element.113), channel_id=1, source_target_pairs={{1,2},{5,6},{9,10},{13,14},{17,18},{21,22},{25,26},{29,30}} | collective-permute-start | bytes 589832 | tf_op jit(solution)/shard_map/ppermute | solution.py:318
  19.4 3.9 %collective-permute-start.9 = (bf16[32,3072]{1,0:T(8,128)(2,1)S(1)}, bf16[32,3072]{1,0:T(8,128)(2,1)S(1)}, u32[]{:S(2)}, u32[]{:S(2)}) collective-permute-start(bf16[32,3072]{1,0:T(8,128)(2,1)S(1)} %get-tuple-element.114), channel_id=1, source_target_pairs={{2,3},{6,7},{10,11},{14,15},{18,19},{22,23},{26,27},{30,31}} | collective-permute-start | bytes 589832 | tf_op jit(solution)/shard_map/ppermute | solution.py:318
  21.8 2.5 %collective-permute-start.5 = (bf16[32,3072]{1,0:T(8,128)(2,1)S(1)}, bf16[32,3072]{1,0:T(8,128)(2,1)S(1)}, u32[]{:S(2)}, u32[]{:S(2)}) collective-permute-start(bf16[32,3072]{1,0:T(8,128)(2,1)S(1)} %get-tuple-element.108), channel_id=1, source_target_pairs={{1,2},{5,6},{9,10},{13,14},{17,18},{21,22},{25,26},{29,30}} | collective-permute-start | bytes 589832 | tf_op jit(solution)/shard_map/ppermute | solution.py:318
  22.5 1.1 %copy-start = (bf16[128,3072]{1,0:T(8,128)(2,1)S(1)}, bf16[128,3072]{1,0:T(8,128)(2,1)}, u32[]{:S(2)}) copy-start(bf16[128,3072]{1,0:T(8,128)(2,1)} %seeds.7) | copy-start | bytes 2359300
  22.5 1.8 %collective-permute-start.7 = (bf16[32,3072]{1,0:T(8,128)(2,1)S(1)}, bf16[32,3072]{1,0:T(8,128)(2,1)S(1)}, u32[]{:S(2)}, u32[]{:S(2)}) collective-permute-start(bf16[32,3072]{1,0:T(8,128)(2,1)S(1)} %get-tuple-element.112), channel_id=1, source_target_pairs={{2,3},{6,7},{10,11},{14,15},{18,19},{22,23},{26,27},{30,31}} | collective-permute-start | bytes 589832 | tf_op jit(solution)/shard_map/ppermute | solution.py:318
  23.6 1.4 %collective-permute-start.11 = (bf16[32,3072]{1,0:T(8,128)(2,1)S(1)}, bf16[32,3072]{1,0:T(8,128)(2,1)S(1)}, u32[]{:S(2)}, u32[]{:S(2)}) collective-permute-start(bf16[32,3072]{1,0:T(8,128)(2,1)S(1)} %get-tuple-element.122), channel_id=1, source_target_pairs={{2,3},{3,2},{6,7},{7,6},{10,11},{11,10},{14,15},{15,14},{18,19},{1... | collective-permute-start | bytes 589832 | tf_op jit(solution)/shard_map/ppermute | solution.py:403
  24.3 2.3 %collective-permute-start.10 = (bf16[32,3072]{1,0:T(8,128)(2,1)S(1)}, bf16[32,3072]{1,0:T(8,128)(2,1)S(1)}, u32[]{:S(2)}, u32[]{:S(2)}) collective-permute-start(bf16[32,3072]{1,0:T(8,128)(2,1)S(1)} %get-tuple-element.121), channel_id=1, source_target_pairs={{2,3},{3,2},{6,7},{7,6},{10,11},{11,10},{14,15},{15,14},{18,19},{1... | collective-permute-start | bytes 589832 | tf_op jit(solution)/shard_map/ppermute | solution.py:403
  25.2 2.8 %collective-permute-start.12 = (bf16[32,3072]{1,0:T(8,128)(2,1)S(1)}, bf16[32,3072]{1,0:T(8,128)(2,1)S(1)}, u32[]{:S(2)}, u32[]{:S(2)}) collective-permute-start(bf16[32,3072]{1,0:T(8,128)(2,1)S(1)} %get-tuple-element.132), channel_id=1, source_target_pairs={{3,2},{7,6},{11,10},{15,14},{19,18},{23,22},{27,26},{31,30}} | collective-permute-start | bytes 589832 | tf_op jit(solution)/shard_map/ppermute | solution.py:318
  25.9 2.8 %collective-permute-start.16 = (bf16[32,3072]{1,0:T(8,128)(2,1)S(1)}, bf16[32,3072]{1,0:T(8,128)(2,1)S(1)}, u32[]{:S(2)}, u32[]{:S(2)}) collective-permute-start(bf16[32,3072]{1,0:T(8,128)(2,1)S(1)} %get-tuple-element.138), channel_id=1, source_target_pairs={{2,1},{6,5},{10,9},{14,13},{18,17},{22,21},{26,25},{30,29}} | collective-permute-start | bytes 589832 | tf_op jit(solution)/shard_map/ppermute | solution.py:318
  26.7 3.4 %collective-permute-start.15 = (bf16[32,3072]{1,0:T(8,128)(2,1)S(1)}, bf16[32,3072]{1,0:T(8,128)(2,1)S(1)}, u32[]{:S(2)}, u32[]{:S(2)}) collective-permute-start(bf16[32,3072]{1,0:T(8,128)(2,1)S(1)} %get-tuple-element.137), channel_id=1, source_target_pairs={{3,2},{7,6},{11,10},{15,14},{19,18},{23,22},{27,26},{31,30}} | collective-permute-start | bytes 589832 | tf_op jit(solution)/shard_map/ppermute | solution.py:318
  27.4 3.4 %collective-permute-start.14 = (bf16[32,3072]{1,0:T(8,128)(2,1)S(1)}, bf16[32,3072]{1,0:T(8,128)(2,1)S(1)}, u32[]{:S(2)}, u32[]{:S(2)}) collective-permute-start(bf16[32,3072]{1,0:T(8,128)(2,1)S(1)} %get-tuple-element.136), channel_id=1, source_target_pairs={{2,1},{6,5},{10,9},{14,13},{18,17},{22,21},{26,25},{30,29}} | collective-permute-start | bytes 589832 | tf_op jit(solution)/shard_map/ppermute | solution.py:318
  28.1 4.1 %collective-permute-start.13 = (bf16[32,3072]{1,0:T(8,128)(2,1)S(1)}, bf16[32,3072]{1,0:T(8,128)(2,1)S(1)}, u32[]{:S(2)}, u32[]{:S(2)}) collective-permute-start(bf16[32,3072]{1,0:T(8,128)(2,1)S(1)} %get-tuple-element.135), channel_id=1, source_target_pairs={{2,1},{6,5},{10,9},{14,13},{18,17},{22,21},{26,25},{30,29}} | collective-permute-start | bytes 589832 | tf_op jit(solution)/shard_map/ppermute | solution.py:318
  28.8 25.9 %collective-permute-start.20 = (bf16[32,3072]{1,0:T(8,128)(2,1)S(1)}, bf16[32,3072]{1,0:T(8,128)(2,1)S(1)}, u32[]{:S(2)}, u32[]{:S(2)}) collective-permute-start(bf16[32,3072]{1,0:T(8,128)(2,1)S(1)} %get-tuple-element.146), channel_id=1, source_target_pairs={{1,0},{5,4},{9,8},{13,12},{17,16},{21,20},{25,24},{29,28}} | collective-permute-start | bytes 589832 | tf_op jit(solution)/shard_map/ppermute | solution.py:318
  30.1 24.6 %collective-permute-start.19 = (bf16[32,3072]{1,0:T(8,128)(2,1)S(1)}, bf16[32,3072]{1,0:T(8,128)(2,1)S(1)}, u32[]{:S(2)}, u32[]{:S(2)}) collective-permute-start(bf16[32,3072]{1,0:T(8,128)(2,1)S(1)} %get-tuple-element.145), channel_id=1, source_target_pairs={{2,1},{6,5},{10,9},{14,13},{18,17},{22,21},{26,25},{30,29}} | collective-permute-start | bytes 589832 | tf_op jit(solution)/shard_map/ppermute | solution.py:318
  30.8 28.0 %collective-permute-start.18 = (bf16[32,3072]{1,0:T(8,128)(2,1)S(1)}, bf16[32,3072]{1,0:T(8,128)(2,1)S(1)}, u32[]{:S(2)}, u32[]{:S(2)}) collective-permute-start(bf16[32,3072]{1,0:T(8,128)(2,1)S(1)} %get-tuple-element.144), channel_id=1, source_target_pairs={{1,0},{5,4},{9,8},{13,12},{17,16},{21,20},{25,24},{29,28}} | collective-permute-start | bytes 589832 | tf_op jit(solution)/shard_map/ppermute | solution.py:318
  32.2 31.1 %collective-permute-start.17 = (bf16[32,3072]{1,0:T(8,128)(2,1)S(1)}, bf16[32,3072]{1,0:T(8,128)(2,1)S(1)}, u32[]{:S(2)}, u32[]{:S(2)}) collective-permute-start(bf16[32,3072]{1,0:T(8,128)(2,1)S(1)} %get-tuple-element.143), channel_id=1, source_target_pairs={{1,0},{5,4},{9,8},{13,12},{17,16},{21,20},{25,24},{29,28}} | collective-permute-start | bytes 589832 | tf_op jit(solution)/shard_map/ppermute | solution.py:318
  54.8 10.5 %collective-permute-start.22 = (bf16[32,3072]{1,0:T(8,128)(2,1)S(1)}, bf16[32,3072]{1,0:T(8,128)(2,1)S(1)}, u32[]{:S(2)}, u32[]{:S(2)}) collective-permute-start(bf16[32,3072]{1,0:T(8,128)(2,1)S(1)} %get-tuple-element.151), channel_id=1, source_target_pairs={{1,0},{5,4},{9,8},{13,12},{17,16},{21,20},{25,24},{29,28}} | collective-permute-start | bytes 589832 | tf_op jit(solution)/shard_map/ppermute | solution.py:318
  63.9 3.0 %collective-permute-start.21 = (bf16[24,4,16,128]{3,2,1,0:T(8,128)(2,1)S(1)}, bf16[24,4,16,128]{3,2,1,0:T(8,128)(2,1)S(1)}, u32[]{:S(2)}, u32[]{:S(2)}) collective-permute-start(bf16[24,4,16,128]{3,2,1,0:T(8,128)(2,1)S(1)} %get-tuple-element.150), channel_id=1, source_target_pairs={{0,4},{4,0},{8,12},{12,8},{16,20},{20,16},{24,28},{28,24},{1,5},{5... | collective-permute-start | bytes 1179656 | tf_op jit(solution)/shard_map/ppermute | solution.py:390
  64.0 2.9 %collective-permute-start.23 = (bf16[3,32,3072]{2,1,0:T(8,128)(2,1)S(1)}, bf16[3,32,3072]{2,1,0:T(8,128)(2,1)S(1)}, u32[]{:S(2)}, u32[]{:S(2)}) collective-permute-start(bf16[3,32,3072]{2,1,0:T(8,128)(2,1)S(1)} %get-tuple-element.154), channel_id=1, source_target_pairs={{0,4},{4,0},{8,12},{12,8},{16,20},{20,16},{24,28},{28,24},{1,5},{5... | collective-permute-start | bytes 1769480 | tf_op jit(solution)/shard_map/ppermute | solution.py:391
  65.4 1.5 %collective-permute-start.24 = (bf16[32,3072]{1,0:T(8,128)(2,1)S(1)}, bf16[32,3072]{1,0:T(8,128)(2,1)S(1)}, u32[]{:S(2)}, u32[]{:S(2)}) collective-permute-start(bf16[32,3072]{1,0:T(8,128)(2,1)S(1)} %get-tuple-element.155), channel_id=1, source_target_pairs={{0,4},{4,0},{8,12},{12,8},{16,20},{20,16},{24,28},{28,24},{1,5},{5... | collective-permute-start | bytes 589832 | tf_op jit(solution)/shard_map/ppermute | solution.py:428
  67.4 6.8 %collective-permute-start.25 = (bf16[2,18,16,128]{3,2,1,0:T(8,128)(2,1)S(1)}, bf16[2,18,16,128]{3,2,1,0:T(8,128)(2,1)S(1)}, u32[]{:S(2)}, u32[]{:S(2)}) collective-permute-start(bf16[2,18,16,128]{3,2,1,0:T(8,128)(2,1)S(1)} %get-tuple-element.157), channel_id=1, source_target_pairs={{0,8},{4,12},{8,0},{12,4},{16,24},{20,28},{24,16},{28,20},{1,9},{5... | collective-permute-start | bytes 442376 | tf_op jit(solution)/shard_map/ppermute | solution.py:457
  67.8 6.8 %collective-permute-start.26 = (bf16[2,18,16,128]{3,2,1,0:T(8,128)(2,1)S(1)}, bf16[2,18,16,128]{3,2,1,0:T(8,128)(2,1)S(1)}, u32[]{:S(2)}, u32[]{:S(2)}) collective-permute-start(bf16[2,18,16,128]{3,2,1,0:T(8,128)(2,1)S(1)} %get-tuple-element.158), channel_id=1, source_target_pairs={{0,16},{4,20},{8,24},{12,28},{16,0},{20,4},{24,8},{28,12},{1,17},{... | collective-permute-start | bytes 442376 | tf_op jit(solution)/shard_map/ppermute | solution.py:457
  69.3 8.0 %collective-permute-start.27 = (bf16[2,18,16,128]{3,2,1,0:T(8,128)(2,1)S(1)}, bf16[2,18,16,128]{3,2,1,0:T(8,128)(2,1)S(1)}, u32[]{:S(2)}, u32[]{:S(2)}) collective-permute-start(bf16[2,18,16,128]{3,2,1,0:T(8,128)(2,1)S(1)} %get-tuple-element.159), channel_id=1, source_target_pairs={{0,8},{4,12},{8,0},{12,4},{16,24},{20,28},{24,16},{28,20},{1,9},{5... | collective-permute-start | bytes 442376 | tf_op jit(solution)/shard_map/ppermute | solution.py:457
  69.9 7.5 %collective-permute-start.28 = (bf16[2,18,16,128]{3,2,1,0:T(8,128)(2,1)S(1)}, bf16[2,18,16,128]{3,2,1,0:T(8,128)(2,1)S(1)}, u32[]{:S(2)}, u32[]{:S(2)}) collective-permute-start(bf16[2,18,16,128]{3,2,1,0:T(8,128)(2,1)S(1)} %get-tuple-element.160), channel_id=1, source_target_pairs={{0,16},{4,20},{8,24},{12,28},{16,0},{20,4},{24,8},{28,12},{1,17},{... | collective-permute-start | bytes 442376 | tf_op jit(solution)/shard_map/ppermute | solution.py:457
  74.2 5.2 %collective-permute-start.29 = (bf16[18,16,128]{2,1,0:T(8,128)(2,1)S(1)}, bf16[18,16,128]{2,1,0:T(8,128)(2,1)S(1)}, u32[]{:S(2)}, u32[]{:S(2)}) collective-permute-start(bf16[18,16,128]{2,1,0:T(8,128)(2,1)S(1)} %shard_map.76), channel_id=1, source_target_pairs={{0,16},{4,20},{8,24},{12,28},{16,0},{20,4},{24,8},{28,12},{1,17},{... | collective-permute-start | bytes 221192 | tf_op jit(solution)/shard_map/ppermute | solution.py:457
  74.7 4.9 %collective-permute-start.30 = (bf16[18,16,128]{2,1,0:T(8,128)(2,1)S(1)}, bf16[18,16,128]{2,1,0:T(8,128)(2,1)S(1)}, u32[]{:S(2)}, u32[]{:S(2)}) collective-permute-start(bf16[18,16,128]{2,1,0:T(8,128)(2,1)S(1)} %shard_map.77), channel_id=1, source_target_pairs={{0,8},{4,12},{8,0},{12,4},{16,24},{20,28},{24,16},{28,20},{1,9},{5... | collective-permute-start | bytes 221192 | tf_op jit(solution)/shard_map/ppermute | solution.py:457
  77.3 4.4 %collective-permute-start.31 = (bf16[18,16,128]{2,1,0:T(8,128)(2,1)S(1)}, bf16[18,16,128]{2,1,0:T(8,128)(2,1)S(1)}, u32[]{:S(2)}, u32[]{:S(2)}) collective-permute-start(bf16[18,16,128]{2,1,0:T(8,128)(2,1)S(1)} %shard_map.78), channel_id=1, source_target_pairs={{0,16},{4,20},{8,24},{12,28},{16,0},{20,4},{24,8},{28,12},{1,17},{... | collective-permute-start | bytes 221192 | tf_op jit(solution)/shard_map/ppermute | solution.py:457
  77.5 4.4 %collective-permute-start.32 = (bf16[18,16,128]{2,1,0:T(8,128)(2,1)S(1)}, bf16[18,16,128]{2,1,0:T(8,128)(2,1)S(1)}, u32[]{:S(2)}, u32[]{:S(2)}) collective-permute-start(bf16[18,16,128]{2,1,0:T(8,128)(2,1)S(1)} %shard_map.79), channel_id=1, source_target_pairs={{0,8},{4,12},{8,0},{12,4},{16,24},{20,28},{24,16},{28,20},{1,9},{5... | collective-permute-start | bytes 221192 | tf_op jit(solution)/shard_map/ppermute | solution.py:457

commit v8 on v7

--- a/solution.py
+++ b/solution.py
@@ -63,7 +63,7 @@
 def mix(n, rows, tiles, u3, kpc, blk):
     x = jnp.concatenate([u3[rows[0, n * kpc + k]] for k in range(kpc)], axis=1)
     w = tiles[n * kpc : (n + 1) * kpc].reshape(kpc * blk, blk)
-    return jnp.tanh(jnp.dot(x, w, preferred_element_type=F32))
+    return jnp.dot(x, w, preferred_element_type=F32)
 
 
 def tile_loads(tiles, tiles_v, sems):
@@ -112,7 +112,7 @@
         for c in range(CHUNKS):
             loads[c].wait()
             for n in range(c * nb // CHUNKS, (c + 1) * nb // CHUNKS):
-                a = mix(n, rows, tiles_v, u3, kpc, blk)
+                a = jnp.tanh(mix(n, rows, tiles_v, u3, kpc, blk))
                 s = columns(n, blk)
                 hout[:, s] = (hf[:, s] + a).astype(BF16)
                 kd[0, :, s] = 1.0 - a * a
@@ -129,8 +129,10 @@
     hf = h.astype(F32)
     normalise(hf, u3, nb, blk)
     for n in range(nb):
-        a = mix(n, rows, tiles, u3, kpc, blk)
+        kd[m, :, columns(n, blk)] = mix(n, rows, tiles, u3, kpc, blk)
+    for n in range(nb):
         c = columns(n, blk)
+        a = jnp.tanh(kd[m, :, c])
         hout[:, c] = (hf[:, c] + a).astype(BF16)
         kd[m, :, c] = 1.0 - a * a
 
@@ -178,8 +180,10 @@
     normalise(hf, u3, nb, blk)
     g = seeds.at[pl.ds(m * R, R)]
     for n in range(nb):
-        a = mix(n, rows, tiles, u3, kpc, blk)
+        v3[n] = mix(n, rows, tiles, u3, kpc, blk)
+    for n in range(nb):
         c = columns(n, blk)
+        a = jnp.tanh(v3[n])
         kz[m, :, c] = (g[:, c].astype(F32) * (1.0 - a * a)).astype(BF16)
     spread(rows, tiles_t, lambda n: kz[m, :, columns(n, blk)], v3, nb, kpc, blk)
     finish(kh.at[m], g, v3, gout, nb, blk)

time: 83.4 us -> 83.4 us (level)
  no operation moved by 1% of the time
where the time goes in v8:
time: 83.4 us; the launch traced here: 83 us
  waiting for transfers between devices  39.9 us (48%)
  starting transfers between devices  34 us (41%)
  Pallas kernels  8.15 us (10%)
    ppermute x20, waiting for transfers between devices, hop(): return lax.ppermute(array, 'section', [(a, b)])  32.7 us
    ppermute x20, starting transfers between devices, hop(): return lax.ppermute(array, 'section', [(a, b)])  23.8 us
    ppermute x8, starting transfers between devices, across(): return lax.ppermute(array, 'dp', [(i, i ^ 2 * j) for i in range(groups)])  8.19 us
    pallas_call x35, Pallas kernels, call(): pl.pallas_call(body, out_shape=out_shape, in_specs=in_specs, out_specs=ou...  8.15 us
    ppermute x8, waiting for transfers between devices, across(): return lax.ppermute(array, 'dp', [(i, i ^ 2 * j) for i in range(groups)])  5.68 us
  transfers between devices with their start and end apart: 33, of which 13 were waited for; matrix products, arithmetic and copies ran while one was open for 0% of the time, Pallas kernels for 5%

profile of v8, /device:TPU:0, one launch (start us, length us, event | category | flops | bytes accessed | tf_op | source)
XLA Modules:
  0.0 83.0 jit_solution(17624034227181157436)
XLA Ops:
  0.0 2.2 %shard_map.46 = (bf16[72,128,128]{2,1,0:T(8,128)(2,1)S(1)}, s32[1,72]{1,0:T(1,128)S(4)}, bf16[4,32,3072]{2,1,0:T(8,128)(2,1)S(1)}, f32[4,32,3072]{2,1,0:T(8,128)...) custom-call(bf16[1,72,128,128]{3,2,1,0:T(8,128)(2,1)} %tiles.3, s32[1,72]{1,0:T(1,128)} %rows_h.3, ...), custom_call_target="tpu_custom_call" | custom-call | flops 100000000 | bytes 3000000 | tf_op jit(solution)/shard_map/pallas_call | solution.py:36
  2.2 2.8 %collective-permute-start = (bf16[32,3072]{1,0:T(8,128)(2,1)S(1)}, bf16[32,3072]{1,0:T(8,128)(2,1)S(1)}, u32[]{:S(2)}, u32[]{:S(2)}) collective-permute-start(bf16[32,3072]{1,0:T(8,128)(2,1)S(1)} %get-tuple-element.89), channel_id=1, source_target_pairs={{0,1},{4,5},{8,9},{12,13},{16,17},{20,21},{24,25},{28,29}} | collective-permute-start | bytes 589832 | tf_op jit(solution)/shard_map/ppermute | solution.py:322
  5.0 0.7 shard_map.48
  5.7 1.3 %collective-permute-start.4 = (bf16[32,3072]{1,0:T(8,128)(2,1)S(1)}, bf16[32,3072]{1,0:T(8,128)(2,1)S(1)}, u32[]{:S(2)}, u32[]{:S(2)}) collective-permute-start(bf16[32,3072]{1,0:T(8,128)(2,1)S(1)} %get-tuple-element.100), channel_id=1, source_target_pairs={{0,1},{4,5},{8,9},{12,13},{16,17},{20,21},{24,25},{28,29}} | collective-permute-start | bytes 589832 | tf_op jit(solution)/shard_map/ppermute | solution.py:322
  7.0 0.7 shard_map.47
  7.8 0.7 shard_map.49
  8.4 1.3 %collective-permute-start.3 = (bf16[32,3072]{1,0:T(8,128)(2,1)S(1)}, bf16[32,3072]{1,0:T(8,128)(2,1)S(1)}, u32[]{:S(2)}, u32[]{:S(2)}) collective-permute-start(bf16[32,3072]{1,0:T(8,128)(2,1)S(1)} %get-tuple-element.99), channel_id=1, source_target_pairs={{0,1},{4,5},{8,9},{12,13},{16,17},{20,21},{24,25},{28,29}} | collective-permute-start | bytes 589832 | tf_op jit(solution)/shard_map/ppermute | solution.py:322
  9.8 0.6 collective-permute-done.refs_2_
  10.3 0.7 collective-permute-start.2
  11.0 0.7 shard_map.51
  11.7 5.1 %collective-permute-start.1 = (bf16[32,3072]{1,0:T(8,128)(2,1)S(1)}, bf16[32,3072]{1,0:T(8,128)(2,1)S(1)}, u32[]{:S(2)}, u32[]{:S(2)}) collective-permute-start(bf16[32,3072]{1,0:T(8,128)(2,1)S(1)} %get-tuple-element.97), channel_id=1, source_target_pairs={{0,1},{4,5},{8,9},{12,13},{16,17},{20,21},{24,25},{28,29}} | collective-permute-start | bytes 589832 | tf_op jit(solution)/shard_map/ppermute | solution.py:322
  16.8 0.7 collective-permute-start.6
  17.4 1.3 %collective-permute-done.3.refs_2_ = bf16[32,3072]{1,0:T(8,128)(2,1)S(1)} collective-permute-done((bf16[32,3072]{1,0:T(8,128)(2,1)S(1)}, bf16[32,3072]{1,0:T(8,128)(2,1)S(1)}, u32[]{:S(2)}, u32[]{:S(2)}) %collective-permute-start.3) | collective-permute-done | bytes 196640 | tf_op jit(solution)/shard_map/ppermute | solution.py:322
  18.7 0.7 collective-permute-start.8
  19.4 0.7 collective-permute-start.9
  20.1 1.7 %collective-permute-done.1.refs_2_ = bf16[32,3072]{1,0:T(8,128)(2,1)S(1)} collective-permute-done((bf16[32,3072]{1,0:T(8,128)(2,1)S(1)}, bf16[32,3072]{1,0:T(8,128)(2,1)S(1)}, u32[]{:S(2)}, u32[]{:S(2)}) %collective-permute-start.1) | collective-permute-done | bytes 196640 | tf_op jit(solution)/shard_map/ppermute | solution.py:322
  21.8 0.7 collective-permute-start.5
  22.5 0.8 collective-permute-start.7
  23.6 0.7 collective-permute-start.11
  24.3 0.7 collective-permute-start.10
  25.2 0.7 collective-permute-start.12
  25.9 0.7 collective-permute-start.16
  26.7 0.7 collective-permute-start.15
  27.4 0.7 collective-permute-start.14
  28.1 0.7 collective-permute-start.13
  28.8 1.3 %collective-permute-start.20 = (bf16[32,3072]{1,0:T(8,128)(2,1)S(1)}, bf16[32,3072]{1,0:T(8,128)(2,1)S(1)}, u32[]{:S(2)}, u32[]{:S(2)}) collective-permute-start(bf16[32,3072]{1,0:T(8,128)(2,1)S(1)} %get-tuple-element.146), channel_id=1, source_target_pairs={{1,0},{5,4},{9,8},{13,12},{17,16},{21,20},{25,24},{29,28}} | collective-permute-start | bytes 589832 | tf_op jit(solution)/shard_map/ppermute | solution.py:322
  30.1 0.7 collective-permute-start.19
  30.8 1.3 %collective-permute-start.18 = (bf16[32,3072]{1,0:T(8,128)(2,1)S(1)}, bf16[32,3072]{1,0:T(8,128)(2,1)S(1)}, u32[]{:S(2)}, u32[]{:S(2)}) collective-permute-start(bf16[32,3072]{1,0:T(8,128)(2,1)S(1)} %get-tuple-element.144), channel_id=1, source_target_pairs={{1,0},{5,4},{9,8},{13,12},{17,16},{21,20},{25,24},{29,28}} | collective-permute-start | bytes 589832 | tf_op jit(solution)/shard_map/ppermute | solution.py:322
  32.2 1.3 %collective-permute-start.17 = (bf16[32,3072]{1,0:T(8,128)(2,1)S(1)}, bf16[32,3072]{1,0:T(8,128)(2,1)S(1)}, u32[]{:S(2)}, u32[]{:S(2)}) collective-permute-start(bf16[32,3072]{1,0:T(8,128)(2,1)S(1)} %get-tuple-element.143), channel_id=1, source_target_pairs={{1,0},{5,4},{9,8},{13,12},{17,16},{21,20},{25,24},{29,28}} | collective-permute-start | bytes 589832 | tf_op jit(solution)/shard_map/ppermute | solution.py:322
  33.5 21.2 %collective-permute-done.20.gin = bf16[32,3072]{1,0:T(8,128)(2,1)S(1)} collective-permute-done((bf16[32,3072]{1,0:T(8,128)(2,1)S(1)}, bf16[32,3072]{1,0:T(8,128)(2,1)S(1)}, u32[]{:S(2)}, u32[]{:S(2)}) %collective-permute-start.20) | collective-permute-done | bytes 196640 | tf_op jit(solution)/shard_map/ppermute | solution.py:322
  54.8 1.3 %collective-permute-start.22 = (bf16[32,3072]{1,0:T(8,128)(2,1)S(1)}, bf16[32,3072]{1,0:T(8,128)(2,1)S(1)}, u32[]{:S(2)}, u32[]{:S(2)}) collective-permute-start(bf16[32,3072]{1,0:T(8,128)(2,1)S(1)} %get-tuple-element.151), channel_id=1, source_target_pairs={{1,0},{5,4},{9,8},{13,12},{17,16},{21,20},{25,24},{29,28}} | collective-permute-start | bytes 589832 | tf_op jit(solution)/shard_map/ppermute | solution.py:322
  56.1 2.8 %collective-permute-done.18.gin = bf16[32,3072]{1,0:T(8,128)(2,1)S(1)} collective-permute-done((bf16[32,3072]{1,0:T(8,128)(2,1)S(1)}, bf16[32,3072]{1,0:T(8,128)(2,1)S(1)}, u32[]{:S(2)}, u32[]{:S(2)}) %collective-permute-start.18) | collective-permute-done | bytes 196640 | tf_op jit(solution)/shard_map/ppermute | solution.py:322
  58.9 4.3 %collective-permute-done.17.gin = bf16[32,3072]{1,0:T(8,128)(2,1)S(1)} collective-permute-done((bf16[32,3072]{1,0:T(8,128)(2,1)S(1)}, bf16[32,3072]{1,0:T(8,128)(2,1)S(1)}, u32[]{:S(2)}, u32[]{:S(2)}) %collective-permute-start.17) | collective-permute-done | bytes 196640 | tf_op jit(solution)/shard_map/ppermute | solution.py:322
  63.3 0.6 shard_map.72
  64.0 0.5 collective-permute-start.23
  64.5 0.8 %collective-permute-done.22.gin = bf16[32,3072]{1,0:T(8,128)(2,1)S(1)} collective-permute-done((bf16[32,3072]{1,0:T(8,128)(2,1)S(1)}, bf16[32,3072]{1,0:T(8,128)(2,1)S(1)}, u32[]{:S(2)}, u32[]{:S(2)}) %collective-permute-start.22) | collective-permute-done | bytes 196640 | tf_op jit(solution)/shard_map/ppermute | solution.py:322
  65.5 1.4 %collective-permute-done.24.zlast = bf16[32,3072]{1,0:T(8,128)(2,1)S(1)} collective-permute-done((bf16[32,3072]{1,0:T(8,128)(2,1)S(1)}, bf16[32,3072]{1,0:T(8,128)(2,1)S(1)}, u32[]{:S(2)}, u32[]{:S(2)}) %collective-permute-start.24) | collective-permute-done | bytes 196640 | tf_op jit(solution)/shard_map/ppermute | solution.py:432
  66.9 0.5 shard_map.75
  67.8 1.5 %collective-permute-start.26 = (bf16[2,18,16,128]{3,2,1,0:T(8,128)(2,1)S(1)}, bf16[2,18,16,128]{3,2,1,0:T(8,128)(2,1)S(1)}, u32[]{:S(2)}, u32[]{:S(2)}) collective-permute-start(bf16[2,18,16,128]{3,2,1,0:T(8,128)(2,1)S(1)} %get-tuple-element.158), channel_id=1, source_target_pairs={{0,16},{4,20},{8,24},{12,28},{16,0},{20,4},{24,8},{28,12},{1,17},{... | collective-permute-start | bytes 442376 | tf_op jit(solution)/shard_map/ppermute | solution.py:461
  69.3 0.5 collective-permute-start.27
  69.9 1.6 %collective-permute-start.28 = (bf16[2,18,16,128]{3,2,1,0:T(8,128)(2,1)S(1)}, bf16[2,18,16,128]{3,2,1,0:T(8,128)(2,1)S(1)}, u32[]{:S(2)}, u32[]{:S(2)}) collective-permute-start(bf16[2,18,16,128]{3,2,1,0:T(8,128)(2,1)S(1)} %get-tuple-element.160), channel_id=1, source_target_pairs={{0,16},{4,20},{8,24},{12,28},{16,0},{20,4},{24,8},{28,12},{1,17},{... | collective-permute-start | bytes 442376 | tf_op jit(solution)/shard_map/ppermute | solution.py:461
  71.5 0.5 shard_map.74
  72.0 2.2 %collective-permute-done.25.got.refs_0_ = bf16[2,18,16,128]{3,2,1,0:T(8,128)(2,1)S(1)} collective-permute-done((bf16[2,18,16,128]{3,2,1,0:T(8,128)(2,1)S(1)}, bf16[2,18,16,128]{3,2,1,0:T(8,128)(2,1)S(1)}, u32[]{:S(2)}, u32[]{:S(2)}) %collective-permute-start.25) | collective-permute-done | bytes 147488 | tf_op jit(solution)/shard_map/ppermute | solution.py:461
  74.7 1.7 %collective-permute-start.30 = (bf16[18,16,128]{2,1,0:T(8,128)(2,1)S(1)}, bf16[18,16,128]{2,1,0:T(8,128)(2,1)S(1)}, u32[]{:S(2)}, u32[]{:S(2)}) collective-permute-start(bf16[18,16,128]{2,1,0:T(8,128)(2,1)S(1)} %shard_map.77), channel_id=1, source_target_pairs={{0,8},{4,12},{8,0},{12,4},{16,24},{20,28},{24,16},{28,20},{1,9},{5... | collective-permute-start | bytes 221192 | tf_op jit(solution)/shard_map/ppermute | solution.py:461
  76.3 1.0 %collective-permute-done.27.got.refs_2_ = bf16[2,18,16,128]{3,2,1,0:T(8,128)(2,1)S(1)} collective-permute-done((bf16[2,18,16,128]{3,2,1,0:T(8,128)(2,1)S(1)}, bf16[2,18,16,128]{3,2,1,0:T(8,128)(2,1)S(1)}, u32[]{:S(2)}, u32[]{:S(2)}) %collective-permute-start.27) | collective-permute-done | bytes 147488 | tf_op jit(solution)/shard_map/ppermute | solution.py:461
  77.5 1.9 %collective-permute-start.32 = (bf16[18,16,128]{2,1,0:T(8,128)(2,1)S(1)}, bf16[18,16,128]{2,1,0:T(8,128)(2,1)S(1)}, u32[]{:S(2)}, u32[]{:S(2)}) collective-permute-start(bf16[18,16,128]{2,1,0:T(8,128)(2,1)S(1)} %shard_map.79), channel_id=1, source_target_pairs={{0,8},{4,12},{8,0},{12,4},{16,24},{20,28},{24,16},{28,20},{1,9},{5... | collective-permute-start | bytes 221192 | tf_op jit(solution)/shard_map/ppermute | solution.py:461
  79.5 2.2 %collective-permute-done.31.refs_6_ = bf16[18,16,128]{2,1,0:T(8,128)(2,1)S(1)} collective-permute-done((bf16[18,16,128]{2,1,0:T(8,128)(2,1)S(1)}, bf16[18,16,128]{2,1,0:T(8,128)(2,1)S(1)}, u32[]{:S(2)}, u32[]{:S(2)}) %collective-permute-start.31) | collective-permute-done | bytes 73760 | tf_op jit(solution)/shard_map/ppermute | solution.py:461
  81.9 1.0 %shard_map.80 = f32[16,1,72,128]{3,2,1,0:T(8,128)} custom-call(f32[1,72,16,128]{3,2,1,0:T(8,128)S(1)} %get-tuple-element.156.mine, bf16[2,18,16,128]{3,2,1,0:T(8,128)(2,1)S(1)} %collective-permute-done.25.got.refs_0_, bf16[2,18,16,128]{3,2,1,0:T(8,128)(2,1)S(1)} %collective-permute-done.26.got.refs_1_, ...), custom_call_target="tpu_custom_call" | custom-call | flops 100000000 | bytes 3000000 | tf_op jit(solution)/shard_map/pallas_call | solution.py:36
  (55 shorter events, 2.3 us)
Async XLA Ops:
  2.2 8.1 %collective-permute-start = (bf16[32,3072]{1,0:T(8,128)(2,1)S(1)}, bf16[32,3072]{1,0:T(8,128)(2,1)S(1)}, u32[]{:S(2)}, u32[]{:S(2)}) collective-permute-start(bf16[32,3072]{1,0:T(8,128)(2,1)S(1)} %get-tuple-element.89), channel_id=1, source_target_pairs={{0,1},{4,5},{8,9},{12,13},{16,17},{20,21},{24,25},{28,29}} | collective-permute-start | bytes 589832 | tf_op jit(solution)/shard_map/ppermute | solution.py:322
  5.7 11.0 %collective-permute-start.4 = (bf16[32,3072]{1,0:T(8,128)(2,1)S(1)}, bf16[32,3072]{1,0:T(8,128)(2,1)S(1)}, u32[]{:S(2)}, u32[]{:S(2)}) collective-permute-start(bf16[32,3072]{1,0:T(8,128)(2,1)S(1)} %get-tuple-element.100), channel_id=1, source_target_pairs={{0,1},{4,5},{8,9},{12,13},{16,17},{20,21},{24,25},{28,29}} | collective-permute-start | bytes 589832 | tf_op jit(solution)/shard_map/ppermute | solution.py:322
  8.4 10.3 %collective-permute-start.3 = (bf16[32,3072]{1,0:T(8,128)(2,1)S(1)}, bf16[32,3072]{1,0:T(8,128)(2,1)S(1)}, u32[]{:S(2)}, u32[]{:S(2)}) collective-permute-start(bf16[32,3072]{1,0:T(8,128)(2,1)S(1)} %get-tuple-element.99), channel_id=1, source_target_pairs={{0,1},{4,5},{8,9},{12,13},{16,17},{20,21},{24,25},{28,29}} | collective-permute-start | bytes 589832 | tf_op jit(solution)/shard_map/ppermute | solution.py:322
  10.3 9.1 %collective-permute-start.2 = (bf16[32,3072]{1,0:T(8,128)(2,1)S(1)}, bf16[32,3072]{1,0:T(8,128)(2,1)S(1)}, u32[]{:S(2)}, u32[]{:S(2)}) collective-permute-start(bf16[32,3072]{1,0:T(8,128)(2,1)S(1)} %get-tuple-element.98), channel_id=1, source_target_pairs={{1,2},{5,6},{9,10},{13,14},{17,18},{21,22},{25,26},{29,30}} | collective-permute-start | bytes 589832 | tf_op jit(solution)/shard_map/ppermute | solution.py:322
  11.7 10.1 %collective-permute-start.1 = (bf16[32,3072]{1,0:T(8,128)(2,1)S(1)}, bf16[32,3072]{1,0:T(8,128)(2,1)S(1)}, u32[]{:S(2)}, u32[]{:S(2)}) collective-permute-start(bf16[32,3072]{1,0:T(8,128)(2,1)S(1)} %get-tuple-element.97), channel_id=1, source_target_pairs={{0,1},{4,5},{8,9},{12,13},{16,17},{20,21},{24,25},{28,29}} | collective-permute-start | bytes 589832 | tf_op jit(solution)/shard_map/ppermute | solution.py:322
  16.8 5.7 %collective-permute-start.6 = (bf16[32,3072]{1,0:T(8,128)(2,1)S(1)}, bf16[32,3072]{1,0:T(8,128)(2,1)S(1)}, u32[]{:S(2)}, u32[]{:S(2)}) collective-permute-start(bf16[32,3072]{1,0:T(8,128)(2,1)S(1)} %get-tuple-element.109), channel_id=1, source_target_pairs={{1,2},{5,6},{9,10},{13,14},{17,18},{21,22},{25,26},{29,30}} | collective-permute-start | bytes 589832 | tf_op jit(solution)/shard_map/ppermute | solution.py:322
  18.7 4.6 %collective-permute-start.8 = (bf16[32,3072]{1,0:T(8,128)(2,1)S(1)}, bf16[32,3072]{1,0:T(8,128)(2,1)S(1)}, u32[]{:S(2)}, u32[]{:S(2)}) collective-permute-start(bf16[32,3072]{1,0:T(8,128)(2,1)S(1)} %get-tuple-element.113), channel_id=1, source_target_pairs={{1,2},{5,6},{9,10},{13,14},{17,18},{21,22},{25,26},{29,30}} | collective-permute-start | bytes 589832 | tf_op jit(solution)/shard_map/ppermute | solution.py:322
  19.4 3.9 %collective-permute-start.9 = (bf16[32,3072]{1,0:T(8,128)(2,1)S(1)}, bf16[32,3072]{1,0:T(8,128)(2,1)S(1)}, u32[]{:S(2)}, u32[]{:S(2)}) collective-permute-start(bf16[32,3072]{1,0:T(8,128)(2,1)S(1)} %get-tuple-element.114), channel_id=1, source_target_pairs={{2,3},{6,7},{10,11},{14,15},{18,19},{22,23},{26,27},{30,31}} | collective-permute-start | bytes 589832 | tf_op jit(solution)/shard_map/ppermute | solution.py:322
  21.8 2.5 %collective-permute-start.5 = (bf16[32,3072]{1,0:T(8,128)(2,1)S(1)}, bf16[32,3072]{1,0:T(8,128)(2,1)S(1)}, u32[]{:S(2)}, u32[]{:S(2)}) collective-permute-start(bf16[32,3072]{1,0:T(8,128)(2,1)S(1)} %get-tuple-element.108), channel_id=1, source_target_pairs={{1,2},{5,6},{9,10},{13,14},{17,18},{21,22},{25,26},{29,30}} | collective-permute-start | bytes 589832 | tf_op jit(solution)/shard_map/ppermute | solution.py:322
  22.5 1.1 %copy-start = (bf16[128,3072]{1,0:T(8,128)(2,1)S(1)}, bf16[128,3072]{1,0:T(8,128)(2,1)}, u32[]{:S(2)}) copy-start(bf16[128,3072]{1,0:T(8,128)(2,1)} %seeds.7) | copy-start | bytes 2359300
  22.5 1.8 %collective-permute-start.7 = (bf16[32,3072]{1,0:T(8,128)(2,1)S(1)}, bf16[32,3072]{1,0:T(8,128)(2,1)S(1)}, u32[]{:S(2)}, u32[]{:S(2)}) collective-permute-start(bf16[32,3072]{1,0:T(8,128)(2,1)S(1)} %get-tuple-element.112), channel_id=1, source_target_pairs={{2,3},{6,7},{10,11},{14,15},{18,19},{22,23},{26,27},{30,31}} | collective-permute-start | bytes 589832 | tf_op jit(solution)/shard_map/ppermute | solution.py:322
  23.6 1.4 %collective-permute-start.11 = (bf16[32,3072]{1,0:T(8,128)(2,1)S(1)}, bf16[32,3072]{1,0:T(8,128)(2,1)S(1)}, u32[]{:S(2)}, u32[]{:S(2)}) collective-permute-start(bf16[32,3072]{1,0:T(8,128)(2,1)S(1)} %get-tuple-element.122), channel_id=1, source_target_pairs={{2,3},{3,2},{6,7},{7,6},{10,11},{11,10},{14,15},{15,14},{18,19},{1... | collective-permute-start | bytes 589832 | tf_op jit(solution)/shard_map/ppermute | solution.py:407
  24.3 2.3 %collective-permute-start.10 = (bf16[32,3072]{1,0:T(8,128)(2,1)S(1)}, bf16[32,3072]{1,0:T(8,128)(2,1)S(1)}, u32[]{:S(2)}, u32[]{:S(2)}) collective-permute-start(bf16[32,3072]{1,0:T(8,128)(2,1)S(1)} %get-tuple-element.121), channel_id=1, source_target_pairs={{2,3},{3,2},{6,7},{7,6},{10,11},{11,10},{14,15},{15,14},{18,19},{1... | collective-permute-start | bytes 589832 | tf_op jit(solution)/shard_map/ppermute | solution.py:407
  25.2 2.8 %collective-permute-start.12 = (bf16[32,3072]{1,0:T(8,128)(2,1)S(1)}, bf16[32,3072]{1,0:T(8,128)(2,1)S(1)}, u32[]{:S(2)}, u32[]{:S(2)}) collective-permute-start(bf16[32,3072]{1,0:T(8,128)(2,1)S(1)} %get-tuple-element.132), channel_id=1, source_target_pairs={{3,2},{7,6},{11,10},{15,14},{19,18},{23,22},{27,26},{31,30}} | collective-permute-start | bytes 589832 | tf_op jit(solution)/shard_map/ppermute | solution.py:322
  25.9 2.8 %collective-permute-start.16 = (bf16[32,3072]{1,0:T(8,128)(2,1)S(1)}, bf16[32,3072]{1,0:T(8,128)(2,1)S(1)}, u32[]{:S(2)}, u32[]{:S(2)}) collective-permute-start(bf16[32,3072]{1,0:T(8,128)(2,1)S(1)} %get-tuple-element.138), channel_id=1, source_target_pairs={{2,1},{6,5},{10,9},{14,13},{18,17},{22,21},{26,25},{30,29}} | collective-permute-start | bytes 589832 | tf_op jit(solution)/shard_map/ppermute | solution.py:322
  26.7 3.4 %collective-permute-start.15 = (bf16[32,3072]{1,0:T(8,128)(2,1)S(1)}, bf16[32,3072]{1,0:T(8,128)(2,1)S(1)}, u32[]{:S(2)}, u32[]{:S(2)}) collective-permute-start(bf16[32,3072]{1,0:T(8,128)(2,1)S(1)} %get-tuple-element.137), channel_id=1, source_target_pairs={{3,2},{7,6},{11,10},{15,14},{19,18},{23,22},{27,26},{31,30}} | collective-permute-start | bytes 589832 | tf_op jit(solution)/shard_map/ppermute | solution.py:322
  27.4 3.4 %collective-permute-start.14 = (bf16[32,3072]{1,0:T(8,128)(2,1)S(1)}, bf16[32,3072]{1,0:T(8,128)(2,1)S(1)}, u32[]{:S(2)}, u32[]{:S(2)}) collective-permute-start(bf16[32,3072]{1,0:T(8,128)(2,1)S(1)} %get-tuple-element.136), channel_id=1, source_target_pairs={{2,1},{6,5},{10,9},{14,13},{18,17},{22,21},{26,25},{30,29}} | collective-permute-start | bytes 589832 | tf_op jit(solution)/shard_map/ppermute | solution.py:322
  28.1 4.1 %collective-permute-start.13 = (bf16[32,3072]{1,0:T(8,128)(2,1)S(1)}, bf16[32,3072]{1,0:T(8,128)(2,1)S(1)}, u32[]{:S(2)}, u32[]{:S(2)}) collective-permute-start(bf16[32,3072]{1,0:T(8,128)(2,1)S(1)} %get-tuple-element.135), channel_id=1, source_target_pairs={{2,1},{6,5},{10,9},{14,13},{18,17},{22,21},{26,25},{30,29}} | collective-permute-start | bytes 589832 | tf_op jit(solution)/shard_map/ppermute | solution.py:322
  28.8 25.9 %collective-permute-start.20 = (bf16[32,3072]{1,0:T(8,128)(2,1)S(1)}, bf16[32,3072]{1,0:T(8,128)(2,1)S(1)}, u32[]{:S(2)}, u32[]{:S(2)}) collective-permute-start(bf16[32,3072]{1,0:T(8,128)(2,1)S(1)} %get-tuple-element.146), channel_id=1, source_target_pairs={{1,0},{5,4},{9,8},{13,12},{17,16},{21,20},{25,24},{29,28}} | collective-permute-start | bytes 589832 | tf_op jit(solution)/shard_map/ppermute | solution.py:322
  30.1 24.6 %collective-permute-start.19 = (bf16[32,3072]{1,0:T(8,128)(2,1)S(1)}, bf16[32,3072]{1,0:T(8,128)(2,1)S(1)}, u32[]{:S(2)}, u32[]{:S(2)}) collective-permute-start(bf16[32,3072]{1,0:T(8,128)(2,1)S(1)} %get-tuple-element.145), channel_id=1, source_target_pairs={{2,1},{6,5},{10,9},{14,13},{18,17},{22,21},{26,25},{30,29}} | collective-permute-start | bytes 589832 | tf_op jit(solution)/shard_map/ppermute | solution.py:322
  30.8 28.0 %collective-permute-start.18 = (bf16[32,3072]{1,0:T(8,128)(2,1)S(1)}, bf16[32,3072]{1,0:T(8,128)(2,1)S(1)}, u32[]{:S(2)}, u32[]{:S(2)}) collective-permute-start(bf16[32,3072]{1,0:T(8,128)(2,1)S(1)} %get-tuple-element.144), channel_id=1, source_target_pairs={{1,0},{5,4},{9,8},{13,12},{17,16},{21,20},{25,24},{29,28}} | collective-permute-start | bytes 589832 | tf_op jit(solution)/shard_map/ppermute | solution.py:322
  32.2 31.0 %collective-permute-start.17 = (bf16[32,3072]{1,0:T(8,128)(2,1)S(1)}, bf16[32,3072]{1,0:T(8,128)(2,1)S(1)}, u32[]{:S(2)}, u32[]{:S(2)}) collective-permute-start(bf16[32,3072]{1,0:T(8,128)(2,1)S(1)} %get-tuple-element.143), channel_id=1, source_target_pairs={{1,0},{5,4},{9,8},{13,12},{17,16},{21,20},{25,24},{29,28}} | collective-permute-start | bytes 589832 | tf_op jit(solution)/shard_map/ppermute | solution.py:322
  54.8 10.5 %collective-permute-start.22 = (bf16[32,3072]{1,0:T(8,128)(2,1)S(1)}, bf16[32,3072]{1,0:T(8,128)(2,1)S(1)}, u32[]{:S(2)}, u32[]{:S(2)}) collective-permute-start(bf16[32,3072]{1,0:T(8,128)(2,1)S(1)} %get-tuple-element.151), channel_id=1, source_target_pairs={{1,0},{5,4},{9,8},{13,12},{17,16},{21,20},{25,24},{29,28}} | collective-permute-start | bytes 589832 | tf_op jit(solution)/shard_map/ppermute | solution.py:322
  63.9 3.0 %collective-permute-start.21 = (bf16[24,4,16,128]{3,2,1,0:T(8,128)(2,1)S(1)}, bf16[24,4,16,128]{3,2,1,0:T(8,128)(2,1)S(1)}, u32[]{:S(2)}, u32[]{:S(2)}) collective-permute-start(bf16[24,4,16,128]{3,2,1,0:T(8,128)(2,1)S(1)} %get-tuple-element.150), channel_id=1, source_target_pairs={{0,4},{4,0},{8,12},{12,8},{16,20},{20,16},{24,28},{28,24},{1,5},{5... | collective-permute-start | bytes 1179656 | tf_op jit(solution)/shard_map/ppermute | solution.py:394
  64.0 2.9 %collective-permute-start.23 = (bf16[3,32,3072]{2,1,0:T(8,128)(2,1)S(1)}, bf16[3,32,3072]{2,1,0:T(8,128)(2,1)S(1)}, u32[]{:S(2)}, u32[]{:S(2)}) collective-permute-start(bf16[3,32,3072]{2,1,0:T(8,128)(2,1)S(1)} %get-tuple-element.154), channel_id=1, source_target_pairs={{0,4},{4,0},{8,12},{12,8},{16,20},{20,16},{24,28},{28,24},{1,5},{5... | collective-permute-start | bytes 1769480 | tf_op jit(solution)/shard_map/ppermute | solution.py:395
  65.4 1.5 %collective-permute-start.24 = (bf16[32,3072]{1,0:T(8,128)(2,1)S(1)}, bf16[32,3072]{1,0:T(8,128)(2,1)S(1)}, u32[]{:S(2)}, u32[]{:S(2)}) collective-permute-start(bf16[32,3072]{1,0:T(8,128)(2,1)S(1)} %get-tuple-element.155), channel_id=1, source_target_pairs={{0,4},{4,0},{8,12},{12,8},{16,20},{20,16},{24,28},{28,24},{1,5},{5... | collective-permute-start | bytes 589832 | tf_op jit(solution)/shard_map/ppermute | solution.py:432
  67.4 6.8 %collective-permute-start.25 = (bf16[2,18,16,128]{3,2,1,0:T(8,128)(2,1)S(1)}, bf16[2,18,16,128]{3,2,1,0:T(8,128)(2,1)S(1)}, u32[]{:S(2)}, u32[]{:S(2)}) collective-permute-start(bf16[2,18,16,128]{3,2,1,0:T(8,128)(2,1)S(1)} %get-tuple-element.157), channel_id=1, source_target_pairs={{0,8},{4,12},{8,0},{12,4},{16,24},{20,28},{24,16},{28,20},{1,9},{5... | collective-permute-start | bytes 442376 | tf_op jit(solution)/shard_map/ppermute | solution.py:461
  67.8 6.8 %collective-permute-start.26 = (bf16[2,18,16,128]{3,2,1,0:T(8,128)(2,1)S(1)}, bf16[2,18,16,128]{3,2,1,0:T(8,128)(2,1)S(1)}, u32[]{:S(2)}, u32[]{:S(2)}) collective-permute-start(bf16[2,18,16,128]{3,2,1,0:T(8,128)(2,1)S(1)} %get-tuple-element.158), channel_id=1, source_target_pairs={{0,16},{4,20},{8,24},{12,28},{16,0},{20,4},{24,8},{28,12},{1,17},{... | collective-permute-start | bytes 442376 | tf_op jit(solution)/shard_map/ppermute | solution.py:461
  69.3 8.0 %collective-permute-start.27 = (bf16[2,18,16,128]{3,2,1,0:T(8,128)(2,1)S(1)}, bf16[2,18,16,128]{3,2,1,0:T(8,128)(2,1)S(1)}, u32[]{:S(2)}, u32[]{:S(2)}) collective-permute-start(bf16[2,18,16,128]{3,2,1,0:T(8,128)(2,1)S(1)} %get-tuple-element.159), channel_id=1, source_target_pairs={{0,8},{4,12},{8,0},{12,4},{16,24},{20,28},{24,16},{28,20},{1,9},{5... | collective-permute-start | bytes 442376 | tf_op jit(solution)/shard_map/ppermute | solution.py:461
  69.9 7.5 %collective-permute-start.28 = (bf16[2,18,16,128]{3,2,1,0:T(8,128)(2,1)S(1)}, bf16[2,18,16,128]{3,2,1,0:T(8,128)(2,1)S(1)}, u32[]{:S(2)}, u32[]{:S(2)}) collective-permute-start(bf16[2,18,16,128]{3,2,1,0:T(8,128)(2,1)S(1)} %get-tuple-element.160), channel_id=1, source_target_pairs={{0,16},{4,20},{8,24},{12,28},{16,0},{20,4},{24,8},{28,12},{1,17},{... | collective-permute-start | bytes 442376 | tf_op jit(solution)/shard_map/ppermute | solution.py:461
  74.2 5.2 %collective-permute-start.29 = (bf16[18,16,128]{2,1,0:T(8,128)(2,1)S(1)}, bf16[18,16,128]{2,1,0:T(8,128)(2,1)S(1)}, u32[]{:S(2)}, u32[]{:S(2)}) collective-permute-start(bf16[18,16,128]{2,1,0:T(8,128)(2,1)S(1)} %shard_map.76), channel_id=1, source_target_pairs={{0,16},{4,20},{8,24},{12,28},{16,0},{20,4},{24,8},{28,12},{1,17},{... | collective-permute-start | bytes 221192 | tf_op jit(solution)/shard_map/ppermute | solution.py:461
  74.7 4.9 %collective-permute-start.30 = (bf16[18,16,128]{2,1,0:T(8,128)(2,1)S(1)}, bf16[18,16,128]{2,1,0:T(8,128)(2,1)S(1)}, u32[]{:S(2)}, u32[]{:S(2)}) collective-permute-start(bf16[18,16,128]{2,1,0:T(8,128)(2,1)S(1)} %shard_map.77), channel_id=1, source_target_pairs={{0,8},{4,12},{8,0},{12,4},{16,24},{20,28},{24,16},{28,20},{1,9},{5... | collective-permute-start | bytes 221192 | tf_op jit(solution)/shard_map/ppermute | solution.py:461
  77.3 4.4 %collective-permute-start.31 = (bf16[18,16,128]{2,1,0:T(8,128)(2,1)S(1)}, bf16[18,16,128]{2,1,0:T(8,128)(2,1)S(1)}, u32[]{:S(2)}, u32[]{:S(2)}) collective-permute-start(bf16[18,16,128]{2,1,0:T(8,128)(2,1)S(1)} %shard_map.78), channel_id=1, source_target_pairs={{0,16},{4,20},{8,24},{12,28},{16,0},{20,4},{24,8},{28,12},{1,17},{... | collective-permute-start | bytes 221192 | tf_op jit(solution)/shard_map/ppermute | solution.py:461
  77.5 4.4 %collective-permute-start.32 = (bf16[18,16,128]{2,1,0:T(8,128)(2,1)S(1)}, bf16[18,16,128]{2,1,0:T(8,128)(2,1)S(1)}, u32[]{:S(2)}, u32[]{:S(2)}) collective-permute-start(bf16[18,16,128]{2,1,0:T(8,128)(2,1)S(1)} %shard_map.79), channel_id=1, source_target_pairs={{0,8},{4,12},{8,0},{12,4},{16,24},{20,28},{24,16},{28,20},{1,9},{5... | collective-permute-start | bytes 221192 | tf_op jit(solution)/shard_map/ppermute | solution.py:461
